TPU v7x, 32 devices: a whole 2x2x4 slice. The times are simulated.
32 devices in a mesh: groups: 2 (over x), blk: 8 (over z, core), dim: 2 (over y).
Axes of the slice: x: 2, y: 2, z: 4, core: 2. Of those that a mesh axis runs over, the one named last changes fastest.
Arguments:
- grad_codes: bfloat16 [32768, 16384], P(('groups', 'blk'), 'dim'), parts along dimension 0, may hold values from -6 to 6
- scale_exps: int32 [32768, 128], P(('groups', 'blk'), 'dim'), parts along dimension 0, may hold values from -2 to 2
- val_grads: bfloat16 [2048, 16384], P(('groups', 'blk'), 'dim'), parts along dimension 0, may hold values from -0.046875 to 0.046875
- fisher: float32 [16384], P('dim'), may hold values from 0.5 to 4
Outputs:
- scores: float32 [1024, 32768], P('dim', ('groups', 'blk')), parts along dimension 1
There are 2 independent parts, one for each index of `groups`. A program takes and returns all parts, laid end to end along the dimension named above; an argument that names none is the same for every part. Nothing has to cross between parts.
All inputs are finite; a program needn't handle non-finite values.
Results may differ from a plain program's by a relative error of at most 0.0029.
Values may be sent and summed in bfloat16 or wider, within the bound.
No kernel may reach another device: no remote copies, remote signals or barrier semaphores. Data moves between devices by JAX's collectives and lax.ppermute only.
A program may use at most 320 MiB of HBM per device.

v0:
```python
import jax
import jax.numpy as jnp
from jax import lax
from jax.sharding import PartitionSpec as P

damping = 0.05


def dequantize(grad_codes, scale_exps):
    count, width = grad_codes.shape
    factor = jnp.exp2(scale_exps.astype(jnp.float32))
    blocks = grad_codes.astype(jnp.float32).reshape(count, width // 128, 128) * factor[:, :, None]
    return blocks.reshape(count, width).astype(jnp.bfloat16)


def shards(grad_codes, scale_exps, val_grads, fisher):
    train = dequantize(grad_codes, scale_exps)
    panel = (val_grads.astype(jnp.float32) / (fisher + damping)[None, :]).astype(jnp.bfloat16)
    gathered = lax.all_gather(panel, "blk", axis=0, tiled=True)
    return lax.psum_scatter(
        lax.dot_general(
            gathered, train, (((1,), (1,)), ((), ())), preferred_element_type=jnp.float32
        ),
        "dim",
        scatter_dimension=0,
        tiled=True,
    )


def solution(mesh):
    in_specs = (
        P(("groups", "blk"), "dim"),
        P(("groups", "blk"), "dim"),
        P(("groups", "blk"), "dim"),
        P("dim"),
    )
    out_specs = P("dim", ("groups", "blk"))
    return jax.shard_map(shards, mesh=mesh, in_specs=in_specs, out_specs=out_specs, check_vma=False)
```

profile of v0, /device:TPU:0, one launch (start us, length us, event | category | flops | bytes accessed | tf_op | source)
XLA Modules:
  0.0 360.5 jit_solution(7179717188302142076)
XLA Ops:
  6.5 0.0 all-gather.2.cloned.1.call-start
  6.5 0.8 broadcast_add_fusion
  7.3 3.3 divide_convert_fusion
  10.6 0.0 all-gather.2.cloned.1.call-update
  10.7 0.0 reduce-scatter.2.cloned.1.call-start
  10.7 1.1 multiply_exponential_fusion
  11.8 0.3 copy.5
  12.2 152.5 %all-gather.2.cloned.1.call-done = bf16[1024,8192]{1,0:T(8,128)(2,1)} async-done(((bf16[128,8192]{1,0:T(8,128)(2,1)}), bf16[1024,8192]{1,0:T(8,128)(2,1)}) %all-gather.2.cloned.1.call-update) | async-done | bytes 16777232 | tf_op jit(solution)/shard_map/all_gather | solution.py:19
  164.6 21.3 %mul.11 = f32[2048,64,128]{2,1,0:T(8,128)} broadcast(f32[2048,64]{1,0:T(8,128)S(1)} %copy.5), dimensions={0,1} | broadcast | bytes 67633152 | tf_op jit(solution)/shard_map/mul | solution.py:12
  186.0 70.0 %fusion.1 = f32[1024,2048]{1,0:T(8,128)} fusion(bf16[1024,8192]{1,0:T(8,128)(2,1)} %all-gather.2.cloned.1.call-done, f32[256,8,64,128]{3,2,1,0:T(8,128)} %bitcast, bf16[2048,8192]{1,0:T(8,128)(2,1)} %param.4), kind=kOutput, calls=%fused_computation.2 | convolution fusion | flops 34410070016 | bytes 125829120 | tf_op jit(solution)/shard_map/dot_general | solution.py:21
  256.0 0.0 reduce-scatter.2.cloned.1.call-update
  256.1 97.6 %reduce-scatter.2.cloned.1.call-done = f32[512,2048]{1,0:T(8,128)} async-done(((f32[1024,2048]{1,0:T(8,128)}), f32[512,2048]{1,0:T(8,128)}) %reduce-scatter.2.cloned.1.call-update) | async-done | bytes 4194320 | tf_op jit(solution)/shard_map/reduce_scatter | solution.py:20
Async XLA Ops:
  6.5 158.1 %all-gather.2.cloned.1.call-start = ((), (), s32[]{:S(2)}) async-start(), calls=%async_computation.1 | async-start | bytes 18874368 | tf_op jit(solution)/shard_map/all_gather | solution.py:19
  10.7 343.0 %reduce-scatter.2.cloned.1.call-start = ((), (), s32[]{:S(2)}) async-start(), calls=%async_computation.2 | async-start | bytes 12582912 | tf_op jit(solution)/shard_map/reduce_scatter | solution.py:20
Sparse Core Ops, SparseCore 0:
  10.8 153.7 all-gather.1
  256.2 97.4 reduce-scatter.1
where the time goes:
time: 361 us
  waiting for transfers between devices  250 us (69%)
  matrix products  70 us (19%)
  local copies, waits for them, and re-layouts  21.7 us (6%)
  between operations  13.4 us (4%)
  other arithmetic  5.23 us (1%)
    all_gather x1, waiting for transfers between devices, shards(): gathered = lax.all_gather(panel, 'blk', axis=0, tiled=True)  152 us
    reduce_scatter x1, waiting for transfers between devices, shards(): lax.psum_scatter(lax.dot_general(gathered, train, (((1,), (1,)), ((), ())...  97.6 us
    dot_general x1, matrix products, shards(): lax.dot_general(gathered, train, (((1,), (1,)), ((), ())), preferred_elem...  70 us
    mul x1, local copies, waits for them, and re-layouts, dequantize(): grad_codes.astype(jnp.float32).reshape(count, width // 128, 128)  21.3 us
  transfers between devices with their start and end apart: 2, of which 2 were waited for; matrix products, arithmetic and copies ran while one was open for 0% of the time, Pallas kernels for 0%

commit v1 on v0

v1 whole, which is shorter than its diff:
```python
import functools

import jax
import jax.numpy as jnp
from jax import lax
from jax.experimental import pallas as pl
from jax.experimental.pallas import tpu as pltpu
from jax.sharding import PartitionSpec as P

damping = 0.05
lanes = 128
mib = 1 << 20


def dequantize_kernel(codes_ref, exps_ref, train_ref):
    exps = exps_ref[...]
    up = jnp.left_shift(1, jnp.maximum(exps, 0)).astype(jnp.float32)
    down = jnp.left_shift(1, jnp.maximum(-exps, 0)).astype(jnp.float32)
    factor = up / down
    for block in range(exps.shape[1]):
        cols = slice(block * lanes, (block + 1) * lanes)
        codes = codes_ref[:, cols].astype(jnp.float32)
        train_ref[:, cols] = (codes * factor[:, block:block + 1]).astype(jnp.bfloat16)


def dequantize(codes, exps):
    count, width = codes.shape
    rows = min(count, 256)
    return pl.pallas_call(
        dequantize_kernel,
        grid=(count // rows,),
        in_specs=[
            pl.BlockSpec((rows, width), lambda i: (i, 0)),
            pl.BlockSpec((rows, width // lanes), lambda i: (i, 0)),
        ],
        out_specs=pl.BlockSpec((rows, width), lambda i: (i, 0)),
        out_shape=jax.ShapeDtypeStruct((count, width), jnp.bfloat16),
        compiler_params=pltpu.CompilerParams(vmem_limit_bytes=40 * mib),
        cost_estimate=pl.CostEstimate(
            flops=2 * count * width, bytes_accessed=4 * count * width, transcendentals=0
        ),
        name="dequantize",
    )(codes, exps)


def partial_kernel(owners, me_ref, *refs):
    panels = refs[:owners]
    fisher_ref, train_ref, keep_ref, send_ref, left = refs[owners:]
    rows = panels[0].shape[0]

    @pl.when(pl.program_id(0) == 0)
    def _():
        scale = 1.0 / (fisher_ref[...] + damping)
        for owner in range(owners):
            vals = panels[owner][...].astype(jnp.float32)
            left[owner * rows:(owner + 1) * rows, :] = (vals * scale).astype(jnp.bfloat16)

    sums = lax.dot_general(
        left[...], train_ref[...], (((1,), (1,)), ((), ())), preferred_element_type=jnp.float32
    )
    keep_ref[...] = sums[:rows]
    send_ref[...] = sums[rows:].astype(jnp.bfloat16)


def partials(me, owners, panel, fisher, train):
    count, width = train.shape
    queries = panel.shape[0]
    rows = queries // owners
    tile = min(count, 256)

    def of_owner(step):
        return pl.BlockSpec((rows, width), lambda i, me_ref: (lax.rem(me_ref[0] + step, owners), 0))

    return pl.pallas_call(
        functools.partial(partial_kernel, owners),
        grid_spec=pltpu.PrefetchScalarGridSpec(
            num_scalar_prefetch=1,
            grid=(count // tile,),
            in_specs=[of_owner(step) for step in range(owners)] + [
                pl.BlockSpec((1, width), lambda i, me_ref: (0, 0)),
                pl.BlockSpec((tile, width), lambda i, me_ref: (i, 0)),
            ],
            out_specs=[
                pl.BlockSpec((rows, tile), lambda i, me_ref: (0, i)),
                pl.BlockSpec((queries - rows, tile), lambda i, me_ref: (0, i)),
            ],
            scratch_shapes=[pltpu.VMEM((queries, width), jnp.bfloat16)],
        ),
        out_shape=[
            jax.ShapeDtypeStruct((rows, count), jnp.float32),
            jax.ShapeDtypeStruct((queries - rows, count), jnp.bfloat16),
        ],
        compiler_params=pltpu.CompilerParams(vmem_limit_bytes=40 * mib),
        cost_estimate=pl.CostEstimate(
            flops=2 * queries * count * width, bytes_accessed=2 * count * width, transcendentals=0
        ),
        name="partials",
    )(me, *([panel] * owners), fisher, train)


def shards(blks, owners, grad_codes, scale_exps, val_grads, fisher):
    me = lax.axis_index("dim")[None]
    own, width = val_grads.shape
    count = grad_codes.shape[0]
    per_owner = blks // owners
    chunks = 4
    rows = own // chunks
    fisher = fisher[None, :]
    gathered = [
        lax.all_gather(val_grads[chunk * rows:(chunk + 1) * rows], "blk", axis=0, tiled=True)
        for chunk in range(chunks)
    ]
    train = dequantize(grad_codes, scale_exps)
    scores = jnp.zeros((per_owner, own, count), jnp.float32)
    for chunk in range(chunks):
        keep, send = partials(me, owners, gathered[chunk], fisher, train)
        total = keep
        for step in range(1, owners):
            part = send[(step - 1) * per_owner * rows:step * per_owner * rows]
            pairs = [(dev, (dev + step) % owners) for dev in range(owners)]
            total = total + lax.ppermute(part, "dim", pairs).astype(jnp.float32)
        scores = lax.dynamic_update_slice(
            scores, total.reshape(per_owner, rows, count), (0, chunk * rows, 0)
        )
    return scores.reshape(per_owner * own, count)


def solution(mesh):
    in_specs = (
        P(("groups", "blk"), "dim"),
        P(("groups", "blk"), "dim"),
        P(("groups", "blk"), "dim"),
        P("dim"),
    )
    out_specs = P("dim", ("groups", "blk"))
    body = functools.partial(shards, mesh.shape["blk"], mesh.shape["dim"])
    return jax.shard_map(body, mesh=mesh, in_specs=in_specs, out_specs=out_specs, check_vma=False)
```

time: 361 us -> 245 us (0.68)
  waiting for transfers between devices: 250 us -> 105 us
  Pallas kernels: 0 us -> 101 us
  matrix products: 70 us -> 0 us
  local copies, waits for them, and re-layouts: 21.7 us -> 14.7 us
  starting transfers between devices: 0.04 us -> 6.17 us
    pallas_call x0 -> x5, Pallas kernels: none -> 101 us  [the longest x4 70.1 us: partials(): pl.pallas_call(functools.partial(partial_kernel, owners), grid_spec=pltpu...]
    reduce_scatter x1 -> x0, waiting for transfers between devices: 97.6 us -> none  [shards(): lax.psum_scatter(lax.dot_general(gathered, train, (((1,), (1,)), ((), ())...]
    dot_general x1 -> x0, matrix products: 70 us -> none  [shards(): lax.dot_general(gathered, train, (((1,), (1,)), ((), ())), preferred_elem...]
    all_gather x1 -> x4, waiting for transfers between devices: 152 us -> 94.7 us  [shards(): lax.all_gather(val_grads[chunk * rows:(chunk + 1) * rows], 'blk', axis=0,...]
    mul x1 -> x0, local copies, waits for them, and re-layouts: 21.3 us -> none  [dequantize(): grad_codes.astype(jnp.float32).reshape(count, width // 128, 128)]
    unnamed x0 -> x15, local copies, waits for them, and re-layouts: none -> 11.1 us
    ppermute x0 -> x4, waiting for transfers between devices: none -> 8.46 us  [shards(): total = total + lax.ppermute(part, 'dim', pairs).astype(jnp.float32)]
    ppermute x0 -> x4, starting transfers between devices: none -> 6.05 us  [shards(): total = total + lax.ppermute(part, 'dim', pairs).astype(jnp.float32)]
  transfers between devices with their start and end apart: 2 -> 8, of which waited for: 2 -> 5; matrix products, arithmetic and copies ran while one was open for 0% -> 2% of each run, Pallas kernels for 0% -> 41%
where the time goes in v1:
time: 245 us; the launch traced here: 244 us
  waiting for transfers between devices  105 us (43%)
  Pallas kernels  101 us (41%)
  local copies, waits for them, and re-layouts  14.7 us (6%)
  between operations  13.3 us (5%)
  starting transfers between devices  6.17 us (3%)
  other arithmetic  3.53 us (1%)
    all_gather x4, waiting for transfers between devices, shards(): lax.all_gather(val_grads[chunk * rows:(chunk + 1) * rows], 'blk', axis=0,...  94.7 us
    pallas_call x4, Pallas kernels, partials(): pl.pallas_call(functools.partial(partial_kernel, owners), grid_spec=pltpu...  70.1 us
    pallas_call x1, Pallas kernels, dequantize(): pl.pallas_call(dequantize_kernel, grid=(count // rows,), in_specs=[pl.Blo...  30.6 us
    unnamed x15, local copies, waits for them, and re-layouts  11.1 us
    ppermute x4, waiting for transfers between devices, shards(): total = total + lax.ppermute(part, 'dim', pairs).astype(jnp.float32)  8.46 us
    ppermute x4, starting transfers between devices, shards(): total = total + lax.ppermute(part, 'dim', pairs).astype(jnp.float32)  6.05 us
  transfers between devices with their start and end apart: 8, of which 5 were waited for; matrix products, arithmetic and copies ran while one was open for 2% of the time, Pallas kernels for 41%

profile of v1, /device:TPU:0, one launch (start us, length us, event | category | flops | bytes accessed | tf_op | source)
XLA Modules:
  0.0 243.5 jit_solution(776689818779770562)
XLA Ops:
  6.5 0.0 all-gather.7.cloned.1.call-start
  6.5 2.9 %fusion = (bf16[32,8192]{1,0:T(8,128)(2,1)}, bf16[32,8192]{1,0:T(8,128)(2,1)}, bf16[32,8192]{1,0:T(8,128)(2,1)}, bf16[32,8192]{1,0:T(8,128)(2,1)}) fusion(bf16[128,8192]{1,0:T(8,128)(2,1)} %param.6), kind=kLoop, calls=%fused_computation.7 | loop fusion | bytes 4194304 | tf_op jit(solution)/shard_map/slice | solution.py:110
  9.5 0.0 all-gather.7.cloned.1.call-update
  9.5 0.0 all-gather.5.cloned.1.call-start
  9.5 0.7 all-gather.5.cloned.1.call-update
  10.2 0.0 all-gather.9.cloned.1.call-start
  10.3 0.7 all-gather.9.cloned.1.call-update
  11.0 0.0 all-gather.11.cloned.1.call-start
  11.0 0.5 all-gather.11.cloned.1.call-update
  11.5 0.0 copy-done.6
  11.6 0.3 copy.5.exps_ref
  11.9 0.0 copy-start.4
  11.9 30.6 %dequantize.1.refs_3_ = bf16[2048,8192]{1,0:T(8,128)(2,1)} custom-call(bf16[2048,8192]{1,0:T(8,128)(2,1)} %codes_ref.1, s32[2048,64]{1,0:T(8,128)S(1)} %copy.5.exps_ref), custom_call_target="tpu_custom_call" | custom-call | flops 33554432 | bytes 67108864 | tf_op jit(solution)/shard_map/dequantize/pallas_call | solution.py:29
  42.5 17.0 %all-gather.7.cloned.1.call-done.refs_0_.refs_1_ = bf16[256,8192]{1,0:T(8,128)(2,1)} async-done(((bf16[32,8192]{1,0:T(8,128)(2,1)}), bf16[256,8192]{1,0:T(8,128)(2,1)}) %all-gather.7.cloned.1.call-update) | async-done | bytes 4194320 | tf_op jit(solution)/shard_map/all_gather | solution.py:110
  59.5 0.0 copy-done.4
  59.5 0.0 copy-start.3
  59.5 2.2 copy-done.3
  61.7 17.8 %partials.5 = (f32[128,2048]{1,0:T(8,128)S(1)}, bf16[128,2048]{1,0:T(8,128)(2,1)}) custom-call(s32[1]{0:T(128)} %bitcast.me_ref, bf16[256,8192]{1,0:T(8,128)(2,1)S(1)} %copy-done.3, bf16[256,8192]{1,0:T(8,128)(2,1)S(1)} %copy-done.3, f32[1,8192]{1,0:T(1,128)S(1)} %bitcast.7, bf16[2048,8192]{1,0:T(8,128)(2,1)} %dequantize.1.refs_3_), custom_call_target="tpu_custom_call" | custom-call | flops 8589934592 | bytes 33554432 | tf_op jit(solution)/shard_map/partials/pallas_call | solution.py:74
  79.5 1.5 collective-permute-start.1
  81.0 25.9 %all-gather.5.cloned.1.call-done.refs_0_.refs_1_ = bf16[256,8192]{1,0:T(8,128)(2,1)} async-done(((bf16[32,8192]{1,0:T(8,128)(2,1)}), bf16[256,8192]{1,0:T(8,128)(2,1)}) %all-gather.5.cloned.1.call-update) | async-done | bytes 4194320 | tf_op jit(solution)/shard_map/all_gather | solution.py:110
  107.0 0.0 copy-start.2
  107.0 2.2 copy-done.2
  109.2 17.9 %partials.4 = (f32[128,2048]{1,0:T(8,128)S(1)}, bf16[128,2048]{1,0:T(8,128)(2,1)}) custom-call(s32[1]{0:T(128)} %bitcast.me_ref, bf16[256,8192]{1,0:T(8,128)(2,1)S(1)} %copy-done.2, bf16[256,8192]{1,0:T(8,128)(2,1)S(1)} %copy-done.2, f32[1,8192]{1,0:T(1,128)S(1)} %bitcast.8, bf16[2048,8192]{1,0:T(8,128)(2,1)} %dequantize.1.refs_3_), custom_call_target="tpu_custom_call" | custom-call | flops 8589934592 | bytes 33554432 | tf_op jit(solution)/shard_map/partials/pallas_call | solution.py:74
  127.0 1.5 collective-permute-start
  128.5 25.9 %all-gather.9.cloned.1.call-done.refs_0_.refs_1_ = bf16[256,8192]{1,0:T(8,128)(2,1)} async-done(((bf16[32,8192]{1,0:T(8,128)(2,1)}), bf16[256,8192]{1,0:T(8,128)(2,1)}) %all-gather.9.cloned.1.call-update) | async-done | bytes 4194320 | tf_op jit(solution)/shard_map/all_gather | solution.py:110
  154.5 0.0 copy-start.1
  154.5 2.2 copy-done.1
  156.7 17.8 %partials.6 = (f32[128,2048]{1,0:T(8,128)S(1)}, bf16[128,2048]{1,0:T(8,128)(2,1)}) custom-call(s32[1]{0:T(128)} %bitcast.me_ref, bf16[256,8192]{1,0:T(8,128)(2,1)S(1)} %copy-done.1, bf16[256,8192]{1,0:T(8,128)(2,1)S(1)} %copy-done.1, f32[1,8192]{1,0:T(1,128)S(1)} %bitcast.9, bf16[2048,8192]{1,0:T(8,128)(2,1)} %dequantize.1.refs_3_), custom_call_target="tpu_custom_call" | custom-call | flops 8589934592 | bytes 33554432 | tf_op jit(solution)/shard_map/partials/pallas_call | solution.py:74
  174.5 1.5 collective-permute-start.2
  176.0 25.9 %all-gather.11.cloned.1.call-done.refs_0_.refs_1_ = bf16[256,8192]{1,0:T(8,128)(2,1)} async-done(((bf16[32,8192]{1,0:T(8,128)(2,1)}), bf16[256,8192]{1,0:T(8,128)(2,1)}) %all-gather.11.cloned.1.call-update) | async-done | bytes 4194320 | tf_op jit(solution)/shard_map/all_gather | solution.py:110
  201.8 0.0 copy-start
  201.8 2.2 copy-done
  204.0 16.6 %partials.7 = (f32[128,2048]{1,0:T(8,128)S(1)}, bf16[128,2048]{1,0:T(8,128)(2,1)S(1)}) custom-call(s32[1]{0:T(128)} %bitcast.me_ref, bf16[256,8192]{1,0:T(8,128)(2,1)S(1)} %copy-done, bf16[256,8192]{1,0:T(8,128)(2,1)S(1)} %copy-done, f32[1,8192]{1,0:T(1,128)S(1)} %bitcast.10, bf16[2048,8192]{1,0:T(8,128)(2,1)} %dequantize.1.refs_3_), custom_call_target="tpu_custom_call" | custom-call | flops 8589934592 | bytes 33554432 | tf_op jit(solution)/shard_map/partials/pallas_call | solution.py:74
  220.6 1.5 collective-permute-start.3
  222.2 0.0 collective-permute-done.1
  222.2 1.1 convert_add_fusion.2
  223.3 0.0 collective-permute-done
  223.3 1.1 convert_add_fusion.3
  224.5 0.0 collective-permute-done.2
  224.5 1.1 convert_add_fusion.1
  225.6 0.5 dynamic_update_slice.12
  226.1 0.1 constant_dynamic-update-slice_fusion.2
  226.2 0.1 constant_dynamic-update-slice_fusion.1
  226.3 8.5 %collective-permute-done.3 = bf16[128,2048]{1,0:T(8,128)(2,1)S(1)} collective-permute-done((bf16[128,2048]{1,0:T(8,128)(2,1)S(1)}, bf16[128,2048]{1,0:T(8,128)(2,1)S(1)}, u32[]{:S(2)}, u32[]{:S(2)}) %collective-permute-start.3) | collective-permute-done | bytes 524320 | tf_op jit(solution)/shard_map/ppermute | solution.py:121
  234.8 0.1 convert_add_fusion
  234.9 0.1 constant_dynamic-update-slice_fusion
  235.0 0.0 copy-start.5
  235.0 2.0 copy-done.5
  (1 shorter events, 0.0 us)
Async XLA Ops:
  6.5 5.0 %copy-start.6 = (s32[2048,64]{0,1:T(8,128)S(1)}, s32[2048,64]{0,1:T(8,128)}, u32[]{:S(2)}) copy-start(s32[2048,64]{0,1:T(8,128)} %param.5) | copy-start | bytes 1572868
  6.5 52.9 %all-gather.7.cloned.1.call-start = ((), (), s32[]{:S(2)}) async-start(), calls=%async_computation.1 | async-start | bytes 4718592 | tf_op jit(solution)/shard_map/all_gather | solution.py:110
  9.5 97.5 %all-gather.5.cloned.1.call-start = ((), (), s32[]{:S(2)}) async-start(), calls=%async_computation | async-start | bytes 4718592 | tf_op jit(solution)/shard_map/all_gather | solution.py:110
  10.2 144.3 %all-gather.9.cloned.1.call-start = ((), (), s32[]{:S(2)}) async-start(), calls=%async_computation.2 | async-start | bytes 4718592 | tf_op jit(solution)/shard_map/all_gather | solution.py:110
  11.0 190.9 %all-gather.11.cloned.1.call-start = ((), (), s32[]{:S(2)}) async-start(), calls=%async_computation.3 | async-start | bytes 4718592 | tf_op jit(solution)/shard_map/all_gather | solution.py:110
  11.9 47.6 %copy-start.4 = (f32[8192]{0:T(1024)S(1)}, f32[8192]{0:T(1024)}, u32[]{:S(2)}) copy-start(f32[8192]{0:T(1024)} %param.7) | copy-start | bytes 98308
  59.5 2.2 copy-start.3
  79.5 142.7 %collective-permute-start.1 = (bf16[128,2048]{1,0:T(8,128)(2,1)}, bf16[128,2048]{1,0:T(8,128)(2,1)}, u32[]{:S(2)}, u32[]{:S(2)}) collective-permute-start(bf16[128,2048]{1,0:T(8,128)(2,1)} %get-tuple-element.16), channel_id=1, source_target_pairs={{0,1},{1,0},{2,3},{3,2},{4,5},{5,4},{6,7},{7,6},{8,9},{9,8},{10,11... | collective-permute-start | bytes 1572872 | tf_op jit(solution)/shard_map/ppermute | solution.py:121
  107.0 2.2 copy-start.2
  127.0 96.3 %collective-permute-start = (bf16[128,2048]{1,0:T(8,128)(2,1)}, bf16[128,2048]{1,0:T(8,128)(2,1)}, u32[]{:S(2)}, u32[]{:S(2)}) collective-permute-start(bf16[128,2048]{1,0:T(8,128)(2,1)} %get-tuple-element.14), channel_id=1, source_target_pairs={{0,1},{1,0},{2,3},{3,2},{4,5},{5,4},{6,7},{7,6},{8,9},{9,8},{10,11... | collective-permute-start | bytes 1572872 | tf_op jit(solution)/shard_map/ppermute | solution.py:121
  154.5 2.2 copy-start.1
  174.5 50.0 %collective-permute-start.2 = (bf16[128,2048]{1,0:T(8,128)(2,1)}, bf16[128,2048]{1,0:T(8,128)(2,1)}, u32[]{:S(2)}, u32[]{:S(2)}) collective-permute-start(bf16[128,2048]{1,0:T(8,128)(2,1)} %get-tuple-element.18), channel_id=1, source_target_pairs={{0,1},{1,0},{2,3},{3,2},{4,5},{5,4},{6,7},{7,6},{8,9},{9,8},{10,11... | collective-permute-start | bytes 1572872 | tf_op jit(solution)/shard_map/ppermute | solution.py:121
  201.8 2.2 copy-start
  220.6 14.1 %collective-permute-start.3 = (bf16[128,2048]{1,0:T(8,128)(2,1)S(1)}, bf16[128,2048]{1,0:T(8,128)(2,1)S(1)}, u32[]{:S(2)}, u32[]{:S(2)}) collective-permute-start(bf16[128,2048]{1,0:T(8,128)(2,1)S(1)} %get-tuple-element.20), channel_id=1, source_target_pairs={{0,1},{1,0},{2,3},{3,2},{4,5},{5,4},{6,7},{7,6},{8,9},{9,8},{10,11... | collective-permute-start | bytes 1572872 | tf_op jit(solution)/shard_map/ppermute | solution.py:121
  235.0 2.0 copy-start.5
Sparse Core Ops, SparseCore 0:
  9.6 49.8 all-gather.6
  61.1 45.8 all-gather.4
  108.6 45.8 all-gather.8
  155.9 45.8 all-gather.10

commit v2 on v1

v2 whole, which is shorter than its diff:
```python
import functools

import jax
import jax.numpy as jnp
from jax import lax
from jax.experimental import pallas as pl
from jax.experimental.pallas import tpu as pltpu
from jax.sharding import PartitionSpec as P

damping = 0.05
lanes = 128
cores = 2
mib = 1 << 20


def dequantize_kernel(codes_ref, exps_ref, train_ref):
    exps = exps_ref[...]
    up = jnp.left_shift(1, jnp.maximum(exps, 0)).astype(jnp.float32)
    down = jnp.left_shift(1, jnp.maximum(-exps, 0)).astype(jnp.float32)
    factor = up / down
    for block in range(exps.shape[1]):
        cols = slice(block * lanes, (block + 1) * lanes)
        codes = codes_ref[:, cols].astype(jnp.float32)
        train_ref[:, cols] = (codes * factor[:, block:block + 1]).astype(jnp.bfloat16)


def dequantize(codes, exps):
    count, width = codes.shape
    rows = min(count, 256)
    return pl.pallas_call(
        dequantize_kernel,
        grid=(count // rows,),
        in_specs=[
            pl.BlockSpec((rows, width), lambda i: (i, 0)),
            pl.BlockSpec((rows, width // lanes), lambda i: (i, 0)),
        ],
        out_specs=pl.BlockSpec((rows, width), lambda i: (i, 0)),
        out_shape=jax.ShapeDtypeStruct((count, width), jnp.bfloat16),
        compiler_params=pltpu.CompilerParams(vmem_limit_bytes=40 * mib),
        cost_estimate=pl.CostEstimate(
            flops=2 * count * width, bytes_accessed=4 * count * width, transcendentals=0
        ),
        name="dequantize",
    )(codes, exps)


def partial_kernel(keep_rows, spots_ref, *refs):
    panels = refs[:-6]
    fisher_ref, train_ref, keep_ref, send_ref, left, sums = refs[-6:]
    rows = panels[0].shape[0]
    step = pl.program_id(0)

    scale = 1.0 / (fisher_ref[...] + damping)
    for index, panel in enumerate(panels):
        spot = pl.ds(pl.multiple_of(spots_ref[index] * rows, rows), rows)
        left[spot, :] = (panel[...].astype(jnp.float32) * scale).astype(jnp.bfloat16)
    term = lax.dot_general(
        train_ref[...], left[...], (((1,), (1,)), ((), ())), preferred_element_type=jnp.float32
    )

    @pl.when(step == 0)
    def _():
        sums[...] = term

    @pl.when(step > 0)
    def _():
        sums[...] += term

    @pl.when(step == pl.num_programs(0) - 1)
    def _():
        turned = sums[...].T
        keep_ref[...] = turned[:keep_rows]
        send_ref[...] = turned[keep_rows:].astype(jnp.bfloat16)


def partials(spots, panels, keep_rows, rows, fisher, train):
    count, width = train.shape
    queries = rows * len(panels)
    depth = min(width, 1024)

    def spec(block):
        return pl.BlockSpec((rows, depth), lambda k, spots_ref: (block, k))

    return pl.pallas_call(
        functools.partial(partial_kernel, keep_rows),
        grid_spec=pltpu.PrefetchScalarGridSpec(
            num_scalar_prefetch=1,
            grid=(width // depth,),
            in_specs=[spec(block) for _, block in panels] + [
                pl.BlockSpec((1, depth), lambda k, spots_ref: (0, k)),
                pl.BlockSpec((count, depth), lambda k, spots_ref: (0, k)),
            ],
            out_specs=[
                pl.BlockSpec((keep_rows, count), lambda k, spots_ref: (0, 0)),
                pl.BlockSpec((queries - keep_rows, count), lambda k, spots_ref: (0, 0)),
            ],
            scratch_shapes=[
                pltpu.VMEM((queries, depth), jnp.bfloat16),
                pltpu.VMEM((count, queries), jnp.float32),
            ],
        ),
        out_shape=[
            jax.ShapeDtypeStruct((keep_rows, count), jnp.float32),
            jax.ShapeDtypeStruct((queries - keep_rows, count), jnp.bfloat16),
        ],
        compiler_params=pltpu.CompilerParams(vmem_limit_bytes=40 * mib),
        cost_estimate=pl.CostEstimate(
            flops=2 * queries * count * width, bytes_accessed=2 * count * width, transcendentals=0
        ),
        name="partials",
    )(spots, *[panel for panel, _ in panels], fisher, train)


def shards(blks, owners, grad_codes, scale_exps, val_grads, fisher):
    chips = blks // cores
    per_owner = blks // owners
    me = lax.axis_index("dim")
    blk = lax.axis_index("blk")
    chip, core = blk // cores, lax.rem(blk, cores)
    own, width = val_grads.shape
    count = grad_codes.shape[0]
    fisher = fisher[None, :]

    def shift(panel, by):
        pairs = [
            (z * cores + c, (z + by) % chips * cores + c) for z in range(chips) for c in range(cores)
        ]
        return lax.ppermute(panel, "blk", pairs)

    def swap(panel):
        return lax.ppermute(panel, "blk", [(b, b ^ 1) for b in range(blks)])

    ups = chips // 2
    pieces = 4
    rows = own // pieces
    held = {0: val_grads}
    for by in range(1, ups):
        held[by] = shift(held[by - 1], 1)
    for by in range(1, chips - ups):
        held[-by] = shift(held[1 - by], -1)
    last = [shift(held[ups - 1][piece * rows:(piece + 1) * rows], 1) for piece in range(pieces)]
    other = {by: swap(panel) for by, panel in held.items()}
    last_other = [swap(panel) for panel in last]
    train = dequantize(grad_codes, scale_exps)

    spots = []
    for by in list(held) + [ups]:
        spot = lax.rem(chip - by + 2 * chips - me * (per_owner // cores), chips)
        spots += [spot * cores + core, spot * cores + 1 - core]
    spots = jnp.stack(spots).astype(jnp.int32)

    scores = jnp.zeros((per_owner, own, count), jnp.float32)
    for piece in range(pieces):
        panels = []
        for by in held:
            panels += [(held[by], piece), (other[by], piece)]
        panels += [(last[piece], 0), (last_other[piece], 0)]
        keep, send = partials(spots, panels, per_owner * rows, rows, fisher, train)
        total = keep
        for step in range(1, owners):
            part = send[(step - 1) * per_owner * rows:step * per_owner * rows]
            pairs = [(dev, (dev + step) % owners) for dev in range(owners)]
            total = total + lax.ppermute(part, "dim", pairs).astype(jnp.float32)
        scores = lax.dynamic_update_slice(
            scores, total.reshape(per_owner, rows, count), (0, piece * rows, 0)
        )
    return scores.reshape(per_owner * own, count)


def solution(mesh):
    in_specs = (
        P(("groups", "blk"), "dim"),
        P(("groups", "blk"), "dim"),
        P(("groups", "blk"), "dim"),
        P("dim"),
    )
    out_specs = P("dim", ("groups", "blk"))
    body = functools.partial(shards, mesh.shape["blk"], mesh.shape["dim"])
    return jax.shard_map(body, mesh=mesh, in_specs=in_specs, out_specs=out_specs, check_vma=False)
```

time: 245 us -> 253 us (1.033)
  waiting for transfers between devices: 105 us -> 125 us
  between operations: 13.3 us -> 0.18 us
  starting transfers between devices: 6.17 us -> 14.3 us
  local copies, waits for them, and re-layouts: 14.7 us -> 6.63 us
  Pallas kernels: 101 us -> 105 us
  other arithmetic: 3.53 us -> 0.44 us
    ppermute x0 -> x13, waiting for transfers between devices: none -> 113 us  [the longest x6 113 us: shift(): return lax.ppermute(panel, 'blk', pairs)]
    all_gather x4 -> x0, waiting for transfers between devices: 94.7 us -> none  [shards(): lax.all_gather(val_grads[chunk * rows:(chunk + 1) * rows], 'blk', axis=0,...]
    ppermute x0 -> x13, starting transfers between devices: none -> 9.92 us  [the longest x6 8.89 us: shift(): return lax.ppermute(panel, 'blk', pairs)]
    unnamed x15 -> x11, local copies, waits for them, and re-layouts: 11.1 us -> 4.71 us
    pallas_call x4, Pallas kernels: 70.1 us -> 75 us  [partials(): pl.pallas_call(functools.partial(partial_kernel, keep_rows), grid_spec=pl...]
    ppermute x4, waiting for transfers between devices: 8.46 us -> 12.3 us  [shards(): total = total + lax.ppermute(part, 'dim', pairs).astype(jnp.float32)]
    add x4, other arithmetic: 3.53 us -> 0.44 us  [shards(): total = total + lax.ppermute(part, 'dim', pairs).astype(jnp.float32)]
  transfers between devices with their start and end apart: 8 -> 17, of which waited for: 5 -> 5; matrix products, arithmetic and copies ran while one was open for 2% -> 1% of each run, Pallas kernels for 41% -> 42%
where the time goes in v2:
time: 253 us; the launch traced here: 252 us
  waiting for transfers between devices  125 us (49%)
  Pallas kernels  105 us (42%)
  starting transfers between devices  14.3 us (6%)
  local copies, waits for them, and re-layouts  6.63 us (3%)
    ppermute x6, waiting for transfers between devices, shift(): return lax.ppermute(panel, 'blk', pairs)  113 us
    pallas_call x4, Pallas kernels, partials(): pl.pallas_call(functools.partial(partial_kernel, keep_rows), grid_spec=pl...  75 us
    pallas_call x1, Pallas kernels, dequantize(): pl.pallas_call(dequantize_kernel, grid=(count // rows,), in_specs=[pl.Blo...  30.3 us
    ppermute x4, waiting for transfers between devices, shards(): total = total + lax.ppermute(part, 'dim', pairs).astype(jnp.float32)  12.3 us
    ppermute x6, starting transfers between devices, shift(): return lax.ppermute(panel, 'blk', pairs)  8.89 us
  transfers between devices with their start and end apart: 17, of which 5 were waited for; matrix products, arithmetic and copies ran while one was open for 1% of the time, Pallas kernels for 42%

profile of v2, /device:TPU:0, one launch (start us, length us, event | category | flops | bytes accessed | tf_op | source)
XLA Modules:
  0.0 252.1 jit_solution(4047031222606469033)
XLA Ops:
  0.0 3.0 %collective-permute-start.1 = (bf16[128,8192]{1,0:T(8,128)(2,1)}, bf16[128,8192]{1,0:T(8,128)(2,1)S(1)}, u32[]{:S(2)}, u32[]{:S(2)}) collective-permute-start(bf16[128,8192]{1,0:T(8,128)(2,1)} %refs_0_.7), channel_id=1, source_target_pairs={{0,4},{2,6},{4,8},{6,10},{8,12},{10,14},{12,0},{14,2},{1,5},{3,7},... | collective-permute-start | bytes 6291464 | tf_op jit(solution)/shard_map/ppermute | solution.py:128
  3.0 2.0 collective-permute-start.3
  5.1 0.0 collective-permute-start
  5.1 46.7 %collective-permute-done.1.refs_2_ = bf16[128,8192]{1,0:T(8,128)(2,1)S(1)} collective-permute-done((bf16[128,8192]{1,0:T(8,128)(2,1)}, bf16[128,8192]{1,0:T(8,128)(2,1)S(1)}, u32[]{:S(2)}, u32[]{:S(2)}) %collective-permute-start.1) | collective-permute-done | bytes 2097184 | tf_op jit(solution)/shard_map/ppermute | solution.py:128
  51.8 0.0 collective-permute-start.2
  51.8 43.6 %collective-permute-done.3.refs_4_ = bf16[128,8192]{1,0:T(8,128)(2,1)} collective-permute-done((bf16[128,8192]{1,0:T(8,128)(2,1)}, bf16[128,8192]{1,0:T(8,128)(2,1)}, u32[]{:S(2)}, u32[]{:S(2)}) %collective-permute-start.3) | collective-permute-done | bytes 2097184 | tf_op jit(solution)/shard_map/ppermute | solution.py:128
  95.4 0.0 collective-permute-start.4
  95.4 1.1 fusion
  96.5 1.1 collective-permute-start.14
  97.7 1.1 collective-permute-start.11
  98.8 1.3 copy-done.1
  100.1 1.6 collective-permute-start.8
  101.7 11.5 %collective-permute-done.14.refs_6_ = bf16[32,8192]{1,0:T(8,128)(2,1)} collective-permute-done((bf16[32,8192]{1,0:T(8,128)(2,1)S(1)}, bf16[32,8192]{1,0:T(8,128)(2,1)}, u32[]{:S(2)}, u32[]{:S(2)}) %collective-permute-start.14) | collective-permute-done | bytes 524320 | tf_op jit(solution)/shard_map/ppermute | solution.py:128
  113.1 11.2 %collective-permute-done.11.refs_6_ = bf16[32,8192]{1,0:T(8,128)(2,1)} collective-permute-done((bf16[32,8192]{1,0:T(8,128)(2,1)S(1)}, bf16[32,8192]{1,0:T(8,128)(2,1)}, u32[]{:S(2)}, u32[]{:S(2)}) %collective-permute-start.11) | collective-permute-done | bytes 524320 | tf_op jit(solution)/shard_map/ppermute | solution.py:128
  124.4 0.0 collective-permute-start.15
  124.4 1.4 copy.5.exps_ref
  125.8 0.1 stack.35.spots_ref
  125.8 0.0 copy-start.3
  125.9 30.3 %dequantize.1.refs_9_ = bf16[2048,8192]{1,0:T(8,128)(2,1)} custom-call(bf16[2048,8192]{1,0:T(8,128)(2,1)} %codes_ref.1, s32[2048,64]{1,0:T(8,128)S(1)} %copy.5.exps_ref), custom_call_target="tpu_custom_call" | custom-call | flops 33554432 | bytes 67108864 | tf_op jit(solution)/shard_map/dequantize/pallas_call | solution.py:30
  156.1 0.0 collective-permute-done.8.refs_6_
  156.1 0.5 collective-permute-start.12
  156.6 0.1 collective-permute-start.9
  156.7 0.0 collective-permute-done.15.refs_7_
  156.7 0.4 collective-permute-start.6
  157.2 18.8 %partials.7 = (f32[128,2048]{1,0:T(8,128)S(1)}, bf16[128,2048]{1,0:T(8,128)(2,1)S(1)}) custom-call(s32[8]{0:T(128)S(1)} %stack.35.spots_ref, bf16[128,8192]{1,0:T(8,128)(2,1)S(1)} %copy-done, bf16[128,8192]{1,0:T(8,128)(2,1)S(1)} %copy-done.2, bf16[128,8192]{1,0:T(8,128)(2,1)S(1)} %collective-permute-done.1.refs_2_, ...), custom_call_target="tpu_custom_call" | custom-call | flops 8589934592 | bytes 33554432 | tf_op jit(solution)/shard_map/partials/pallas_call | solution.py:84
  176.0 1.6 collective-permute-start.16
  177.6 0.0 collective-permute-done.12.refs_7_
  177.6 18.7 %partials.6 = (f32[128,2048]{1,0:T(8,128)S(1)}, bf16[128,2048]{1,0:T(8,128)(2,1)S(1)}) custom-call(s32[8]{0:T(128)S(1)} %stack.35.spots_ref, bf16[128,8192]{1,0:T(8,128)(2,1)S(1)} %copy-done, bf16[128,8192]{1,0:T(8,128)(2,1)S(1)} %copy-done.2, bf16[128,8192]{1,0:T(8,128)(2,1)S(1)} %collective-permute-done.1.refs_2_, ...), custom_call_target="tpu_custom_call" | custom-call | flops 8589934592 | bytes 33554432 | tf_op jit(solution)/shard_map/partials/pallas_call | solution.py:84
  196.3 0.6 collective-permute-start.13
  196.9 0.0 collective-permute-done.9.refs_7_
  196.9 18.7 %partials.5 = (f32[128,2048]{1,0:T(8,128)S(1)}, bf16[128,2048]{1,0:T(8,128)(2,1)S(1)}) custom-call(s32[8]{0:T(128)S(1)} %stack.35.spots_ref, bf16[128,8192]{1,0:T(8,128)(2,1)S(1)} %copy-done, bf16[128,8192]{1,0:T(8,128)(2,1)S(1)} %copy-done.2, bf16[128,8192]{1,0:T(8,128)(2,1)S(1)} %collective-permute-done.1.refs_2_, ...), custom_call_target="tpu_custom_call" | custom-call | flops 8589934592 | bytes 33554432 | tf_op jit(solution)/shard_map/partials/pallas_call | solution.py:84
  215.7 1.6 collective-permute-start.10
  217.2 0.0 collective-permute-done.6.refs_7_
  217.2 18.7 %partials.4 = (f32[128,2048]{1,0:T(8,128)S(1)}, bf16[128,2048]{1,0:T(8,128)(2,1)S(1)}) custom-call(s32[8]{0:T(128)S(1)} %stack.35.spots_ref, bf16[128,8192]{1,0:T(8,128)(2,1)S(1)} %copy-done, bf16[128,8192]{1,0:T(8,128)(2,1)S(1)} %copy-done.2, bf16[128,8192]{1,0:T(8,128)(2,1)S(1)} %collective-permute-done.1.refs_2_, ...), custom_call_target="tpu_custom_call" | custom-call | flops 8589934592 | bytes 33554432 | tf_op jit(solution)/shard_map/partials/pallas_call | solution.py:84
  236.0 0.6 collective-permute-start.7
  236.5 0.0 collective-permute-done.13
  236.6 0.1 convert_add_fusion.1
  236.7 0.0 collective-permute-done.10
  236.7 0.1 convert_add_fusion.2
  236.8 12.3 %collective-permute-done.7 = bf16[128,2048]{1,0:T(8,128)(2,1)S(1)} collective-permute-done((bf16[128,2048]{1,0:T(8,128)(2,1)S(1)}, bf16[128,2048]{1,0:T(8,128)(2,1)S(1)}, u32[]{:S(2)}, u32[]{:S(2)}) %collective-permute-start.7) | collective-permute-done | bytes 524320 | tf_op jit(solution)/shard_map/ppermute | solution.py:163
  249.1 0.1 convert_add_fusion.3
  249.2 0.5 dynamic_update_slice.12
  249.7 0.1 constant_dynamic-update-slice_fusion.2
  249.8 0.1 constant_dynamic-update-slice_fusion.1
  249.9 0.1 convert_add_fusion
  250.0 0.1 constant_dynamic-update-slice_fusion
  250.1 0.0 copy-start.4
  250.1 2.0 copy-done.4
  (12 shorter events, 0.0 us)
Async XLA Ops:
  0.0 51.8 %collective-permute-start.1 = (bf16[128,8192]{1,0:T(8,128)(2,1)}, bf16[128,8192]{1,0:T(8,128)(2,1)S(1)}, u32[]{:S(2)}, u32[]{:S(2)}) collective-permute-start(bf16[128,8192]{1,0:T(8,128)(2,1)} %refs_0_.7), channel_id=1, source_target_pairs={{0,4},{2,6},{4,8},{6,10},{8,12},{10,14},{12,0},{14,2},{1,5},{3,7},... | collective-permute-start | bytes 6291464 | tf_op jit(solution)/shard_map/ppermute | solution.py:128
  3.0 92.3 %collective-permute-start.3 = (bf16[128,8192]{1,0:T(8,128)(2,1)}, bf16[128,8192]{1,0:T(8,128)(2,1)}, u32[]{:S(2)}, u32[]{:S(2)}) collective-permute-start(bf16[128,8192]{1,0:T(8,128)(2,1)} %refs_0_.7), channel_id=1, source_target_pairs={{0,12},{2,14},{4,0},{6,2},{8,4},{10,6},{12,8},{14,10},{1,13},{3,15... | collective-permute-start | bytes 6291464 | tf_op jit(solution)/shard_map/ppermute | solution.py:128
  5.1 93.7 %collective-permute-start = (bf16[128,8192]{1,0:T(8,128)(2,1)}, bf16[128,8192]{1,0:T(8,128)(2,1)S(1)}, u32[]{:S(2)}, u32[]{:S(2)}) collective-permute-start(bf16[128,8192]{1,0:T(8,128)(2,1)} %refs_0_.7), channel_id=1, source_target_pairs={{0,2},{2,0},{4,6},{6,4},{8,10},{10,8},{12,14},{14,12},{1,3},{3,1},... | collective-permute-start | bytes 6291464 | tf_op jit(solution)/shard_map/ppermute | solution.py:131
  51.8 105.4 %collective-permute-start.2 = (bf16[128,8192]{1,0:T(8,128)(2,1)S(1)}, bf16[128,8192]{1,0:T(8,128)(2,1)}, u32[]{:S(2)}, u32[]{:S(2)}) collective-permute-start(bf16[128,8192]{1,0:T(8,128)(2,1)S(1)} %collective-permute-done.1.refs_2_), channel_id=1, source_target_pairs={{0,2},{2,0},{4,6},{6,4},{8,10},{10,8},{12,14},{14,12},{1,3},{3,1},... | collective-permute-start | bytes 6291464 | tf_op jit(solution)/shard_map/ppermute | solution.py:131
  95.4 61.8 %collective-permute-start.4 = (bf16[128,8192]{1,0:T(8,128)(2,1)}, bf16[128,8192]{1,0:T(8,128)(2,1)}, u32[]{:S(2)}, u32[]{:S(2)}) collective-permute-start(bf16[128,8192]{1,0:T(8,128)(2,1)} %collective-permute-done.3.refs_4_), channel_id=1, source_target_pairs={{0,2},{2,0},{4,6},{6,4},{8,10},{10,8},{12,14},{14,12},{1,3},{3,1},... | collective-permute-start | bytes 6291464 | tf_op jit(solution)/shard_map/ppermute | solution.py:131
  96.5 16.6 %collective-permute-start.14 = (bf16[32,8192]{1,0:T(8,128)(2,1)S(1)}, bf16[32,8192]{1,0:T(8,128)(2,1)}, u32[]{:S(2)}, u32[]{:S(2)}) collective-permute-start(bf16[32,8192]{1,0:T(8,128)(2,1)S(1)} %get-tuple-element.21), channel_id=1, source_target_pairs={{0,4},{2,6},{4,8},{6,10},{8,12},{10,14},{12,0},{14,2},{1,5},{3,7},... | collective-permute-start | bytes 1572872 | tf_op jit(solution)/shard_map/ppermute | solution.py:128
  97.7 26.7 %collective-permute-start.11 = (bf16[32,8192]{1,0:T(8,128)(2,1)S(1)}, bf16[32,8192]{1,0:T(8,128)(2,1)}, u32[]{:S(2)}, u32[]{:S(2)}) collective-permute-start(bf16[32,8192]{1,0:T(8,128)(2,1)S(1)} %get-tuple-element.22), channel_id=1, source_target_pairs={{0,4},{2,6},{4,8},{6,10},{8,12},{10,14},{12,0},{14,2},{1,5},{3,7},... | collective-permute-start | bytes 1572872 | tf_op jit(solution)/shard_map/ppermute | solution.py:128
  98.8 1.3 copy-start.1
  100.1 56.0 %collective-permute-start.8 = (bf16[32,8192]{1,0:T(8,128)(2,1)}, bf16[32,8192]{1,0:T(8,128)(2,1)}, u32[]{:S(2)}, u32[]{:S(2)}) collective-permute-start(bf16[32,8192]{1,0:T(8,128)(2,1)} %get-tuple-element.23), channel_id=1, source_target_pairs={{0,4},{2,6},{4,8},{6,10},{8,12},{10,14},{12,0},{14,2},{1,5},{3,7},... | collective-permute-start | bytes 1572872 | tf_op jit(solution)/shard_map/ppermute | solution.py:128
  113.1 43.5 %collective-permute-start.5 = (bf16[32,8192]{1,0:T(8,128)(2,1)}, bf16[32,8192]{1,0:T(8,128)(2,1)}, u32[]{:S(2)}, u32[]{:S(2)}) collective-permute-start(bf16[32,8192]{1,0:T(8,128)(2,1)} %get-tuple-element.24), channel_id=1, source_target_pairs={{0,4},{2,6},{4,8},{6,10},{8,12},{10,14},{12,0},{14,2},{1,5},{3,7},... | collective-permute-start | bytes 1572872 | tf_op jit(solution)/shard_map/ppermute | solution.py:128
  124.4 32.3 %collective-permute-start.15 = (bf16[32,8192]{1,0:T(8,128)(2,1)}, bf16[32,8192]{1,0:T(8,128)(2,1)}, u32[]{:S(2)}, u32[]{:S(2)}) collective-permute-start(bf16[32,8192]{1,0:T(8,128)(2,1)} %collective-permute-done.14.refs_6_), channel_id=1, source_target_pairs={{0,2},{2,0},{4,6},{6,4},{8,10},{10,8},{12,14},{14,12},{1,3},{3,1},... | collective-permute-start | bytes 1572872 | tf_op jit(solution)/shard_map/ppermute | solution.py:131
  125.8 31.3 %copy-start = (bf16[128,8192]{1,0:T(8,128)(2,1)S(1)}, bf16[128,8192]{1,0:T(8,128)(2,1)}, u32[]{:S(2)}) copy-start(bf16[128,8192]{1,0:T(8,128)(2,1)} %refs_0_.7) | copy-start | bytes 6291460
  125.8 31.3 %copy-start.2 = (bf16[128,8192]{1,0:T(8,128)(2,1)S(1)}, bf16[128,8192]{1,0:T(8,128)(2,1)}, u32[]{:S(2)}) copy-start(bf16[128,8192]{1,0:T(8,128)(2,1)} %copy-done.1) | copy-start | bytes 6291460
  125.8 31.3 %copy-start.3 = (f32[8192]{0:T(1024)S(1)}, f32[8192]{0:T(1024)}, u32[]{:S(2)}) copy-start(f32[8192]{0:T(1024)} %param.7) | copy-start | bytes 98308
  156.1 21.5 %collective-permute-start.12 = (bf16[32,8192]{1,0:T(8,128)(2,1)}, bf16[32,8192]{1,0:T(8,128)(2,1)S(1)}, u32[]{:S(2)}, u32[]{:S(2)}) collective-permute-start(bf16[32,8192]{1,0:T(8,128)(2,1)} %collective-permute-done.11.refs_6_), channel_id=1, source_target_pairs={{0,2},{2,0},{4,6},{6,4},{8,10},{10,8},{12,14},{14,12},{1,3},{3,1},... | collective-permute-start | bytes 1572872 | tf_op jit(solution)/shard_map/ppermute | solution.py:131
  156.6 40.3 %collective-permute-start.9 = (bf16[32,8192]{1,0:T(8,128)(2,1)}, bf16[32,8192]{1,0:T(8,128)(2,1)S(1)}, u32[]{:S(2)}, u32[]{:S(2)}) collective-permute-start(bf16[32,8192]{1,0:T(8,128)(2,1)} %collective-permute-done.8.refs_6_), channel_id=1, source_target_pairs={{0,2},{2,0},{4,6},{6,4},{8,10},{10,8},{12,14},{14,12},{1,3},{3,1},... | collective-permute-start | bytes 1572872 | tf_op jit(solution)/shard_map/ppermute | solution.py:131
  156.7 60.5 %collective-permute-start.6 = (bf16[32,8192]{1,0:T(8,128)(2,1)}, bf16[32,8192]{1,0:T(8,128)(2,1)S(1)}, u32[]{:S(2)}, u32[]{:S(2)}) collective-permute-start(bf16[32,8192]{1,0:T(8,128)(2,1)} %collective-permute-done.5.refs_6_), channel_id=1, source_target_pairs={{0,2},{2,0},{4,6},{6,4},{8,10},{10,8},{12,14},{14,12},{1,3},{3,1},... | collective-permute-start | bytes 1572872 | tf_op jit(solution)/shard_map/ppermute | solution.py:131
  176.0 73.9 %collective-permute-start.16 = (bf16[128,2048]{1,0:T(8,128)(2,1)S(1)}, bf16[128,2048]{1,0:T(8,128)(2,1)S(1)}, u32[]{:S(2)}, u32[]{:S(2)}) collective-permute-start(bf16[128,2048]{1,0:T(8,128)(2,1)S(1)} %get-tuple-element.20), channel_id=1, source_target_pairs={{0,1},{1,0},{2,3},{3,2},{4,5},{5,4},{6,7},{7,6},{8,9},{9,8},{10,11... | collective-permute-start | bytes 1572872 | tf_op jit(solution)/shard_map/ppermute | solution.py:163
  196.3 40.2 %collective-permute-start.13 = (bf16[128,2048]{1,0:T(8,128)(2,1)S(1)}, bf16[128,2048]{1,0:T(8,128)(2,1)S(1)}, u32[]{:S(2)}, u32[]{:S(2)}) collective-permute-start(bf16[128,2048]{1,0:T(8,128)(2,1)S(1)} %get-tuple-element.18), channel_id=1, source_target_pairs={{0,1},{1,0},{2,3},{3,2},{4,5},{5,4},{6,7},{7,6},{8,9},{9,8},{10,11... | collective-permute-start | bytes 1572872 | tf_op jit(solution)/shard_map/ppermute | solution.py:163
  215.7 21.0 %collective-permute-start.10 = (bf16[128,2048]{1,0:T(8,128)(2,1)S(1)}, bf16[128,2048]{1,0:T(8,128)(2,1)S(1)}, u32[]{:S(2)}, u32[]{:S(2)}) collective-permute-start(bf16[128,2048]{1,0:T(8,128)(2,1)S(1)} %get-tuple-element.16), channel_id=1, source_target_pairs={{0,1},{1,0},{2,3},{3,2},{4,5},{5,4},{6,7},{7,6},{8,9},{9,8},{10,11... | collective-permute-start | bytes 1572872 | tf_op jit(solution)/shard_map/ppermute | solution.py:163
  236.0 13.2 %collective-permute-start.7 = (bf16[128,2048]{1,0:T(8,128)(2,1)S(1)}, bf16[128,2048]{1,0:T(8,128)(2,1)S(1)}, u32[]{:S(2)}, u32[]{:S(2)}) collective-permute-start(bf16[128,2048]{1,0:T(8,128)(2,1)S(1)} %get-tuple-element.14), channel_id=1, source_target_pairs={{0,1},{1,0},{2,3},{3,2},{4,5},{5,4},{6,7},{7,6},{8,9},{9,8},{10,11... | collective-permute-start | bytes 1572872 | tf_op jit(solution)/shard_map/ppermute | solution.py:163
  250.1 2.0 copy-start.4

commit v3 on v0

v3 whole, which is shorter than its diff:
```python
import functools

import jax
import jax.numpy as jnp
from jax import lax
from jax.experimental import pallas as pl
from jax.experimental.pallas import tpu as pltpu
from jax.sharding import PartitionSpec as P

damping = 0.05
lanes = 128
cores = 2
mib = 1 << 20


def dequantize_kernel(codes_ref, exps_ref, train_ref):
    exps = exps_ref[...]
    up = jnp.left_shift(1, jnp.maximum(exps, 0)).astype(jnp.float32)
    down = jnp.left_shift(1, jnp.maximum(-exps, 0)).astype(jnp.float32)
    factor = up / down
    for block in range(exps.shape[1]):
        cols = slice(block * lanes, (block + 1) * lanes)
        codes = codes_ref[:, cols].astype(jnp.float32)
        train_ref[:, cols] = (codes * factor[:, block:block + 1]).astype(jnp.bfloat16)


def dequantize(codes, exps):
    count, width = codes.shape
    rows = min(count, 256)
    return pl.pallas_call(
        dequantize_kernel,
        grid=(count // rows,),
        in_specs=[
            pl.BlockSpec((rows, width), lambda i: (i, 0)),
            pl.BlockSpec((rows, width // lanes), lambda i: (i, 0)),
        ],
        out_specs=pl.BlockSpec((rows, width), lambda i: (i, 0)),
        out_shape=jax.ShapeDtypeStruct((count, width), jnp.bfloat16),
        compiler_params=pltpu.CompilerParams(vmem_limit_bytes=40 * mib),
        cost_estimate=pl.CostEstimate(
            flops=2 * count * width, bytes_accessed=4 * count * width, transcendentals=0
        ),
        name="dequantize",
    )(codes, exps)


def after(array, *others):
    return lax.optimization_barrier((array, *others))[0]


def shards(blks, owners, grad_codes, scale_exps, val_grads, fisher):
    chips = blks // cores
    chips_per_owner = chips // owners
    me = lax.axis_index("dim")
    blk = lax.axis_index("blk")
    chip, core = blk // cores, lax.rem(blk, cores)
    own, width = val_grads.shape
    count = grad_codes.shape[0]
    scale = 1.0 / (fisher + damping)[None, :]

    def shift(panel, by):
        pairs = [
            (z * cores + c, (z + by) % chips * cores + c) for z in range(chips) for c in range(cores)
        ]
        return lax.ppermute(panel, "blk", pairs)

    def swap(panel):
        return lax.ppermute(panel, "blk", [(b, b ^ 1) for b in range(blks)])

    def partial(mine, theirs, train):
        both = jnp.stack([jnp.where(core == 0, mine, theirs), jnp.where(core == 0, theirs, mine)])
        both = (both.astype(jnp.float32) * scale).astype(jnp.bfloat16).reshape(-1, width)
        return lax.dot_general(
            both, train, (((1,), (1,)), ((), ())), preferred_element_type=jnp.float32
        )

    def collect(scores, part, by, start):
        total = part
        sent = part.astype(jnp.bfloat16)
        for step in range(1, owners):
            pairs = []
            for b in range(blks):
                owner = (b // cores - by) % chips // chips_per_owner
                pairs.append((b * owners + (owner + step) % owners, b * owners + owner))
            total = total + lax.ppermute(sent, ("blk", "dim"), pairs).astype(jnp.float32)
        source = lax.rem(chip - by + chips, chips)
        spot = (lax.rem(source, chips_per_owner), 0, start, 0)
        total = total.reshape(1, cores, -1, count)
        before = lax.dynamic_slice(scores, spot, total.shape)
        total = jnp.where(source // chips_per_owner == me, total, before)
        return lax.dynamic_update_slice(scores, total, spot)

    ups = chips // 2
    pieces = 4
    rows = own // pieces
    scores = jnp.zeros((chips_per_owner, cores, own, count), jnp.float32)
    held = {0: val_grads}
    for by in range(1, chips - ups):
        held[by] = shift(held[by - 1], 1)
        held[-by] = shift(held[1 - by], -1)
    if ups - 1 not in held:
        held[ups - 1] = shift(held[ups - 2], 1)
    train = dequantize(grad_codes, scale_exps)
    part = partial(val_grads, swap(val_grads), train)
    scores = collect(scores, part, 0, 0)
    for by in [by for by in held if by != 0]:
        panel = after(held[by], part)
        if by == ups - 1:
            last = [shift(panel[piece * rows:(piece + 1) * rows], 1) for piece in range(pieces)]
        part = partial(panel, swap(panel), train)
        scores = collect(scores, part, by, 0)
    for piece in range(pieces):
        panel = after(last[piece], part)
        part = partial(panel, swap(panel), train)
        scores = collect(scores, part, ups, piece * rows)
    return scores.reshape(chips_per_owner * cores * own, count)


def solution(mesh):
    in_specs = (
        P(("groups", "blk"), "dim"),
        P(("groups", "blk"), "dim"),
        P(("groups", "blk"), "dim"),
        P("dim"),
    )
    out_specs = P("dim", ("groups", "blk"))
    body = functools.partial(shards, mesh.shape["blk"], mesh.shape["dim"])
    return jax.shard_map(body, mesh=mesh, in_specs=in_specs, out_specs=out_specs, check_vma=False)
```

time: 361 us -> 258 us (0.71)
  the two profiles are of different devices: /device:TPU:0 before, /device:TPU:26 now
where the time goes in v3:
time: 258 us; the launch traced here: 257 us
  matrix products  114 us (44%)
  waiting for transfers between devices  49.8 us (19%)
  other arithmetic  34.5 us (13%)
  Pallas kernels  30.3 us (12%)
  starting transfers between devices  21.4 us (8%)
  local copies, waits for them, and re-layouts  6.83 us (3%)
    dot_general x7, matrix products, partial(): lax.dot_general(both, train, (((1,), (1,)), ((), ())), preferred_element_...  114 us
    pallas_call x1, Pallas kernels, dequantize(): pl.pallas_call(dequantize_kernel, grid=(count // rows,), in_specs=[pl.Blo...  30.3 us
    ppermute x7, waiting for transfers between devices, collect(): lax.ppermute(sent, ('blk', 'dim'), pairs).astype(jnp.float32)  26.7 us
    ppermute x6, waiting for transfers between devices, shift(): return lax.ppermute(panel, 'blk', pairs)  23.1 us
    another operation x14, other arithmetic, partial(): jnp.stack([jnp.where(core == 0, mine, theirs), jnp.where(core == 0, their...  17.6 us
    dynamic_update_slice x6, other arithmetic, collect(): return lax.dynamic_update_slice(scores, total, spot)  14.2 us
    ppermute x7, starting transfers between devices, collect(): lax.ppermute(sent, ('blk', 'dim'), pairs).astype(jnp.float32)  13.7 us
    ppermute x6, starting transfers between devices, shift(): return lax.ppermute(panel, 'blk', pairs)  6.92 us
  transfers between devices with their start and end apart: 20, of which 6 were waited for; matrix products, arithmetic and copies ran while one was open for 53% of the time, Pallas kernels for 12%

profile of v3, /device:TPU:26, one launch (start us, length us, event | category | flops | bytes accessed | tf_op | source)
XLA Modules:
  0.0 257.0 jit_solution(11792560557998670442)
XLA Ops:
  0.2 1.4 copy.5.exps_ref
  1.6 30.3 %dequantize.1 = bf16[2048,8192]{1,0:T(8,128)(2,1)} custom-call(bf16[2048,8192]{1,0:T(8,128)(2,1)} %codes_ref.1, s32[2048,64]{1,0:T(8,128)S(1)} %copy.5.exps_ref), custom_call_target="tpu_custom_call" | custom-call | flops 33554432 | bytes 67108864 | tf_op jit(solution)/shard_map/dequantize/pallas_call | solution.py:30
  31.9 1.9 select_bitcast_fusion.5
  33.8 2.4 pad_maximum_fusion
  36.2 17.3 %fusion.29 = (bf16[256,2048]{1,0:T(8,128)(2,1)}, f32[256,2048]{1,0:T(8,128)}) fusion(bf16[2048,8192]{1,0:T(8,128)(2,1)} %dequantize.1, bf16[256,8192]{1,0:T(8,128)(2,1)} %bitcast.64, f32[8192]{0:T(1024)S(1)} %add_divide_fusion), kind=kOutput, calls=%fused_computation.65 | convolution fusion | flops 8596750336 | bytes 40927232 | tf_op jit(solution)/shard_map/dot_general | solution.py:73
  53.5 0.3 collective-permute-start.3
  53.8 1.8 collective-permute-start.5
  55.6 3.5 %collective-permute-start.1 = (bf16[256,2048]{1,0:T(8,128)(2,1)}, bf16[256,2048]{1,0:T(8,128)(2,1)S(1)}, u32[]{:S(2)}, u32[]{:S(2)}) collective-permute-start(bf16[256,2048]{1,0:T(8,128)(2,1)} %get-tuple-element.35), channel_id=1, source_target_pairs={{1,0},{3,2},{5,4},{7,6},{8,9},{10,11},{12,13},{14,15},{17,16},{19,... | collective-permute-start | bytes 3145736 | tf_op jit(solution)/shard_map/ppermute | solution.py:85
  59.0 1.9 select_bitcast_fusion.3
  60.9 2.4 pad_maximum_fusion.1
  63.3 17.3 %fusion.30 = (bf16[256,2048]{1,0:T(8,128)(2,1)}, f32[256,2048]{1,0:T(8,128)}) fusion(bf16[2048,8192]{1,0:T(8,128)(2,1)} %dequantize.1, bf16[256,8192]{1,0:T(8,128)(2,1)} %bitcast.65, f32[8192]{0:T(1024)S(1)} %add_divide_fusion), kind=kOutput, calls=%fused_computation.66 | convolution fusion | flops 8596750336 | bytes 40927232 | tf_op jit(solution)/shard_map/dot_general | solution.py:73
  80.6 23.1 %collective-permute-done.5 = bf16[128,8192]{1,0:T(8,128)(2,1)} collective-permute-done((bf16[128,8192]{1,0:T(8,128)(2,1)}, bf16[128,8192]{1,0:T(8,128)(2,1)}, u32[]{:S(2)}, u32[]{:S(2)}) %collective-permute-start.5) | collective-permute-done | bytes 2097184 | tf_op jit(solution)/shard_map/ppermute | solution.py:65
  103.7 1.4 fusion.28
  105.0 1.4 collective-permute-start.11
  106.4 1.6 collective-permute-start.14
  108.0 2.0 collective-permute-start.17
  110.0 0.3 add_select_fusion
  110.3 2.5 broadcast_in_dim.2
  112.8 1.5 constant_dynamic-update-slice_fusion
  114.4 3.7 %collective-permute-start.4 = (bf16[256,2048]{1,0:T(8,128)(2,1)}, bf16[256,2048]{1,0:T(8,128)(2,1)S(1)}, u32[]{:S(2)}, u32[]{:S(2)}) collective-permute-start(bf16[256,2048]{1,0:T(8,128)(2,1)} %get-tuple-element.37), channel_id=1, source_target_pairs={{0,1},{2,3},{5,4},{7,6},{9,8},{11,10},{12,13},{14,15},{16,17},{18,... | collective-permute-start | bytes 3145736 | tf_op jit(solution)/shard_map/ppermute | solution.py:85
  118.0 1.9 select_bitcast_fusion.1
  119.9 2.4 pad_maximum_fusion.2
  122.3 17.4 %fusion.31 = (bf16[256,2048]{1,0:T(8,128)(2,1)}, f32[256,2048]{1,0:T(8,128)}) fusion(bf16[2048,8192]{1,0:T(8,128)(2,1)} %dequantize.1, bf16[256,8192]{1,0:T(8,128)(2,1)} %bitcast.66, f32[8192]{0:T(1024)S(1)} %add_divide_fusion), kind=kOutput, calls=%fused_computation.67 | convolution fusion | flops 8596750336 | bytes 40927232 | tf_op jit(solution)/shard_map/dot_general | solution.py:73
  140.1 1.9 convert_add_fusion.1
  142.0 1.3 collective-permute-start.7
  143.3 1.1 select_bitcast_fusion.13
  144.6 15.4 %fusion.32 = (bf16[64,2048]{1,0:T(8,128)(2,1)S(1)}, f32[64,2048]{1,0:T(8,128)S(1)}) fusion(bf16[2048,8192]{1,0:T(8,128)(2,1)} %dequantize.1, bf16[64,8192]{1,0:T(8,128)(2,1)S(1)} %bitcast.61, f32[8192]{0:T(1024)S(1)} %add_divide_fusion), kind=kOutput, calls=%fused_computation.68 | convolution fusion | flops 2149187584 | bytes 35422208 | tf_op jit(solution)/shard_map/dot_general | solution.py:73
  160.0 1.4 collective-permute-start.10
  161.5 3.3 %select_dynamic-update-slice_fusion.1 = f32[2,2,128,2048]{3,2,1,0:T(8,128)} fusion(f32[2,2,128,2048]{3,2,1,0:T(8,128)} %constant_dynamic-update-slice_fusion, s32[]{:T(128)S(6)} %select_n.169, f32[1,2,128,2048]{3,2,1,0:T(8,128)S(1)} %bitcast.57, pred[]{:T(512)S(6)} %eq.12), kind=kLoop, calls=%fused_computation.27 | loop fusion | flops 524288 | bytes 6291461 | tf_op jit(solution)/shard_map/dynamic_update_slice | solution.py:91
  165.0 9.9 %collective-permute-done.10 = bf16[64,2048]{1,0:T(8,128)(2,1)S(1)} collective-permute-done((bf16[64,2048]{1,0:T(8,128)(2,1)S(1)}, bf16[64,2048]{1,0:T(8,128)(2,1)S(1)}, u32[]{:S(2)}, u32[]{:S(2)}) %collective-permute-start.10) | collective-permute-done | bytes 262176 | tf_op jit(solution)/shard_map/ppermute | solution.py:85
  174.9 0.3 convert_add_fusion
  175.2 3.3 %select_dynamic-update-slice_fusion = f32[2,2,128,2048]{3,2,1,0:T(8,128)} fusion(f32[2,2,128,2048]{3,2,1,0:T(8,128)} %select_dynamic-update-slice_fusion.1, s32[]{:T(128)S(6)} %select_n.175, f32[1,2,128,2048]{3,2,1,0:T(8,128)S(1)} %bitcast.59, pred[]{:T(512)S(6)} %eq.13), kind=kLoop, calls=%fused_computation.23 | loop fusion | flops 524288 | bytes 6291461 | tf_op jit(solution)/shard_map/dynamic_update_slice | solution.py:91
  178.5 1.1 select_bitcast_fusion.11
  179.7 15.4 %fusion.33 = (bf16[64,2048]{1,0:T(8,128)(2,1)S(1)}, f32[64,2048]{1,0:T(8,128)S(1)}) fusion(bf16[2048,8192]{1,0:T(8,128)(2,1)} %dequantize.1, bf16[64,8192]{1,0:T(8,128)(2,1)S(1)} %bitcast.62, f32[8192]{0:T(1024)S(1)} %add_divide_fusion), kind=kOutput, calls=%fused_computation.69 | convolution fusion | flops 2149187584 | bytes 35422208 | tf_op jit(solution)/shard_map/dot_general | solution.py:73
  195.1 1.3 collective-permute-start.13
  196.5 1.9 select_dynamic-update-slice_fusion.5
  198.4 6.2 %collective-permute-done.13 = bf16[64,2048]{1,0:T(8,128)(2,1)S(1)} collective-permute-done((bf16[64,2048]{1,0:T(8,128)(2,1)S(1)}, bf16[64,2048]{1,0:T(8,128)(2,1)S(1)}, u32[]{:S(2)}, u32[]{:S(2)}) %collective-permute-start.13) | collective-permute-done | bytes 262176 | tf_op jit(solution)/shard_map/ppermute | solution.py:85
  204.7 1.1 select_bitcast_fusion.9
  206.0 15.4 %fusion.34 = (bf16[64,2048]{1,0:T(8,128)(2,1)S(1)}, f32[64,2048]{1,0:T(8,128)S(1)}) fusion(bf16[2048,8192]{1,0:T(8,128)(2,1)} %dequantize.1, bf16[64,8192]{1,0:T(8,128)(2,1)S(1)} %bitcast.63, f32[8192]{0:T(1024)S(1)} %add_divide_fusion), kind=kOutput, calls=%fused_computation.70 | convolution fusion | flops 2149187584 | bytes 35422208 | tf_op jit(solution)/shard_map/dot_general | solution.py:73
  221.4 1.3 collective-permute-start.16
  222.8 1.9 select_dynamic-update-slice_fusion.4
  224.7 5.3 %collective-permute-done.16 = bf16[64,2048]{1,0:T(8,128)(2,1)S(1)} collective-permute-done((bf16[64,2048]{1,0:T(8,128)(2,1)S(1)}, bf16[64,2048]{1,0:T(8,128)(2,1)S(1)}, u32[]{:S(2)}, u32[]{:S(2)}) %collective-permute-start.16) | collective-permute-done | bytes 262176 | tf_op jit(solution)/shard_map/ppermute | solution.py:85
  230.1 1.1 select_bitcast_fusion.7
  231.3 15.4 %fusion.35 = (bf16[64,2048]{1,0:T(8,128)(2,1)S(1)}, f32[64,2048]{1,0:T(8,128)S(1)}) fusion(bf16[2048,8192]{1,0:T(8,128)(2,1)} %dequantize.1, bf16[64,8192]{1,0:T(8,128)(2,1)S(1)} %bitcast.60, f32[8192]{0:T(1024)S(1)} %add_divide_fusion), kind=kOutput, calls=%fused_computation.71 | convolution fusion | flops 2149187584 | bytes 35422208 | tf_op jit(solution)/shard_map/dot_general | solution.py:73
  246.8 1.3 collective-permute-start.19
  248.1 1.9 select_dynamic-update-slice_fusion.3
  250.0 5.0 %collective-permute-done.19 = bf16[64,2048]{1,0:T(8,128)(2,1)S(1)} collective-permute-done((bf16[64,2048]{1,0:T(8,128)(2,1)S(1)}, bf16[64,2048]{1,0:T(8,128)(2,1)S(1)}, u32[]{:S(2)}, u32[]{:S(2)}) %collective-permute-start.19) | collective-permute-done | bytes 262176 | tf_op jit(solution)/shard_map/ppermute | solution.py:85
  255.1 1.9 select_dynamic-update-slice_fusion.2
  (42 shorter events, 1.6 us)
Async XLA Ops:
  0.0 31.9 %collective-permute-start = (bf16[128,8192]{1,0:T(8,128)(2,1)}, bf16[128,8192]{1,0:T(8,128)(2,1)}, u32[]{:S(2)}, u32[]{:S(2)}) collective-permute-start(bf16[128,8192]{1,0:T(8,128)(2,1)} %param.6), channel_id=1, source_target_pairs={{0,2},{2,0},{4,6},{6,4},{8,10},{10,8},{12,14},{14,12},{1,3},{3,1},... | collective-permute-start | bytes 6291464 | tf_op jit(solution)/shard_map/ppermute | solution.py:68
  0.0 53.5 %collective-permute-start.2 = (bf16[128,8192]{1,0:T(8,128)(2,1)}, bf16[128,8192]{1,0:T(8,128)(2,1)S(1)}, u32[]{:S(2)}, u32[]{:S(2)}) collective-permute-start(bf16[128,8192]{1,0:T(8,128)(2,1)} %param.6), channel_id=1, source_target_pairs={{0,4},{2,6},{4,8},{6,10},{8,12},{10,14},{12,0},{14,2},{1,5},{3,7},... | collective-permute-start | bytes 6291464 | tf_op jit(solution)/shard_map/ppermute | solution.py:65
  1.6 30.3 %copy-start.3 = (f32[8192]{0:T(1024)S(1)}, f32[8192]{0:T(1024)}, u32[]{:S(2)}) copy-start(f32[8192]{0:T(1024)} %param.7) | copy-start | bytes 98308
  1.6 30.3 %copy-start.2 = (bf16[128,8192]{1,0:T(8,128)(2,1)S(1)}, bf16[128,8192]{1,0:T(8,128)(2,1)}, u32[]{:S(2)}) copy-start(bf16[128,8192]{1,0:T(8,128)(2,1)} %param.6) | copy-start | bytes 6291460
  53.5 5.5 %collective-permute-start.3 = (bf16[128,8192]{1,0:T(8,128)(2,1)S(1)}, bf16[128,8192]{1,0:T(8,128)(2,1)}, u32[]{:S(2)}, u32[]{:S(2)}) collective-permute-start(bf16[128,8192]{1,0:T(8,128)(2,1)S(1)} %collective-permute-done.2), channel_id=1, source_target_pairs={{0,2},{2,0},{4,6},{6,4},{8,10},{10,8},{12,14},{14,12},{1,3},{3,1},... | collective-permute-start | bytes 6291464 | tf_op jit(solution)/shard_map/ppermute | solution.py:68
  53.8 49.9 %collective-permute-start.5 = (bf16[128,8192]{1,0:T(8,128)(2,1)}, bf16[128,8192]{1,0:T(8,128)(2,1)}, u32[]{:S(2)}, u32[]{:S(2)}) collective-permute-start(bf16[128,8192]{1,0:T(8,128)(2,1)} %param.6), channel_id=1, source_target_pairs={{0,12},{2,14},{4,0},{6,2},{8,4},{10,6},{12,8},{14,10},{1,13},{3,15... | collective-permute-start | bytes 6291464 | tf_op jit(solution)/shard_map/ppermute | solution.py:65
  55.6 52.4 %collective-permute-start.1 = (bf16[256,2048]{1,0:T(8,128)(2,1)}, bf16[256,2048]{1,0:T(8,128)(2,1)S(1)}, u32[]{:S(2)}, u32[]{:S(2)}) collective-permute-start(bf16[256,2048]{1,0:T(8,128)(2,1)} %get-tuple-element.35), channel_id=1, source_target_pairs={{1,0},{3,2},{5,4},{7,6},{8,9},{10,11},{12,13},{14,15},{17,16},{19,... | collective-permute-start | bytes 3145736 | tf_op jit(solution)/shard_map/ppermute | solution.py:85
  80.6 29.4 %copy-start = (f32[256,2048]{1,0:T(8,128)S(1)}, f32[256,2048]{1,0:T(8,128)}, u32[]{:S(2)}) copy-start(f32[256,2048]{1,0:T(8,128)} %get-tuple-element.36) | copy-start | bytes 6291460
  103.7 10.7 %collective-permute-start.6 = (bf16[128,8192]{1,0:T(8,128)(2,1)}, bf16[128,8192]{1,0:T(8,128)(2,1)S(1)}, u32[]{:S(2)}, u32[]{:S(2)}) collective-permute-start(bf16[128,8192]{1,0:T(8,128)(2,1)} %collective-permute-done.5), channel_id=1, source_target_pairs={{0,2},{2,0},{4,6},{6,4},{8,10},{10,8},{12,14},{14,12},{1,3},{3,1},... | collective-permute-start | bytes 6291464 | tf_op jit(solution)/shard_map/ppermute | solution.py:68
  105.0 34.7 %collective-permute-start.8 = (bf16[32,8192]{1,0:T(8,128)(2,1)}, bf16[32,8192]{1,0:T(8,128)(2,1)}, u32[]{:S(2)}, u32[]{:S(2)}) collective-permute-start(bf16[32,8192]{1,0:T(8,128)(2,1)} %get-tuple-element.26), channel_id=1, source_target_pairs={{0,4},{2,6},{4,8},{6,10},{8,12},{10,14},{12,0},{14,2},{1,5},{3,7},... | collective-permute-start | bytes 1572872 | tf_op jit(solution)/shard_map/ppermute | solution.py:65
  105.0 59.7 %collective-permute-start.11 = (bf16[32,8192]{1,0:T(8,128)(2,1)}, bf16[32,8192]{1,0:T(8,128)(2,1)}, u32[]{:S(2)}, u32[]{:S(2)}) collective-permute-start(bf16[32,8192]{1,0:T(8,128)(2,1)} %get-tuple-element.25), channel_id=1, source_target_pairs={{0,4},{2,6},{4,8},{6,10},{8,12},{10,14},{12,0},{14,2},{1,5},{3,7},... | collective-permute-start | bytes 1572872 | tf_op jit(solution)/shard_map/ppermute | solution.py:65
  106.4 90.0 %collective-permute-start.14 = (bf16[32,8192]{1,0:T(8,128)(2,1)}, bf16[32,8192]{1,0:T(8,128)(2,1)}, u32[]{:S(2)}, u32[]{:S(2)}) collective-permute-start(bf16[32,8192]{1,0:T(8,128)(2,1)} %get-tuple-element.24), channel_id=1, source_target_pairs={{0,4},{2,6},{4,8},{6,10},{8,12},{10,14},{12,0},{14,2},{1,5},{3,7},... | collective-permute-start | bytes 1572872 | tf_op jit(solution)/shard_map/ppermute | solution.py:65
  108.0 114.7 %collective-permute-start.17 = (bf16[32,8192]{1,0:T(8,128)(2,1)}, bf16[32,8192]{1,0:T(8,128)(2,1)}, u32[]{:S(2)}, u32[]{:S(2)}) collective-permute-start(bf16[32,8192]{1,0:T(8,128)(2,1)} %get-tuple-element.23), channel_id=1, source_target_pairs={{0,4},{2,6},{4,8},{6,10},{8,12},{10,14},{12,0},{14,2},{1,5},{3,7},... | collective-permute-start | bytes 1572872 | tf_op jit(solution)/shard_map/ppermute | solution.py:65
  114.4 25.7 %collective-permute-start.4 = (bf16[256,2048]{1,0:T(8,128)(2,1)}, bf16[256,2048]{1,0:T(8,128)(2,1)S(1)}, u32[]{:S(2)}, u32[]{:S(2)}) collective-permute-start(bf16[256,2048]{1,0:T(8,128)(2,1)} %get-tuple-element.37), channel_id=1, source_target_pairs={{0,1},{2,3},{5,4},{7,6},{9,8},{11,10},{12,13},{14,15},{16,17},{18,... | collective-permute-start | bytes 3145736 | tf_op jit(solution)/shard_map/ppermute | solution.py:85
  139.7 2.3 copy-start.4
  139.7 3.6 %collective-permute-start.9 = (bf16[32,8192]{1,0:T(8,128)(2,1)}, bf16[32,8192]{1,0:T(8,128)(2,1)S(1)}, u32[]{:S(2)}, u32[]{:S(2)}) collective-permute-start(bf16[32,8192]{1,0:T(8,128)(2,1)} %collective-permute-done.8), channel_id=1, source_target_pairs={{0,2},{2,0},{4,6},{6,4},{8,10},{10,8},{12,14},{14,12},{1,3},{3,1},... | collective-permute-start | bytes 1572872 | tf_op jit(solution)/shard_map/ppermute | solution.py:68
  142.0 32.9 %collective-permute-start.7 = (bf16[256,2048]{1,0:T(8,128)(2,1)S(1)}, bf16[256,2048]{1,0:T(8,128)(2,1)S(1)}, u32[]{:S(2)}, u32[]{:S(2)}) collective-permute-start(bf16[256,2048]{1,0:T(8,128)(2,1)S(1)} %copy-done.4), channel_id=1, source_target_pairs={{1,0},{3,2},{4,5},{6,7},{8,9},{10,11},{13,12},{15,14},{17,16},{19,... | collective-permute-start | bytes 3145736 | tf_op jit(solution)/shard_map/ppermute | solution.py:85
  160.0 14.9 %copy-start.1 = (f32[256,2048]{1,0:T(8,128)S(1)}, f32[256,2048]{1,0:T(8,128)}, u32[]{:S(2)}) copy-start(f32[256,2048]{1,0:T(8,128)} %get-tuple-element.40) | copy-start | bytes 6291460
  160.0 14.8 %collective-permute-start.10 = (bf16[64,2048]{1,0:T(8,128)(2,1)S(1)}, bf16[64,2048]{1,0:T(8,128)(2,1)S(1)}, u32[]{:S(2)}, u32[]{:S(2)}) collective-permute-start(bf16[64,2048]{1,0:T(8,128)(2,1)S(1)} %get-tuple-element.41), channel_id=1, source_target_pairs={{0,1},{2,3},{4,5},{6,7},{9,8},{11,10},{13,12},{15,14},{16,17},{18,... | collective-permute-start | bytes 786440 | tf_op jit(solution)/shard_map/ppermute | solution.py:85
  164.7 13.7 %collective-permute-start.12 = (bf16[32,8192]{1,0:T(8,128)(2,1)}, bf16[32,8192]{1,0:T(8,128)(2,1)S(1)}, u32[]{:S(2)}, u32[]{:S(2)}) collective-permute-start(bf16[32,8192]{1,0:T(8,128)(2,1)} %collective-permute-done.11), channel_id=1, source_target_pairs={{0,2},{2,0},{4,6},{6,4},{8,10},{10,8},{12,14},{14,12},{1,3},{3,1},... | collective-permute-start | bytes 1572872 | tf_op jit(solution)/shard_map/ppermute | solution.py:68
  195.1 9.5 %collective-permute-start.13 = (bf16[64,2048]{1,0:T(8,128)(2,1)S(1)}, bf16[64,2048]{1,0:T(8,128)(2,1)S(1)}, u32[]{:S(2)}, u32[]{:S(2)}) collective-permute-start(bf16[64,2048]{1,0:T(8,128)(2,1)S(1)} %get-tuple-element.43), channel_id=1, source_target_pairs={{0,1},{2,3},{4,5},{6,7},{9,8},{11,10},{13,12},{15,14},{16,17},{18,... | collective-permute-start | bytes 786440 | tf_op jit(solution)/shard_map/ppermute | solution.py:85
  196.4 8.3 %collective-permute-start.15 = (bf16[32,8192]{1,0:T(8,128)(2,1)}, bf16[32,8192]{1,0:T(8,128)(2,1)S(1)}, u32[]{:S(2)}, u32[]{:S(2)}) collective-permute-start(bf16[32,8192]{1,0:T(8,128)(2,1)} %collective-permute-done.14), channel_id=1, source_target_pairs={{0,2},{2,0},{4,6},{6,4},{8,10},{10,8},{12,14},{14,12},{1,3},{3,1},... | collective-permute-start | bytes 1572872 | tf_op jit(solution)/shard_map/ppermute | solution.py:68
  221.4 8.6 %collective-permute-start.16 = (bf16[64,2048]{1,0:T(8,128)(2,1)S(1)}, bf16[64,2048]{1,0:T(8,128)(2,1)S(1)}, u32[]{:S(2)}, u32[]{:S(2)}) collective-permute-start(bf16[64,2048]{1,0:T(8,128)(2,1)S(1)} %get-tuple-element.45), channel_id=1, source_target_pairs={{0,1},{2,3},{4,5},{6,7},{9,8},{11,10},{13,12},{15,14},{16,17},{18,... | collective-permute-start | bytes 786440 | tf_op jit(solution)/shard_map/ppermute | solution.py:85
  222.7 7.4 %collective-permute-start.18 = (bf16[32,8192]{1,0:T(8,128)(2,1)}, bf16[32,8192]{1,0:T(8,128)(2,1)S(1)}, u32[]{:S(2)}, u32[]{:S(2)}) collective-permute-start(bf16[32,8192]{1,0:T(8,128)(2,1)} %collective-permute-done.17), channel_id=1, source_target_pairs={{0,2},{2,0},{4,6},{6,4},{8,10},{10,8},{12,14},{14,12},{1,3},{3,1},... | collective-permute-start | bytes 1572872 | tf_op jit(solution)/shard_map/ppermute | solution.py:68
  246.8 8.3 %collective-permute-start.19 = (bf16[64,2048]{1,0:T(8,128)(2,1)S(1)}, bf16[64,2048]{1,0:T(8,128)(2,1)S(1)}, u32[]{:S(2)}, u32[]{:S(2)}) collective-permute-start(bf16[64,2048]{1,0:T(8,128)(2,1)S(1)} %get-tuple-element.47), channel_id=1, source_target_pairs={{0,1},{2,3},{4,5},{6,7},{9,8},{11,10},{13,12},{15,14},{16,17},{18,... | collective-permute-start | bytes 786440 | tf_op jit(solution)/shard_map/ppermute | solution.py:85

commit v4 on v3

v4 whole, which is shorter than its diff:
```python
import functools

import jax
import jax.numpy as jnp
from jax import lax
from jax.experimental import pallas as pl
from jax.experimental.pallas import tpu as pltpu
from jax.sharding import PartitionSpec as P

damping = 0.05
lanes = 128
cores = 2
mib = 1 << 20
in_vmem = pl.BlockSpec(memory_space=pltpu.VMEM)
in_smem = pl.BlockSpec(memory_space=pltpu.SMEM)
anywhere = pl.BlockSpec(memory_space=pl.ANY)
small = pl.CostEstimate(flops=1, bytes_accessed=1, transcendentals=0)


def dequantize_kernel(codes_ref, exps_ref, train_ref):
    exps = exps_ref[...]
    up = jnp.left_shift(1, jnp.maximum(exps, 0)).astype(jnp.float32)
    down = jnp.left_shift(1, jnp.maximum(-exps, 0)).astype(jnp.float32)
    factor = up / down
    for block in range(exps.shape[1]):
        cols = slice(block * lanes, (block + 1) * lanes)
        codes = codes_ref[:, cols].astype(jnp.float32)
        train_ref[:, cols] = (codes * factor[:, block:block + 1]).astype(jnp.bfloat16)


def dequantize(codes, exps):
    count, width = codes.shape
    rows = min(count, 256)
    return pl.pallas_call(
        dequantize_kernel,
        grid=(count // rows,),
        in_specs=[
            pl.BlockSpec((rows, width), lambda i: (i, 0)),
            pl.BlockSpec((rows, width // lanes), lambda i: (i, 0)),
        ],
        out_specs=pl.BlockSpec((rows, width), lambda i: (i, 0)),
        out_shape=jax.ShapeDtypeStruct((count, width), jnp.bfloat16),
        compiler_params=pltpu.CompilerParams(vmem_limit_bytes=32 * mib),
        cost_estimate=small,
        name="dequantize",
    )(codes, exps)


def multiply_kernel(core_ref, *refs):
    mine_ref, *parts = refs[:-12]
    fisher_ref, train_ref, keep_ref, send_ref = refs[-12:-8]
    left, keep, send, held, in_sems, keep_sems, send_sems, train_sems = refs[-8:]
    rows, width = mine_ref.shape
    count = train_ref.shape[0]
    slots, tile, _ = held.shape
    tiles = count // tile
    half = tile // 2
    depth = min(width, 1024)
    core = core_ref[0]

    def fetches(i):
        slot = lax.rem(i, slots)
        return [
            pltpu.make_async_copy(
                train_ref.at[pl.ds(pl.multiple_of(i * tile, tile) + part * half, half)],
                held.at[slot, pl.ds(part * half, half)],
                train_sems.at[slot, part],
            )
            for part in range(2)
        ]

    mine_spot = pl.ds(pl.multiple_of(core * rows, rows), rows)
    loads = [pltpu.make_async_copy(mine_ref, left.at[mine_spot], in_sems.at[0])]
    offset = 0
    for index, ref in enumerate(parts):
        spot = pl.ds(pl.multiple_of((1 - core) * rows, rows) + offset, ref.shape[0])
        loads.append(pltpu.make_async_copy(ref, left.at[spot], in_sems.at[index + 1]))
        offset += ref.shape[0]
    for load in loads:
        load.start()
    for i in range(min(slots, tiles)):
        for fetch in fetches(i):
            fetch.start()
    for load in loads:
        load.wait()

    @pl.loop(0, width // depth)
    def _(k):
        cols = pl.ds(pl.multiple_of(k * depth, depth), depth)
        scale = 1.0 / (fisher_ref[:, cols] + damping)
        left[:, cols] = (left[:, cols].astype(jnp.float32) * scale).astype(jnp.bfloat16)

    def stores(i):
        cols = pl.ds(pl.multiple_of(i * tile, tile), tile)
        return (
            pltpu.make_async_copy(keep.at[:, cols], keep_ref.at[:, cols], keep_sems.at[i]),
            pltpu.make_async_copy(send.at[:, cols], send_ref.at[:, cols], send_sems.at[i]),
        )

    @pl.loop(0, tiles)
    def _(i):
        cols = pl.ds(pl.multiple_of(i * tile, tile), tile)
        for fetch in fetches(i):
            fetch.wait()
        sums = lax.dot_general(
            left[...], held[lax.rem(i, slots)], (((1,), (1,)), ((), ())),
            preferred_element_type=jnp.float32,
        )
        keep[:, cols] = sums
        send[:, cols] = sums.astype(jnp.bfloat16)
        for store in stores(i):
            store.start()

        @pl.when(i + slots < tiles)
        def _():
            for fetch in fetches(i + slots):
                fetch.start()

    @pl.loop(0, tiles)
    def _(i):
        for store in stores(i):
            store.wait()


def multiply(core, mine, parts, fisher, train):
    rows, width = mine.shape
    count = train.shape[0]
    tile = min(count, 256)
    shape = (cores * rows, count)
    return pl.pallas_call(
        multiply_kernel,
        in_specs=[in_smem] + [anywhere] * (1 + len(parts)) + [in_vmem, anywhere],
        out_specs=[anywhere] * 2,
        out_shape=[
            jax.ShapeDtypeStruct(shape, jnp.float32), jax.ShapeDtypeStruct(shape, jnp.bfloat16),
        ],
        scratch_shapes=[
            pltpu.VMEM((cores * rows, width), jnp.bfloat16),
            pltpu.VMEM(shape, jnp.float32),
            pltpu.VMEM(shape, jnp.bfloat16),
            pltpu.VMEM((4, tile, width), jnp.bfloat16),
            pltpu.SemaphoreType.DMA((1 + len(parts),)),
            pltpu.SemaphoreType.DMA((count // tile,)),
            pltpu.SemaphoreType.DMA((count // tile,)),
            pltpu.SemaphoreType.DMA((4, 2)),
        ],
        compiler_params=pltpu.CompilerParams(vmem_limit_bytes=32 * mib),
        cost_estimate=small,
        name="multiply",
    )(core, mine, *parts, fisher, train)


def place_kernel(start, parts, mine_ref, spot_ref, *refs):
    keep_ref, received = refs[0], refs[1:1 + parts]
    scores_ref, total, terms, in_sems, out_sems = refs[-5:]
    rows = keep_ref.shape[0] // cores

    @pl.when(mine_ref[0] == 1)
    def _():
        loads = [pltpu.make_async_copy(keep_ref, total, in_sems.at[0])]
        for index, ref in enumerate(received):
            loads.append(pltpu.make_async_copy(ref, terms.at[index], in_sems.at[index + 1]))
        for load in loads:
            load.start()
        for load in loads:
            load.wait()
        for index in range(parts):
            total[...] += terms[index].astype(jnp.float32)
        copies = [
            pltpu.make_async_copy(
                total.at[pl.ds(c * rows, rows)],
                scores_ref.at[spot_ref[0], c, pl.ds(start, rows)],
                out_sems.at[c],
            )
            for c in range(cores)
        ]
        for copy in copies:
            copy.start()
        for copy in copies:
            copy.wait()


def place(scores, shape, mine, spot, keep, received, start):
    given = [] if scores is None else [scores]
    parts = len(received)
    return pl.pallas_call(
        functools.partial(place_kernel, start, parts),
        in_specs=[in_smem] * 2 + [anywhere] * (1 + parts + len(given)),
        out_specs=anywhere,
        out_shape=jax.ShapeDtypeStruct(shape, jnp.float32),
        scratch_shapes=[
            pltpu.VMEM(keep.shape, jnp.float32),
            pltpu.VMEM((parts, *keep.shape), jnp.bfloat16),
            pltpu.SemaphoreType.DMA((1 + parts,)),
            pltpu.SemaphoreType.DMA((cores,)),
        ],
        input_output_aliases={3 + parts: 0} if given else {},
        compiler_params=pltpu.CompilerParams(vmem_limit_bytes=12 * mib),
        cost_estimate=small,
        name="place",
    )(mine, spot, keep, *received, *given)


def cut_kernel(lows, whole_ref, *refs):
    sems = refs[-1]
    copies = [
        pltpu.make_async_copy(whole_ref.at[pl.ds(low, ref.shape[0])], ref, sems.at[index])
        for index, (low, ref) in enumerate(zip(lows, refs[:-1]))
    ]
    for copy in copies:
        copy.start()
    for copy in copies:
        copy.wait()


def cut(whole, cuts):
    return pl.pallas_call(
        functools.partial(cut_kernel, [low for low, _ in cuts]),
        in_specs=[anywhere],
        out_specs=[anywhere] * len(cuts),
        out_shape=[
            jax.ShapeDtypeStruct((high - low, whole.shape[1]), whole.dtype) for low, high in cuts
        ],
        scratch_shapes=[pltpu.SemaphoreType.DMA((len(cuts),))],
        compiler_params=pltpu.CompilerParams(vmem_limit_bytes=2 * mib),
        cost_estimate=small,
        name="cut",
    )(whole)


def after(array, *others):
    return lax.optimization_barrier((array, *others))[0]


def shards(blks, owners, grad_codes, scale_exps, val_grads, fisher):
    chips = blks // cores
    chips_per_owner = chips // owners
    me = lax.axis_index("dim")
    blk = lax.axis_index("blk")
    chip, core = blk // cores, lax.rem(blk, cores)[None]
    own = val_grads.shape[0]
    count = grad_codes.shape[0]
    fisher = fisher[None, :]
    shape = (chips_per_owner, cores, own, count)

    def shift(panel, by):
        pairs = [
            (z * cores + c, (z + by) % chips * cores + c) for z in range(chips) for c in range(cores)
        ]
        return lax.ppermute(panel, "blk", pairs)

    def swap(parts):
        pairs = [(b, b ^ 1) for b in range(blks)]
        return [lax.ppermute(part, "blk", pairs) for part in parts]

    def collect(scores, part, by, start):
        keep, send = part
        received = []
        for step in range(1, owners):
            pairs = []
            for b in range(blks):
                owner = (b // cores - by) % chips // chips_per_owner
                pairs.append((b * owners + (owner + step) % owners, b * owners + owner))
            received.append(lax.ppermute(send, ("blk", "dim"), pairs))
        source = lax.rem(chip - by + chips, chips)
        mine = (source // chips_per_owner == me).astype(jnp.int32)[None]
        return place(scores, shape, mine, lax.rem(source, chips_per_owner)[None], keep, received, start)

    ups = chips // 2
    cuts = [0, own * 3 // 4, own]
    held = {0: val_grads}
    for by in range(1, chips - ups):
        held[by] = shift(held[by - 1], 1)
        held[-by] = shift(held[1 - by], -1)
    if ups - 1 not in held:
        held[ups - 1] = shift(held[ups - 2], 1)
    train = dequantize(grad_codes, scale_exps)
    part = multiply(core, val_grads, swap([val_grads]), fisher, train)
    pending = [(part, 0, 0)]
    scores = None
    order = [by for by in held if by != 0] + [ups] * (len(cuts) - 1)
    lows = [0] * (len(held) - 1) + cuts[:-1]
    halves = [(0, own // 2), (own // 2, own)]
    for by, lo in zip(order, lows):
        panel = held[by] if by != ups else last[cuts.index(lo)]
        panel = after(panel, part) if scores is None else after(panel, part, scores)
        if by == ups - 1:
            *parts, low_part, high_part = cut(panel, halves + list(zip(cuts, cuts[1:])))
            last = [shift(low_part, 1), shift(high_part, 1)]
        elif by == ups and lo > 0:
            parts = [panel]
        else:
            half = max(panel.shape[0] // 32 * 16, 16)
            parts = cut(panel, [(0, half), (half, panel.shape[0])])
        part = multiply(core, panel, swap(parts), fisher, train)
        scores = collect(scores, *pending.pop())
        pending.append((part, by, lo))
    scores = collect(scores, *pending.pop())
    return scores.reshape(chips_per_owner * cores * own, count)


def solution(mesh):
    in_specs = (
        P(("groups", "blk"), "dim"),
        P(("groups", "blk"), "dim"),
        P(("groups", "blk"), "dim"),
        P("dim"),
    )
    out_specs = P("dim", ("groups", "blk"))
    body = functools.partial(shards, mesh.shape["blk"], mesh.shape["dim"])
    return jax.shard_map(body, mesh=mesh, in_specs=in_specs, out_specs=out_specs, check_vma=False)
```

time: 258 us -> 388 us (1.50)
  the two profiles are of different devices: /device:TPU:26 before, /device:TPU:0 now
where the time goes in v4:
time: 388 us; the launch traced here: 383 us
  Pallas kernels  293 us (76%)
  waiting for transfers between devices  43.7 us (11%)
  starting transfers between devices  34.7 us (9%)
  local copies, waits for them, and re-layouts  11.3 us (3%)
    pallas_call x3, Pallas kernels, cut(): pl.pallas_call(functools.partial(cut_kernel, [low for low, _ in cuts]), i...  177 us
    pallas_call x5, Pallas kernels, multiply(): pl.pallas_call(multiply_kernel, in_specs=[in_smem] + [anywhere] * (1 + le...  80.8 us
    pallas_call x1, Pallas kernels, dequantize(): pl.pallas_call(dequantize_kernel, grid=(count // rows,), in_specs=[pl.Blo...  30.1 us
    ppermute x4, starting transfers between devices, shift(): return lax.ppermute(panel, 'blk', pairs)  24.1 us
    ppermute x4, waiting for transfers between devices, shift(): return lax.ppermute(panel, 'blk', pairs)  22.4 us
    ppermute x5, waiting for transfers between devices, collect(): received.append(lax.ppermute(send, ('blk', 'dim'), pairs))  15.4 us
    unnamed x25, local copies, waits for them, and re-layouts  11.3 us
    ppermute x5, starting transfers between devices, collect(): received.append(lax.ppermute(send, ('blk', 'dim'), pairs))  8.31 us
  transfers between devices with their start and end apart: 17, of which 8 were waited for; matrix products, arithmetic and copies ran while one was open for 0% of the time, Pallas kernels for 76%

profile of v4, /device:TPU:0, one launch (start us, length us, event | category | flops | bytes accessed | tf_op | source)
XLA Modules:
  0.0 382.8 jit_solution(369607230516495059)
XLA Ops:
  0.0 0.5 collective-permute-start.1
  0.5 2.6 collective-permute-start
  3.0 2.1 collective-permute-start.4
  5.1 1.4 copy.9.exps_ref
  6.5 0.0 copy-start.7
  6.5 30.1 %dequantize.1.refs_3_.refs_4_ = bf16[2048,8192]{1,0:T(8,128)(2,1)} custom-call(bf16[2048,8192]{1,0:T(8,128)(2,1)} %codes_ref.1, s32[2048,64]{1,0:T(8,128)S(1)} %copy.9.exps_ref), custom_call_target="tpu_custom_call" | custom-call | flops 1 | bytes 1 | tf_op jit(solution)/shard_map/dequantize/pallas_call | solution.py:34
  36.6 1.6 copy-done
  38.2 18.2 %multiply.5 = (f32[256,2048]{1,0:T(8,128)S(1)}, bf16[256,2048]{1,0:T(8,128)(2,1)}) custom-call(s32[1]{0:T(128)} %bitcast.2.core_ref, bf16[128,8192]{1,0:T(8,128)(2,1)S(1)} %copy-done, bf16[128,8192]{1,0:T(8,128)(2,1)} %collective-permute-done.1.refs_1_, f32[1,8192]{1,0:T(1,128)S(1)} %bitcast.11, bf16[2048,8192]{1,0:T(8,128)(2,1)} %dequantize.1.refs_3_.refs_4_), custom_call_target="tpu_custom_call" | custom-call | flops 1 | bytes 1 | tf_op jit(solution)/shard_map/multiply/pallas_call | solution.py:130
  56.4 0.0 copy-start.3
  56.4 1.3 copy-done.3
  57.7 128.2 %cut.3 = (bf16[64,8192]{1,0:T(8,128)(2,1)}, bf16[64,8192]{1,0:T(8,128)(2,1)}, bf16[96,8192]{1,0:T(8,128)(2,1)}, bf16[32,8192]{1,0:T(8,128)(2,1)}) custom-call(bf16[128,8192]{1,0:T(8,128)(2,1)} %collective-permute-done.whole_ref.refs_0_), custom_call_target="tpu_custom_call" | custom-call | flops 1 | bytes 1 | tf_op jit(solution)/shard_map/cut/pallas_call | solution.py:217
  185.9 0.2 collective-permute-start.5
  186.2 0.3 collective-permute-start.6
  186.5 1.3 collective-permute-start.7
  187.8 0.1 collective-permute-start.3
  187.9 0.0 copy-start.4
  187.9 0.9 collective-permute-done.5.refs_1_
  188.9 1.6 collective-permute-done.6.refs_2_
  190.5 18.3 %multiply.6 = (f32[256,2048]{1,0:T(8,128)S(1)}, bf16[256,2048]{1,0:T(8,128)(2,1)}) custom-call(s32[1]{0:T(128)} %bitcast.2.core_ref, bf16[128,8192]{1,0:T(8,128)(2,1)} %collective-permute-done.whole_ref.refs_0_, bf16[64,8192]{1,0:T(8,128)(2,1)S(1)} %collective-permute-done.5.refs_1_, bf16[64,8192]{1,0:T(8,128)(2,1)} %collective-permute-done.6.refs_2_, ...), custom_call_target="tpu_custom_call" | custom-call | flops 1 | bytes 1 | tf_op jit(solution)/shard_map/multiply/pallas_call | solution.py:130
  208.8 5.2 %collective-permute-done.7.refs_1_ = bf16[256,2048]{1,0:T(8,128)(2,1)} collective-permute-done((bf16[256,2048]{1,0:T(8,128)(2,1)}, bf16[256,2048]{1,0:T(8,128)(2,1)}, u32[]{:S(2)}, u32[]{:S(2)}) %collective-permute-start.7) | collective-permute-done | bytes 1048608 | tf_op jit(solution)/shard_map/ppermute | solution.py:264
  213.9 2.9 place.5.refs_2_
  216.9 0.2 cut.4
  217.0 0.1 collective-permute-start.8
  217.1 0.5 collective-permute-start.9
  217.6 2.3 collective-permute-start.10
  219.9 1.4 collective-permute-done.9.refs_2_
  221.3 14.0 %multiply.7 = (f32[256,2048]{1,0:T(8,128)S(1)}, bf16[256,2048]{1,0:T(8,128)(2,1)}) custom-call(s32[1]{0:T(128)} %bitcast.2.core_ref, bf16[128,8192]{1,0:T(8,128)(2,1)S(1)} %collective-permute-done.4.whole_ref.refs_0_, bf16[64,8192]{1,0:T(8,128)(2,1)S(1)} %collective-permute-done.8.refs_1_, bf16[64,8192]{1,0:T(8,128)(2,1)S(1)} %collective-permute-done.9.refs_2_, ...), custom_call_target="tpu_custom_call" | custom-call | flops 1 | bytes 1 | tf_op jit(solution)/shard_map/multiply/pallas_call | solution.py:130
  235.3 1.3 copy-done.1
  236.5 1.3 collective-permute-start.13
  237.9 4.3 %collective-permute-done.10.refs_1_ = bf16[256,2048]{1,0:T(8,128)(2,1)} collective-permute-done((bf16[256,2048]{1,0:T(8,128)(2,1)}, bf16[256,2048]{1,0:T(8,128)(2,1)}, u32[]{:S(2)}, u32[]{:S(2)}) %collective-permute-start.10) | collective-permute-done | bytes 1048608 | tf_op jit(solution)/shard_map/ppermute | solution.py:264
  242.1 1.6 copy-done.6
  243.8 22.4 %collective-permute-done.3.whole_ref.refs_0_ = bf16[96,8192]{1,0:T(8,128)(2,1)} collective-permute-done((bf16[96,8192]{1,0:T(8,128)(2,1)}, bf16[96,8192]{1,0:T(8,128)(2,1)}, u32[]{:S(2)}, u32[]{:S(2)}) %collective-permute-start.3) | collective-permute-done | bytes 1572896 | tf_op jit(solution)/shard_map/ppermute | solution.py:250
  266.2 48.8 %cut.5 = (bf16[48,8192]{1,0:T(8,128)(2,1)}, bf16[48,8192]{1,0:T(8,128)(2,1)}) custom-call(bf16[96,8192]{1,0:T(8,128)(2,1)} %collective-permute-done.3.whole_ref.refs_0_), custom_call_target="tpu_custom_call" | custom-call | flops 1 | bytes 1 | tf_op jit(solution)/shard_map/cut/pallas_call | solution.py:217
  315.0 0.1 collective-permute-start.11
  315.0 0.5 collective-permute-start.12
  315.5 19.4 %collective-permute-start.2 = (bf16[32,8192]{1,0:T(8,128)(2,1)}, bf16[32,8192]{1,0:T(8,128)(2,1)S(1)}, u32[]{:S(2)}, u32[]{:S(2)}) collective-permute-start(bf16[32,8192]{1,0:T(8,128)(2,1)} %get-tuple-element.30), channel_id=1, source_target_pairs={{0,4},{2,6},{4,8},{6,10},{8,12},{10,14},{12,0},{14,2},{1,5},{3,7},... | collective-permute-start | bytes 1572872 | tf_op jit(solution)/shard_map/ppermute | solution.py:250
  335.0 0.9 copy-done.8
  335.9 0.9 copy-done.10
  336.8 1.1 copy-done.9
  337.9 1.1 copy-done.11
  339.1 16.4 %multiply.8 = (f32[192,2048]{1,0:T(8,128)S(1)}, bf16[192,2048]{1,0:T(8,128)(2,1)}) custom-call(s32[1]{0:T(128)} %bitcast.2.core_ref, bf16[96,8192]{1,0:T(8,128)(2,1)} %collective-permute-done.3.whole_ref.refs_0_, bf16[48,8192]{1,0:T(8,128)(2,1)S(1)} %copy-done.9, bf16[48,8192]{1,0:T(8,128)(2,1)S(1)} %copy-done.11, f32[1,8192]{1,0:T(1,128)S(1)} %bitcast.14, ...), custom_call_target="tpu_custom_call" | custom-call | flops 1 | bytes 1 | tf_op jit(solution)/shard_map/multiply/pallas_call | solution.py:130
  355.4 2.2 collective-permute-start.16
  357.6 1.7 place.7.refs_2_
  359.4 0.1 collective-permute-start.14
  359.5 1.9 collective-permute-done.14.refs_1_
  361.4 14.0 %multiply.9 = (f32[64,2048]{1,0:T(8,128)S(1)}, bf16[64,2048]{1,0:T(8,128)(2,1)S(1)}) custom-call(s32[1]{0:T(128)} %bitcast.2.core_ref, bf16[32,8192]{1,0:T(8,128)(2,1)S(1)} %collective-permute-done.2.refs_0_, bf16[32,8192]{1,0:T(8,128)(2,1)S(1)} %collective-permute-done.14.refs_1_, f32[1,8192]{1,0:T(1,128)S(1)} %bitcast.15, ...), custom_call_target="tpu_custom_call" | custom-call | flops 1 | bytes 1 | tf_op jit(solution)/shard_map/multiply/pallas_call | solution.py:130
  375.3 1.3 collective-permute-start.15
  376.7 6.0 %collective-permute-done.15.refs_1_ = bf16[64,2048]{1,0:T(8,128)(2,1)S(1)} collective-permute-done((bf16[64,2048]{1,0:T(8,128)(2,1)S(1)}, bf16[64,2048]{1,0:T(8,128)(2,1)S(1)}, u32[]{:S(2)}, u32[]{:S(2)}) %collective-permute-start.15) | collective-permute-done | bytes 262176 | tf_op jit(solution)/shard_map/ppermute | solution.py:264
  (25 shorter events, 0.2 us)
Async XLA Ops:
  0.0 36.6 %collective-permute-start.1 = (bf16[128,8192]{1,0:T(8,128)(2,1)}, bf16[128,8192]{1,0:T(8,128)(2,1)}, u32[]{:S(2)}, u32[]{:S(2)}) collective-permute-start(bf16[128,8192]{1,0:T(8,128)(2,1)} %refs_0_.1), channel_id=1, source_target_pairs={{0,2},{2,0},{4,6},{6,4},{8,10},{10,8},{12,14},{14,12},{1,3},{3,1},... | collective-permute-start | bytes 6291464 | tf_op jit(solution)/shard_map/ppermute | solution.py:254
  0.5 57.3 %collective-permute-start = (bf16[128,8192]{1,0:T(8,128)(2,1)}, bf16[128,8192]{1,0:T(8,128)(2,1)}, u32[]{:S(2)}, u32[]{:S(2)}) collective-permute-start(bf16[128,8192]{1,0:T(8,128)(2,1)} %refs_0_.1), channel_id=1, source_target_pairs={{0,4},{2,6},{4,8},{6,10},{8,12},{10,14},{12,0},{14,2},{1,5},{3,7},... | collective-permute-start | bytes 6291464 | tf_op jit(solution)/shard_map/ppermute | solution.py:250
  3.0 213.8 %collective-permute-start.4 = (bf16[128,8192]{1,0:T(8,128)(2,1)}, bf16[128,8192]{1,0:T(8,128)(2,1)S(1)}, u32[]{:S(2)}, u32[]{:S(2)}) collective-permute-start(bf16[128,8192]{1,0:T(8,128)(2,1)} %refs_0_.1), channel_id=1, source_target_pairs={{0,12},{2,14},{4,0},{6,2},{8,4},{10,6},{12,8},{14,10},{1,13},{3,15... | collective-permute-start | bytes 6291464 | tf_op jit(solution)/shard_map/ppermute | solution.py:250
  6.5 30.1 %copy-start.7 = (f32[8192]{0:T(1024)S(1)}, f32[8192]{0:T(1024)}, u32[]{:S(2)}) copy-start(f32[8192]{0:T(1024)} %param.7) | copy-start | bytes 98308
  36.6 1.6 copy-start
  56.4 1.3 copy-start.3
  185.9 2.9 collective-permute-start.5
  186.2 4.3 %collective-permute-start.6 = (bf16[64,8192]{1,0:T(8,128)(2,1)}, bf16[64,8192]{1,0:T(8,128)(2,1)}, u32[]{:S(2)}, u32[]{:S(2)}) collective-permute-start(bf16[64,8192]{1,0:T(8,128)(2,1)} %get-tuple-element.33), channel_id=1, source_target_pairs={{0,2},{2,0},{4,6},{6,4},{8,10},{10,8},{12,14},{14,12},{1,3},{3,1},... | collective-permute-start | bytes 3145736 | tf_op jit(solution)/shard_map/ppermute | solution.py:254
  186.5 27.4 %collective-permute-start.7 = (bf16[256,2048]{1,0:T(8,128)(2,1)}, bf16[256,2048]{1,0:T(8,128)(2,1)}, u32[]{:S(2)}, u32[]{:S(2)}) collective-permute-start(bf16[256,2048]{1,0:T(8,128)(2,1)} %get-tuple-element.28), channel_id=1, source_target_pairs={{1,0},{3,2},{5,4},{7,6},{8,9},{10,11},{12,13},{14,15},{17,16},{19,... | collective-permute-start | bytes 3145736 | tf_op jit(solution)/shard_map/ppermute | solution.py:264
  187.8 78.4 %collective-permute-start.3 = (bf16[96,8192]{1,0:T(8,128)(2,1)}, bf16[96,8192]{1,0:T(8,128)(2,1)}, u32[]{:S(2)}, u32[]{:S(2)}) collective-permute-start(bf16[96,8192]{1,0:T(8,128)(2,1)} %get-tuple-element.31), channel_id=1, source_target_pairs={{0,4},{2,6},{4,8},{6,10},{8,12},{10,14},{12,0},{14,2},{1,5},{3,7},... | collective-permute-start | bytes 4718600 | tf_op jit(solution)/shard_map/ppermute | solution.py:250
  187.9 26.0 %copy-start.4 = (f32[256,2048]{1,0:T(8,128)S(1)}, f32[256,2048]{1,0:T(8,128)}, u32[]{:S(2)}) copy-start(f32[256,2048]{1,0:T(8,128)} %copy-done.3) | copy-start | bytes 6291460
  208.8 8.1 %copy-start.5 = (f32[256,2048]{1,0:T(8,128)}, f32[256,2048]{1,0:T(8,128)S(1)}, u32[]{:S(2)}) copy-start(f32[256,2048]{1,0:T(8,128)S(1)} %get-tuple-element.34.refs_0_) | copy-start | bytes 6291460
  217.0 2.8 collective-permute-start.8
  217.1 4.1 %collective-permute-start.9 = (bf16[64,8192]{1,0:T(8,128)(2,1)S(1)}, bf16[64,8192]{1,0:T(8,128)(2,1)S(1)}, u32[]{:S(2)}, u32[]{:S(2)}) collective-permute-start(bf16[64,8192]{1,0:T(8,128)(2,1)S(1)} %get-tuple-element.38), channel_id=1, source_target_pairs={{0,2},{2,0},{4,6},{6,4},{8,10},{10,8},{12,14},{14,12},{1,3},{3,1},... | collective-permute-start | bytes 3145736 | tf_op jit(solution)/shard_map/ppermute | solution.py:254
  217.6 24.5 %collective-permute-start.10 = (bf16[256,2048]{1,0:T(8,128)(2,1)}, bf16[256,2048]{1,0:T(8,128)(2,1)}, u32[]{:S(2)}, u32[]{:S(2)}) collective-permute-start(bf16[256,2048]{1,0:T(8,128)(2,1)} %get-tuple-element.35), channel_id=1, source_target_pairs={{0,1},{2,3},{5,4},{7,6},{9,8},{11,10},{12,13},{14,15},{16,17},{18,... | collective-permute-start | bytes 3145736 | tf_op jit(solution)/shard_map/ppermute | solution.py:264
  235.2 1.3 copy-start.1
  236.5 121.1 %collective-permute-start.13 = (bf16[256,2048]{1,0:T(8,128)(2,1)}, bf16[256,2048]{1,0:T(8,128)(2,1)S(1)}, u32[]{:S(2)}, u32[]{:S(2)}) collective-permute-start(bf16[256,2048]{1,0:T(8,128)(2,1)} %get-tuple-element.40), channel_id=1, source_target_pairs={{1,0},{3,2},{4,5},{6,7},{8,9},{10,11},{13,12},{15,14},{17,16},{19,... | collective-permute-start | bytes 3145736 | tf_op jit(solution)/shard_map/ppermute | solution.py:264
  242.1 1.6 copy-start.6
  315.0 20.0 %collective-permute-start.11 = (bf16[48,8192]{1,0:T(8,128)(2,1)}, bf16[48,8192]{1,0:T(8,128)(2,1)S(1)}, u32[]{:S(2)}, u32[]{:S(2)}) collective-permute-start(bf16[48,8192]{1,0:T(8,128)(2,1)} %get-tuple-element.42), channel_id=1, source_target_pairs={{0,2},{2,0},{4,6},{6,4},{8,10},{10,8},{12,14},{14,12},{1,3},{3,1},... | collective-permute-start | bytes 2359304 | tf_op jit(solution)/shard_map/ppermute | solution.py:254
  315.0 20.8 %collective-permute-start.12 = (bf16[48,8192]{1,0:T(8,128)(2,1)}, bf16[48,8192]{1,0:T(8,128)(2,1)S(1)}, u32[]{:S(2)}, u32[]{:S(2)}) collective-permute-start(bf16[48,8192]{1,0:T(8,128)(2,1)} %get-tuple-element.43), channel_id=1, source_target_pairs={{0,2},{2,0},{4,6},{6,4},{8,10},{10,8},{12,14},{14,12},{1,3},{3,1},... | collective-permute-start | bytes 2359304 | tf_op jit(solution)/shard_map/ppermute | solution.py:254
  315.5 43.8 %collective-permute-start.2 = (bf16[32,8192]{1,0:T(8,128)(2,1)}, bf16[32,8192]{1,0:T(8,128)(2,1)S(1)}, u32[]{:S(2)}, u32[]{:S(2)}) collective-permute-start(bf16[32,8192]{1,0:T(8,128)(2,1)} %get-tuple-element.30), channel_id=1, source_target_pairs={{0,4},{2,6},{4,8},{6,10},{8,12},{10,14},{12,0},{14,2},{1,5},{3,7},... | collective-permute-start | bytes 1572872 | tf_op jit(solution)/shard_map/ppermute | solution.py:250
  335.0 22.7 %copy-start.2 = (f32[256,2048]{1,0:T(8,128)S(1)}, f32[256,2048]{1,0:T(8,128)}, u32[]{:S(2)}) copy-start(f32[256,2048]{1,0:T(8,128)} %copy-done.1) | copy-start | bytes 6291460
  335.0 0.9 copy-start.8
  335.9 0.9 copy-start.10
  336.8 1.1 copy-start.9
  337.9 1.1 copy-start.11
  355.4 21.2 %collective-permute-start.16 = (bf16[192,2048]{1,0:T(8,128)(2,1)}, bf16[192,2048]{1,0:T(8,128)(2,1)}, u32[]{:S(2)}, u32[]{:S(2)}) collective-permute-start(bf16[192,2048]{1,0:T(8,128)(2,1)} %get-tuple-element.45), channel_id=1, source_target_pairs={{0,1},{2,3},{4,5},{6,7},{9,8},{11,10},{13,12},{15,14},{16,17},{18,... | collective-permute-start | bytes 2359304 | tf_op jit(solution)/shard_map/ppermute | solution.py:264
  359.4 2.0 collective-permute-start.14
  375.3 7.4 %collective-permute-start.15 = (bf16[64,2048]{1,0:T(8,128)(2,1)S(1)}, bf16[64,2048]{1,0:T(8,128)(2,1)S(1)}, u32[]{:S(2)}, u32[]{:S(2)}) collective-permute-start(bf16[64,2048]{1,0:T(8,128)(2,1)S(1)} %get-tuple-element.48), channel_id=1, source_target_pairs={{0,1},{2,3},{4,5},{6,7},{9,8},{11,10},{13,12},{15,14},{16,17},{18,... | collective-permute-start | bytes 786440 | tf_op jit(solution)/shard_map/ppermute | solution.py:264

commit v5 on v4

--- a/solution.py
+++ b/solution.py
@@ -201,31 +201,8 @@
     )(mine, spot, keep, *received, *given)
 
 
-def cut_kernel(lows, whole_ref, *refs):
-    sems = refs[-1]
-    copies = [
-        pltpu.make_async_copy(whole_ref.at[pl.ds(low, ref.shape[0])], ref, sems.at[index])
-        for index, (low, ref) in enumerate(zip(lows, refs[:-1]))
-    ]
-    for copy in copies:
-        copy.start()
-    for copy in copies:
-        copy.wait()
-
-
 def cut(whole, cuts):
-    return pl.pallas_call(
-        functools.partial(cut_kernel, [low for low, _ in cuts]),
-        in_specs=[anywhere],
-        out_specs=[anywhere] * len(cuts),
-        out_shape=[
-            jax.ShapeDtypeStruct((high - low, whole.shape[1]), whole.dtype) for low, high in cuts
-        ],
-        scratch_shapes=[pltpu.SemaphoreType.DMA((len(cuts),))],
-        compiler_params=pltpu.CompilerParams(vmem_limit_bytes=2 * mib),
-        cost_estimate=small,
-        name="cut",
-    )(whole)
+    return [whole[low:high] for low, high in cuts]
 
 
 def after(array, *others):

time: 388 us -> 216 us (0.56)
  the two profiles are of different devices: /device:TPU:0 before, /device:TPU:16 now
where the time goes in v5:
time: 216 us
  Pallas kernels  125 us (58%)
  waiting for transfers between devices  57.2 us (26%)
  starting transfers between devices  20.8 us (10%)
  local copies, waits for them, and re-layouts  12.5 us (6%)
    pallas_call x5, Pallas kernels, multiply(): pl.pallas_call(multiply_kernel, in_specs=[in_smem] + [anywhere] * (1 + le...  88.6 us
    ppermute x4, waiting for transfers between devices, shift(): return lax.ppermute(panel, 'blk', pairs)  39.6 us
    pallas_call x1, Pallas kernels, dequantize(): pl.pallas_call(dequantize_kernel, grid=(count // rows,), in_specs=[pl.Blo...  30.1 us
    ppermute x5, starting transfers between devices, collect(): received.append(lax.ppermute(send, ('blk', 'dim'), pairs))  15.3 us
    ppermute x5, waiting for transfers between devices, collect(): received.append(lax.ppermute(send, ('blk', 'dim'), pairs))  10.9 us
    slice x5, local copies, waits for them, and re-layouts, cut(): return [whole[low:high] for low, high in cuts]  9.26 us
    ppermute x8, waiting for transfers between devices, swap(): return [lax.ppermute(part, 'blk', pairs) for part in parts]  6.82 us
    pallas_call x5, Pallas kernels, place(): pl.pallas_call(functools.partial(place_kernel, start, parts), in_specs=[i...  6.42 us
  transfers between devices with their start and end apart: 17, of which 10 were waited for; matrix products, arithmetic and copies ran while one was open for 5% of the time, Pallas kernels for 58%

profile of v5, /device:TPU:16, one launch (start us, length us, event | category | flops | bytes accessed | tf_op | source)
XLA Modules:
  0.0 215.9 jit_solution(1769427833845900952)
XLA Ops:
  0.0 1.6 collective-permute-start
  1.6 0.4 collective-permute-start.4
  2.0 1.4 copy.9.exps_ref
  3.4 0.0 copy-start.7
  3.4 30.1 %dequantize.1.refs_3_.refs_4_ = bf16[2048,8192]{1,0:T(8,128)(2,1)} custom-call(bf16[2048,8192]{1,0:T(8,128)(2,1)} %codes_ref.1, s32[2048,64]{1,0:T(8,128)S(1)} %copy.9.exps_ref), custom_call_target="tpu_custom_call" | custom-call | flops 1 | bytes 1 | tf_op jit(solution)/shard_map/dequantize/pallas_call | solution.py:34
  33.5 0.0 collective-permute-done.1.refs_1_
  33.5 1.6 copy-done
  35.1 18.2 %multiply.5 = (f32[256,2048]{1,0:T(8,128)S(1)}, bf16[256,2048]{1,0:T(8,128)(2,1)}) custom-call(s32[1]{0:T(128)} %bitcast.2.core_ref, bf16[128,8192]{1,0:T(8,128)(2,1)S(1)} %copy-done, bf16[128,8192]{1,0:T(8,128)(2,1)} %collective-permute-done.1.refs_1_, f32[1,8192]{1,0:T(1,128)S(1)} %bitcast.11, bf16[2048,8192]{1,0:T(8,128)(2,1)} %dequantize.1.refs_3_.refs_4_), custom_call_target="tpu_custom_call" | custom-call | flops 1 | bytes 1 | tf_op jit(solution)/shard_map/multiply/pallas_call | solution.py:130
  53.3 0.0 copy-start.1
  53.3 39.6 %collective-permute-done.refs_0_ = bf16[128,8192]{1,0:T(8,128)(2,1)S(1)} collective-permute-done((bf16[128,8192]{1,0:T(8,128)(2,1)}, bf16[128,8192]{1,0:T(8,128)(2,1)S(1)}, u32[]{:S(2)}, u32[]{:S(2)}) %collective-permute-start) | collective-permute-done | bytes 2097184 | tf_op jit(solution)/shard_map/ppermute | solution.py:227
  92.9 1.5 fusion.1
  94.4 0.0 collective-permute-start.5
  94.4 0.5 collective-permute-start.6
  94.9 4.4 %collective-permute-start.7 = (bf16[256,2048]{1,0:T(8,128)(2,1)}, bf16[256,2048]{1,0:T(8,128)(2,1)}, u32[]{:S(2)}, u32[]{:S(2)}) collective-permute-start(bf16[256,2048]{1,0:T(8,128)(2,1)} %get-tuple-element.20), channel_id=1, source_target_pairs={{1,0},{3,2},{5,4},{7,6},{8,9},{10,11},{12,13},{14,15},{17,16},{19,... | collective-permute-start | bytes 3145736 | tf_op jit(solution)/shard_map/ppermute | solution.py:241
  99.3 1.2 slice.25
  100.5 1.7 collective-permute-start.3
  102.2 0.0 collective-permute-done.5.refs_1_
  102.2 0.0 collective-permute-done.6.refs_2_
  102.2 17.9 %multiply.6 = (f32[256,2048]{1,0:T(8,128)S(1)}, bf16[256,2048]{1,0:T(8,128)(2,1)}) custom-call(s32[1]{0:T(128)} %bitcast.2.core_ref, bf16[128,8192]{1,0:T(8,128)(2,1)S(1)} %collective-permute-done.refs_0_, bf16[64,8192]{1,0:T(8,128)(2,1)S(1)} %collective-permute-done.5.refs_1_, bf16[64,8192]{1,0:T(8,128)(2,1)} %collective-permute-done.6.refs_2_, ...), custom_call_target="tpu_custom_call" | custom-call | flops 1 | bytes 1 | tf_op jit(solution)/shard_map/multiply/pallas_call | solution.py:130
  120.1 1.0 collective-permute-done.7.refs_1_
  121.2 0.3 copy-done.5
  121.5 3.0 %fusion = (bf16[64,8192]{1,0:T(8,128)(2,1)}, bf16[64,8192]{1,0:T(8,128)(2,1)}) fusion(bf16[128,8192]{1,0:T(8,128)(2,1)} %collective-permute-done.4.refs_0_), kind=kLoop, calls=%fused_computation | loop fusion | bytes 4194304 | tf_op jit(solution)/shard_map/slice | solution.py:205
  124.5 0.0 collective-permute-start.8
  124.5 0.5 collective-permute-start.9
  125.0 1.3 collective-permute-start.10
  126.4 2.5 %collective-permute-done.8.refs_1_ = bf16[64,8192]{1,0:T(8,128)(2,1)S(1)} collective-permute-done((bf16[64,8192]{1,0:T(8,128)(2,1)}, bf16[64,8192]{1,0:T(8,128)(2,1)S(1)}, u32[]{:S(2)}, u32[]{:S(2)}) %collective-permute-start.8) | collective-permute-done | bytes 1048608 | tf_op jit(solution)/shard_map/ppermute | solution.py:231
  128.8 0.2 collective-permute-done.9.refs_2_
  129.0 18.3 %multiply.7 = (f32[256,2048]{1,0:T(8,128)S(1)}, bf16[256,2048]{1,0:T(8,128)(2,1)}) custom-call(s32[1]{0:T(128)} %bitcast.2.core_ref, bf16[128,8192]{1,0:T(8,128)(2,1)} %collective-permute-done.4.refs_0_, bf16[64,8192]{1,0:T(8,128)(2,1)S(1)} %collective-permute-done.8.refs_1_, bf16[64,8192]{1,0:T(8,128)(2,1)} %collective-permute-done.9.refs_2_, ...), custom_call_target="tpu_custom_call" | custom-call | flops 1 | bytes 1 | tf_op jit(solution)/shard_map/multiply/pallas_call | solution.py:130
  147.3 7.0 %collective-permute-start.13 = (bf16[256,2048]{1,0:T(8,128)(2,1)}, bf16[256,2048]{1,0:T(8,128)(2,1)S(1)}, u32[]{:S(2)}, u32[]{:S(2)}) collective-permute-start(bf16[256,2048]{1,0:T(8,128)(2,1)} %get-tuple-element.26), channel_id=1, source_target_pairs={{1,0},{3,2},{4,5},{6,7},{8,9},{10,11},{13,12},{15,14},{17,16},{19,... | collective-permute-start | bytes 3145736 | tf_op jit(solution)/shard_map/ppermute | solution.py:241
  154.4 0.6 collective-permute-done.10.refs_1_
  155.0 2.9 %place.6.refs_2_ = f32[2,2,128,2048]{3,2,1,0:T(8,128)} custom-call(s32[1]{0:T(128)} %bitcast.6.mine_ref, s32[1]{0:T(128)} %bitcast.7.spot_ref, f32[256,2048]{1,0:T(8,128)S(1)} %copy-done.6, bf16[256,2048]{1,0:T(8,128)(2,1)} %collective-permute-done.10.refs_1_, f32[2,2,128,2048]{3,2,1,0:T(8,128)} %place.5.refs_2_), custom_call_target="tpu_custom_call", output_to_operand_aliasing={{}: (4, {})} | custom-call | flops 1 | bytes 1 | tf_op jit(solution)/shard_map/place/pallas_call | solution.py:186
  157.9 2.6 %fusion.2 = (bf16[48,8192]{1,0:T(8,128)(2,1)}, bf16[48,8192]{1,0:T(8,128)(2,1)}) fusion(bf16[96,8192]{1,0:T(8,128)(2,1)} %collective-permute-done.3.refs_0_), kind=kLoop, calls=%fused_computation.2 | loop fusion | bytes 3145728 | tf_op jit(solution)/shard_map/slice | solution.py:205
  160.6 0.5 collective-permute-start.12
  161.1 0.9 slice.24
  161.9 1.3 collective-permute-done.11.refs_1_
  163.2 1.1 collective-permute-done.12.refs_2_
  164.3 20.3 %multiply.8 = (f32[192,2048]{1,0:T(8,128)S(1)}, bf16[192,2048]{1,0:T(8,128)(2,1)}) custom-call(s32[1]{0:T(128)} %bitcast.2.core_ref, bf16[96,8192]{1,0:T(8,128)(2,1)} %collective-permute-done.3.refs_0_, bf16[48,8192]{1,0:T(8,128)(2,1)} %collective-permute-done.11.refs_1_, bf16[48,8192]{1,0:T(8,128)(2,1)} %collective-permute-done.12.refs_2_, ...), custom_call_target="tpu_custom_call" | custom-call | flops 1 | bytes 1 | tf_op jit(solution)/shard_map/multiply/pallas_call | solution.py:130
  184.6 1.3 collective-permute-start.16
  185.9 0.0 collective-permute-done.13.refs_1_
  186.0 0.0 collective-permute-done.2.refs_0_
  186.0 0.2 collective-permute-start.14
  186.2 1.8 collective-permute-done.14.refs_1_
  188.0 14.0 %multiply.9 = (f32[64,2048]{1,0:T(8,128)S(1)}, bf16[64,2048]{1,0:T(8,128)(2,1)S(1)}) custom-call(s32[1]{0:T(128)} %bitcast.2.core_ref, bf16[32,8192]{1,0:T(8,128)(2,1)S(1)} %collective-permute-done.2.refs_0_, bf16[32,8192]{1,0:T(8,128)(2,1)S(1)} %collective-permute-done.14.refs_1_, f32[1,8192]{1,0:T(1,128)S(1)} %bitcast.15, ...), custom_call_target="tpu_custom_call" | custom-call | flops 1 | bytes 1 | tf_op jit(solution)/shard_map/multiply/pallas_call | solution.py:130
  201.9 1.3 collective-permute-start.15
  203.3 3.1 %collective-permute-done.16.refs_1_ = bf16[192,2048]{1,0:T(8,128)(2,1)} collective-permute-done((bf16[192,2048]{1,0:T(8,128)(2,1)}, bf16[192,2048]{1,0:T(8,128)(2,1)}, u32[]{:S(2)}, u32[]{:S(2)}) %collective-permute-start.16) | collective-permute-done | bytes 786464 | tf_op jit(solution)/shard_map/ppermute | solution.py:241
  206.4 2.5 %place.8.refs_2_ = f32[2,2,128,2048]{3,2,1,0:T(8,128)} custom-call(s32[1]{0:T(128)} %bitcast.mine_ref, s32[1]{0:T(128)} %bitcast.1.spot_ref, f32[192,2048]{1,0:T(8,128)S(1)} %get-tuple-element.28.refs_0_, bf16[192,2048]{1,0:T(8,128)(2,1)} %collective-permute-done.16.refs_1_, f32[2,2,128,2048]{3,2,1,0:T(8,128)} %place.7.refs_2_), custom_call_target="tpu_custom_call", output_to_operand_aliasing={{}: (4, {})} | custom-call | flops 1 | bytes 1 | tf_op jit(solution)/shard_map/place/pallas_call | solution.py:186
  208.9 6.0 %collective-permute-done.15.refs_1_ = bf16[64,2048]{1,0:T(8,128)(2,1)S(1)} collective-permute-done((bf16[64,2048]{1,0:T(8,128)(2,1)S(1)}, bf16[64,2048]{1,0:T(8,128)(2,1)S(1)}, u32[]{:S(2)}, u32[]{:S(2)}) %collective-permute-start.15) | collective-permute-done | bytes 262176 | tf_op jit(solution)/shard_map/ppermute | solution.py:241
  215.0 0.9 place.9
  (19 shorter events, 0.1 us)
Async XLA Ops:
  0.0 33.5 %collective-permute-start.1 = (bf16[128,8192]{1,0:T(8,128)(2,1)}, bf16[128,8192]{1,0:T(8,128)(2,1)}, u32[]{:S(2)}, u32[]{:S(2)}) collective-permute-start(bf16[128,8192]{1,0:T(8,128)(2,1)} %refs_0_.1), channel_id=1, source_target_pairs={{0,2},{2,0},{4,6},{6,4},{8,10},{10,8},{12,14},{14,12},{1,3},{3,1},... | collective-permute-start | bytes 6291464 | tf_op jit(solution)/shard_map/ppermute | solution.py:231
  0.0 92.9 %collective-permute-start = (bf16[128,8192]{1,0:T(8,128)(2,1)}, bf16[128,8192]{1,0:T(8,128)(2,1)S(1)}, u32[]{:S(2)}, u32[]{:S(2)}) collective-permute-start(bf16[128,8192]{1,0:T(8,128)(2,1)} %refs_0_.1), channel_id=1, source_target_pairs={{0,4},{2,6},{4,8},{6,10},{8,12},{10,14},{12,0},{14,2},{1,5},{3,7},... | collective-permute-start | bytes 6291464 | tf_op jit(solution)/shard_map/ppermute | solution.py:227
  1.6 119.9 %collective-permute-start.4 = (bf16[128,8192]{1,0:T(8,128)(2,1)}, bf16[128,8192]{1,0:T(8,128)(2,1)}, u32[]{:S(2)}, u32[]{:S(2)}) collective-permute-start(bf16[128,8192]{1,0:T(8,128)(2,1)} %refs_0_.1), channel_id=1, source_target_pairs={{0,12},{2,14},{4,0},{6,2},{8,4},{10,6},{12,8},{14,10},{1,13},{3,15... | collective-permute-start | bytes 6291464 | tf_op jit(solution)/shard_map/ppermute | solution.py:227
  3.4 30.1 %copy-start.7 = (f32[8192]{0:T(1024)S(1)}, f32[8192]{0:T(1024)}, u32[]{:S(2)}) copy-start(f32[8192]{0:T(1024)} %param.7) | copy-start | bytes 98308
  33.5 1.6 copy-start
  53.3 41.1 %copy-start.1 = (f32[256,2048]{1,0:T(8,128)}, f32[256,2048]{1,0:T(8,128)S(1)}, u32[]{:S(2)}) copy-start(f32[256,2048]{1,0:T(8,128)S(1)} %get-tuple-element.19.refs_0_) | copy-start | bytes 6291460
  94.4 7.9 %collective-permute-start.5 = (bf16[64,8192]{1,0:T(8,128)(2,1)}, bf16[64,8192]{1,0:T(8,128)(2,1)S(1)}, u32[]{:S(2)}, u32[]{:S(2)}) collective-permute-start(bf16[64,8192]{1,0:T(8,128)(2,1)} %get-tuple-element.36), channel_id=1, source_target_pairs={{0,2},{2,0},{4,6},{6,4},{8,10},{10,8},{12,14},{14,12},{1,3},{3,1},... | collective-permute-start | bytes 3145736 | tf_op jit(solution)/shard_map/ppermute | solution.py:231
  94.4 7.9 %collective-permute-start.6 = (bf16[64,8192]{1,0:T(8,128)(2,1)}, bf16[64,8192]{1,0:T(8,128)(2,1)}, u32[]{:S(2)}, u32[]{:S(2)}) collective-permute-start(bf16[64,8192]{1,0:T(8,128)(2,1)} %get-tuple-element.35), channel_id=1, source_target_pairs={{0,2},{2,0},{4,6},{6,4},{8,10},{10,8},{12,14},{14,12},{1,3},{3,1},... | collective-permute-start | bytes 3145736 | tf_op jit(solution)/shard_map/ppermute | solution.py:231
  94.9 26.3 %collective-permute-start.7 = (bf16[256,2048]{1,0:T(8,128)(2,1)}, bf16[256,2048]{1,0:T(8,128)(2,1)}, u32[]{:S(2)}, u32[]{:S(2)}) collective-permute-start(bf16[256,2048]{1,0:T(8,128)(2,1)} %get-tuple-element.20), channel_id=1, source_target_pairs={{1,0},{3,2},{5,4},{7,6},{8,9},{10,11},{12,13},{14,15},{17,16},{19,... | collective-permute-start | bytes 3145736 | tf_op jit(solution)/shard_map/ppermute | solution.py:241
  100.5 20.6 %copy-start.2 = (f32[256,2048]{1,0:T(8,128)S(1)}, f32[256,2048]{1,0:T(8,128)}, u32[]{:S(2)}) copy-start(f32[256,2048]{1,0:T(8,128)} %copy-done.1) | copy-start | bytes 6291460
  100.5 57.4 %collective-permute-start.3 = (bf16[96,8192]{1,0:T(8,128)(2,1)}, bf16[96,8192]{1,0:T(8,128)(2,1)}, u32[]{:S(2)}, u32[]{:S(2)}) collective-permute-start(bf16[96,8192]{1,0:T(8,128)(2,1)} %slice.25), channel_id=1, source_target_pairs={{0,4},{2,6},{4,8},{6,10},{8,12},{10,14},{12,0},{14,2},{1,5},{3,7},... | collective-permute-start | bytes 4718600 | tf_op jit(solution)/shard_map/ppermute | solution.py:227
  120.1 1.4 copy-start.5
  124.5 4.3 %collective-permute-start.8 = (bf16[64,8192]{1,0:T(8,128)(2,1)}, bf16[64,8192]{1,0:T(8,128)(2,1)S(1)}, u32[]{:S(2)}, u32[]{:S(2)}) collective-permute-start(bf16[64,8192]{1,0:T(8,128)(2,1)} %get-tuple-element.34), channel_id=1, source_target_pairs={{0,2},{2,0},{4,6},{6,4},{8,10},{10,8},{12,14},{14,12},{1,3},{3,1},... | collective-permute-start | bytes 3145736 | tf_op jit(solution)/shard_map/ppermute | solution.py:231
  124.5 4.5 %collective-permute-start.9 = (bf16[64,8192]{1,0:T(8,128)(2,1)}, bf16[64,8192]{1,0:T(8,128)(2,1)}, u32[]{:S(2)}, u32[]{:S(2)}) collective-permute-start(bf16[64,8192]{1,0:T(8,128)(2,1)} %get-tuple-element.33), channel_id=1, source_target_pairs={{0,2},{2,0},{4,6},{6,4},{8,10},{10,8},{12,14},{14,12},{1,3},{3,1},... | collective-permute-start | bytes 3145736 | tf_op jit(solution)/shard_map/ppermute | solution.py:231
  125.0 30.0 %collective-permute-start.10 = (bf16[256,2048]{1,0:T(8,128)(2,1)}, bf16[256,2048]{1,0:T(8,128)(2,1)}, u32[]{:S(2)}, u32[]{:S(2)}) collective-permute-start(bf16[256,2048]{1,0:T(8,128)(2,1)} %get-tuple-element.23), channel_id=1, source_target_pairs={{0,1},{2,3},{5,4},{7,6},{9,8},{11,10},{12,13},{14,15},{16,17},{18,... | collective-permute-start | bytes 3145736 | tf_op jit(solution)/shard_map/ppermute | solution.py:241
  126.3 28.7 %copy-start.6 = (f32[256,2048]{1,0:T(8,128)S(1)}, f32[256,2048]{1,0:T(8,128)}, u32[]{:S(2)}) copy-start(f32[256,2048]{1,0:T(8,128)} %copy-done.5) | copy-start | bytes 6291460
  147.3 10.6 %copy-start.3 = (f32[256,2048]{1,0:T(8,128)}, f32[256,2048]{1,0:T(8,128)S(1)}, u32[]{:S(2)}) copy-start(f32[256,2048]{1,0:T(8,128)S(1)} %get-tuple-element.25.refs_0_) | copy-start | bytes 6291460
  147.3 38.6 %collective-permute-start.13 = (bf16[256,2048]{1,0:T(8,128)(2,1)}, bf16[256,2048]{1,0:T(8,128)(2,1)S(1)}, u32[]{:S(2)}, u32[]{:S(2)}) collective-permute-start(bf16[256,2048]{1,0:T(8,128)(2,1)} %get-tuple-element.26), channel_id=1, source_target_pairs={{1,0},{3,2},{4,5},{6,7},{8,9},{10,11},{13,12},{15,14},{17,16},{19,... | collective-permute-start | bytes 3145736 | tf_op jit(solution)/shard_map/ppermute | solution.py:241
  160.6 2.6 %collective-permute-start.11 = (bf16[48,8192]{1,0:T(8,128)(2,1)}, bf16[48,8192]{1,0:T(8,128)(2,1)}, u32[]{:S(2)}, u32[]{:S(2)}) collective-permute-start(bf16[48,8192]{1,0:T(8,128)(2,1)} %get-tuple-element.38), channel_id=1, source_target_pairs={{0,2},{2,0},{4,6},{6,4},{8,10},{10,8},{12,14},{14,12},{1,3},{3,1},... | collective-permute-start | bytes 2359304 | tf_op jit(solution)/shard_map/ppermute | solution.py:231
  160.6 3.7 %collective-permute-start.12 = (bf16[48,8192]{1,0:T(8,128)(2,1)}, bf16[48,8192]{1,0:T(8,128)(2,1)}, u32[]{:S(2)}, u32[]{:S(2)}) collective-permute-start(bf16[48,8192]{1,0:T(8,128)(2,1)} %get-tuple-element.37), channel_id=1, source_target_pairs={{0,2},{2,0},{4,6},{6,4},{8,10},{10,8},{12,14},{14,12},{1,3},{3,1},... | collective-permute-start | bytes 2359304 | tf_op jit(solution)/shard_map/ppermute | solution.py:231
  161.9 24.0 %collective-permute-start.2 = (bf16[32,8192]{1,0:T(8,128)(2,1)}, bf16[32,8192]{1,0:T(8,128)(2,1)S(1)}, u32[]{:S(2)}, u32[]{:S(2)}) collective-permute-start(bf16[32,8192]{1,0:T(8,128)(2,1)} %slice.24), channel_id=1, source_target_pairs={{0,4},{2,6},{4,8},{6,10},{8,12},{10,14},{12,0},{14,2},{1,5},{3,7},... | collective-permute-start | bytes 1572872 | tf_op jit(solution)/shard_map/ppermute | solution.py:227
  161.9 24.0 %copy-start.4 = (f32[256,2048]{1,0:T(8,128)S(1)}, f32[256,2048]{1,0:T(8,128)}, u32[]{:S(2)}) copy-start(f32[256,2048]{1,0:T(8,128)} %copy-done.3) | copy-start | bytes 6291460
  184.6 21.8 %collective-permute-start.16 = (bf16[192,2048]{1,0:T(8,128)(2,1)}, bf16[192,2048]{1,0:T(8,128)(2,1)}, u32[]{:S(2)}, u32[]{:S(2)}) collective-permute-start(bf16[192,2048]{1,0:T(8,128)(2,1)} %get-tuple-element.29), channel_id=1, source_target_pairs={{0,1},{2,3},{4,5},{6,7},{9,8},{11,10},{13,12},{15,14},{16,17},{18,... | collective-permute-start | bytes 2359304 | tf_op jit(solution)/shard_map/ppermute | solution.py:241
  186.0 2.0 collective-permute-start.14
  201.9 13.1 %collective-permute-start.15 = (bf16[64,2048]{1,0:T(8,128)(2,1)S(1)}, bf16[64,2048]{1,0:T(8,128)(2,1)S(1)}, u32[]{:S(2)}, u32[]{:S(2)}) collective-permute-start(bf16[64,2048]{1,0:T(8,128)(2,1)S(1)} %get-tuple-element.32), channel_id=1, source_target_pairs={{0,1},{2,3},{4,5},{6,7},{9,8},{11,10},{13,12},{15,14},{16,17},{18,... | collective-permute-start | bytes 786440 | tf_op jit(solution)/shard_map/ppermute | solution.py:241

commit v6 on v5

--- a/solution.py
+++ b/solution.py
@@ -244,34 +244,38 @@
         return place(scores, shape, mine, lax.rem(source, chips_per_owner)[None], keep, received, start)
 
     ups = chips // 2
-    cuts = [0, own * 3 // 4, own]
-    held = {0: val_grads}
-    for by in range(1, chips - ups):
-        held[by] = shift(held[by - 1], 1)
-        held[-by] = shift(held[1 - by], -1)
-    if ups - 1 not in held:
-        held[ups - 1] = shift(held[ups - 2], 1)
+    order = list(range(1, ups + 1)) + list(range(-1, ups - chips, -1))
+    pieces = [(0, own * 3 // 4), (own * 3 // 4, own)]
+    halves = [(0, own // 2), (own // 2, own)]
+
+    arriving = shift(val_grads, 1)
+    beside = swap([val_grads])
     train = dequantize(grad_codes, scale_exps)
-    part = multiply(core, val_grads, swap([val_grads]), fisher, train)
-    pending = [(part, 0, 0)]
-    scores = None
-    order = [by for by in held if by != 0] + [ups] * (len(cuts) - 1)
-    lows = [0] * (len(held) - 1) + cuts[:-1]
-    halves = [(0, own // 2), (own // 2, own)]
-    for by, lo in zip(order, lows):
-        panel = held[by] if by != ups else last[cuts.index(lo)]
-        panel = after(panel, part) if scores is None else after(panel, part, scores)
-        if by == ups - 1:
-            *parts, low_part, high_part = cut(panel, halves + list(zip(cuts, cuts[1:])))
-            last = [shift(low_part, 1), shift(high_part, 1)]
-        elif by == ups and lo > 0:
-            parts = [panel]
-        else:
-            half = max(panel.shape[0] // 32 * 16, 16)
-            parts = cut(panel, [(0, half), (half, panel.shape[0])])
+    scores, part, pending = None, train, []
+    for index, by in enumerate(order[:-1]):
+        panel = after(arriving, part, *([] if scores is None else [scores]))
+        if index == 0:
+            part = multiply(core, after(val_grads, panel), beside, fisher, train)
+            pending.append((part, 0, 0))
+        following = order[index + 1]
+        source = panel if abs(following) > 1 else val_grads
+        parts = swap(cut(panel, halves))
+        if index + 2 < len(order):
+            arriving = shift(source, 1 if following > 0 else -1)
+        done = part
+        part = multiply(core, after(panel, part), parts, fisher, train)
+        if index + 2 == len(order):
+            arriving = [shift(after(piece, done), 1 if following > 0 else -1) for piece in cut(source, pieces)]
+        scores = collect(scores, *pending.pop())
+        pending.append((part, by, 0))
+    by = order[-1]
+    for (low, high), panel in zip(pieces, arriving):
+        panel = after(panel, part, scores)
+        half = max((high - low) // 32 * 16, 16)
+        parts = [panel] if low > 0 else cut(panel, [(0, half), (half, high - low)])
         part = multiply(core, panel, swap(parts), fisher, train)
         scores = collect(scores, *pending.pop())
-        pending.append((part, by, lo))
+        pending.append((part, by, low))
     scores = collect(scores, *pending.pop())
     return scores.reshape(chips_per_owner * cores * own, count)
 

time: 216 us -> 208 us (0.963)
  the two profiles are of different devices: /device:TPU:16 before, /device:TPU:0 now
where the time goes in v6:
time: 208 us
  Pallas kernels  126 us (61%)
  waiting for transfers between devices  43.2 us (21%)
  starting transfers between devices  23 us (11%)
  local copies, waits for them, and re-layouts  15.2 us (7%)
    pallas_call x5, Pallas kernels, multiply(): pl.pallas_call(multiply_kernel, in_specs=[in_smem] + [anywhere] * (1 + le...  89.4 us
    pallas_call x1, Pallas kernels, dequantize(): pl.pallas_call(dequantize_kernel, grid=(count // rows,), in_specs=[pl.Blo...  30.1 us
    ppermute x5, waiting for transfers between devices, collect(): received.append(lax.ppermute(send, ('blk', 'dim'), pairs))  22.6 us
    ppermute x4, waiting for transfers between devices, shift(): return lax.ppermute(panel, 'blk', pairs)  16.5 us
    ppermute x5, starting transfers between devices, collect(): received.append(lax.ppermute(send, ('blk', 'dim'), pairs))  15.4 us
    slice x5, local copies, waits for them, and re-layouts, cut(): return [whole[low:high] for low, high in cuts]  10.9 us
    pallas_call x5, Pallas kernels, place(): pl.pallas_call(functools.partial(place_kernel, start, parts), in_specs=[i...  6.42 us
    ppermute x4, starting transfers between devices, shift(): return lax.ppermute(panel, 'blk', pairs)  5.78 us
  transfers between devices with their start and end apart: 17, of which 7 were waited for; matrix products, arithmetic and copies ran while one was open for 6% of the time, Pallas kernels for 60%

profile of v6, /device:TPU:0, one launch (start us, length us, event | category | flops | bytes accessed | tf_op | source)
XLA Modules:
  0.0 207.5 jit_solution(10269238727660444966)
XLA Ops:
  0.0 3.0 %collective-permute-start = (bf16[128,8192]{1,0:T(8,128)(2,1)}, bf16[128,8192]{1,0:T(8,128)(2,1)}, u32[]{:S(2)}, u32[]{:S(2)}) collective-permute-start(bf16[128,8192]{1,0:T(8,128)(2,1)} %refs_0_), channel_id=1, source_target_pairs={{0,4},{2,6},{4,8},{6,10},{8,12},{10,14},{12,0},{14,2},{1,5},{3,7},... | collective-permute-start | bytes 6291464 | tf_op jit(solution)/shard_map/ppermute | solution.py:227
  3.0 0.0 collective-permute-start.1
  3.0 1.4 copy.9.exps_ref
  4.4 30.1 %dequantize.1.refs_3_.refs_4_ = bf16[2048,8192]{1,0:T(8,128)(2,1)} custom-call(bf16[2048,8192]{1,0:T(8,128)(2,1)} %codes_ref.1, s32[2048,64]{1,0:T(8,128)S(1)} %copy.9.exps_ref), custom_call_target="tpu_custom_call" | custom-call | flops 1 | bytes 1 | tf_op jit(solution)/shard_map/dequantize/pallas_call | solution.py:34
  34.5 16.5 %collective-permute-done.refs_0_ = bf16[128,8192]{1,0:T(8,128)(2,1)} collective-permute-done((bf16[128,8192]{1,0:T(8,128)(2,1)}, bf16[128,8192]{1,0:T(8,128)(2,1)}, u32[]{:S(2)}, u32[]{:S(2)}) %collective-permute-start) | collective-permute-done | bytes 2097184 | tf_op jit(solution)/shard_map/ppermute | solution.py:227
  51.0 3.1 %fusion.1 = (bf16[64,8192]{1,0:T(8,128)(2,1)}, bf16[64,8192]{1,0:T(8,128)(2,1)}) fusion(bf16[128,8192]{1,0:T(8,128)(2,1)} %collective-permute-done.refs_0_), kind=kLoop, calls=%fused_computation.1 | loop fusion | bytes 4194304 | tf_op jit(solution)/shard_map/slice | solution.py:205
  54.1 0.0 collective-permute-start.2
  54.1 0.5 collective-permute-start.3
  54.6 18.2 %multiply.5 = (f32[256,2048]{1,0:T(8,128)S(1)}, bf16[256,2048]{1,0:T(8,128)(2,1)}) custom-call(s32[1]{0:T(128)} %bitcast.2.core_ref, bf16[128,8192]{1,0:T(8,128)(2,1)S(1)} %copy-done, bf16[128,8192]{1,0:T(8,128)(2,1)} %collective-permute-done.1.refs_1_, f32[1,8192]{1,0:T(1,128)S(1)} %bitcast.11, bf16[2048,8192]{1,0:T(8,128)(2,1)} %dequantize.1.refs_3_.refs_4_), custom_call_target="tpu_custom_call" | custom-call | flops 1 | bytes 1 | tf_op jit(solution)/shard_map/multiply/pallas_call | solution.py:130
  72.7 0.0 copy-start.1
  72.8 1.3 copy-done.1
  74.1 1.3 collective-permute-start.7
  75.4 1.3 slice.27
  76.7 0.0 collective-permute-done.2.refs_1_
  76.7 0.0 collective-permute-done.3.refs_2_
  76.7 18.4 %multiply.6 = (f32[256,2048]{1,0:T(8,128)S(1)}, bf16[256,2048]{1,0:T(8,128)(2,1)}) custom-call(s32[1]{0:T(128)} %bitcast.2.core_ref, bf16[128,8192]{1,0:T(8,128)(2,1)} %collective-permute-done.refs_0_, bf16[64,8192]{1,0:T(8,128)(2,1)S(1)} %collective-permute-done.2.refs_1_, bf16[64,8192]{1,0:T(8,128)(2,1)} %collective-permute-done.3.refs_2_, ...), custom_call_target="tpu_custom_call" | custom-call | flops 1 | bytes 1 | tf_op jit(solution)/shard_map/multiply/pallas_call | solution.py:130
  95.1 5.6 %collective-permute-start.10 = (bf16[256,2048]{1,0:T(8,128)(2,1)}, bf16[256,2048]{1,0:T(8,128)(2,1)S(1)}, u32[]{:S(2)}, u32[]{:S(2)}) collective-permute-start(bf16[256,2048]{1,0:T(8,128)(2,1)} %get-tuple-element.30), channel_id=1, source_target_pairs={{0,1},{2,3},{5,4},{7,6},{9,8},{11,10},{12,13},{14,15},{16,17},{18,... | collective-permute-start | bytes 3145736 | tf_op jit(solution)/shard_map/ppermute | solution.py:241
  100.7 2.8 %collective-permute-start.5 = (bf16[96,8192]{1,0:T(8,128)(2,1)}, bf16[96,8192]{1,0:T(8,128)(2,1)}, u32[]{:S(2)}, u32[]{:S(2)}) collective-permute-start(bf16[96,8192]{1,0:T(8,128)(2,1)} %slice.27), channel_id=1, source_target_pairs={{0,12},{2,14},{4,0},{6,2},{8,4},{10,6},{12,8},{14,10},{1,13},{3,15... | collective-permute-start | bytes 4718600 | tf_op jit(solution)/shard_map/ppermute | solution.py:227
  103.4 0.0 collective-permute-done.7.refs_1_
  103.4 2.9 %place.5.refs_2_ = f32[2,2,128,2048]{3,2,1,0:T(8,128)} custom-call(s32[1]{0:T(128)} %bitcast.4.mine_ref, s32[1]{0:T(128)} %bitcast.5.spot_ref, f32[256,2048]{1,0:T(8,128)S(1)} %copy-done.2, bf16[256,2048]{1,0:T(8,128)(2,1)} %collective-permute-done.7.refs_1_), custom_call_target="tpu_custom_call" | custom-call | flops 1 | bytes 1 | tf_op jit(solution)/shard_map/place/pallas_call | solution.py:186
  106.3 0.0 collective-permute-done.6.refs_0_
  106.3 3.0 %fusion = (bf16[64,8192]{1,0:T(8,128)(2,1)}, bf16[64,8192]{1,0:T(8,128)(2,1)}) fusion(bf16[128,8192]{1,0:T(8,128)(2,1)} %collective-permute-done.6.refs_0_), kind=kLoop, calls=%fused_computation | loop fusion | bytes 4194304 | tf_op jit(solution)/shard_map/slice | solution.py:205
  109.4 0.0 collective-permute-start.8
  109.4 0.5 collective-permute-start.9
  109.9 13.4 %collective-permute-done.10.refs_1_ = bf16[256,2048]{1,0:T(8,128)(2,1)S(1)} collective-permute-done((bf16[256,2048]{1,0:T(8,128)(2,1)}, bf16[256,2048]{1,0:T(8,128)(2,1)S(1)}, u32[]{:S(2)}, u32[]{:S(2)}) %collective-permute-start.10) | collective-permute-done | bytes 1048608 | tf_op jit(solution)/shard_map/ppermute | solution.py:241
  123.2 1.6 copy-done.6
  124.9 0.0 collective-permute-done.9.refs_2_
  124.9 18.6 %multiply.7 = (f32[256,2048]{1,0:T(8,128)S(1)}, bf16[256,2048]{1,0:T(8,128)(2,1)}) custom-call(s32[1]{0:T(128)} %bitcast.2.core_ref, bf16[128,8192]{1,0:T(8,128)(2,1)} %collective-permute-done.6.refs_0_, bf16[64,8192]{1,0:T(8,128)(2,1)} %collective-permute-done.8.refs_1_, bf16[64,8192]{1,0:T(8,128)(2,1)} %collective-permute-done.9.refs_2_, ...), custom_call_target="tpu_custom_call" | custom-call | flops 1 | bytes 1 | tf_op jit(solution)/shard_map/multiply/pallas_call | solution.py:130
  143.5 6.0 %collective-permute-start.13 = (bf16[256,2048]{1,0:T(8,128)(2,1)}, bf16[256,2048]{1,0:T(8,128)(2,1)S(1)}, u32[]{:S(2)}, u32[]{:S(2)}) collective-permute-start(bf16[256,2048]{1,0:T(8,128)(2,1)} %get-tuple-element.36), channel_id=1, source_target_pairs={{0,1},{2,3},{4,5},{6,7},{9,8},{11,10},{13,12},{15,14},{16,17},{18,... | collective-permute-start | bytes 3145736 | tf_op jit(solution)/shard_map/ppermute | solution.py:241
  149.5 2.7 %fusion.2 = (bf16[48,8192]{1,0:T(8,128)(2,1)}, bf16[48,8192]{1,0:T(8,128)(2,1)}) fusion(bf16[96,8192]{1,0:T(8,128)(2,1)} %collective-permute-done.5.refs_0_), kind=kLoop, calls=%fused_computation.2 | loop fusion | bytes 3145728 | tf_op jit(solution)/shard_map/slice | solution.py:205
  152.2 0.0 collective-permute-start.11
  152.2 0.5 collective-permute-start.12
  152.7 0.9 slice.24
  153.6 0.0 collective-permute-start.4
  153.6 1.2 collective-permute-done.11.refs_1_
  154.8 1.1 collective-permute-done.12.refs_2_
  156.0 20.2 %multiply.8 = (f32[192,2048]{1,0:T(8,128)S(1)}, bf16[192,2048]{1,0:T(8,128)(2,1)}) custom-call(s32[1]{0:T(128)} %bitcast.2.core_ref, bf16[96,8192]{1,0:T(8,128)(2,1)} %collective-permute-done.5.refs_0_, bf16[48,8192]{1,0:T(8,128)(2,1)} %collective-permute-done.11.refs_1_, bf16[48,8192]{1,0:T(8,128)(2,1)} %collective-permute-done.12.refs_2_, ...), custom_call_target="tpu_custom_call" | custom-call | flops 1 | bytes 1 | tf_op jit(solution)/shard_map/multiply/pallas_call | solution.py:130
  176.2 1.3 collective-permute-start.16
  177.5 0.0 collective-permute-done.13.refs_1_
  177.6 0.0 collective-permute-done.4.refs_0_
  177.6 0.2 collective-permute-start.14
  177.8 1.8 collective-permute-done.14.refs_1_
  179.6 14.0 %multiply.9 = (f32[64,2048]{1,0:T(8,128)S(1)}, bf16[64,2048]{1,0:T(8,128)(2,1)S(1)}) custom-call(s32[1]{0:T(128)} %bitcast.2.core_ref, bf16[32,8192]{1,0:T(8,128)(2,1)S(1)} %collective-permute-done.4.refs_0_, bf16[32,8192]{1,0:T(8,128)(2,1)S(1)} %collective-permute-done.14.refs_1_, f32[1,8192]{1,0:T(1,128)S(1)} %bitcast.15, ...), custom_call_target="tpu_custom_call" | custom-call | flops 1 | bytes 1 | tf_op jit(solution)/shard_map/multiply/pallas_call | solution.py:130
  193.5 1.3 collective-permute-start.15
  194.9 3.1 %collective-permute-done.16.refs_1_ = bf16[192,2048]{1,0:T(8,128)(2,1)} collective-permute-done((bf16[192,2048]{1,0:T(8,128)(2,1)}, bf16[192,2048]{1,0:T(8,128)(2,1)}, u32[]{:S(2)}, u32[]{:S(2)}) %collective-permute-start.16) | collective-permute-done | bytes 786464 | tf_op jit(solution)/shard_map/ppermute | solution.py:241
  198.0 2.5 %place.8.refs_2_ = f32[2,2,128,2048]{3,2,1,0:T(8,128)} custom-call(s32[1]{0:T(128)} %bitcast.mine_ref, s32[1]{0:T(128)} %bitcast.1.spot_ref, f32[192,2048]{1,0:T(8,128)S(1)} %get-tuple-element.38.refs_0_, bf16[192,2048]{1,0:T(8,128)(2,1)} %collective-permute-done.16.refs_1_, f32[2,2,128,2048]{3,2,1,0:T(8,128)} %place.7.refs_2_), custom_call_target="tpu_custom_call", output_to_operand_aliasing={{}: (4, {})} | custom-call | flops 1 | bytes 1 | tf_op jit(solution)/shard_map/place/pallas_call | solution.py:186
  200.5 6.1 %collective-permute-done.15.refs_1_ = bf16[64,2048]{1,0:T(8,128)(2,1)S(1)} collective-permute-done((bf16[64,2048]{1,0:T(8,128)(2,1)S(1)}, bf16[64,2048]{1,0:T(8,128)(2,1)S(1)}, u32[]{:S(2)}, u32[]{:S(2)}) %collective-permute-start.15) | collective-permute-done | bytes 262176 | tf_op jit(solution)/shard_map/ppermute | solution.py:241
  206.6 0.9 place.9
  (19 shorter events, 0.1 us)
Async XLA Ops:
  0.0 51.0 %collective-permute-start = (bf16[128,8192]{1,0:T(8,128)(2,1)}, bf16[128,8192]{1,0:T(8,128)(2,1)}, u32[]{:S(2)}, u32[]{:S(2)}) collective-permute-start(bf16[128,8192]{1,0:T(8,128)(2,1)} %refs_0_), channel_id=1, source_target_pairs={{0,4},{2,6},{4,8},{6,10},{8,12},{10,14},{12,0},{14,2},{1,5},{3,7},... | collective-permute-start | bytes 6291464 | tf_op jit(solution)/shard_map/ppermute | solution.py:227
  3.0 51.5 %collective-permute-start.1 = (bf16[128,8192]{1,0:T(8,128)(2,1)}, bf16[128,8192]{1,0:T(8,128)(2,1)}, u32[]{:S(2)}, u32[]{:S(2)}) collective-permute-start(bf16[128,8192]{1,0:T(8,128)(2,1)} %refs_0_), channel_id=1, source_target_pairs={{0,2},{2,0},{4,6},{6,4},{8,10},{10,8},{12,14},{14,12},{1,3},{3,1},... | collective-permute-start | bytes 6291464 | tf_op jit(solution)/shard_map/ppermute | solution.py:231
  34.5 20.1 %copy-start = (bf16[128,8192]{1,0:T(8,128)(2,1)S(1)}, bf16[128,8192]{1,0:T(8,128)(2,1)}, u32[]{:S(2)}) copy-start(bf16[128,8192]{1,0:T(8,128)(2,1)} %refs_0_) | copy-start | bytes 6291460
  34.5 20.1 %copy-start.7 = (f32[8192]{0:T(1024)S(1)}, f32[8192]{0:T(1024)}, u32[]{:S(2)}) copy-start(f32[8192]{0:T(1024)} %param.7) | copy-start | bytes 98308
  51.0 55.3 %collective-permute-start.6 = (bf16[128,8192]{1,0:T(8,128)(2,1)}, bf16[128,8192]{1,0:T(8,128)(2,1)}, u32[]{:S(2)}, u32[]{:S(2)}) collective-permute-start(bf16[128,8192]{1,0:T(8,128)(2,1)} %collective-permute-done.refs_0_), channel_id=1, source_target_pairs={{0,4},{2,6},{4,8},{6,10},{8,12},{10,14},{12,0},{14,2},{1,5},{3,7},... | collective-permute-start | bytes 6291464 | tf_op jit(solution)/shard_map/ppermute | solution.py:227
  54.1 22.6 %collective-permute-start.2 = (bf16[64,8192]{1,0:T(8,128)(2,1)}, bf16[64,8192]{1,0:T(8,128)(2,1)S(1)}, u32[]{:S(2)}, u32[]{:S(2)}) collective-permute-start(bf16[64,8192]{1,0:T(8,128)(2,1)} %get-tuple-element.46), channel_id=1, source_target_pairs={{0,2},{2,0},{4,6},{6,4},{8,10},{10,8},{12,14},{14,12},{1,3},{3,1},... | collective-permute-start | bytes 3145736 | tf_op jit(solution)/shard_map/ppermute | solution.py:231
  54.1 22.6 %collective-permute-start.3 = (bf16[64,8192]{1,0:T(8,128)(2,1)}, bf16[64,8192]{1,0:T(8,128)(2,1)}, u32[]{:S(2)}, u32[]{:S(2)}) collective-permute-start(bf16[64,8192]{1,0:T(8,128)(2,1)} %get-tuple-element.45), channel_id=1, source_target_pairs={{0,2},{2,0},{4,6},{6,4},{8,10},{10,8},{12,14},{14,12},{1,3},{3,1},... | collective-permute-start | bytes 3145736 | tf_op jit(solution)/shard_map/ppermute | solution.py:231
  72.7 1.3 copy-start.1
  74.1 29.3 %collective-permute-start.7 = (bf16[256,2048]{1,0:T(8,128)(2,1)}, bf16[256,2048]{1,0:T(8,128)(2,1)}, u32[]{:S(2)}, u32[]{:S(2)}) collective-permute-start(bf16[256,2048]{1,0:T(8,128)(2,1)} %get-tuple-element.27), channel_id=1, source_target_pairs={{1,0},{3,2},{5,4},{7,6},{8,9},{10,11},{12,13},{14,15},{17,16},{19,... | collective-permute-start | bytes 3145736 | tf_op jit(solution)/shard_map/ppermute | solution.py:241
  76.7 26.8 %copy-start.2 = (f32[256,2048]{1,0:T(8,128)S(1)}, f32[256,2048]{1,0:T(8,128)}, u32[]{:S(2)}) copy-start(f32[256,2048]{1,0:T(8,128)} %copy-done.1) | copy-start | bytes 6291460
  95.1 11.2 %copy-start.5 = (f32[256,2048]{1,0:T(8,128)}, f32[256,2048]{1,0:T(8,128)S(1)}, u32[]{:S(2)}) copy-start(f32[256,2048]{1,0:T(8,128)S(1)} %get-tuple-element.29.refs_0_) | copy-start | bytes 6291460
  95.1 28.1 %collective-permute-start.10 = (bf16[256,2048]{1,0:T(8,128)(2,1)}, bf16[256,2048]{1,0:T(8,128)(2,1)S(1)}, u32[]{:S(2)}, u32[]{:S(2)}) collective-permute-start(bf16[256,2048]{1,0:T(8,128)(2,1)} %get-tuple-element.30), channel_id=1, source_target_pairs={{0,1},{2,3},{5,4},{7,6},{9,8},{11,10},{12,13},{14,15},{16,17},{18,... | collective-permute-start | bytes 3145736 | tf_op jit(solution)/shard_map/ppermute | solution.py:241
  100.7 48.9 %collective-permute-start.5 = (bf16[96,8192]{1,0:T(8,128)(2,1)}, bf16[96,8192]{1,0:T(8,128)(2,1)}, u32[]{:S(2)}, u32[]{:S(2)}) collective-permute-start(bf16[96,8192]{1,0:T(8,128)(2,1)} %slice.27), channel_id=1, source_target_pairs={{0,12},{2,14},{4,0},{6,2},{8,4},{10,6},{12,8},{14,10},{1,13},{3,15... | collective-permute-start | bytes 4718600 | tf_op jit(solution)/shard_map/ppermute | solution.py:227
  109.4 15.5 %collective-permute-start.8 = (bf16[64,8192]{1,0:T(8,128)(2,1)}, bf16[64,8192]{1,0:T(8,128)(2,1)}, u32[]{:S(2)}, u32[]{:S(2)}) collective-permute-start(bf16[64,8192]{1,0:T(8,128)(2,1)} %get-tuple-element.44), channel_id=1, source_target_pairs={{0,2},{2,0},{4,6},{6,4},{8,10},{10,8},{12,14},{14,12},{1,3},{3,1},... | collective-permute-start | bytes 3145736 | tf_op jit(solution)/shard_map/ppermute | solution.py:231
  109.4 15.5 %collective-permute-start.9 = (bf16[64,8192]{1,0:T(8,128)(2,1)}, bf16[64,8192]{1,0:T(8,128)(2,1)}, u32[]{:S(2)}, u32[]{:S(2)}) collective-permute-start(bf16[64,8192]{1,0:T(8,128)(2,1)} %get-tuple-element.43), channel_id=1, source_target_pairs={{0,2},{2,0},{4,6},{6,4},{8,10},{10,8},{12,14},{14,12},{1,3},{3,1},... | collective-permute-start | bytes 3145736 | tf_op jit(solution)/shard_map/ppermute | solution.py:231
  123.2 1.6 copy-start.6
  143.5 10.1 %copy-start.3 = (f32[256,2048]{1,0:T(8,128)}, f32[256,2048]{1,0:T(8,128)S(1)}, u32[]{:S(2)}) copy-start(f32[256,2048]{1,0:T(8,128)S(1)} %get-tuple-element.35.refs_0_) | copy-start | bytes 6291460
  143.5 34.0 %collective-permute-start.13 = (bf16[256,2048]{1,0:T(8,128)(2,1)}, bf16[256,2048]{1,0:T(8,128)(2,1)S(1)}, u32[]{:S(2)}, u32[]{:S(2)}) collective-permute-start(bf16[256,2048]{1,0:T(8,128)(2,1)} %get-tuple-element.36), channel_id=1, source_target_pairs={{0,1},{2,3},{4,5},{6,7},{9,8},{11,10},{13,12},{15,14},{16,17},{18,... | collective-permute-start | bytes 3145736 | tf_op jit(solution)/shard_map/ppermute | solution.py:241
  152.2 2.6 %collective-permute-start.11 = (bf16[48,8192]{1,0:T(8,128)(2,1)}, bf16[48,8192]{1,0:T(8,128)(2,1)}, u32[]{:S(2)}, u32[]{:S(2)}) collective-permute-start(bf16[48,8192]{1,0:T(8,128)(2,1)} %get-tuple-element.48), channel_id=1, source_target_pairs={{0,2},{2,0},{4,6},{6,4},{8,10},{10,8},{12,14},{14,12},{1,3},{3,1},... | collective-permute-start | bytes 2359304 | tf_op jit(solution)/shard_map/ppermute | solution.py:231
  152.2 3.7 %collective-permute-start.12 = (bf16[48,8192]{1,0:T(8,128)(2,1)}, bf16[48,8192]{1,0:T(8,128)(2,1)}, u32[]{:S(2)}, u32[]{:S(2)}) collective-permute-start(bf16[48,8192]{1,0:T(8,128)(2,1)} %get-tuple-element.47), channel_id=1, source_target_pairs={{0,2},{2,0},{4,6},{6,4},{8,10},{10,8},{12,14},{14,12},{1,3},{3,1},... | collective-permute-start | bytes 2359304 | tf_op jit(solution)/shard_map/ppermute | solution.py:231
  153.6 24.0 %collective-permute-start.4 = (bf16[32,8192]{1,0:T(8,128)(2,1)}, bf16[32,8192]{1,0:T(8,128)(2,1)S(1)}, u32[]{:S(2)}, u32[]{:S(2)}) collective-permute-start(bf16[32,8192]{1,0:T(8,128)(2,1)} %slice.24), channel_id=1, source_target_pairs={{0,12},{2,14},{4,0},{6,2},{8,4},{10,6},{12,8},{14,10},{1,13},{3,15... | collective-permute-start | bytes 1572872 | tf_op jit(solution)/shard_map/ppermute | solution.py:227
  153.6 23.9 %copy-start.4 = (f32[256,2048]{1,0:T(8,128)S(1)}, f32[256,2048]{1,0:T(8,128)}, u32[]{:S(2)}) copy-start(f32[256,2048]{1,0:T(8,128)} %copy-done.3) | copy-start | bytes 6291460
  176.2 21.8 %collective-permute-start.16 = (bf16[192,2048]{1,0:T(8,128)(2,1)}, bf16[192,2048]{1,0:T(8,128)(2,1)}, u32[]{:S(2)}, u32[]{:S(2)}) collective-permute-start(bf16[192,2048]{1,0:T(8,128)(2,1)} %get-tuple-element.39), channel_id=1, source_target_pairs={{1,0},{3,2},{4,5},{6,7},{8,9},{10,11},{13,12},{15,14},{17,16},{19,... | collective-permute-start | bytes 2359304 | tf_op jit(solution)/shard_map/ppermute | solution.py:241
  177.6 2.0 collective-permute-start.14
  193.5 13.1 %collective-permute-start.15 = (bf16[64,2048]{1,0:T(8,128)(2,1)S(1)}, bf16[64,2048]{1,0:T(8,128)(2,1)S(1)}, u32[]{:S(2)}, u32[]{:S(2)}) collective-permute-start(bf16[64,2048]{1,0:T(8,128)(2,1)S(1)} %get-tuple-element.42), channel_id=1, source_target_pairs={{1,0},{3,2},{4,5},{6,7},{8,9},{10,11},{13,12},{15,14},{17,16},{19,... | collective-permute-start | bytes 786440 | tf_op jit(solution)/shard_map/ppermute | solution.py:241

commit v7 on v6

--- a/solution.py
+++ b/solution.py
@@ -17,33 +17,74 @@
 small = pl.CostEstimate(flops=1, bytes_accessed=1, transcendentals=0)
 
 
-def dequantize_kernel(codes_ref, exps_ref, train_ref):
+def first_kernel(core_ref, mine_ref, other_ref, fisher_ref, codes_ref, exps_ref, train_ref, keep_ref,
+                 send_ref, left, spread):
+    rows, width = mine_ref.shape
+    depth = min(width, 1024)
+    core = core_ref[0]
+
+    @pl.when(pl.program_id(0) == 0)
+    def _():
+        block = lax.broadcasted_iota(jnp.int32, spread.shape, 0)
+        col = lax.broadcasted_iota(jnp.int32, spread.shape, 1)
+        spread[...] = jnp.where(col // lanes == block, 1.0, 0.0).astype(jnp.bfloat16)
+        for ref, place in ((mine_ref, core), (other_ref, 1 - core)):
+            spot = pl.ds(pl.multiple_of(place * rows, rows), rows)
+            for start in range(0, width, depth):
+                cols = slice(start, start + depth)
+                scale = 1.0 / (fisher_ref[:, cols] + damping)
+                left[spot, cols] = (ref[:, cols].astype(jnp.float32) * scale).astype(jnp.bfloat16)
+
     exps = exps_ref[...]
     up = jnp.left_shift(1, jnp.maximum(exps, 0)).astype(jnp.float32)
     down = jnp.left_shift(1, jnp.maximum(-exps, 0)).astype(jnp.float32)
-    factor = up / down
-    for block in range(exps.shape[1]):
-        cols = slice(block * lanes, (block + 1) * lanes)
-        codes = codes_ref[:, cols].astype(jnp.float32)
-        train_ref[:, cols] = (codes * factor[:, block:block + 1]).astype(jnp.bfloat16)
-
-
-def dequantize(codes, exps):
-    count, width = codes.shape
-    rows = min(count, 256)
+    factor = (up / down).astype(jnp.bfloat16)
+    for start in range(0, width, depth):
+        cols = slice(start, start + depth)
+        wide = jnp.dot(factor, spread[:, cols], preferred_element_type=jnp.float32)
+        train_ref[:, cols] = codes_ref[:, cols] * wide.astype(jnp.bfloat16)
+    sums = lax.dot_general(
+        left[...], train_ref[...], (((1,), (1,)), ((), ())), preferred_element_type=jnp.float32
+    )
+    keep_ref[...] = sums
+    send_ref[...] = sums.astype(jnp.bfloat16)
+
+
+def first(core, mine, other, fisher, codes, exps):
+    rows, width = mine.shape
+    count = codes.shape[0]
+    blocks = width // lanes
+    tile = min(count, 256)
+    shape = (cores * rows, count)
     return pl.pallas_call(
-        dequantize_kernel,
-        grid=(count // rows,),
+        first_kernel,
+        grid=(count // tile,),
         in_specs=[
-            pl.BlockSpec((rows, width), lambda i: (i, 0)),
-            pl.BlockSpec((rows, width // lanes), lambda i: (i, 0)),
-        ],
-        out_specs=pl.BlockSpec((rows, width), lambda i: (i, 0)),
-        out_shape=jax.ShapeDtypeStruct((count, width), jnp.bfloat16),
-        compiler_params=pltpu.CompilerParams(vmem_limit_bytes=32 * mib),
+            in_smem,
+            pl.BlockSpec((rows, width), lambda i: (0, 0)),
+            pl.BlockSpec((rows, width), lambda i: (0, 0)),
+            pl.BlockSpec((1, width), lambda i: (0, 0)),
+            pl.BlockSpec((tile, width), lambda i: (i, 0)),
+            pl.BlockSpec((tile, blocks), lambda i: (i, 0)),
+        ],
+        out_specs=[
+            pl.BlockSpec((tile, width), lambda i: (i, 0)),
+            pl.BlockSpec((cores * rows, tile), lambda i: (0, i)),
+            pl.BlockSpec((cores * rows, tile), lambda i: (0, i)),
+        ],
+        out_shape=[
+            jax.ShapeDtypeStruct((count, width), jnp.bfloat16),
+            jax.ShapeDtypeStruct(shape, jnp.float32),
+            jax.ShapeDtypeStruct(shape, jnp.bfloat16),
+        ],
+        scratch_shapes=[
+            pltpu.VMEM((cores * rows, width), jnp.bfloat16),
+            pltpu.VMEM((blocks, width), jnp.bfloat16),
+        ],
+        compiler_params=pltpu.CompilerParams(vmem_limit_bytes=40 * mib),
         cost_estimate=small,
-        name="dequantize",
-    )(codes, exps)
+        name="first",
+    )(core, mine, other, fisher, codes, exps)
 
 
 def multiply_kernel(core_ref, *refs):
@@ -249,24 +290,22 @@
     halves = [(0, own // 2), (own // 2, own)]
 
     arriving = shift(val_grads, 1)
-    beside = swap([val_grads])
-    train = dequantize(grad_codes, scale_exps)
-    scores, part, pending = None, train, []
+    train, *part = first(core, val_grads, *swap([val_grads]), fisher, grad_codes, scale_exps)
+    scores, pending = None, [(part, 0, 0)]
     for index, by in enumerate(order[:-1]):
-        panel = after(arriving, part, *([] if scores is None else [scores]))
-        if index == 0:
-            part = multiply(core, after(val_grads, panel), beside, fisher, train)
-            pending.append((part, 0, 0))
-        following = order[index + 1]
-        source = panel if abs(following) > 1 else val_grads
-        parts = swap(cut(panel, halves))
-        if index + 2 < len(order):
-            arriving = shift(source, 1 if following > 0 else -1)
-        done = part
-        part = multiply(core, after(panel, part), parts, fisher, train)
-        if index + 2 == len(order):
-            arriving = [shift(after(piece, done), 1 if following > 0 else -1) for piece in cut(source, pieces)]
-        scores = collect(scores, *pending.pop())
+        last = index + 2 == len(order)
+        following = 1 if order[index + 1] > 0 else -1
+        if last:
+            scores = collect(scores, *pending.pop())
+        panel = after(arriving, part)
+        source = panel if abs(order[index + 1]) > 1 else val_grads
+        if last:
+            arriving = [shift(after(piece, scores), following) for piece in cut(source, pieces)]
+        else:
+            arriving = shift(source, following)
+        part = multiply(core, panel, swap(cut(panel, halves)), fisher, train)
+        if not last:
+            scores = collect(scores, *pending.pop())
         pending.append((part, by, 0))
     by = order[-1]
     for (low, high), panel in zip(pieces, arriving):

time: 208 us -> 209 us (level)
  Pallas kernels: 126 us -> 98 us
  waiting for transfers between devices: 43.2 us -> 64.1 us
  starting transfers between devices: 23 us -> 27.6 us
  local copies, waits for them, and re-layouts: 15.2 us -> 18.6 us
    pallas_call x5 -> x4, Pallas kernels: 89.4 us -> 62.8 us  [multiply(): pl.pallas_call(multiply_kernel, in_specs=[in_smem] + [anywhere] * (1 + le...]
    ppermute x5, waiting for transfers between devices: 22.6 us -> 33.1 us  [collect(): received.append(lax.ppermute(send, ('blk', 'dim'), pairs))]
    ppermute x4, starting transfers between devices: 5.78 us -> 13.4 us  [shift(): return lax.ppermute(panel, 'blk', pairs)]
    unnamed x17 -> x31, local copies, waits for them, and re-layouts: 4.3 us -> 11.7 us
    ppermute x4, waiting for transfers between devices: 16.5 us -> 22.8 us  [shift(): return lax.ppermute(panel, 'blk', pairs)]
    ppermute x8, waiting for transfers between devices: 4.16 us -> 8.16 us  [swap(): return [lax.ppermute(part, 'blk', pairs) for part in parts]]
    slice x5, local copies, waits for them, and re-layouts: 10.9 us -> 6.89 us  [cut(): return [whole[low:high] for low, high in cuts]]
    ppermute x5, starting transfers between devices: 15.4 us -> 12.1 us  [collect(): received.append(lax.ppermute(send, ('blk', 'dim'), pairs))]
  transfers between devices with their start and end apart: 17 -> 17, of which waited for: 7 -> 12; matrix products, arithmetic and copies ran while one was open for 6% -> 3% of each run, Pallas kernels for 60% -> 47%
where the time goes in v7:
time: 209 us
  Pallas kernels  98 us (47%)
  waiting for transfers between devices  64.1 us (31%)
  starting transfers between devices  27.6 us (13%)
  local copies, waits for them, and re-layouts  18.6 us (9%)
    pallas_call x4, Pallas kernels, multiply(): pl.pallas_call(multiply_kernel, in_specs=[in_smem] + [anywhere] * (1 + le...  62.8 us
    ppermute x5, waiting for transfers between devices, collect(): received.append(lax.ppermute(send, ('blk', 'dim'), pairs))  33.1 us
    pallas_call x1, Pallas kernels, first(): pl.pallas_call(first_kernel, grid=(count // tile,), in_specs=[in_smem, pl...  29.7 us
    ppermute x4, waiting for transfers between devices, shift(): return lax.ppermute(panel, 'blk', pairs)  22.8 us
    ppermute x4, starting transfers between devices, shift(): return lax.ppermute(panel, 'blk', pairs)  13.4 us
    ppermute x5, starting transfers between devices, collect(): received.append(lax.ppermute(send, ('blk', 'dim'), pairs))  12.1 us
    unnamed x31, local copies, waits for them, and re-layouts  11.7 us
    ppermute x8, waiting for transfers between devices, swap(): return [lax.ppermute(part, 'blk', pairs) for part in parts]  8.16 us
  transfers between devices with their start and end apart: 17, of which 12 were waited for; matrix products, arithmetic and copies ran while one was open for 3% of the time, Pallas kernels for 47%

profile of v7, /device:TPU:0, one launch (start us, length us, event | category | flops | bytes accessed | tf_op | source)
XLA Modules:
  0.0 208.6 jit_solution(6212031165413436436)
XLA Ops:
  0.0 0.5 collective-permute-start.1
  0.5 2.6 %collective-permute-start = (bf16[128,8192]{1,0:T(8,128)(2,1)}, bf16[128,8192]{1,0:T(8,128)(2,1)}, u32[]{:S(2)}, u32[]{:S(2)}) collective-permute-start(bf16[128,8192]{1,0:T(8,128)(2,1)} %mine_ref.1), channel_id=1, source_target_pairs={{0,4},{2,6},{4,8},{6,10},{8,12},{10,14},{12,0},{14,2},{1,5},{3,7},... | collective-permute-start | bytes 6291464 | tf_op jit(solution)/shard_map/ppermute | solution.py:268
  3.0 1.4 copy.9.exps_ref
  4.5 1.6 copy-done
  6.0 0.8 copy-done.10
  6.8 29.7 %first.1 = (bf16[2048,8192]{1,0:T(8,128)(2,1)}, f32[256,2048]{1,0:T(8,128)S(1)}, bf16[256,2048]{1,0:T(8,128)(2,1)}) custom-call(s32[1]{0:T(128)} %bitcast.2.core_ref, bf16[128,8192]{1,0:T(8,128)(2,1)S(1)} %copy-done, bf16[128,8192]{1,0:T(8,128)(2,1)S(1)} %collective-permute-done.1.other_ref, f32[1,8192]{1,0:T(1,128)S(1)} %bitcast.11, ...), custom_call_target="tpu_custom_call" | custom-call | flops 1 | bytes 1 | tf_op jit(solution)/shard_map/first/pallas_call | solution.py:59
  36.5 15.1 %collective-permute-done.refs_0_ = bf16[128,8192]{1,0:T(8,128)(2,1)} collective-permute-done((bf16[128,8192]{1,0:T(8,128)(2,1)}, bf16[128,8192]{1,0:T(8,128)(2,1)}, u32[]{:S(2)}, u32[]{:S(2)}) %collective-permute-start) | collective-permute-done | bytes 2097184 | tf_op jit(solution)/shard_map/ppermute | solution.py:268
  51.7 1.7 fusion.1
  53.4 0.1 collective-permute-start.2
  53.5 0.5 collective-permute-start.3
  54.0 1.3 collective-permute-start.5
  55.3 0.9 collective-permute-done.2.refs_1_
  56.1 1.5 collective-permute-done.3.refs_2_
  57.6 14.5 %multiply.4 = (f32[256,2048]{1,0:T(8,128)S(1)}, bf16[256,2048]{1,0:T(8,128)(2,1)}) custom-call(s32[1]{0:T(128)} %bitcast.2.core_ref, bf16[128,8192]{1,0:T(8,128)(2,1)} %collective-permute-done.refs_0_, bf16[64,8192]{1,0:T(8,128)(2,1)S(1)} %collective-permute-done.2.refs_1_, bf16[64,8192]{1,0:T(8,128)(2,1)S(1)} %collective-permute-done.3.refs_2_, ...), custom_call_target="tpu_custom_call" | custom-call | flops 1 | bytes 1 | tf_op jit(solution)/shard_map/multiply/pallas_call | solution.py:171
  72.1 1.3 copy-done.6
  73.4 3.5 %collective-permute-start.4 = (bf16[256,2048]{1,0:T(8,128)(2,1)}, bf16[256,2048]{1,0:T(8,128)(2,1)S(1)}, u32[]{:S(2)}, u32[]{:S(2)}) collective-permute-start(bf16[256,2048]{1,0:T(8,128)(2,1)} %get-tuple-element.27), channel_id=1, source_target_pairs={{0,1},{2,3},{5,4},{7,6},{9,8},{11,10},{12,13},{14,15},{16,17},{18,... | collective-permute-start | bytes 3145736 | tf_op jit(solution)/shard_map/ppermute | solution.py:282
  77.0 1.3 slice.27
  78.2 3.1 %collective-permute-done.5.refs_1_ = bf16[256,2048]{1,0:T(8,128)(2,1)} collective-permute-done((bf16[256,2048]{1,0:T(8,128)(2,1)}, bf16[256,2048]{1,0:T(8,128)(2,1)}, u32[]{:S(2)}, u32[]{:S(2)}) %collective-permute-start.5) | collective-permute-done | bytes 1048608 | tf_op jit(solution)/shard_map/ppermute | solution.py:282
  81.3 1.6 copy-done.5
  82.9 3.0 %place.5.refs_2_ = f32[2,2,128,2048]{3,2,1,0:T(8,128)} custom-call(s32[1]{0:T(128)} %bitcast.6.mine_ref, s32[1]{0:T(128)} %bitcast.7.spot_ref, f32[256,2048]{1,0:T(8,128)S(1)} %copy-done.5, bf16[256,2048]{1,0:T(8,128)(2,1)} %collective-permute-done.5.refs_1_), custom_call_target="tpu_custom_call" | custom-call | flops 1 | bytes 1 | tf_op jit(solution)/shard_map/place/pallas_call | solution.py:227
  85.9 13.9 %collective-permute-done.4.refs_1_ = bf16[256,2048]{1,0:T(8,128)(2,1)S(1)} collective-permute-done((bf16[256,2048]{1,0:T(8,128)(2,1)}, bf16[256,2048]{1,0:T(8,128)(2,1)S(1)}, u32[]{:S(2)}, u32[]{:S(2)}) %collective-permute-start.4) | collective-permute-done | bytes 1048608 | tf_op jit(solution)/shard_map/ppermute | solution.py:282
  99.9 1.4 copy-done.14
  101.3 6.5 %collective-permute-start.7 = (bf16[96,8192]{1,0:T(8,128)(2,1)S(1)}, bf16[96,8192]{1,0:T(8,128)(2,1)S(1)}, u32[]{:S(2)}, u32[]{:S(2)}) collective-permute-start(bf16[96,8192]{1,0:T(8,128)(2,1)S(1)} %copy-done.14), channel_id=1, source_target_pairs={{0,12},{2,14},{4,0},{6,2},{8,4},{10,6},{12,8},{14,10},{1,13},{3,15... | collective-permute-start | bytes 4718600 | tf_op jit(solution)/shard_map/ppermute | solution.py:268
  107.8 1.7 fusion
  109.5 0.1 collective-permute-start.9
  109.6 0.5 collective-permute-start.10
  110.0 2.1 %collective-permute-done.9.refs_1_ = bf16[64,8192]{1,0:T(8,128)(2,1)S(1)} collective-permute-done((bf16[64,8192]{1,0:T(8,128)(2,1)S(1)}, bf16[64,8192]{1,0:T(8,128)(2,1)S(1)}, u32[]{:S(2)}, u32[]{:S(2)}) %collective-permute-start.9) | collective-permute-done | bytes 1048608 | tf_op jit(solution)/shard_map/ppermute | solution.py:272
  112.2 1.5 collective-permute-done.10.refs_2_
  113.7 14.4 %multiply.5 = (f32[256,2048]{1,0:T(8,128)S(1)}, bf16[256,2048]{1,0:T(8,128)(2,1)}) custom-call(s32[1]{0:T(128)} %bitcast.2.core_ref, bf16[128,8192]{1,0:T(8,128)(2,1)} %collective-permute-done.8.refs_0_, bf16[64,8192]{1,0:T(8,128)(2,1)S(1)} %collective-permute-done.9.refs_1_, bf16[64,8192]{1,0:T(8,128)(2,1)S(1)} %collective-permute-done.10.refs_2_, ...), custom_call_target="tpu_custom_call" | custom-call | flops 1 | bytes 1 | tf_op jit(solution)/shard_map/multiply/pallas_call | solution.py:171
  128.1 4.7 %collective-permute-start.13 = (bf16[256,2048]{1,0:T(8,128)(2,1)}, bf16[256,2048]{1,0:T(8,128)(2,1)S(1)}, u32[]{:S(2)}, u32[]{:S(2)}) collective-permute-start(bf16[256,2048]{1,0:T(8,128)(2,1)} %get-tuple-element.32), channel_id=1, source_target_pairs={{0,1},{2,3},{4,5},{6,7},{9,8},{11,10},{13,12},{15,14},{16,17},{18,... | collective-permute-start | bytes 3145736 | tf_op jit(solution)/shard_map/ppermute | solution.py:282
  132.8 7.7 %collective-permute-done.7.refs_0_ = bf16[96,8192]{1,0:T(8,128)(2,1)S(1)} collective-permute-done((bf16[96,8192]{1,0:T(8,128)(2,1)S(1)}, bf16[96,8192]{1,0:T(8,128)(2,1)S(1)}, u32[]{:S(2)}, u32[]{:S(2)}) %collective-permute-start.7) | collective-permute-done | bytes 1572896 | tf_op jit(solution)/shard_map/ppermute | solution.py:268
  140.5 1.4 fusion.2
  141.9 0.5 collective-permute-start.12
  142.4 0.8 slice.24
  143.3 4.3 %collective-permute-start.6 = (bf16[32,8192]{1,0:T(8,128)(2,1)}, bf16[32,8192]{1,0:T(8,128)(2,1)}, u32[]{:S(2)}, u32[]{:S(2)}) collective-permute-start(bf16[32,8192]{1,0:T(8,128)(2,1)} %slice.24), channel_id=1, source_target_pairs={{0,12},{2,14},{4,0},{6,2},{8,4},{10,6},{12,8},{14,10},{1,13},{3,15... | collective-permute-start | bytes 1572872 | tf_op jit(solution)/shard_map/ppermute | solution.py:268
  147.6 8.2 %collective-permute-done.13.refs_1_ = bf16[256,2048]{1,0:T(8,128)(2,1)S(1)} collective-permute-done((bf16[256,2048]{1,0:T(8,128)(2,1)}, bf16[256,2048]{1,0:T(8,128)(2,1)S(1)}, u32[]{:S(2)}, u32[]{:S(2)}) %collective-permute-start.13) | collective-permute-done | bytes 1048608 | tf_op jit(solution)/shard_map/ppermute | solution.py:282
  155.8 1.6 copy-done.9
  157.4 1.3 copy-done.3
  158.8 19.9 %multiply.6 = (f32[192,2048]{1,0:T(8,128)S(1)}, bf16[192,2048]{1,0:T(8,128)(2,1)}) custom-call(s32[1]{0:T(128)} %bitcast.2.core_ref, bf16[96,8192]{1,0:T(8,128)(2,1)S(1)} %copy-done.3, bf16[48,8192]{1,0:T(8,128)(2,1)} %collective-permute-done.11.refs_1_, bf16[48,8192]{1,0:T(8,128)(2,1)} %collective-permute-done.12.refs_2_, f32[1,8192]{1,0:T(1,128)S(1)} %bitcast.14, ...), custom_call_target="tpu_custom_call" | custom-call | flops 1 | bytes 1 | tf_op jit(solution)/shard_map/multiply/pallas_call | solution.py:171
  178.7 1.3 collective-permute-start.16
  180.0 2.1 %collective-permute-done.14.refs_1_ = bf16[32,8192]{1,0:T(8,128)(2,1)S(1)} collective-permute-done((bf16[32,8192]{1,0:T(8,128)(2,1)}, bf16[32,8192]{1,0:T(8,128)(2,1)S(1)}, u32[]{:S(2)}, u32[]{:S(2)}) %collective-permute-start.14) | collective-permute-done | bytes 524320 | tf_op jit(solution)/shard_map/ppermute | solution.py:272
  182.1 14.1 %multiply.7 = (f32[64,2048]{1,0:T(8,128)S(1)}, bf16[64,2048]{1,0:T(8,128)(2,1)S(1)}) custom-call(s32[1]{0:T(128)} %bitcast.2.core_ref, bf16[32,8192]{1,0:T(8,128)(2,1)} %collective-permute-done.6.refs_0_, bf16[32,8192]{1,0:T(8,128)(2,1)S(1)} %collective-permute-done.14.refs_1_, f32[1,8192]{1,0:T(1,128)S(1)} %bitcast.15, ...), custom_call_target="tpu_custom_call" | custom-call | flops 1 | bytes 1 | tf_op jit(solution)/shard_map/multiply/pallas_call | solution.py:171
  196.2 0.8 copy-done.12
  197.0 1.3 collective-permute-start.15
  198.3 1.7 collective-permute-done.16.refs_1_
  200.0 1.5 place.8.refs_2_
  201.5 6.2 %collective-permute-done.15.refs_1_ = bf16[64,2048]{1,0:T(8,128)(2,1)S(1)} collective-permute-done((bf16[64,2048]{1,0:T(8,128)(2,1)S(1)}, bf16[64,2048]{1,0:T(8,128)(2,1)S(1)}, u32[]{:S(2)}, u32[]{:S(2)}) %collective-permute-start.15) | collective-permute-done | bytes 262176 | tf_op jit(solution)/shard_map/ppermute | solution.py:282
  207.7 0.9 place.9
  (32 shorter events, 0.2 us)
Async XLA Ops:
  0.0 4.5 %collective-permute-start.1 = (bf16[128,8192]{1,0:T(8,128)(2,1)}, bf16[128,8192]{1,0:T(8,128)(2,1)S(1)}, u32[]{:S(2)}, u32[]{:S(2)}) collective-permute-start(bf16[128,8192]{1,0:T(8,128)(2,1)} %mine_ref.1), channel_id=1, source_target_pairs={{0,2},{2,0},{4,6},{6,4},{8,10},{10,8},{12,14},{14,12},{1,3},{3,1},... | collective-permute-start | bytes 6291464 | tf_op jit(solution)/shard_map/ppermute | solution.py:272
  0.5 51.2 %collective-permute-start = (bf16[128,8192]{1,0:T(8,128)(2,1)}, bf16[128,8192]{1,0:T(8,128)(2,1)}, u32[]{:S(2)}, u32[]{:S(2)}) collective-permute-start(bf16[128,8192]{1,0:T(8,128)(2,1)} %mine_ref.1), channel_id=1, source_target_pairs={{0,4},{2,6},{4,8},{6,10},{8,12},{10,14},{12,0},{14,2},{1,5},{3,7},... | collective-permute-start | bytes 6291464 | tf_op jit(solution)/shard_map/ppermute | solution.py:268
  4.5 1.6 copy-start
  6.0 0.8 copy-start.10
  36.5 16.8 %copy-start.4 = (f32[256,2048]{1,0:T(8,128)}, f32[256,2048]{1,0:T(8,128)S(1)}, u32[]{:S(2)}) copy-start(f32[256,2048]{1,0:T(8,128)S(1)} %get-tuple-element.22.refs_0_) | copy-start | bytes 6291460
  53.4 2.7 %collective-permute-start.2 = (bf16[64,8192]{1,0:T(8,128)(2,1)S(1)}, bf16[64,8192]{1,0:T(8,128)(2,1)S(1)}, u32[]{:S(2)}, u32[]{:S(2)}) collective-permute-start(bf16[64,8192]{1,0:T(8,128)(2,1)S(1)} %get-tuple-element.42), channel_id=1, source_target_pairs={{0,2},{2,0},{4,6},{6,4},{8,10},{10,8},{12,14},{14,12},{1,3},{3,1},... | collective-permute-start | bytes 3145736 | tf_op jit(solution)/shard_map/ppermute | solution.py:272
  53.5 4.1 %collective-permute-start.3 = (bf16[64,8192]{1,0:T(8,128)(2,1)S(1)}, bf16[64,8192]{1,0:T(8,128)(2,1)S(1)}, u32[]{:S(2)}, u32[]{:S(2)}) collective-permute-start(bf16[64,8192]{1,0:T(8,128)(2,1)S(1)} %get-tuple-element.41), channel_id=1, source_target_pairs={{0,2},{2,0},{4,6},{6,4},{8,10},{10,8},{12,14},{14,12},{1,3},{3,1},... | collective-permute-start | bytes 3145736 | tf_op jit(solution)/shard_map/ppermute | solution.py:272
  54.0 53.8 %collective-permute-start.8 = (bf16[128,8192]{1,0:T(8,128)(2,1)}, bf16[128,8192]{1,0:T(8,128)(2,1)}, u32[]{:S(2)}, u32[]{:S(2)}) collective-permute-start(bf16[128,8192]{1,0:T(8,128)(2,1)} %collective-permute-done.refs_0_), channel_id=1, source_target_pairs={{0,4},{2,6},{4,8},{6,10},{8,12},{10,14},{12,0},{14,2},{1,5},{3,7},... | collective-permute-start | bytes 6291464 | tf_op jit(solution)/shard_map/ppermute | solution.py:268
  54.0 27.3 %collective-permute-start.5 = (bf16[256,2048]{1,0:T(8,128)(2,1)}, bf16[256,2048]{1,0:T(8,128)(2,1)}, u32[]{:S(2)}, u32[]{:S(2)}) collective-permute-start(bf16[256,2048]{1,0:T(8,128)(2,1)} %get-tuple-element.23), channel_id=1, source_target_pairs={{1,0},{3,2},{5,4},{7,6},{8,9},{10,11},{12,13},{14,15},{17,16},{19,... | collective-permute-start | bytes 3145736 | tf_op jit(solution)/shard_map/ppermute | solution.py:282
  57.6 19.3 %copy-start.1 = (bf16[128,8192]{1,0:T(8,128)(2,1)S(1)}, bf16[128,8192]{1,0:T(8,128)(2,1)}, u32[]{:S(2)}) copy-start(bf16[128,8192]{1,0:T(8,128)(2,1)} %mine_ref.1) | copy-start | bytes 6291460
  72.1 1.3 copy-start.6
  73.4 26.4 %collective-permute-start.4 = (bf16[256,2048]{1,0:T(8,128)(2,1)}, bf16[256,2048]{1,0:T(8,128)(2,1)S(1)}, u32[]{:S(2)}, u32[]{:S(2)}) collective-permute-start(bf16[256,2048]{1,0:T(8,128)(2,1)} %get-tuple-element.27), channel_id=1, source_target_pairs={{0,1},{2,3},{5,4},{7,6},{9,8},{11,10},{12,13},{14,15},{16,17},{18,... | collective-permute-start | bytes 3145736 | tf_op jit(solution)/shard_map/ppermute | solution.py:282
  81.3 1.6 copy-start.5
  82.9 16.9 %copy-start.7 = (f32[256,2048]{1,0:T(8,128)S(1)}, f32[256,2048]{1,0:T(8,128)}, u32[]{:S(2)}) copy-start(f32[256,2048]{1,0:T(8,128)} %copy-done.6) | copy-start | bytes 6291460
  99.9 1.4 copy-start.14
  101.3 12.4 %copy-start.11 = (f32[8192]{0:T(1024)S(1)}, f32[8192]{0:T(1024)}, u32[]{:S(2)}) copy-start(f32[8192]{0:T(1024)} %param.7) | copy-start | bytes 98308
  101.3 39.3 %collective-permute-start.7 = (bf16[96,8192]{1,0:T(8,128)(2,1)S(1)}, bf16[96,8192]{1,0:T(8,128)(2,1)S(1)}, u32[]{:S(2)}, u32[]{:S(2)}) collective-permute-start(bf16[96,8192]{1,0:T(8,128)(2,1)S(1)} %copy-done.14), channel_id=1, source_target_pairs={{0,12},{2,14},{4,0},{6,2},{8,4},{10,6},{12,8},{14,10},{1,13},{3,15... | collective-permute-start | bytes 4718600 | tf_op jit(solution)/shard_map/ppermute | solution.py:268
  109.5 2.7 %collective-permute-start.9 = (bf16[64,8192]{1,0:T(8,128)(2,1)S(1)}, bf16[64,8192]{1,0:T(8,128)(2,1)S(1)}, u32[]{:S(2)}, u32[]{:S(2)}) collective-permute-start(bf16[64,8192]{1,0:T(8,128)(2,1)S(1)} %get-tuple-element.40), channel_id=1, source_target_pairs={{0,2},{2,0},{4,6},{6,4},{8,10},{10,8},{12,14},{14,12},{1,3},{3,1},... | collective-permute-start | bytes 3145736 | tf_op jit(solution)/shard_map/ppermute | solution.py:272
  109.6 4.1 %collective-permute-start.10 = (bf16[64,8192]{1,0:T(8,128)(2,1)S(1)}, bf16[64,8192]{1,0:T(8,128)(2,1)S(1)}, u32[]{:S(2)}, u32[]{:S(2)}) collective-permute-start(bf16[64,8192]{1,0:T(8,128)(2,1)S(1)} %get-tuple-element.39), channel_id=1, source_target_pairs={{0,2},{2,0},{4,6},{6,4},{8,10},{10,8},{12,14},{14,12},{1,3},{3,1},... | collective-permute-start | bytes 3145736 | tf_op jit(solution)/shard_map/ppermute | solution.py:272
  128.1 15.2 %copy-start.8 = (f32[256,2048]{1,0:T(8,128)}, f32[256,2048]{1,0:T(8,128)S(1)}, u32[]{:S(2)}) copy-start(f32[256,2048]{1,0:T(8,128)S(1)} %get-tuple-element.31.refs_0_) | copy-start | bytes 6291460
  128.1 27.7 %collective-permute-start.13 = (bf16[256,2048]{1,0:T(8,128)(2,1)}, bf16[256,2048]{1,0:T(8,128)(2,1)S(1)}, u32[]{:S(2)}, u32[]{:S(2)}) collective-permute-start(bf16[256,2048]{1,0:T(8,128)(2,1)} %get-tuple-element.32), channel_id=1, source_target_pairs={{0,1},{2,3},{4,5},{6,7},{9,8},{11,10},{13,12},{15,14},{16,17},{18,... | collective-permute-start | bytes 3145736 | tf_op jit(solution)/shard_map/ppermute | solution.py:282
  140.5 2.8 %copy-start.2 = (bf16[96,8192]{1,0:T(8,128)(2,1)}, bf16[96,8192]{1,0:T(8,128)(2,1)S(1)}, u32[]{:S(2)}) copy-start(bf16[96,8192]{1,0:T(8,128)(2,1)S(1)} %collective-permute-done.7.refs_0_) | copy-start | bytes 4718596
  141.9 15.5 %collective-permute-start.11 = (bf16[48,8192]{1,0:T(8,128)(2,1)}, bf16[48,8192]{1,0:T(8,128)(2,1)}, u32[]{:S(2)}, u32[]{:S(2)}) collective-permute-start(bf16[48,8192]{1,0:T(8,128)(2,1)} %get-tuple-element.44), channel_id=1, source_target_pairs={{0,2},{2,0},{4,6},{6,4},{8,10},{10,8},{12,14},{14,12},{1,3},{3,1},... | collective-permute-start | bytes 2359304 | tf_op jit(solution)/shard_map/ppermute | solution.py:272
  141.9 15.5 %collective-permute-start.12 = (bf16[48,8192]{1,0:T(8,128)(2,1)}, bf16[48,8192]{1,0:T(8,128)(2,1)}, u32[]{:S(2)}, u32[]{:S(2)}) collective-permute-start(bf16[48,8192]{1,0:T(8,128)(2,1)} %get-tuple-element.43), channel_id=1, source_target_pairs={{0,2},{2,0},{4,6},{6,4},{8,10},{10,8},{12,14},{14,12},{1,3},{3,1},... | collective-permute-start | bytes 2359304 | tf_op jit(solution)/shard_map/ppermute | solution.py:272
  143.3 36.7 %collective-permute-start.6 = (bf16[32,8192]{1,0:T(8,128)(2,1)}, bf16[32,8192]{1,0:T(8,128)(2,1)}, u32[]{:S(2)}, u32[]{:S(2)}) collective-permute-start(bf16[32,8192]{1,0:T(8,128)(2,1)} %slice.24), channel_id=1, source_target_pairs={{0,12},{2,14},{4,0},{6,2},{8,4},{10,6},{12,8},{14,10},{1,13},{3,15... | collective-permute-start | bytes 1572872 | tf_op jit(solution)/shard_map/ppermute | solution.py:268
  155.8 1.6 copy-start.9
  157.4 1.4 copy-start.3
  178.7 21.4 %collective-permute-start.16 = (bf16[192,2048]{1,0:T(8,128)(2,1)}, bf16[192,2048]{1,0:T(8,128)(2,1)S(1)}, u32[]{:S(2)}, u32[]{:S(2)}) collective-permute-start(bf16[192,2048]{1,0:T(8,128)(2,1)} %get-tuple-element.35), channel_id=1, source_target_pairs={{1,0},{3,2},{4,5},{6,7},{8,9},{10,11},{13,12},{15,14},{17,16},{19,... | collective-permute-start | bytes 2359304 | tf_op jit(solution)/shard_map/ppermute | solution.py:282
  180.0 2.2 %collective-permute-start.14 = (bf16[32,8192]{1,0:T(8,128)(2,1)}, bf16[32,8192]{1,0:T(8,128)(2,1)S(1)}, u32[]{:S(2)}, u32[]{:S(2)}) collective-permute-start(bf16[32,8192]{1,0:T(8,128)(2,1)} %collective-permute-done.6.refs_0_), channel_id=1, source_target_pairs={{0,2},{2,0},{4,6},{6,4},{8,10},{10,8},{12,14},{14,12},{1,3},{3,1},... | collective-permute-start | bytes 1572872 | tf_op jit(solution)/shard_map/ppermute | solution.py:272
  196.2 0.8 copy-start.12
  197.0 10.7 %collective-permute-start.15 = (bf16[64,2048]{1,0:T(8,128)(2,1)S(1)}, bf16[64,2048]{1,0:T(8,128)(2,1)S(1)}, u32[]{:S(2)}, u32[]{:S(2)}) collective-permute-start(bf16[64,2048]{1,0:T(8,128)(2,1)S(1)} %get-tuple-element.38), channel_id=1, source_target_pairs={{1,0},{3,2},{4,5},{6,7},{8,9},{10,11},{13,12},{15,14},{17,16},{19,... | collective-permute-start | bytes 786440 | tf_op jit(solution)/shard_map/ppermute | solution.py:282
  200.0 7.7 %copy-start.13 = (f32[64,2048]{1,0:T(8,128)S(1)}, f32[64,2048]{1,0:T(8,128)}, u32[]{:S(2)}) copy-start(f32[64,2048]{1,0:T(8,128)} %copy-done.12) | copy-start | bytes 1572868

commit v8 on v7

--- a/solution.py
+++ b/solution.py
@@ -1,4 +1,5 @@
 import functools
+import math
 
 import jax
 import jax.numpy as jnp
@@ -87,36 +88,40 @@
     )(core, mine, other, fisher, codes, exps)
 
 
-def multiply_kernel(core_ref, *refs):
-    mine_ref, *parts = refs[:-12]
-    fisher_ref, train_ref, keep_ref, send_ref = refs[-12:-8]
-    left, keep, send, held, in_sems, keep_sems, send_sems, train_sems = refs[-8:]
-    rows, width = mine_ref.shape
-    count = train_ref.shape[0]
-    slots, tile, _ = held.shape
-    tiles = count // tile
+def multiply_kernel(counts, low, core_ref, *refs):
+    refs = list(refs)
+    mine_refs, other_refs, given = [[refs.pop(0) for _ in range(size)] for size in counts]
+    fisher_ref, train_ref, keep_ref, send_ref = refs[:4]
+    left, held, keep, send, in_sems, train_sems, keep_sems, send_sems = refs[4:]
+    rows = sum(ref.shape[0] for ref in mine_refs)
+    slots, tile, width = held.shape
+    tiles = train_ref.shape[0] // tile
     half = tile // 2
-    depth = min(width, 1024)
+    depth = math.gcd(width, 1024)
     core = core_ref[0]
 
     def fetches(i):
         slot = lax.rem(i, slots)
         return [
             pltpu.make_async_copy(
-                train_ref.at[pl.ds(pl.multiple_of(i * tile, tile) + part * half, half)],
+                train_ref.at[
+                    pl.ds(pl.multiple_of(i * tile, tile) + part * half, half), pl.ds(low, width)
+                ],
                 held.at[slot, pl.ds(part * half, half)],
                 train_sems.at[slot, part],
             )
             for part in range(2)
         ]
 
-    mine_spot = pl.ds(pl.multiple_of(core * rows, rows), rows)
-    loads = [pltpu.make_async_copy(mine_ref, left.at[mine_spot], in_sems.at[0])]
-    offset = 0
-    for index, ref in enumerate(parts):
-        spot = pl.ds(pl.multiple_of((1 - core) * rows, rows) + offset, ref.shape[0])
-        loads.append(pltpu.make_async_copy(ref, left.at[spot], in_sems.at[index + 1]))
-        offset += ref.shape[0]
+    loads = []
+    for group, place in ((mine_refs, core), (other_refs, 1 - core)):
+        offset = 0
+        for ref in group:
+            spot = pl.ds(pl.multiple_of(place * rows, rows) + offset, ref.shape[0])
+            loads.append(pltpu.make_async_copy(ref, left.at[spot], in_sems.at[len(loads)]))
+            offset += ref.shape[0]
+    for ref in given:
+        loads.append(pltpu.make_async_copy(ref, keep, in_sems.at[len(loads)]))
     for load in loads:
         load.start()
     for i in range(min(slots, tiles)):
@@ -147,6 +152,8 @@
             left[...], held[lax.rem(i, slots)], (((1,), (1,)), ((), ())),
             preferred_element_type=jnp.float32,
         )
+        if given:
+            sums += keep[:, cols]
         keep[:, cols] = sums
         send[:, cols] = sums.astype(jnp.bfloat16)
         for store in stores(i):
@@ -163,32 +170,35 @@
             store.wait()
 
 
-def multiply(core, mine, parts, fisher, train):
-    rows, width = mine.shape
+def multiply(core, mine, other, fisher, train, low=0, given=()):
+    rows = sum(part.shape[0] for part in mine)
+    width = mine[0].shape[1]
     count = train.shape[0]
     tile = min(count, 256)
+    slots = 4
     shape = (cores * rows, count)
+    counts = (len(mine), len(other), len(given))
     return pl.pallas_call(
-        multiply_kernel,
-        in_specs=[in_smem] + [anywhere] * (1 + len(parts)) + [in_vmem, anywhere],
+        functools.partial(multiply_kernel, counts, low),
+        in_specs=[in_smem] + [anywhere] * sum(counts) + [in_vmem, anywhere],
         out_specs=[anywhere] * 2,
         out_shape=[
             jax.ShapeDtypeStruct(shape, jnp.float32), jax.ShapeDtypeStruct(shape, jnp.bfloat16),
         ],
         scratch_shapes=[
             pltpu.VMEM((cores * rows, width), jnp.bfloat16),
+            pltpu.VMEM((slots, tile, width), jnp.bfloat16),
             pltpu.VMEM(shape, jnp.float32),
             pltpu.VMEM(shape, jnp.bfloat16),
-            pltpu.VMEM((4, tile, width), jnp.bfloat16),
-            pltpu.SemaphoreType.DMA((1 + len(parts),)),
+            pltpu.SemaphoreType.DMA((sum(counts),)),
+            pltpu.SemaphoreType.DMA((slots, 2)),
             pltpu.SemaphoreType.DMA((count // tile,)),
             pltpu.SemaphoreType.DMA((count // tile,)),
-            pltpu.SemaphoreType.DMA((4, 2)),
         ],
         compiler_params=pltpu.CompilerParams(vmem_limit_bytes=32 * mib),
         cost_estimate=small,
         name="multiply",
-    )(core, mine, *parts, fisher, train)
+    )(core, *mine, *other, *given, fisher[:, low:low + width], train)
 
 
 def place_kernel(start, parts, mine_ref, spot_ref, *refs):
@@ -242,8 +252,9 @@
     )(mine, spot, keep, *received, *given)
 
 
-def cut(whole, cuts):
-    return [whole[low:high] for low, high in cuts]
+def cut(whole, count):
+    rows = whole.shape[0] // count
+    return [whole[part * rows:(part + 1) * rows] for part in range(count)]
 
 
 def after(array, *others):
@@ -256,14 +267,14 @@
     me = lax.axis_index("dim")
     blk = lax.axis_index("blk")
     chip, core = blk // cores, lax.rem(blk, cores)[None]
-    own = val_grads.shape[0]
+    own, width = val_grads.shape
     count = grad_codes.shape[0]
     fisher = fisher[None, :]
     shape = (chips_per_owner, cores, own, count)
 
-    def shift(panel, by):
+    def shift(panel):
         pairs = [
-            (z * cores + c, (z + by) % chips * cores + c) for z in range(chips) for c in range(cores)
+            (z * cores + c, (z + 1) % chips * cores + c) for z in range(chips) for c in range(cores)
         ]
         return lax.ppermute(panel, "blk", pairs)
 
@@ -271,51 +282,60 @@
         pairs = [(b, b ^ 1) for b in range(blks)]
         return [lax.ppermute(part, "blk", pairs) for part in parts]
 
-    def collect(scores, part, by, start):
-        keep, send = part
+    def exchange(part, by):
         received = []
         for step in range(1, owners):
             pairs = []
             for b in range(blks):
                 owner = (b // cores - by) % chips // chips_per_owner
                 pairs.append((b * owners + (owner + step) % owners, b * owners + owner))
-            received.append(lax.ppermute(send, ("blk", "dim"), pairs))
+            received.append(lax.ppermute(part[1], ("blk", "dim"), pairs))
+        return received
+
+    def collect(scores, latest, part, received, by, start):
         source = lax.rem(chip - by + chips, chips)
         mine = (source // chips_per_owner == me).astype(jnp.int32)[None]
-        return place(scores, shape, mine, lax.rem(source, chips_per_owner)[None], keep, received, start)
-
-    ups = chips // 2
-    order = list(range(1, ups + 1)) + list(range(-1, ups - chips, -1))
-    pieces = [(0, own * 3 // 4), (own * 3 // 4, own)]
-    halves = [(0, own // 2), (own // 2, own)]
-
-    arriving = shift(val_grads, 1)
+        received = [after(term, latest) for term in received]
+        return place(
+            scores, shape, mine, lax.rem(source, chips_per_owner)[None], part[0], received, start
+        )
+
+    hops = chips - 1
+    knee = width * 5 // 8
+    low_flow, high_flow = [shift(piece) for piece in cut(val_grads, 2)]
     train, *part = first(core, val_grads, *swap([val_grads]), fisher, grad_codes, scale_exps)
-    scores, pending = None, [(part, 0, 0)]
-    for index, by in enumerate(order[:-1]):
-        last = index + 2 == len(order)
-        following = 1 if order[index + 1] > 0 else -1
-        if last:
-            scores = collect(scores, *pending.pop())
-        panel = after(arriving, part)
-        source = panel if abs(order[index + 1]) > 1 else val_grads
-        if last:
-            arriving = [shift(after(piece, scores), following) for piece in cut(source, pieces)]
+    scores = None
+    for hop in range(1, hops):
+        before, received = part, exchange(part, hop - 1)
+        low_piece = after(low_flow, part)
+        low_flow = shift(low_piece)
+        low_other = swap(cut(low_piece, 2))
+        high_piece = after(high_flow, low_piece)
+        if hop + 1 < hops:
+            high_flow = shift(high_piece)
         else:
-            arriving = shift(source, following)
-        part = multiply(core, panel, swap(cut(panel, halves)), fisher, train)
-        if not last:
-            scores = collect(scores, *pending.pop())
-        pending.append((part, by, 0))
-    by = order[-1]
-    for (low, high), panel in zip(pieces, arriving):
-        panel = after(panel, part, scores)
-        half = max((high - low) // 32 * 16, 16)
-        parts = [panel] if low > 0 else cut(panel, [(0, half), (half, high - low)])
-        part = multiply(core, panel, swap(parts), fisher, train)
-        scores = collect(scores, *pending.pop())
-        pending.append((part, by, low))
-    scores = collect(scores, *pending.pop())
+            high_flow = [shift(high_piece[:, :knee]), shift(high_piece[:, knee:])]
+        high_other = swap(cut(high_piece, 2))
+        low_piece = after(low_piece, *received)
+        part = multiply(
+            core, [low_piece, high_piece], [*low_other, *high_other], fisher, train
+        )
+        scores = collect(scores, part, before, received, hop - 1, 0)
+    before, earlier = part, exchange(part, hops - 1)
+    low_piece = after(low_flow, part, scores)
+    small_cuts = cut(low_piece, max(1, min(4, low_piece.shape[0] // 16)))
+    part = multiply(core, [low_piece], swap(small_cuts), fisher, train)
+    scores = collect(scores, part, before, earlier, hops - 1, 0)
+    before, received = part, exchange(part, hops)
+    left_piece = after(high_flow[0], part)
+    left_other = swap(cut(left_piece, 2))
+    part = multiply(core, [after(left_piece, *earlier)], left_other, fisher, train)
+    right_piece = after(high_flow[1], part)
+    right_other = swap([right_piece])
+    right_piece = after(right_piece, *received)
+    part = multiply(core, [right_piece], right_other, fisher, train, knee, part[:1])
+    scores = collect(scores, part, before, received, hops, 0)
+    scores = collect(scores, part, part, exchange(part, hops), hops, own // 2)
     return scores.reshape(chips_per_owner * cores * own, count)
 
 

time: 209 us -> 208 us (level)
  waiting for transfers between devices: 64.1 us -> 60.3 us
  starting transfers between devices: 27.6 us -> 24.3 us
  Pallas kernels: 98 us -> 101 us
    ppermute x8 -> x16, waiting for transfers between devices: 8.16 us -> 1.66 us  [swap(): return [lax.ppermute(part, 'blk', pairs) for part in parts]]
    ppermute x5, starting transfers between devices: 12.1 us -> 6.7 us  [exchange(): received.append(lax.ppermute(part[1], ('blk', 'dim'), pairs))]
    pallas_call x4 -> x5, Pallas kernels: 62.8 us -> 65.8 us  [multiply(): pl.pallas_call(functools.partial(multiply_kernel, counts, low), in_specs=...]
    ppermute x5, waiting for transfers between devices: 33.1 us -> 35.5 us  [exchange(): received.append(lax.ppermute(part[1], ('blk', 'dim'), pairs))]
    unnamed x31 -> x43, local copies, waits for them, and re-layouts: 11.7 us -> 12.7 us
    ppermute x4 -> x7, starting transfers between devices: 13.4 us -> 14.3 us  [shift(): return lax.ppermute(panel, 'blk', pairs)]
    ppermute x4 -> x7, waiting for transfers between devices: 22.8 us -> 23.1 us  [shift(): return lax.ppermute(panel, 'blk', pairs)]
    slice x5 -> x11, local copies, waits for them, and re-layouts: 6.89 us -> 6.86 us  [the longest x7 6.78 us: cut(): return [whole[part * rows:(part + 1) * rows] for part in range(count)]]
  transfers between devices with their start and end apart: 17 -> 28, of which waited for: 12 -> 9; matrix products, arithmetic and copies ran while one was open for 3% -> 4% of each run, Pallas kernels for 47% -> 44%
where the time goes in v8:
time: 208 us; the launch traced here: 206 us
  Pallas kernels  101 us (49%)
  waiting for transfers between devices  60.3 us (29%)
  starting transfers between devices  24.3 us (12%)
  local copies, waits for them, and re-layouts  19.6 us (9%)
    pallas_call x5, Pallas kernels, multiply(): pl.pallas_call(functools.partial(multiply_kernel, counts, low), in_specs=...  65.8 us
    ppermute x5, waiting for transfers between devices, exchange(): received.append(lax.ppermute(part[1], ('blk', 'dim'), pairs))  35.5 us
    pallas_call x1, Pallas kernels, first(): pl.pallas_call(first_kernel, grid=(count // tile,), in_specs=[in_smem, pl...  29.8 us
    ppermute x7, waiting for transfers between devices, shift(): return lax.ppermute(panel, 'blk', pairs)  23.1 us
    ppermute x7, starting transfers between devices, shift(): return lax.ppermute(panel, 'blk', pairs)  14.3 us
    unnamed x43, local copies, waits for them, and re-layouts  12.7 us
    slice x7, local copies, waits for them, and re-layouts, cut(): return [whole[part * rows:(part + 1) * rows] for part in range(count)]  6.78 us
    ppermute x5, starting transfers between devices, exchange(): received.append(lax.ppermute(part[1], ('blk', 'dim'), pairs))  6.7 us
  transfers between devices with their start and end apart: 28, of which 9 were waited for; matrix products, arithmetic and copies ran while one was open for 4% of the time, Pallas kernels for 44%

profile of v8, /device:TPU:0, one launch (start us, length us, event | category | flops | bytes accessed | tf_op | source)
XLA Modules:
  0.0 205.5 jit_solution(14895094050165395395)
XLA Ops:
  0.0 0.5 collective-permute-start.2
  0.5 3.2 %fusion = (bf16[64,8192]{1,0:T(8,128)(2,1)}, bf16[64,8192]{1,0:T(8,128)(2,1)}) fusion(bf16[128,8192]{1,0:T(8,128)(2,1)} %mine_ref.1), kind=kLoop, calls=%fused_computation | loop fusion | bytes 4194304 | tf_op jit(solution)/shard_map/slice | solution.py:257
  3.7 2.5 %collective-permute-start.1 = (bf16[64,8192]{1,0:T(8,128)(2,1)}, bf16[64,8192]{1,0:T(8,128)(2,1)S(1)}, u32[]{:S(2)}, u32[]{:S(2)}) collective-permute-start(bf16[64,8192]{1,0:T(8,128)(2,1)} %get-tuple-element.61), channel_id=1, source_target_pairs={{0,4},{2,6},{4,8},{6,10},{8,12},{10,14},{12,0},{14,2},{1,5},{3,7},... | collective-permute-start | bytes 3145736 | tf_op jit(solution)/shard_map/ppermute | solution.py:279
  6.2 1.6 collective-permute-start
  7.8 2.4 %copy.9.exps_ref = s32[2048,64]{1,0:T(8,128)} copy(s32[2048,64]{0,1:T(8,128)} %param.5) | data formatting | bytes 1048576 | tf_op args[1]
  10.2 1.2 copy-done.1
  11.4 29.8 %first.1 = (bf16[2048,8192]{1,0:T(8,128)(2,1)}, f32[256,2048]{1,0:T(8,128)S(1)}, bf16[256,2048]{1,0:T(8,128)(2,1)S(1)}) custom-call(s32[1]{0:T(128)} %bitcast.2.core_ref, bf16[128,8192]{1,0:T(8,128)(2,1)S(1)} %copy-done, bf16[128,8192]{1,0:T(8,128)(2,1)} %collective-permute-done.2.other_ref, f32[1,8192]{1,0:T(1,128)S(1)} %bitcast.11, ...), custom_call_target="tpu_custom_call" | custom-call | flops 1 | bytes 1 | tf_op jit(solution)/shard_map/first/pallas_call | solution.py:60
  41.2 1.3 collective-permute-start.5
  42.5 1.6 collective-permute-start.4
  44.2 10.9 %collective-permute-done.refs_1_ = bf16[64,8192]{1,0:T(8,128)(2,1)} collective-permute-done((bf16[64,8192]{1,0:T(8,128)(2,1)}, bf16[64,8192]{1,0:T(8,128)(2,1)}, u32[]{:S(2)}, u32[]{:S(2)}) %collective-permute-start) | collective-permute-done | bytes 1048608 | tf_op jit(solution)/shard_map/ppermute | solution.py:279
  55.0 1.3 fusion.4
  56.4 0.5 collective-permute-start.9
  57.0 10.9 %collective-permute-done.5.refs_1_ = bf16[256,2048]{1,0:T(8,128)(2,1)S(1)} collective-permute-done((bf16[256,2048]{1,0:T(8,128)(2,1)S(1)}, bf16[256,2048]{1,0:T(8,128)(2,1)S(1)}, u32[]{:S(2)}, u32[]{:S(2)}) %collective-permute-start.5) | collective-permute-done | bytes 1048608 | tf_op jit(solution)/shard_map/ppermute | solution.py:292
  67.9 1.6 collective-permute-start.3
  69.8 13.8 %multiply.5 = (f32[256,2048]{1,0:T(8,128)S(1)}, bf16[256,2048]{1,0:T(8,128)(2,1)S(1)}) custom-call(s32[1]{0:T(128)} %bitcast.2.core_ref, bf16[64,8192]{1,0:T(8,128)(2,1)S(1)} %collective-permute-done.1.refs_0_, bf16[64,8192]{1,0:T(8,128)(2,1)} %collective-permute-done.refs_1_, bf16[32,8192]{1,0:T(8,128)(2,1)S(1)} %collective-permute-done.6.refs_2_, ...), custom_call_target="tpu_custom_call" | custom-call | flops 1 | bytes 1 | tf_op jit(solution)/shard_map/multiply/pallas_call | solution.py:181
  83.6 1.5 collective-permute-start.13
  85.1 1.4 collective-permute-start.12
  86.6 1.1 fusion.3
  87.6 12.2 %collective-permute-done.3.refs_1_ = bf16[64,8192]{1,0:T(8,128)(2,1)S(1)} collective-permute-done((bf16[64,8192]{1,0:T(8,128)(2,1)}, bf16[64,8192]{1,0:T(8,128)(2,1)S(1)}, u32[]{:S(2)}, u32[]{:S(2)}) %collective-permute-start.3) | collective-permute-done | bytes 1048608 | tf_op jit(solution)/shard_map/ppermute | solution.py:279
  99.9 1.0 fusion.2
  100.9 0.5 collective-permute-start.17
  101.4 6.5 %collective-permute-done.13.refs_1_ = bf16[256,2048]{1,0:T(8,128)(2,1)S(1)} collective-permute-done((bf16[256,2048]{1,0:T(8,128)(2,1)S(1)}, bf16[256,2048]{1,0:T(8,128)(2,1)S(1)}, u32[]{:S(2)}, u32[]{:S(2)}) %collective-permute-start.13) | collective-permute-done | bytes 1048608 | tf_op jit(solution)/shard_map/ppermute | solution.py:292
  107.9 1.0 copy-done.8
  108.9 1.6 copy-done.5
  110.5 1.2 copy-done.17
  111.7 1.7 place.5.refs_2_
  113.5 4.5 %collective-permute-start.11 = (bf16[64,5120]{1,0:T(8,128)(2,1)S(1)}, bf16[64,5120]{1,0:T(8,128)(2,1)S(1)}, u32[]{:S(2)}, u32[]{:S(2)}) collective-permute-start(bf16[64,5120]{1,0:T(8,128)(2,1)S(1)} %slice.67), channel_id=1, source_target_pairs={{0,4},{2,6},{4,8},{6,10},{8,12},{10,14},{12,0},{14,2},{1,5},{3,7},... | collective-permute-start | bytes 1966088 | tf_op jit(solution)/shard_map/ppermute | solution.py:279
  118.0 17.7 %multiply.6 = (f32[256,2048]{1,0:T(8,128)S(1)}, bf16[256,2048]{1,0:T(8,128)(2,1)S(1)}) custom-call(s32[1]{0:T(128)} %bitcast.2.core_ref, bf16[64,8192]{1,0:T(8,128)(2,1)S(1)} %collective-permute-done.4.refs_0_, bf16[64,8192]{1,0:T(8,128)(2,1)S(1)} %collective-permute-done.3.refs_1_, bf16[32,8192]{1,0:T(8,128)(2,1)} %collective-permute-done.14.refs_2_, ...), custom_call_target="tpu_custom_call" | custom-call | flops 1 | bytes 1 | tf_op jit(solution)/shard_map/multiply/pallas_call | solution.py:181
  135.8 1.3 copy-done.2
  137.1 0.3 collective-permute-start.18
  138.3 0.5 collective-permute-done.18.refs_1_
  138.8 1.0 collective-permute-start.10
  139.8 1.3 collective-permute-start.22
  141.2 15.1 %multiply.7 = (f32[128,2048]{1,0:T(8,128)S(1)}, bf16[128,2048]{1,0:T(8,128)(2,1)S(1)}) custom-call(s32[1]{0:T(128)} %bitcast.2.core_ref, bf16[64,8192]{1,0:T(8,128)(2,1)S(1)} %collective-permute-done.12.refs_0_, bf16[16,8192]{1,0:T(8,128)(2,1)S(1)} %collective-permute-done.18.refs_1_, bf16[16,8192]{1,0:T(8,128)(2,1)S(1)} %collective-permute-done.19.refs_2_, ...), custom_call_target="tpu_custom_call" | custom-call | flops 1 | bytes 1 | tf_op jit(solution)/shard_map/multiply/pallas_call | solution.py:181
  156.5 0.4 collective-permute-start.24
  156.9 1.3 collective-permute-start.25
  158.2 5.8 %collective-permute-done.22.refs_1_ = bf16[256,2048]{1,0:T(8,128)(2,1)S(1)} collective-permute-done((bf16[256,2048]{1,0:T(8,128)(2,1)S(1)}, bf16[256,2048]{1,0:T(8,128)(2,1)S(1)}, u32[]{:S(2)}, u32[]{:S(2)}) %collective-permute-start.22) | collective-permute-done | bytes 1048608 | tf_op jit(solution)/shard_map/ppermute | solution.py:292
  164.0 1.0 copy-done.10
  165.0 11.1 %multiply.8 = (f32[128,2048]{1,0:T(8,128)S(1)}, bf16[128,2048]{1,0:T(8,128)(2,1)}) custom-call(s32[1]{0:T(128)} %bitcast.2.core_ref, bf16[64,5120]{1,0:T(8,128)(2,1)S(1)} %collective-permute-done.11.refs_0_, bf16[32,5120]{1,0:T(8,128)(2,1)S(1)} %collective-permute-done.23.refs_1_, bf16[32,5120]{1,0:T(8,128)(2,1)S(1)} %collective-permute-done.24.refs_2_, ...), custom_call_target="tpu_custom_call" | custom-call | flops 1 | bytes 1 | tf_op jit(solution)/shard_map/multiply/pallas_call | solution.py:181
  176.2 0.8 copy-done.19
  177.0 0.9 collective-permute-done.26.refs_1_
  177.9 8.1 %multiply.9 = (f32[128,2048]{1,0:T(8,128)S(1)}, bf16[128,2048]{1,0:T(8,128)(2,1)}) custom-call(s32[1]{0:T(128)} %bitcast.2.core_ref, bf16[64,3072]{1,0:T(8,128)(2,1)S(1)} %collective-permute-done.10.refs_0_, bf16[64,3072]{1,0:T(8,128)(2,1)S(1)} %collective-permute-done.26.refs_1_, f32[128,2048]{1,0:T(8,128)S(1)} %get-tuple-element.53.refs_2_, ...), custom_call_target="tpu_custom_call" | custom-call | flops 1 | bytes 1 | tf_op jit(solution)/shard_map/multiply/pallas_call | solution.py:181
  186.0 1.0 copy-done.14
  187.1 1.3 collective-permute-start.27
  188.5 1.2 copy-done.13
  189.8 1.2 place.8.refs_2_
  191.0 12.3 %collective-permute-done.27.refs_1_ = bf16[128,2048]{1,0:T(8,128)(2,1)} collective-permute-done((bf16[128,2048]{1,0:T(8,128)(2,1)}, bf16[128,2048]{1,0:T(8,128)(2,1)}, u32[]{:S(2)}, u32[]{:S(2)}) %collective-permute-start.27) | collective-permute-done | bytes 524320 | tf_op jit(solution)/shard_map/ppermute | solution.py:292
  203.3 2.2 %place.9 = f32[2,2,128,2048]{3,2,1,0:T(8,128)} custom-call(s32[1]{0:T(128)} %bitcast.mine_ref, s32[1]{0:T(128)} %bitcast.1.spot_ref, f32[128,2048]{1,0:T(8,128)S(1)} %copy-done.15, bf16[128,2048]{1,0:T(8,128)(2,1)} %collective-permute-done.27.refs_1_, f32[2,2,128,2048]{3,2,1,0:T(8,128)} %place.8.refs_2_), custom_call_target="tpu_custom_call", output_to_operand_aliasing={{}: (4, {})} | custom-call | flops 1 | bytes 1 | tf_op jit(solution)/shard_map/place/pallas_call | solution.py:237
  (73 shorter events, 2.0 us)
Async XLA Ops:
  0.0 10.1 %copy-start = (bf16[128,8192]{1,0:T(8,128)(2,1)S(1)}, bf16[128,8192]{1,0:T(8,128)(2,1)}, u32[]{:S(2)}) copy-start(bf16[128,8192]{1,0:T(8,128)(2,1)} %mine_ref.1) | copy-start | bytes 6291460
  0.0 10.1 %copy-start.18 = (f32[8192]{0:T(1024)S(1)}, f32[8192]{0:T(1024)}, u32[]{:S(2)}) copy-start(f32[8192]{0:T(1024)} %param.7) | copy-start | bytes 98308
  0.0 10.1 %collective-permute-start.2 = (bf16[128,8192]{1,0:T(8,128)(2,1)}, bf16[128,8192]{1,0:T(8,128)(2,1)}, u32[]{:S(2)}, u32[]{:S(2)}) collective-permute-start(bf16[128,8192]{1,0:T(8,128)(2,1)} %mine_ref.1), channel_id=1, source_target_pairs={{0,2},{2,0},{4,6},{6,4},{8,10},{10,8},{12,14},{14,12},{1,3},{3,1},... | collective-permute-start | bytes 6291464 | tf_op jit(solution)/shard_map/ppermute | solution.py:283
  3.7 38.8 %collective-permute-start.1 = (bf16[64,8192]{1,0:T(8,128)(2,1)}, bf16[64,8192]{1,0:T(8,128)(2,1)S(1)}, u32[]{:S(2)}, u32[]{:S(2)}) collective-permute-start(bf16[64,8192]{1,0:T(8,128)(2,1)} %get-tuple-element.61), channel_id=1, source_target_pairs={{0,4},{2,6},{4,8},{6,10},{8,12},{10,14},{12,0},{14,2},{1,5},{3,7},... | collective-permute-start | bytes 3145736 | tf_op jit(solution)/shard_map/ppermute | solution.py:279
  6.2 48.8 %collective-permute-start = (bf16[64,8192]{1,0:T(8,128)(2,1)}, bf16[64,8192]{1,0:T(8,128)(2,1)}, u32[]{:S(2)}, u32[]{:S(2)}) collective-permute-start(bf16[64,8192]{1,0:T(8,128)(2,1)} %get-tuple-element.62), channel_id=1, source_target_pairs={{0,4},{2,6},{4,8},{6,10},{8,12},{10,14},{12,0},{14,2},{1,5},{3,7},... | collective-permute-start | bytes 3145736 | tf_op jit(solution)/shard_map/ppermute | solution.py:279
  10.2 1.2 copy-start.1
  41.2 42.4 %copy-start.4 = (f32[256,2048]{1,0:T(8,128)}, f32[256,2048]{1,0:T(8,128)S(1)}, u32[]{:S(2)}) copy-start(f32[256,2048]{1,0:T(8,128)S(1)} %get-tuple-element.33.refs_0_) | copy-start | bytes 6291460
  41.2 26.7 %collective-permute-start.5 = (bf16[256,2048]{1,0:T(8,128)(2,1)S(1)}, bf16[256,2048]{1,0:T(8,128)(2,1)S(1)}, u32[]{:S(2)}, u32[]{:S(2)}) collective-permute-start(bf16[256,2048]{1,0:T(8,128)(2,1)S(1)} %get-tuple-element.34), channel_id=1, source_target_pairs={{1,0},{3,2},{5,4},{7,6},{8,9},{10,11},{12,13},{14,15},{17,16},{19,... | collective-permute-start | bytes 3145736 | tf_op jit(solution)/shard_map/ppermute | solution.py:292
  42.5 42.7 %collective-permute-start.4 = (bf16[64,8192]{1,0:T(8,128)(2,1)S(1)}, bf16[64,8192]{1,0:T(8,128)(2,1)S(1)}, u32[]{:S(2)}, u32[]{:S(2)}) collective-permute-start(bf16[64,8192]{1,0:T(8,128)(2,1)S(1)} %collective-permute-done.1.refs_0_), channel_id=1, source_target_pairs={{0,4},{2,6},{4,8},{6,10},{8,12},{10,14},{12,0},{14,2},{1,5},{3,7},... | collective-permute-start | bytes 3145736 | tf_op jit(solution)/shard_map/ppermute | solution.py:279
  56.3 11.6 %collective-permute-start.8 = (bf16[32,8192]{1,0:T(8,128)(2,1)S(1)}, bf16[32,8192]{1,0:T(8,128)(2,1)S(1)}, u32[]{:S(2)}, u32[]{:S(2)}) collective-permute-start(bf16[32,8192]{1,0:T(8,128)(2,1)S(1)} %get-tuple-element.72), channel_id=1, source_target_pairs={{0,2},{2,0},{4,6},{6,4},{8,10},{10,8},{12,14},{14,12},{1,3},{3,1},... | collective-permute-start | bytes 1572872 | tf_op jit(solution)/shard_map/ppermute | solution.py:283
  56.4 13.2 %collective-permute-start.9 = (bf16[32,8192]{1,0:T(8,128)(2,1)S(1)}, bf16[32,8192]{1,0:T(8,128)(2,1)S(1)}, u32[]{:S(2)}, u32[]{:S(2)}) collective-permute-start(bf16[32,8192]{1,0:T(8,128)(2,1)S(1)} %get-tuple-element.71), channel_id=1, source_target_pairs={{0,2},{2,0},{4,6},{6,4},{8,10},{10,8},{12,14},{14,12},{1,3},{3,1},... | collective-permute-start | bytes 1572872 | tf_op jit(solution)/shard_map/ppermute | solution.py:283
  56.9 12.7 %collective-permute-start.6 = (bf16[32,8192]{1,0:T(8,128)(2,1)S(1)}, bf16[32,8192]{1,0:T(8,128)(2,1)S(1)}, u32[]{:S(2)}, u32[]{:S(2)}) collective-permute-start(bf16[32,8192]{1,0:T(8,128)(2,1)S(1)} %get-tuple-element.74), channel_id=1, source_target_pairs={{0,2},{2,0},{4,6},{6,4},{8,10},{10,8},{12,14},{14,12},{1,3},{3,1},... | collective-permute-start | bytes 1572872 | tf_op jit(solution)/shard_map/ppermute | solution.py:283
  67.9 15.7 %copy-start.16 = (bf16[256,2048]{1,0:T(8,128)(2,1)}, bf16[256,2048]{1,0:T(8,128)(2,1)S(1)}, u32[]{:S(2)}) copy-start(bf16[256,2048]{1,0:T(8,128)(2,1)S(1)} %collective-permute-done.5.refs_1_) | copy-start | bytes 3145732
  67.9 1.9 collective-permute-start.7
  67.9 32.0 %collective-permute-start.3 = (bf16[64,8192]{1,0:T(8,128)(2,1)}, bf16[64,8192]{1,0:T(8,128)(2,1)S(1)}, u32[]{:S(2)}, u32[]{:S(2)}) collective-permute-start(bf16[64,8192]{1,0:T(8,128)(2,1)} %collective-permute-done.refs_1_), channel_id=1, source_target_pairs={{0,4},{2,6},{4,8},{6,10},{8,12},{10,14},{12,0},{14,2},{1,5},{3,7},... | collective-permute-start | bytes 3145736 | tf_op jit(solution)/shard_map/ppermute | solution.py:279
  83.6 16.3 %copy-start.6 = (f32[256,2048]{1,0:T(8,128)}, f32[256,2048]{1,0:T(8,128)S(1)}, u32[]{:S(2)}) copy-start(f32[256,2048]{1,0:T(8,128)S(1)} %get-tuple-element.39.refs_0_) | copy-start | bytes 6291460
  83.6 24.3 %collective-permute-start.13 = (bf16[256,2048]{1,0:T(8,128)(2,1)S(1)}, bf16[256,2048]{1,0:T(8,128)(2,1)S(1)}, u32[]{:S(2)}, u32[]{:S(2)}) collective-permute-start(bf16[256,2048]{1,0:T(8,128)(2,1)S(1)} %get-tuple-element.40), channel_id=1, source_target_pairs={{0,1},{2,3},{5,4},{7,6},{9,8},{11,10},{12,13},{14,15},{16,17},{18,... | collective-permute-start | bytes 3145736 | tf_op jit(solution)/shard_map/ppermute | solution.py:292
  85.1 51.9 %collective-permute-start.12 = (bf16[64,8192]{1,0:T(8,128)(2,1)S(1)}, bf16[64,8192]{1,0:T(8,128)(2,1)S(1)}, u32[]{:S(2)}, u32[]{:S(2)}) collective-permute-start(bf16[64,8192]{1,0:T(8,128)(2,1)S(1)} %collective-permute-done.4.refs_0_), channel_id=1, source_target_pairs={{0,4},{2,6},{4,8},{6,10},{8,12},{10,14},{12,0},{14,2},{1,5},{3,7},... | collective-permute-start | bytes 3145736 | tf_op jit(solution)/shard_map/ppermute | solution.py:279
  100.9 12.6 %collective-permute-start.16 = (bf16[32,8192]{1,0:T(8,128)(2,1)}, bf16[32,8192]{1,0:T(8,128)(2,1)}, u32[]{:S(2)}, u32[]{:S(2)}) collective-permute-start(bf16[32,8192]{1,0:T(8,128)(2,1)} %get-tuple-element.68), channel_id=1, source_target_pairs={{0,2},{2,0},{4,6},{6,4},{8,10},{10,8},{12,14},{14,12},{1,3},{3,1},... | collective-permute-start | bytes 1572872 | tf_op jit(solution)/shard_map/ppermute | solution.py:283
  100.9 17.0 %collective-permute-start.17 = (bf16[32,8192]{1,0:T(8,128)(2,1)}, bf16[32,8192]{1,0:T(8,128)(2,1)}, u32[]{:S(2)}, u32[]{:S(2)}) collective-permute-start(bf16[32,8192]{1,0:T(8,128)(2,1)} %get-tuple-element.67), channel_id=1, source_target_pairs={{0,2},{2,0},{4,6},{6,4},{8,10},{10,8},{12,14},{14,12},{1,3},{3,1},... | collective-permute-start | bytes 1572872 | tf_op jit(solution)/shard_map/ppermute | solution.py:283
  101.4 16.5 %collective-permute-start.14 = (bf16[32,8192]{1,0:T(8,128)(2,1)}, bf16[32,8192]{1,0:T(8,128)(2,1)}, u32[]{:S(2)}, u32[]{:S(2)}) collective-permute-start(bf16[32,8192]{1,0:T(8,128)(2,1)} %get-tuple-element.70), channel_id=1, source_target_pairs={{0,2},{2,0},{4,6},{6,4},{8,10},{10,8},{12,14},{14,12},{1,3},{3,1},... | collective-permute-start | bytes 1572872 | tf_op jit(solution)/shard_map/ppermute | solution.py:283
  107.9 1.0 copy-start.8
  108.9 9.1 %collective-permute-start.15 = (bf16[32,8192]{1,0:T(8,128)(2,1)}, bf16[32,8192]{1,0:T(8,128)(2,1)}, u32[]{:S(2)}, u32[]{:S(2)}) collective-permute-start(bf16[32,8192]{1,0:T(8,128)(2,1)} %get-tuple-element.69), channel_id=1, source_target_pairs={{0,2},{2,0},{4,6},{6,4},{8,10},{10,8},{12,14},{14,12},{1,3},{3,1},... | collective-permute-start | bytes 1572872 | tf_op jit(solution)/shard_map/ppermute | solution.py:283
  108.9 1.6 copy-start.5
  110.5 1.2 copy-start.17
  113.5 22.2 %copy-start.7 = (f32[256,2048]{1,0:T(8,128)S(1)}, f32[256,2048]{1,0:T(8,128)}, u32[]{:S(2)}) copy-start(f32[256,2048]{1,0:T(8,128)} %copy-done.6) | copy-start | bytes 6291460
  113.5 22.2 %copy-start.9 = (bf16[256,2048]{1,0:T(8,128)(2,1)S(1)}, bf16[256,2048]{1,0:T(8,128)(2,1)}, u32[]{:S(2)}) copy-start(bf16[256,2048]{1,0:T(8,128)(2,1)} %copy-done.8) | copy-start | bytes 3145732
  113.5 42.8 %collective-permute-start.11 = (bf16[64,5120]{1,0:T(8,128)(2,1)S(1)}, bf16[64,5120]{1,0:T(8,128)(2,1)S(1)}, u32[]{:S(2)}, u32[]{:S(2)}) collective-permute-start(bf16[64,5120]{1,0:T(8,128)(2,1)S(1)} %slice.67), channel_id=1, source_target_pairs={{0,4},{2,6},{4,8},{6,10},{8,12},{10,14},{12,0},{14,2},{1,5},{3,7},... | collective-permute-start | bytes 1966088 | tf_op jit(solution)/shard_map/ppermute | solution.py:279
  135.7 1.4 copy-start.2
  137.1 1.6 collective-permute-start.18
  137.4 2.3 %collective-permute-start.19 = (bf16[16,8192]{1,0:T(8,128)(2,1)S(1)}, bf16[16,8192]{1,0:T(8,128)(2,1)S(1)}, u32[]{:S(2)}, u32[]{:S(2)}) collective-permute-start(bf16[16,8192]{1,0:T(8,128)(2,1)S(1)} %get-tuple-element.65), channel_id=1, source_target_pairs={{0,2},{2,0},{4,6},{6,4},{8,10},{10,8},{12,14},{14,12},{1,3},{3,1},... | collective-permute-start | bytes 786440 | tf_op jit(solution)/shard_map/ppermute | solution.py:283
  137.7 3.4 %collective-permute-start.20 = (bf16[16,8192]{1,0:T(8,128)(2,1)S(1)}, bf16[16,8192]{1,0:T(8,128)(2,1)S(1)}, u32[]{:S(2)}, u32[]{:S(2)}) collective-permute-start(bf16[16,8192]{1,0:T(8,128)(2,1)S(1)} %get-tuple-element.64), channel_id=1, source_target_pairs={{0,2},{2,0},{4,6},{6,4},{8,10},{10,8},{12,14},{14,12},{1,3},{3,1},... | collective-permute-start | bytes 786440 | tf_op jit(solution)/shard_map/ppermute | solution.py:283
  137.9 3.2 %collective-permute-start.21 = (bf16[16,8192]{1,0:T(8,128)(2,1)S(1)}, bf16[16,8192]{1,0:T(8,128)(2,1)S(1)}, u32[]{:S(2)}, u32[]{:S(2)}) collective-permute-start(bf16[16,8192]{1,0:T(8,128)(2,1)S(1)} %get-tuple-element.63), channel_id=1, source_target_pairs={{0,2},{2,0},{4,6},{6,4},{8,10},{10,8},{12,14},{14,12},{1,3},{3,1},... | collective-permute-start | bytes 786440 | tf_op jit(solution)/shard_map/ppermute | solution.py:283
  138.8 37.3 %collective-permute-start.10 = (bf16[64,3072]{1,0:T(8,128)(2,1)S(1)}, bf16[64,3072]{1,0:T(8,128)(2,1)S(1)}, u32[]{:S(2)}, u32[]{:S(2)}) collective-permute-start(bf16[64,3072]{1,0:T(8,128)(2,1)S(1)} %slice.66), channel_id=1, source_target_pairs={{0,4},{2,6},{4,8},{6,10},{8,12},{10,14},{12,0},{14,2},{1,5},{3,7},... | collective-permute-start | bytes 1179656 | tf_op jit(solution)/shard_map/ppermute | solution.py:279
  139.8 24.2 %collective-permute-start.22 = (bf16[256,2048]{1,0:T(8,128)(2,1)S(1)}, bf16[256,2048]{1,0:T(8,128)(2,1)S(1)}, u32[]{:S(2)}, u32[]{:S(2)}) collective-permute-start(bf16[256,2048]{1,0:T(8,128)(2,1)S(1)} %get-tuple-element.45), channel_id=1, source_target_pairs={{0,1},{2,3},{4,5},{6,7},{9,8},{11,10},{13,12},{15,14},{16,17},{18,... | collective-permute-start | bytes 3145736 | tf_op jit(solution)/shard_map/ppermute | solution.py:292
  156.3 7.7 %copy-start.12 = (f32[128,2048]{1,0:T(8,128)}, f32[128,2048]{1,0:T(8,128)S(1)}, u32[]{:S(2)}) copy-start(f32[128,2048]{1,0:T(8,128)S(1)} %get-tuple-element.49.refs_0_) | copy-start | bytes 3145732
  156.3 8.6 %collective-permute-start.23 = (bf16[32,5120]{1,0:T(8,128)(2,1)S(1)}, bf16[32,5120]{1,0:T(8,128)(2,1)S(1)}, u32[]{:S(2)}, u32[]{:S(2)}) collective-permute-start(bf16[32,5120]{1,0:T(8,128)(2,1)S(1)} %get-tuple-element.76), channel_id=1, source_target_pairs={{0,2},{2,0},{4,6},{6,4},{8,10},{10,8},{12,14},{14,12},{1,3},{3,1},... | collective-permute-start | bytes 983048 | tf_op jit(solution)/shard_map/ppermute | solution.py:283
  156.5 8.5 %collective-permute-start.24 = (bf16[32,5120]{1,0:T(8,128)(2,1)S(1)}, bf16[32,5120]{1,0:T(8,128)(2,1)S(1)}, u32[]{:S(2)}, u32[]{:S(2)}) collective-permute-start(bf16[32,5120]{1,0:T(8,128)(2,1)S(1)} %get-tuple-element.75), channel_id=1, source_target_pairs={{0,2},{2,0},{4,6},{6,4},{8,10},{10,8},{12,14},{14,12},{1,3},{3,1},... | collective-permute-start | bytes 983048 | tf_op jit(solution)/shard_map/ppermute | solution.py:283
  156.9 19.3 %collective-permute-start.25 = (bf16[128,2048]{1,0:T(8,128)(2,1)S(1)}, bf16[128,2048]{1,0:T(8,128)(2,1)S(1)}, u32[]{:S(2)}, u32[]{:S(2)}) collective-permute-start(bf16[128,2048]{1,0:T(8,128)(2,1)S(1)} %get-tuple-element.50), channel_id=1, source_target_pairs={{1,0},{3,2},{4,5},{6,7},{8,9},{10,11},{13,12},{15,14},{17,16},{19,... | collective-permute-start | bytes 1572872 | tf_op jit(solution)/shard_map/ppermute | solution.py:292
  164.0 1.0 copy-start.10
  176.1 1.8 collective-permute-start.26
  176.2 12.2 %copy-start.3 = (f32[256,2048]{1,0:T(8,128)S(1)}, f32[256,2048]{1,0:T(8,128)}, u32[]{:S(2)}) copy-start(f32[256,2048]{1,0:T(8,128)} %copy-done.2) | copy-start | bytes 6291460
  176.2 12.2 %copy-start.11 = (bf16[256,2048]{1,0:T(8,128)(2,1)S(1)}, bf16[256,2048]{1,0:T(8,128)(2,1)}, u32[]{:S(2)}) copy-start(bf16[256,2048]{1,0:T(8,128)(2,1)} %copy-done.10) | copy-start | bytes 3145732
  186.0 1.0 copy-start.14
  187.1 16.3 %collective-permute-start.27 = (bf16[128,2048]{1,0:T(8,128)(2,1)}, bf16[128,2048]{1,0:T(8,128)(2,1)}, u32[]{:S(2)}, u32[]{:S(2)}) collective-permute-start(bf16[128,2048]{1,0:T(8,128)(2,1)} %get-tuple-element.57), channel_id=1, source_target_pairs={{1,0},{3,2},{4,5},{6,7},{8,9},{10,11},{13,12},{15,14},{17,16},{19,... | collective-permute-start | bytes 1572872 | tf_op jit(solution)/shard_map/ppermute | solution.py:292
  188.4 1.2 copy-start.13
  188.4 1.3 copy-start.20
  189.8 13.6 %copy-start.15 = (f32[128,2048]{1,0:T(8,128)S(1)}, f32[128,2048]{1,0:T(8,128)}, u32[]{:S(2)}) copy-start(f32[128,2048]{1,0:T(8,128)} %copy-done.14) | copy-start | bytes 3145732
  (1 other events, 0.8 us)

commit v9 on v8

--- a/solution.py
+++ b/solution.py
@@ -82,20 +82,20 @@
             pltpu.VMEM((cores * rows, width), jnp.bfloat16),
             pltpu.VMEM((blocks, width), jnp.bfloat16),
         ],
-        compiler_params=pltpu.CompilerParams(vmem_limit_bytes=40 * mib),
+        compiler_params=pltpu.CompilerParams(vmem_limit_bytes=36 * mib),
         cost_estimate=small,
         name="first",
     )(core, mine, other, fisher, codes, exps)
 
 
-def multiply_kernel(counts, low, core_ref, *refs):
+def multiply_kernel(counts, low, top, core_ref, *refs):
     refs = list(refs)
     mine_refs, other_refs, given = [[refs.pop(0) for _ in range(size)] for size in counts]
     fisher_ref, train_ref, keep_ref, send_ref = refs[:4]
     left, held, keep, send, in_sems, train_sems, keep_sems, send_sems = refs[4:]
     rows = sum(ref.shape[0] for ref in mine_refs)
     slots, tile, width = held.shape
-    tiles = train_ref.shape[0] // tile
+    tiles = keep.shape[1] // tile
     half = tile // 2
     depth = math.gcd(width, 1024)
     core = core_ref[0]
@@ -105,7 +105,7 @@
         return [
             pltpu.make_async_copy(
                 train_ref.at[
-                    pl.ds(pl.multiple_of(i * tile, tile) + part * half, half), pl.ds(low, width)
+                    pl.ds(pl.multiple_of(i * tile, tile) + top + part * half, half), pl.ds(low, width)
                 ],
                 held.at[slot, pl.ds(part * half, half)],
                 train_sems.at[slot, part],
@@ -121,7 +121,8 @@
             loads.append(pltpu.make_async_copy(ref, left.at[spot], in_sems.at[len(loads)]))
             offset += ref.shape[0]
     for ref in given:
-        loads.append(pltpu.make_async_copy(ref, keep, in_sems.at[len(loads)]))
+        source = ref.at[:, pl.ds(top, keep.shape[1])]
+        loads.append(pltpu.make_async_copy(source, keep, in_sems.at[len(loads)]))
     for load in loads:
         load.start()
     for i in range(min(slots, tiles)):
@@ -170,16 +171,17 @@
             store.wait()
 
 
-def multiply(core, mine, other, fisher, train, low=0, given=()):
+def multiply(core, mine, other, fisher, train, low=0, given=(), span=None):
     rows = sum(part.shape[0] for part in mine)
     width = mine[0].shape[1]
-    count = train.shape[0]
+    top, bottom = span or (0, train.shape[0])
+    count = bottom - top
     tile = min(count, 256)
     slots = 4
     shape = (cores * rows, count)
     counts = (len(mine), len(other), len(given))
     return pl.pallas_call(
-        functools.partial(multiply_kernel, counts, low),
+        functools.partial(multiply_kernel, counts, low, top),
         in_specs=[in_smem] + [anywhere] * sum(counts) + [in_vmem, anywhere],
         out_specs=[anywhere] * 2,
         out_shape=[
@@ -195,13 +197,13 @@
             pltpu.SemaphoreType.DMA((count // tile,)),
             pltpu.SemaphoreType.DMA((count // tile,)),
         ],
-        compiler_params=pltpu.CompilerParams(vmem_limit_bytes=32 * mib),
+        compiler_params=pltpu.CompilerParams(vmem_limit_bytes=27 * mib),
         cost_estimate=small,
         name="multiply",
     )(core, *mine, *other, *given, fisher[:, low:low + width], train)
 
 
-def place_kernel(start, parts, mine_ref, spot_ref, *refs):
+def place_kernel(start, col, parts, mine_ref, spot_ref, *refs):
     keep_ref, received = refs[0], refs[1:1 + parts]
     scores_ref, total, terms, in_sems, out_sems = refs[-5:]
     rows = keep_ref.shape[0] // cores
@@ -220,7 +222,7 @@
         copies = [
             pltpu.make_async_copy(
                 total.at[pl.ds(c * rows, rows)],
-                scores_ref.at[spot_ref[0], c, pl.ds(start, rows)],
+                scores_ref.at[spot_ref[0], c, pl.ds(start, rows), pl.ds(col, keep_ref.shape[1])],
                 out_sems.at[c],
             )
             for c in range(cores)
@@ -231,11 +233,11 @@
             copy.wait()
 
 
-def place(scores, shape, mine, spot, keep, received, start):
+def place(scores, shape, mine, spot, keep, received, start, col):
     given = [] if scores is None else [scores]
     parts = len(received)
     return pl.pallas_call(
-        functools.partial(place_kernel, start, parts),
+        functools.partial(place_kernel, start, col, parts),
         in_specs=[in_smem] * 2 + [anywhere] * (1 + parts + len(given)),
         out_specs=anywhere,
         out_shape=jax.ShapeDtypeStruct(shape, jnp.float32),
@@ -292,22 +294,22 @@
             received.append(lax.ppermute(part[1], ("blk", "dim"), pairs))
         return received
 
-    def collect(scores, latest, part, received, by, start):
+    def collect(scores, latest, part, received, by, start, col=0):
         source = lax.rem(chip - by + chips, chips)
         mine = (source // chips_per_owner == me).astype(jnp.int32)[None]
         received = [after(term, latest) for term in received]
         return place(
-            scores, shape, mine, lax.rem(source, chips_per_owner)[None], part[0], received, start
+            scores, shape, mine, lax.rem(source, chips_per_owner)[None], part[0], received, start, col
         )
 
     hops = chips - 1
     knee = width * 5 // 8
     low_flow, high_flow = [shift(piece) for piece in cut(val_grads, 2)]
     train, *part = first(core, val_grads, *swap([val_grads]), fisher, grad_codes, scale_exps)
-    scores = None
+    scores, earlier = None, []
     for hop in range(1, hops):
         before, received = part, exchange(part, hop - 1)
-        low_piece = after(low_flow, part)
+        low_piece = after(low_flow, part, *earlier)
         low_flow = shift(low_piece)
         low_other = swap(cut(low_piece, 2))
         high_piece = after(high_flow, low_piece)
@@ -316,26 +318,35 @@
         else:
             high_flow = [shift(high_piece[:, :knee]), shift(high_piece[:, knee:])]
         high_other = swap(cut(high_piece, 2))
-        low_piece = after(low_piece, *received)
+        if hop > 1:
+            low_piece = after(low_piece, *received)
         part = multiply(
             core, [low_piece, high_piece], [*low_other, *high_other], fisher, train
         )
         scores = collect(scores, part, before, received, hop - 1, 0)
+        earlier = received
     before, earlier = part, exchange(part, hops - 1)
     low_piece = after(low_flow, part, scores)
-    small_cuts = cut(low_piece, max(1, min(4, low_piece.shape[0] // 16)))
-    part = multiply(core, [low_piece], swap(small_cuts), fisher, train)
-    scores = collect(scores, part, before, earlier, hops - 1, 0)
-    before, received = part, exchange(part, hops)
+    small = max(1, min(4, low_piece.shape[0] // 16))
+    part = multiply(core, [low_piece], swap(cut(low_piece, small)), fisher, train)
+    low_part, received = part, exchange(part, hops)
     left_piece = after(high_flow[0], part)
-    left_other = swap(cut(left_piece, 2))
-    part = multiply(core, [after(left_piece, *earlier)], left_other, fisher, train)
+    part = multiply(core, [left_piece], swap(cut(left_piece, small)), fisher, train)
     right_piece = after(high_flow[1], part)
     right_other = swap([right_piece])
-    right_piece = after(right_piece, *received)
-    part = multiply(core, [right_piece], right_other, fisher, train, knee, part[:1])
-    scores = collect(scores, part, before, received, hops, 0)
-    scores = collect(scores, part, part, exchange(part, hops), hops, own // 2)
+    right_piece = after(right_piece, *earlier)
+    half = count // 2
+    parts = []
+    for top in (0, half):
+        if parts:
+            right_piece = after(right_piece, *parts, *received)
+        parts.append(multiply(
+            core, [right_piece], right_other, fisher, train, knee, part[:1], (top, top + half)
+        ))
+    scores = collect(scores, parts[-1], before, earlier, hops - 1, 0)
+    scores = collect(scores, parts[-1], low_part, received, hops, 0)
+    for col, part in zip((0, half), parts):
+        scores = collect(scores, parts[-1], part, exchange(part, hops), hops, own // 2, col)
     return scores.reshape(chips_per_owner * cores * own, count)
 
 

time: 208 us -> 194 us (0.933)
  waiting for transfers between devices: 60.3 us -> 44.6 us
  Pallas kernels: 101 us -> 105 us
    ppermute x5 -> x6, waiting for transfers between devices: 35.5 us -> 6.92 us  [exchange(): received.append(lax.ppermute(part[1], ('blk', 'dim'), pairs))]
    ppermute x7, waiting for transfers between devices: 23.1 us -> 31.5 us  [shift(): return lax.ppermute(panel, 'blk', pairs)]
    ppermute x7, starting transfers between devices: 14.3 us -> 6.53 us  [shift(): return lax.ppermute(panel, 'blk', pairs)]
    ppermute x5 -> x6, starting transfers between devices: 6.7 us -> 13.1 us  [exchange(): received.append(lax.ppermute(part[1], ('blk', 'dim'), pairs))]
    ppermute x16 -> x18, waiting for transfers between devices: 1.66 us -> 6.13 us  [swap(): return [lax.ppermute(part, 'blk', pairs) for part in parts]]
    pallas_call x10 -> x12, Pallas kernels: 71.1 us -> 75.3 us  [the longest x6 69.5 us: multiply(): pl.pallas_call(functools.partial(multiply_kernel, counts, low, top), in_s...]
    unnamed x43 -> x47, local copies, waits for them, and re-layouts: 12.7 us -> 11.5 us
    ppermute x16 -> x18, starting transfers between devices: 3.35 us -> 4.53 us  [swap(): return [lax.ppermute(part, 'blk', pairs) for part in parts]]
  transfers between devices with their start and end apart: 28 -> 31, of which waited for: 9 -> 11; matrix products, arithmetic and copies ran while one was open for 4% -> 5% of each run, Pallas kernels for 44% -> 53%
where the time goes in v9:
time: 194 us; the launch traced here: 193 us
  Pallas kernels  105 us (54%)
  waiting for transfers between devices  44.6 us (23%)
  starting transfers between devices  24.2 us (12%)
  local copies, waits for them, and re-layouts  18.5 us (10%)
    pallas_call x6, Pallas kernels, multiply(): pl.pallas_call(functools.partial(multiply_kernel, counts, low, top), in_s...  69.5 us
    ppermute x7, waiting for transfers between devices, shift(): return lax.ppermute(panel, 'blk', pairs)  31.5 us
    pallas_call x1, Pallas kernels, first(): pl.pallas_call(first_kernel, grid=(count // tile,), in_specs=[in_smem, pl...  29.8 us
    ppermute x6, starting transfers between devices, exchange(): received.append(lax.ppermute(part[1], ('blk', 'dim'), pairs))  13.1 us
    unnamed x47, local copies, waits for them, and re-layouts  11.5 us
    ppermute x6, waiting for transfers between devices, exchange(): received.append(lax.ppermute(part[1], ('blk', 'dim'), pairs))  6.92 us
    slice x7, local copies, waits for them, and re-layouts, cut(): return [whole[part * rows:(part + 1) * rows] for part in range(count)]  6.88 us
    ppermute x7, starting transfers between devices, shift(): return lax.ppermute(panel, 'blk', pairs)  6.53 us
  transfers between devices with their start and end apart: 31, of which 11 were waited for; matrix products, arithmetic and copies ran while one was open for 5% of the time, Pallas kernels for 53%

profile of v9, /device:TPU:0, one launch (start us, length us, event | category | flops | bytes accessed | tf_op | source)
XLA Modules:
  0.0 193.2 jit_solution(15486953388491279765)
XLA Ops:
  0.5 3.2 %fusion = (bf16[64,8192]{1,0:T(8,128)(2,1)}, bf16[64,8192]{1,0:T(8,128)(2,1)}) fusion(bf16[128,8192]{1,0:T(8,128)(2,1)} %mine_ref.1), kind=kLoop, calls=%fused_computation | loop fusion | bytes 4194304 | tf_op jit(solution)/shard_map/slice | solution.py:259
  3.7 2.5 %collective-permute-start.1 = (bf16[64,8192]{1,0:T(8,128)(2,1)}, bf16[64,8192]{1,0:T(8,128)(2,1)S(1)}, u32[]{:S(2)}, u32[]{:S(2)}) collective-permute-start(bf16[64,8192]{1,0:T(8,128)(2,1)} %get-tuple-element.65), channel_id=1, source_target_pairs={{0,4},{2,6},{4,8},{6,10},{8,12},{10,14},{12,0},{14,2},{1,5},{3,7},... | collective-permute-start | bytes 3145736 | tf_op jit(solution)/shard_map/ppermute | solution.py:281
  6.2 1.6 collective-permute-start
  7.8 2.4 %copy.10.exps_ref = s32[2048,64]{1,0:T(8,128)} copy(s32[2048,64]{0,1:T(8,128)} %param.5) | data formatting | bytes 1048576 | tf_op args[1]
  10.2 1.2 copy-done.1
  11.4 29.8 %first.1 = (bf16[2048,8192]{1,0:T(8,128)(2,1)}, f32[256,2048]{1,0:T(8,128)S(1)}, bf16[256,2048]{1,0:T(8,128)(2,1)S(1)}) custom-call(s32[1]{0:T(128)} %bitcast.2.core_ref, bf16[128,8192]{1,0:T(8,128)(2,1)S(1)} %copy-done, bf16[128,8192]{1,0:T(8,128)(2,1)} %collective-permute-done.2.other_ref, f32[1,8192]{1,0:T(1,128)S(1)} %bitcast.11, ...), custom_call_target="tpu_custom_call" | custom-call | flops 1 | bytes 1 | tf_op jit(solution)/shard_map/first/pallas_call | solution.py:60
  41.2 1.3 collective-permute-start.9
  42.5 1.6 collective-permute-start.4
  44.1 10.9 %collective-permute-done.refs_1_ = bf16[64,8192]{1,0:T(8,128)(2,1)} collective-permute-done((bf16[64,8192]{1,0:T(8,128)(2,1)}, bf16[64,8192]{1,0:T(8,128)(2,1)}, u32[]{:S(2)}, u32[]{:S(2)}) %collective-permute-start) | collective-permute-done | bytes 1048608 | tf_op jit(solution)/shard_map/ppermute | solution.py:281
  55.0 1.3 fusion.4
  56.5 0.6 collective-permute-start.8
  57.1 1.2 collective-permute-done.7.refs_4_
  58.4 0.6 collective-permute-done.8.refs_5_
  59.0 0.7 collective-permute-done.5.refs_2_
  59.8 0.7 collective-permute-done.6.refs_3_
  60.5 13.8 %multiply.6 = (f32[256,2048]{1,0:T(8,128)S(1)}, bf16[256,2048]{1,0:T(8,128)(2,1)S(1)}) custom-call(s32[1]{0:T(128)} %bitcast.2.core_ref, bf16[64,8192]{1,0:T(8,128)(2,1)S(1)} %collective-permute-done.1.refs_0_, bf16[64,8192]{1,0:T(8,128)(2,1)} %collective-permute-done.refs_1_, bf16[32,8192]{1,0:T(8,128)(2,1)S(1)} %collective-permute-done.5.refs_2_, ...), custom_call_target="tpu_custom_call" | custom-call | flops 1 | bytes 1 | tf_op jit(solution)/shard_map/multiply/pallas_call | solution.py:183
  74.3 3.6 %collective-permute-start.13 = (bf16[256,2048]{1,0:T(8,128)(2,1)S(1)}, bf16[256,2048]{1,0:T(8,128)(2,1)S(1)}, u32[]{:S(2)}, u32[]{:S(2)}) collective-permute-start(bf16[256,2048]{1,0:T(8,128)(2,1)S(1)} %get-tuple-element.41), channel_id=1, source_target_pairs={{0,1},{2,3},{5,4},{7,6},{9,8},{11,10},{12,13},{14,15},{16,17},{18,... | collective-permute-start | bytes 3145736 | tf_op jit(solution)/shard_map/ppermute | solution.py:294
  78.1 1.2 fusion.3
  79.3 20.6 %collective-permute-done.3.refs_1_ = bf16[64,8192]{1,0:T(8,128)(2,1)S(1)} collective-permute-done((bf16[64,8192]{1,0:T(8,128)(2,1)}, bf16[64,8192]{1,0:T(8,128)(2,1)S(1)}, u32[]{:S(2)}, u32[]{:S(2)}) %collective-permute-start.3) | collective-permute-done | bytes 1048608 | tf_op jit(solution)/shard_map/ppermute | solution.py:281
  99.9 1.0 fusion.2
  100.9 0.5 collective-permute-start.17
  101.4 0.9 copy-done.12
  102.4 0.5 collective-permute-start.15
  102.9 1.6 copy-done.5
  104.5 1.2 copy-done.15
  105.7 1.7 place.6.refs_2_
  107.6 17.9 %multiply.7 = (f32[256,2048]{1,0:T(8,128)S(1)}, bf16[256,2048]{1,0:T(8,128)(2,1)S(1)}) custom-call(s32[1]{0:T(128)} %bitcast.2.core_ref, bf16[64,8192]{1,0:T(8,128)(2,1)S(1)} %collective-permute-done.4.refs_0_, bf16[64,8192]{1,0:T(8,128)(2,1)S(1)} %collective-permute-done.3.refs_1_, bf16[32,8192]{1,0:T(8,128)(2,1)} %collective-permute-done.14.refs_2_, ...), custom_call_target="tpu_custom_call" | custom-call | flops 1 | bytes 1 | tf_op jit(solution)/shard_map/multiply/pallas_call | solution.py:183
  125.6 1.3 copy-done.2
  127.0 0.5 collective-permute-start.19
  128.6 0.6 collective-permute-start.10
  129.2 4.2 %collective-permute-start.26 = (bf16[256,2048]{1,0:T(8,128)(2,1)S(1)}, bf16[256,2048]{1,0:T(8,128)(2,1)S(1)}, u32[]{:S(2)}, u32[]{:S(2)}) collective-permute-start(bf16[256,2048]{1,0:T(8,128)(2,1)S(1)} %get-tuple-element.46), channel_id=1, source_target_pairs={{0,1},{2,3},{4,5},{6,7},{9,8},{11,10},{13,12},{15,14},{16,17},{18,... | collective-permute-start | bytes 3145736 | tf_op jit(solution)/shard_map/ppermute | solution.py:294
  133.4 15.1 %multiply.8 = (f32[128,2048]{1,0:T(8,128)S(1)}, bf16[128,2048]{1,0:T(8,128)(2,1)S(1)}) custom-call(s32[1]{0:T(128)} %bitcast.2.core_ref, bf16[64,8192]{1,0:T(8,128)(2,1)S(1)} %collective-permute-done.12.refs_0_, bf16[16,8192]{1,0:T(8,128)(2,1)S(1)} %collective-permute-done.18.refs_1_, bf16[16,8192]{1,0:T(8,128)(2,1)S(1)} %collective-permute-done.19.refs_2_, ...), custom_call_target="tpu_custom_call" | custom-call | flops 1 | bytes 1 | tf_op jit(solution)/shard_map/multiply/pallas_call | solution.py:183
  148.6 0.5 collective-permute-start.23
  149.2 0.8 collective-permute-done.22.refs_1_
  150.3 1.5 collective-permute-start.28
  151.8 11.8 %multiply.9 = (f32[128,2048]{1,0:T(8,128)S(1)}, bf16[128,2048]{1,0:T(8,128)(2,1)}) custom-call(s32[1]{0:T(128)} %bitcast.2.core_ref, bf16[64,5120]{1,0:T(8,128)(2,1)S(1)} %collective-permute-done.11.refs_0_, bf16[16,5120]{1,0:T(8,128)(2,1)S(1)} %collective-permute-done.22.refs_1_, bf16[16,5120]{1,0:T(8,128)(2,1)S(1)} %collective-permute-done.23.refs_2_, ...), custom_call_target="tpu_custom_call" | custom-call | flops 1 | bytes 1 | tf_op jit(solution)/shard_map/multiply/pallas_call | solution.py:183
  164.0 1.4 collective-permute-done.27.refs_1_
  165.4 5.3 %multiply.10 = (f32[128,1024]{1,0:T(8,128)S(1)}, bf16[128,1024]{1,0:T(8,128)(2,1)}) custom-call(s32[1]{0:T(128)} %bitcast.2.core_ref, bf16[64,3072]{1,0:T(8,128)(2,1)S(1)} %collective-permute-done.10.refs_0_, bf16[64,3072]{1,0:T(8,128)(2,1)S(1)} %collective-permute-done.27.refs_1_, f32[128,2048]{1,0:T(8,128)S(1)} %get-tuple-element.53.refs_2_, ...), custom_call_target="tpu_custom_call" | custom-call | flops 1 | bytes 1 | tf_op jit(solution)/shard_map/multiply/pallas_call | solution.py:183
  170.7 0.8 copy-done.19
  171.5 1.3 collective-permute-start.30
  172.8 5.7 %multiply.11 = (f32[128,1024]{1,0:T(8,128)S(1)}, bf16[128,1024]{1,0:T(8,128)(2,1)}) custom-call(s32[1]{0:T(128)} %bitcast.2.core_ref, bf16[64,3072]{1,0:T(8,128)(2,1)S(1)} %collective-permute-done.10.refs_0_, bf16[64,3072]{1,0:T(8,128)(2,1)S(1)} %collective-permute-done.27.refs_1_, f32[128,2048]{1,0:T(8,128)S(1)} %get-tuple-element.53.refs_2_, ...), custom_call_target="tpu_custom_call" | custom-call | flops 1 | bytes 1 | tf_op jit(solution)/shard_map/multiply/pallas_call | solution.py:183
  178.6 0.8 copy-done.21
  179.4 1.3 collective-permute-start.29
  180.8 1.2 copy-done.11
  182.1 1.2 place.9.refs_2_
  183.3 6.9 %collective-permute-done.29.refs_1_ = bf16[128,1024]{1,0:T(8,128)(2,1)} collective-permute-done((bf16[128,1024]{1,0:T(8,128)(2,1)}, bf16[128,1024]{1,0:T(8,128)(2,1)}, u32[]{:S(2)}, u32[]{:S(2)}) %collective-permute-start.29) | collective-permute-done | bytes 262176 | tf_op jit(solution)/shard_map/ppermute | solution.py:294
  190.2 0.9 place.10.refs_2_
  191.2 1.9 place.11
  (85 shorter events, 3.3 us)
Async XLA Ops:
  0.0 10.1 %copy-start = (bf16[128,8192]{1,0:T(8,128)(2,1)S(1)}, bf16[128,8192]{1,0:T(8,128)(2,1)}, u32[]{:S(2)}) copy-start(bf16[128,8192]{1,0:T(8,128)(2,1)} %mine_ref.1) | copy-start | bytes 6291460
  0.0 10.1 %copy-start.16 = (f32[8192]{0:T(1024)S(1)}, f32[8192]{0:T(1024)}, u32[]{:S(2)}) copy-start(f32[8192]{0:T(1024)} %param.7) | copy-start | bytes 98308
  0.0 10.1 %collective-permute-start.2 = (bf16[128,8192]{1,0:T(8,128)(2,1)}, bf16[128,8192]{1,0:T(8,128)(2,1)}, u32[]{:S(2)}, u32[]{:S(2)}) collective-permute-start(bf16[128,8192]{1,0:T(8,128)(2,1)} %mine_ref.1), channel_id=1, source_target_pairs={{0,2},{2,0},{4,6},{6,4},{8,10},{10,8},{12,14},{14,12},{1,3},{3,1},... | collective-permute-start | bytes 6291464 | tf_op jit(solution)/shard_map/ppermute | solution.py:285
  3.7 38.8 %collective-permute-start.1 = (bf16[64,8192]{1,0:T(8,128)(2,1)}, bf16[64,8192]{1,0:T(8,128)(2,1)S(1)}, u32[]{:S(2)}, u32[]{:S(2)}) collective-permute-start(bf16[64,8192]{1,0:T(8,128)(2,1)} %get-tuple-element.65), channel_id=1, source_target_pairs={{0,4},{2,6},{4,8},{6,10},{8,12},{10,14},{12,0},{14,2},{1,5},{3,7},... | collective-permute-start | bytes 3145736 | tf_op jit(solution)/shard_map/ppermute | solution.py:281
  6.2 48.8 %collective-permute-start = (bf16[64,8192]{1,0:T(8,128)(2,1)}, bf16[64,8192]{1,0:T(8,128)(2,1)}, u32[]{:S(2)}, u32[]{:S(2)}) collective-permute-start(bf16[64,8192]{1,0:T(8,128)(2,1)} %get-tuple-element.66), channel_id=1, source_target_pairs={{0,4},{2,6},{4,8},{6,10},{8,12},{10,14},{12,0},{14,2},{1,5},{3,7},... | collective-permute-start | bytes 3145736 | tf_op jit(solution)/shard_map/ppermute | solution.py:281
  41.2 33.1 %copy-start.4 = (f32[256,2048]{1,0:T(8,128)}, f32[256,2048]{1,0:T(8,128)S(1)}, u32[]{:S(2)}) copy-start(f32[256,2048]{1,0:T(8,128)S(1)} %get-tuple-element.35.refs_0_) | copy-start | bytes 6291460
  41.2 36.8 %collective-permute-start.9 = (bf16[256,2048]{1,0:T(8,128)(2,1)S(1)}, bf16[256,2048]{1,0:T(8,128)(2,1)S(1)}, u32[]{:S(2)}, u32[]{:S(2)}) collective-permute-start(bf16[256,2048]{1,0:T(8,128)(2,1)S(1)} %get-tuple-element.36), channel_id=1, source_target_pairs={{1,0},{3,2},{5,4},{7,6},{8,9},{10,11},{12,13},{14,15},{17,16},{19,... | collective-permute-start | bytes 3145736 | tf_op jit(solution)/shard_map/ppermute | solution.py:294
  42.5 35.5 %collective-permute-start.4 = (bf16[64,8192]{1,0:T(8,128)(2,1)S(1)}, bf16[64,8192]{1,0:T(8,128)(2,1)S(1)}, u32[]{:S(2)}, u32[]{:S(2)}) collective-permute-start(bf16[64,8192]{1,0:T(8,128)(2,1)S(1)} %collective-permute-done.1.refs_0_), channel_id=1, source_target_pairs={{0,4},{2,6},{4,8},{6,10},{8,12},{10,14},{12,0},{14,2},{1,5},{3,7},... | collective-permute-start | bytes 3145736 | tf_op jit(solution)/shard_map/ppermute | solution.py:281
  56.3 2.0 %collective-permute-start.7 = (bf16[32,8192]{1,0:T(8,128)(2,1)S(1)}, bf16[32,8192]{1,0:T(8,128)(2,1)S(1)}, u32[]{:S(2)}, u32[]{:S(2)}) collective-permute-start(bf16[32,8192]{1,0:T(8,128)(2,1)S(1)} %get-tuple-element.76), channel_id=1, source_target_pairs={{0,2},{2,0},{4,6},{6,4},{8,10},{10,8},{12,14},{14,12},{1,3},{3,1},... | collective-permute-start | bytes 1572872 | tf_op jit(solution)/shard_map/ppermute | solution.py:285
  56.5 2.6 %collective-permute-start.8 = (bf16[32,8192]{1,0:T(8,128)(2,1)S(1)}, bf16[32,8192]{1,0:T(8,128)(2,1)S(1)}, u32[]{:S(2)}, u32[]{:S(2)}) collective-permute-start(bf16[32,8192]{1,0:T(8,128)(2,1)S(1)} %get-tuple-element.75), channel_id=1, source_target_pairs={{0,2},{2,0},{4,6},{6,4},{8,10},{10,8},{12,14},{14,12},{1,3},{3,1},... | collective-permute-start | bytes 1572872 | tf_op jit(solution)/shard_map/ppermute | solution.py:285
  57.0 2.8 %collective-permute-start.5 = (bf16[32,8192]{1,0:T(8,128)(2,1)S(1)}, bf16[32,8192]{1,0:T(8,128)(2,1)S(1)}, u32[]{:S(2)}, u32[]{:S(2)}) collective-permute-start(bf16[32,8192]{1,0:T(8,128)(2,1)S(1)} %get-tuple-element.78), channel_id=1, source_target_pairs={{0,2},{2,0},{4,6},{6,4},{8,10},{10,8},{12,14},{14,12},{1,3},{3,1},... | collective-permute-start | bytes 1572872 | tf_op jit(solution)/shard_map/ppermute | solution.py:285
  58.3 2.2 %collective-permute-start.6 = (bf16[32,8192]{1,0:T(8,128)(2,1)S(1)}, bf16[32,8192]{1,0:T(8,128)(2,1)S(1)}, u32[]{:S(2)}, u32[]{:S(2)}) collective-permute-start(bf16[32,8192]{1,0:T(8,128)(2,1)S(1)} %get-tuple-element.77), channel_id=1, source_target_pairs={{0,2},{2,0},{4,6},{6,4},{8,10},{10,8},{12,14},{14,12},{1,3},{3,1},... | collective-permute-start | bytes 1572872 | tf_op jit(solution)/shard_map/ppermute | solution.py:285
  59.0 40.8 %collective-permute-start.3 = (bf16[64,8192]{1,0:T(8,128)(2,1)}, bf16[64,8192]{1,0:T(8,128)(2,1)S(1)}, u32[]{:S(2)}, u32[]{:S(2)}) collective-permute-start(bf16[64,8192]{1,0:T(8,128)(2,1)} %collective-permute-done.refs_1_), channel_id=1, source_target_pairs={{0,4},{2,6},{4,8},{6,10},{8,12},{10,14},{12,0},{14,2},{1,5},{3,7},... | collective-permute-start | bytes 3145736 | tf_op jit(solution)/shard_map/ppermute | solution.py:281
  74.3 25.6 %copy-start.6 = (f32[256,2048]{1,0:T(8,128)}, f32[256,2048]{1,0:T(8,128)S(1)}, u32[]{:S(2)}) copy-start(f32[256,2048]{1,0:T(8,128)S(1)} %get-tuple-element.40.refs_0_) | copy-start | bytes 6291460
  74.3 27.1 %collective-permute-start.13 = (bf16[256,2048]{1,0:T(8,128)(2,1)S(1)}, bf16[256,2048]{1,0:T(8,128)(2,1)S(1)}, u32[]{:S(2)}, u32[]{:S(2)}) collective-permute-start(bf16[256,2048]{1,0:T(8,128)(2,1)S(1)} %get-tuple-element.41), channel_id=1, source_target_pairs={{0,1},{2,3},{5,4},{7,6},{9,8},{11,10},{12,13},{14,15},{16,17},{18,... | collective-permute-start | bytes 3145736 | tf_op jit(solution)/shard_map/ppermute | solution.py:294
  78.0 23.4 %copy-start.14 = (bf16[256,2048]{1,0:T(8,128)(2,1)}, bf16[256,2048]{1,0:T(8,128)(2,1)S(1)}, u32[]{:S(2)}) copy-start(bf16[256,2048]{1,0:T(8,128)(2,1)S(1)} %collective-permute-done.9.refs_1_) | copy-start | bytes 3145732
  78.0 48.9 %collective-permute-start.12 = (bf16[64,8192]{1,0:T(8,128)(2,1)S(1)}, bf16[64,8192]{1,0:T(8,128)(2,1)S(1)}, u32[]{:S(2)}, u32[]{:S(2)}) collective-permute-start(bf16[64,8192]{1,0:T(8,128)(2,1)S(1)} %collective-permute-done.4.refs_0_), channel_id=1, source_target_pairs={{0,4},{2,6},{4,8},{6,10},{8,12},{10,14},{12,0},{14,2},{1,5},{3,7},... | collective-permute-start | bytes 3145736 | tf_op jit(solution)/shard_map/ppermute | solution.py:281
  100.9 6.6 %collective-permute-start.16 = (bf16[32,8192]{1,0:T(8,128)(2,1)}, bf16[32,8192]{1,0:T(8,128)(2,1)}, u32[]{:S(2)}, u32[]{:S(2)}) collective-permute-start(bf16[32,8192]{1,0:T(8,128)(2,1)} %get-tuple-element.72), channel_id=1, source_target_pairs={{0,2},{2,0},{4,6},{6,4},{8,10},{10,8},{12,14},{14,12},{1,3},{3,1},... | collective-permute-start | bytes 1572872 | tf_op jit(solution)/shard_map/ppermute | solution.py:285
  100.9 6.7 %collective-permute-start.17 = (bf16[32,8192]{1,0:T(8,128)(2,1)}, bf16[32,8192]{1,0:T(8,128)(2,1)}, u32[]{:S(2)}, u32[]{:S(2)}) collective-permute-start(bf16[32,8192]{1,0:T(8,128)(2,1)} %get-tuple-element.71), channel_id=1, source_target_pairs={{0,2},{2,0},{4,6},{6,4},{8,10},{10,8},{12,14},{14,12},{1,3},{3,1},... | collective-permute-start | bytes 1572872 | tf_op jit(solution)/shard_map/ppermute | solution.py:285
  101.4 6.2 %collective-permute-start.14 = (bf16[32,8192]{1,0:T(8,128)(2,1)}, bf16[32,8192]{1,0:T(8,128)(2,1)}, u32[]{:S(2)}, u32[]{:S(2)}) collective-permute-start(bf16[32,8192]{1,0:T(8,128)(2,1)} %get-tuple-element.74), channel_id=1, source_target_pairs={{0,2},{2,0},{4,6},{6,4},{8,10},{10,8},{12,14},{14,12},{1,3},{3,1},... | collective-permute-start | bytes 1572872 | tf_op jit(solution)/shard_map/ppermute | solution.py:285
  102.4 5.2 %collective-permute-start.15 = (bf16[32,8192]{1,0:T(8,128)(2,1)}, bf16[32,8192]{1,0:T(8,128)(2,1)}, u32[]{:S(2)}, u32[]{:S(2)}) collective-permute-start(bf16[32,8192]{1,0:T(8,128)(2,1)} %get-tuple-element.73), channel_id=1, source_target_pairs={{0,2},{2,0},{4,6},{6,4},{8,10},{10,8},{12,14},{14,12},{1,3},{3,1},... | collective-permute-start | bytes 1572872 | tf_op jit(solution)/shard_map/ppermute | solution.py:285
  102.9 1.6 copy-start.5
  107.5 18.0 %copy-start.7 = (f32[256,2048]{1,0:T(8,128)S(1)}, f32[256,2048]{1,0:T(8,128)}, u32[]{:S(2)}) copy-start(f32[256,2048]{1,0:T(8,128)} %copy-done.6) | copy-start | bytes 6291460
  107.5 18.0 %copy-start.13 = (bf16[256,2048]{1,0:T(8,128)(2,1)S(1)}, bf16[256,2048]{1,0:T(8,128)(2,1)}, u32[]{:S(2)}) copy-start(bf16[256,2048]{1,0:T(8,128)(2,1)} %copy-done.12) | copy-start | bytes 3145732
  107.5 41.0 %collective-permute-start.11 = (bf16[64,5120]{1,0:T(8,128)(2,1)S(1)}, bf16[64,5120]{1,0:T(8,128)(2,1)S(1)}, u32[]{:S(2)}, u32[]{:S(2)}) collective-permute-start(bf16[64,5120]{1,0:T(8,128)(2,1)S(1)} %slice.74), channel_id=1, source_target_pairs={{0,4},{2,6},{4,8},{6,10},{8,12},{10,14},{12,0},{14,2},{1,5},{3,7},... | collective-permute-start | bytes 1966088 | tf_op jit(solution)/shard_map/ppermute | solution.py:281
  125.5 1.4 copy-start.2
  127.0 1.6 collective-permute-start.18
  127.0 2.2 %collective-permute-start.19 = (bf16[16,8192]{1,0:T(8,128)(2,1)S(1)}, bf16[16,8192]{1,0:T(8,128)(2,1)S(1)}, u32[]{:S(2)}, u32[]{:S(2)}) collective-permute-start(bf16[16,8192]{1,0:T(8,128)(2,1)S(1)} %get-tuple-element.69), channel_id=1, source_target_pairs={{0,2},{2,0},{4,6},{6,4},{8,10},{10,8},{12,14},{14,12},{1,3},{3,1},... | collective-permute-start | bytes 786440 | tf_op jit(solution)/shard_map/ppermute | solution.py:285
  127.5 5.9 %collective-permute-start.20 = (bf16[16,8192]{1,0:T(8,128)(2,1)S(1)}, bf16[16,8192]{1,0:T(8,128)(2,1)S(1)}, u32[]{:S(2)}, u32[]{:S(2)}) collective-permute-start(bf16[16,8192]{1,0:T(8,128)(2,1)S(1)} %get-tuple-element.68), channel_id=1, source_target_pairs={{0,2},{2,0},{4,6},{6,4},{8,10},{10,8},{12,14},{14,12},{1,3},{3,1},... | collective-permute-start | bytes 786440 | tf_op jit(solution)/shard_map/ppermute | solution.py:285
  127.6 5.8 %collective-permute-start.21 = (bf16[16,8192]{1,0:T(8,128)(2,1)S(1)}, bf16[16,8192]{1,0:T(8,128)(2,1)S(1)}, u32[]{:S(2)}, u32[]{:S(2)}) collective-permute-start(bf16[16,8192]{1,0:T(8,128)(2,1)S(1)} %get-tuple-element.67), channel_id=1, source_target_pairs={{0,2},{2,0},{4,6},{6,4},{8,10},{10,8},{12,14},{14,12},{1,3},{3,1},... | collective-permute-start | bytes 786440 | tf_op jit(solution)/shard_map/ppermute | solution.py:285
  128.6 35.0 %collective-permute-start.10 = (bf16[64,3072]{1,0:T(8,128)(2,1)S(1)}, bf16[64,3072]{1,0:T(8,128)(2,1)S(1)}, u32[]{:S(2)}, u32[]{:S(2)}) collective-permute-start(bf16[64,3072]{1,0:T(8,128)(2,1)S(1)} %slice.73), channel_id=1, source_target_pairs={{0,4},{2,6},{4,8},{6,10},{8,12},{10,14},{12,0},{14,2},{1,5},{3,7},... | collective-permute-start | bytes 1179656 | tf_op jit(solution)/shard_map/ppermute | solution.py:281
  129.2 34.8 %collective-permute-start.26 = (bf16[256,2048]{1,0:T(8,128)(2,1)S(1)}, bf16[256,2048]{1,0:T(8,128)(2,1)S(1)}, u32[]{:S(2)}, u32[]{:S(2)}) collective-permute-start(bf16[256,2048]{1,0:T(8,128)(2,1)S(1)} %get-tuple-element.46), channel_id=1, source_target_pairs={{0,1},{2,3},{4,5},{6,7},{9,8},{11,10},{13,12},{15,14},{16,17},{18,... | collective-permute-start | bytes 3145736 | tf_op jit(solution)/shard_map/ppermute | solution.py:294
  148.5 3.3 %copy-start.10 = (f32[128,2048]{1,0:T(8,128)}, f32[128,2048]{1,0:T(8,128)S(1)}, u32[]{:S(2)}) copy-start(f32[128,2048]{1,0:T(8,128)S(1)} %get-tuple-element.50.refs_0_) | copy-start | bytes 3145732
  148.6 1.5 collective-permute-start.22
  148.6 1.6 collective-permute-start.23
  149.1 2.6 %collective-permute-start.24 = (bf16[16,5120]{1,0:T(8,128)(2,1)S(1)}, bf16[16,5120]{1,0:T(8,128)(2,1)S(1)}, u32[]{:S(2)}, u32[]{:S(2)}) collective-permute-start(bf16[16,5120]{1,0:T(8,128)(2,1)S(1)} %get-tuple-element.80), channel_id=1, source_target_pairs={{0,2},{2,0},{4,6},{6,4},{8,10},{10,8},{12,14},{14,12},{1,3},{3,1},... | collective-permute-start | bytes 491528 | tf_op jit(solution)/shard_map/ppermute | solution.py:285
  150.0 1.7 collective-permute-start.25
  150.3 22.5 %collective-permute-start.28 = (bf16[128,2048]{1,0:T(8,128)(2,1)S(1)}, bf16[128,2048]{1,0:T(8,128)(2,1)S(1)}, u32[]{:S(2)}, u32[]{:S(2)}) collective-permute-start(bf16[128,2048]{1,0:T(8,128)(2,1)S(1)} %get-tuple-element.51), channel_id=1, source_target_pairs={{1,0},{3,2},{4,5},{6,7},{8,9},{10,11},{13,12},{15,14},{17,16},{19,... | collective-permute-start | bytes 1572872 | tf_op jit(solution)/shard_map/ppermute | solution.py:294
  163.6 1.8 collective-permute-start.27
  164.0 6.7 %copy-start.8 = (bf16[256,2048]{1,0:T(8,128)(2,1)}, bf16[256,2048]{1,0:T(8,128)(2,1)S(1)}, u32[]{:S(2)}) copy-start(bf16[256,2048]{1,0:T(8,128)(2,1)S(1)} %collective-permute-done.26.refs_1_) | copy-start | bytes 3145732
  171.5 11.8 %collective-permute-start.30 = (bf16[128,1024]{1,0:T(8,128)(2,1)}, bf16[128,1024]{1,0:T(8,128)(2,1)S(1)}, u32[]{:S(2)}, u32[]{:S(2)}) collective-permute-start(bf16[128,1024]{1,0:T(8,128)(2,1)} %get-tuple-element.57), channel_id=1, source_target_pairs={{1,0},{3,2},{4,5},{6,7},{8,9},{10,11},{13,12},{15,14},{17,16},{19,... | collective-permute-start | bytes 786440 | tf_op jit(solution)/shard_map/ppermute | solution.py:294
  172.8 5.7 %copy-start.17 = (bf16[128,2048]{1,0:T(8,128)(2,1)}, bf16[128,2048]{1,0:T(8,128)(2,1)S(1)}, u32[]{:S(2)}) copy-start(bf16[128,2048]{1,0:T(8,128)(2,1)S(1)} %collective-permute-done.28.refs_1_) | copy-start | bytes 1572868
  172.8 7.9 %copy-start.3 = (f32[256,2048]{1,0:T(8,128)S(1)}, f32[256,2048]{1,0:T(8,128)}, u32[]{:S(2)}) copy-start(f32[256,2048]{1,0:T(8,128)} %copy-done.2) | copy-start | bytes 6291460
  172.8 7.9 %copy-start.9 = (bf16[256,2048]{1,0:T(8,128)(2,1)S(1)}, bf16[256,2048]{1,0:T(8,128)(2,1)}, u32[]{:S(2)}) copy-start(bf16[256,2048]{1,0:T(8,128)(2,1)} %copy-done.8) | copy-start | bytes 3145732
  179.4 10.9 %collective-permute-start.29 = (bf16[128,1024]{1,0:T(8,128)(2,1)}, bf16[128,1024]{1,0:T(8,128)(2,1)}, u32[]{:S(2)}, u32[]{:S(2)}) collective-permute-start(bf16[128,1024]{1,0:T(8,128)(2,1)} %get-tuple-element.60), channel_id=1, source_target_pairs={{1,0},{3,2},{4,5},{6,7},{8,9},{10,11},{13,12},{15,14},{17,16},{19,... | collective-permute-start | bytes 786440 | tf_op jit(solution)/shard_map/ppermute | solution.py:294
  180.8 1.3 copy-start.18
  182.1 8.1 %copy-start.20 = (f32[128,1024]{1,0:T(8,128)S(1)}, f32[128,1024]{1,0:T(8,128)}, u32[]{:S(2)}) copy-start(f32[128,1024]{1,0:T(8,128)} %copy-done.19) | copy-start | bytes 1572868
  183.3 7.9 %copy-start.22 = (f32[128,1024]{1,0:T(8,128)S(1)}, f32[128,1024]{1,0:T(8,128)}, u32[]{:S(2)}) copy-start(f32[128,1024]{1,0:T(8,128)} %copy-done.21) | copy-start | bytes 1572868
  (6 other events, 6.2 us)

commit v10 on v9

v10 whole, which is shorter than its diff:
```python
import functools

import jax
import jax.numpy as jnp
from jax import lax
from jax.experimental import pallas as pl
from jax.experimental.pallas import tpu as pltpu
from jax.sharding import PartitionSpec as P

damping = 0.05
lanes = 128
cores = 2
mib = 1 << 20
in_vmem = pl.BlockSpec(memory_space=pltpu.VMEM)
in_smem = pl.BlockSpec(memory_space=pltpu.SMEM)
anywhere = pl.BlockSpec(memory_space=pl.ANY)
small = pl.CostEstimate(flops=1, bytes_accessed=1, transcendentals=0)


def first_kernel(core_ref, mine_ref, other_ref, fisher_ref, codes_ref, exps_ref, train_ref, keep_ref,
                 send_ref, left, spread):
    rows, width = mine_ref.shape
    depth = min(width, 1024)
    core = core_ref[0]

    @pl.when(pl.program_id(0) == 0)
    def _():
        block = lax.broadcasted_iota(jnp.int32, spread.shape, 0)
        col = lax.broadcasted_iota(jnp.int32, spread.shape, 1)
        spread[...] = jnp.where(col // lanes == block, 1.0, 0.0).astype(jnp.bfloat16)
        for ref, place in ((mine_ref, core), (other_ref, 1 - core)):
            spot = pl.ds(pl.multiple_of(place * rows, rows), rows)
            for start in range(0, width, depth):
                cols = slice(start, start + depth)
                scale = 1.0 / (fisher_ref[:, cols] + damping)
                left[spot, cols] = (ref[:, cols].astype(jnp.float32) * scale).astype(jnp.bfloat16)

    exps = exps_ref[...]
    up = jnp.left_shift(1, jnp.maximum(exps, 0)).astype(jnp.float32)
    down = jnp.left_shift(1, jnp.maximum(-exps, 0)).astype(jnp.float32)
    factor = (up / down).astype(jnp.bfloat16)
    for start in range(0, width, depth):
        cols = slice(start, start + depth)
        wide = jnp.dot(factor, spread[:, cols], preferred_element_type=jnp.float32)
        train_ref[:, cols] = codes_ref[:, cols] * wide.astype(jnp.bfloat16)
    sums = lax.dot_general(
        left[...], train_ref[...], (((1,), (1,)), ((), ())), preferred_element_type=jnp.float32
    )
    keep_ref[...] = sums
    send_ref[...] = sums.astype(jnp.bfloat16)


def first(core, mine, other, fisher, codes, exps):
    rows, width = mine.shape
    count = codes.shape[0]
    blocks = width // lanes
    tile = min(count, 256)
    shape = (cores * rows, count)
    return pl.pallas_call(
        first_kernel,
        grid=(count // tile,),
        in_specs=[
            in_smem,
            pl.BlockSpec((rows, width), lambda i: (0, 0)),
            pl.BlockSpec((rows, width), lambda i: (0, 0)),
            pl.BlockSpec((1, width), lambda i: (0, 0)),
            pl.BlockSpec((tile, width), lambda i: (i, 0)),
            pl.BlockSpec((tile, blocks), lambda i: (i, 0)),
        ],
        out_specs=[
            pl.BlockSpec((tile, width), lambda i: (i, 0)),
            pl.BlockSpec((cores * rows, tile), lambda i: (0, i)),
            pl.BlockSpec((cores * rows, tile), lambda i: (0, i)),
        ],
        out_shape=[
            jax.ShapeDtypeStruct((count, width), jnp.bfloat16),
            jax.ShapeDtypeStruct(shape, jnp.float32),
            jax.ShapeDtypeStruct(shape, jnp.bfloat16),
        ],
        scratch_shapes=[
            pltpu.VMEM((cores * rows, width), jnp.bfloat16),
            pltpu.VMEM((blocks, width), jnp.bfloat16),
        ],
        compiler_params=pltpu.CompilerParams(vmem_limit_bytes=36 * mib),
        cost_estimate=small,
        name="first",
    )(core, mine, other, fisher, codes, exps)


def multiply_kernel(counts, start, top, mine_ref, spot_ref, core_ref, *refs):
    refs = list(refs)
    mine_refs, other_refs, _ = [[refs.pop(0) for _ in range(size)] for size in counts]
    fisher_ref, train_ref, scores_ref, send_ref = refs[:4]
    left, held, keep, send, in_sems, train_sems, keep_sems, send_sems = refs[4:]
    rows = sum(ref.shape[0] for ref in mine_refs)
    slots, tile, width = held.shape
    tiles = keep.shape[1] // tile
    half = tile // 2
    depth = min(width, 1024)
    core = core_ref[0]

    def fetches(i):
        slot = lax.rem(i, slots)
        return [
            pltpu.make_async_copy(
                train_ref.at[pl.ds(pl.multiple_of(i * tile, tile) + top + part * half, half)],
                held.at[slot, pl.ds(part * half, half)],
                train_sems.at[slot, part],
            )
            for part in range(2)
        ]

    loads = []
    for group, place in ((mine_refs, core), (other_refs, 1 - core)):
        offset = 0
        for ref in group:
            spot = pl.ds(pl.multiple_of(place * rows, rows) + offset, ref.shape[0])
            loads.append(pltpu.make_async_copy(ref, left.at[spot], in_sems.at[len(loads)]))
            offset += ref.shape[0]
    for load in loads:
        load.start()
    for i in range(min(slots, tiles)):
        for fetch in fetches(i):
            fetch.start()
    for load in loads:
        load.wait()

    @pl.loop(0, width // depth)
    def _(k):
        cols = pl.ds(pl.multiple_of(k * depth, depth), depth)
        scale = 1.0 / (fisher_ref[:, cols] + damping)
        left[:, cols] = (left[:, cols].astype(jnp.float32) * scale).astype(jnp.bfloat16)

    def keeps(i):
        cols = pl.ds(pl.multiple_of(i * tile, tile), tile)
        return [
            pltpu.make_async_copy(
                keep.at[pl.ds(c * rows, rows), cols],
                scores_ref.at[
                    spot_ref[0], c, pl.ds(start, rows),
                    pl.ds(pl.multiple_of(i * tile, tile) + top, tile),
                ],
                keep_sems.at[i, c],
            )
            for c in range(cores)
        ]

    def sends(i):
        cols = pl.ds(pl.multiple_of(i * tile, tile), tile)
        return [pltpu.make_async_copy(send.at[:, cols], send_ref.at[:, cols], send_sems.at[i])]

    @pl.loop(0, tiles)
    def _(i):
        cols = pl.ds(pl.multiple_of(i * tile, tile), tile)
        for fetch in fetches(i):
            fetch.wait()
        sums = lax.dot_general(
            left[...], held[lax.rem(i, slots)], (((1,), (1,)), ((), ())),
            preferred_element_type=jnp.float32,
        )

        @pl.when(mine_ref[0] == 1)
        def _():
            keep[:, cols] = sums
            for copy in keeps(i):
                copy.start()

        @pl.when(mine_ref[0] == 0)
        def _():
            send[:, cols] = sums.astype(jnp.bfloat16)
            for copy in sends(i):
                copy.start()

        @pl.when(i + slots < tiles)
        def _():
            for fetch in fetches(i + slots):
                fetch.start()

    @pl.loop(0, tiles)
    def _(i):
        @pl.when(mine_ref[0] == 1)
        def _():
            for copy in keeps(i):
                copy.wait()

        @pl.when(mine_ref[0] == 0)
        def _():
            for copy in sends(i):
                copy.wait()


def multiply(scores, shape, where, core, mine, other, fisher, train, start, span=None):
    rows = sum(part.shape[0] for part in mine)
    width = mine[0].shape[1]
    top, bottom = span or (0, train.shape[0])
    count = bottom - top
    tile = min(count, 256)
    slots = 4
    block = (cores * rows, count)
    given = [] if scores is None else [scores]
    counts = (len(mine), len(other), len(given))
    return pl.pallas_call(
        functools.partial(multiply_kernel, counts, start, top),
        in_specs=[in_smem] * 3 + [anywhere] * sum(counts) + [in_vmem, anywhere],
        out_specs=[anywhere] * 2,
        out_shape=[
            jax.ShapeDtypeStruct(shape, jnp.float32), jax.ShapeDtypeStruct(block, jnp.bfloat16),
        ],
        scratch_shapes=[
            pltpu.VMEM((cores * rows, width), jnp.bfloat16),
            pltpu.VMEM((slots, tile, width), jnp.bfloat16),
            pltpu.VMEM(block, jnp.float32),
            pltpu.VMEM(block, jnp.bfloat16),
            pltpu.SemaphoreType.DMA((len(mine) + len(other),)),
            pltpu.SemaphoreType.DMA((slots, 2)),
            pltpu.SemaphoreType.DMA((count // tile, cores)),
            pltpu.SemaphoreType.DMA((count // tile,)),
        ],
        input_output_aliases={3 + len(mine) + len(other): 0} if given else {},
        compiler_params=pltpu.CompilerParams(vmem_limit_bytes=27 * mib),
        cost_estimate=small,
        name="multiply",
    )(*where, core, *mine, *other, *given, fisher, train)


def place_kernel(start, cols, kept, mine_ref, spot_ref, *refs):
    first_ref, received = refs[:kept], refs[kept:kept + len(cols)]
    scores_ref, total, in_sems, out_sems, *terms = refs[kept + len(cols) + 1:]
    rows = total.shape[0] // cores

    def own(c):
        return scores_ref.at[spot_ref[0], c, pl.ds(start, rows)]

    @pl.when(mine_ref[0] == 1)
    def _():
        if kept:
            loads = [pltpu.make_async_copy(first_ref[0], total, in_sems.at[0])]
        else:
            loads = [
                pltpu.make_async_copy(own(c), total.at[pl.ds(c * rows, rows)], in_sems.at[c])
                for c in range(cores)
            ]
        for index, ref in enumerate(received):
            loads.append(pltpu.make_async_copy(ref, terms[index], in_sems.at[cores + index]))
        for load in loads:
            load.start()
        for load in loads:
            load.wait()
        for col, term in zip(cols, terms):
            span = slice(col, col + term.shape[1])
            total[:, span] += term[...].astype(jnp.float32)
        copies = [
            pltpu.make_async_copy(total.at[pl.ds(c * rows, rows)], own(c), out_sems.at[c])
            for c in range(cores)
        ]
        for copy in copies:
            copy.start()
        for copy in copies:
            copy.wait()


def place(scores, where, kept, received, cols, start):
    count = scores.shape[-1]
    rows = received[0].shape[0]
    operands = [*kept, *received, scores]
    return pl.pallas_call(
        functools.partial(place_kernel, start, cols, len(kept)),
        in_specs=[in_smem] * 2 + [anywhere] * len(operands),
        out_specs=anywhere,
        out_shape=jax.ShapeDtypeStruct(scores.shape, jnp.float32),
        scratch_shapes=[
            pltpu.VMEM((rows, count), jnp.float32),
            pltpu.SemaphoreType.DMA((cores + len(received),)),
            pltpu.SemaphoreType.DMA((cores,)),
        ] + [pltpu.VMEM(term.shape, jnp.bfloat16) for term in received],
        input_output_aliases={1 + len(operands): 0},
        compiler_params=pltpu.CompilerParams(vmem_limit_bytes=12 * mib),
        cost_estimate=small,
        name="place",
    )(*where, *operands)


def cut(whole, count):
    rows = whole.shape[0] // count
    return [whole[part * rows:(part + 1) * rows] for part in range(count)]


def after(array, *others):
    return lax.optimization_barrier((array, *others))[0]


def shards(blks, owners, grad_codes, scale_exps, val_grads, fisher):
    chips = blks // cores
    chips_per_owner = chips // owners
    me = lax.axis_index("dim")
    blk = lax.axis_index("blk")
    chip, core = blk // cores, lax.rem(blk, cores)[None]
    own, width = val_grads.shape
    count = grad_codes.shape[0]
    fisher = fisher[None, :]
    shape = (chips_per_owner, cores, own, count)

    def shift(panel):
        pairs = [
            (z * cores + c, (z + 1) % chips * cores + c) for z in range(chips) for c in range(cores)
        ]
        return lax.ppermute(panel, "blk", pairs)

    def swap(parts):
        pairs = [(b, b ^ 1) for b in range(blks)]
        return [lax.ppermute(part, "blk", pairs) for part in parts]

    def exchange(send, by):
        received = []
        for step in range(1, owners):
            pairs = []
            for b in range(blks):
                owner = (b // cores - by) % chips // chips_per_owner
                pairs.append((b * owners + (owner + step) % owners, b * owners + owner))
            received.append(lax.ppermute(send, ("blk", "dim"), pairs))
        return received

    def whose(by):
        source = lax.rem(chip - by + chips, chips)
        mine = (source // chips_per_owner == me).astype(jnp.int32)[None]
        return mine, lax.rem(source, chips_per_owner)[None]

    hops = chips - 1
    low_flow, high_flow = [shift(piece) for piece in cut(val_grads, 2)]
    train, keep, send = first(core, val_grads, *swap([val_grads]), fisher, grad_codes, scale_exps)
    scores, kept = None, [keep]
    for hop in range(1, hops):
        received = exchange(send, hop - 1)
        low_piece = after(low_flow, send, *([] if scores is None else [scores]))
        low_flow = shift(low_piece)
        low_other = swap(cut(low_piece, 2))
        high_piece = after(high_flow, low_piece)
        high_flow = shift(high_piece)
        high_other = swap(cut(high_piece, 2))
        if hop > 1:
            low_piece = after(low_piece, *received)
        scores, send = multiply(
            scores, shape, whose(hop), core, [low_piece, high_piece], [*low_other, *high_other],
            fisher, train, 0,
        )
        received = [after(term, send) for term in received]
        scores = place(scores, whose(hop - 1), kept, received, [0] * len(received), 0)
        kept = []
    earlier = exchange(send, hops - 1)
    low_piece = after(low_flow, send, scores)
    small = max(1, min(4, low_piece.shape[0] // 16))
    scores, send = multiply(
        scores, shape, whose(hops), core, [low_piece], swap(cut(low_piece, small)), fisher, train, 0
    )
    received = exchange(send, hops)
    high_piece = after(high_flow, send)
    high_other = swap(cut(high_piece, small))
    high_piece = after(high_piece, *earlier)
    half = count // 2
    halves = []
    for top in (0, half):
        if top:
            high_piece = after(high_piece, send, *received)
        scores, send = multiply(
            scores, shape, whose(hops), core, [high_piece], high_other, fisher, train, own // 2,
            (top, top + half),
        )
        halves.append(exchange(send, hops))
    earlier = [after(term, send) for term in earlier]
    scores = place(scores, whose(hops - 1), [], earlier, [0] * len(earlier), 0)
    received = [after(term, scores) for term in received]
    scores = place(scores, whose(hops), [], received, [0] * len(received), 0)
    cols = [0] * len(received) + [half] * len(received)
    scores = place(scores, whose(hops), [], halves[0] + halves[1], cols, own // 2)
    return scores.reshape(chips_per_owner * cores * own, count)


def solution(mesh):
    in_specs = (
        P(("groups", "blk"), "dim"),
        P(("groups", "blk"), "dim"),
        P(("groups", "blk"), "dim"),
        P("dim"),
    )
    out_specs = P("dim", ("groups", "blk"))
    body = functools.partial(shards, mesh.shape["blk"], mesh.shape["dim"])
    return jax.shard_map(body, mesh=mesh, in_specs=in_specs, out_specs=out_specs, check_vma=False)
```

time: 194 us -> 199 us (1.026)
  local copies, waits for them, and re-layouts: 18.5 us -> 26.8 us
  waiting for transfers between devices: 44.6 us -> 40 us
  starting transfers between devices: 24.2 us -> 27.9 us
  Pallas kernels: 105 us -> 103 us
    ppermute x7 -> x6, waiting for transfers between devices: 31.5 us -> 24.4 us  [shift(): return lax.ppermute(panel, 'blk', pairs)]
    ppermute x6, waiting for transfers between devices: 6.92 us -> 12 us  [exchange(): received.append(lax.ppermute(send, ('blk', 'dim'), pairs))]
    slice x7, local copies, waits for them, and re-layouts: 6.88 us -> 11.7 us  [cut(): return [whole[part * rows:(part + 1) * rows] for part in range(count)]]
    unnamed x47 -> x39, local copies, waits for them, and re-layouts: 11.5 us -> 15.1 us
    ppermute x6, starting transfers between devices: 13.1 us -> 16.1 us  [exchange(): received.append(lax.ppermute(send, ('blk', 'dim'), pairs))]
    ppermute x18 -> x17, waiting for transfers between devices: 6.13 us -> 3.61 us  [swap(): return [lax.ppermute(part, 'blk', pairs) for part in parts]]
    pallas_call x12 -> x10, Pallas kernels: 75.3 us -> 73 us  [the longest x5 66.5 us: multiply(): pl.pallas_call(functools.partial(multiply_kernel, counts, start, top), in...]
    ppermute x7 -> x6, starting transfers between devices: 6.53 us -> 7.76 us  [shift(): return lax.ppermute(panel, 'blk', pairs)]
  transfers between devices with their start and end apart: 31 -> 29, of which waited for: 11 -> 12; matrix products, arithmetic and copies ran while one was open for 5% -> 7% of each run, Pallas kernels for 53% -> 51%
where the time goes in v10:
time: 199 us
  Pallas kernels  103 us (52%)
  waiting for transfers between devices  40 us (20%)
  starting transfers between devices  27.9 us (14%)
  local copies, waits for them, and re-layouts  26.8 us (13%)
    pallas_call x5, Pallas kernels, multiply(): pl.pallas_call(functools.partial(multiply_kernel, counts, start, top), in...  66.5 us
    pallas_call x1, Pallas kernels, first(): pl.pallas_call(first_kernel, grid=(count // tile,), in_specs=[in_smem, pl...  30.4 us
    ppermute x6, waiting for transfers between devices, shift(): return lax.ppermute(panel, 'blk', pairs)  24.4 us
    ppermute x6, starting transfers between devices, exchange(): received.append(lax.ppermute(send, ('blk', 'dim'), pairs))  16.1 us
    unnamed x39, local copies, waits for them, and re-layouts  15.1 us
    ppermute x6, waiting for transfers between devices, exchange(): received.append(lax.ppermute(send, ('blk', 'dim'), pairs))  12 us
    slice x7, local copies, waits for them, and re-layouts, cut(): return [whole[part * rows:(part + 1) * rows] for part in range(count)]  11.7 us
    ppermute x6, starting transfers between devices, shift(): return lax.ppermute(panel, 'blk', pairs)  7.76 us
  transfers between devices with their start and end apart: 29, of which 12 were waited for; matrix products, arithmetic and copies ran while one was open for 7% of the time, Pallas kernels for 51%

profile of v10, /device:TPU:0, one launch (start us, length us, event | category | flops | bytes accessed | tf_op | source)
XLA Modules:
  0.0 198.6 jit_solution(928994284455889488)
XLA Ops:
  0.5 3.3 %fusion = (bf16[64,8192]{1,0:T(8,128)(2,1)}, bf16[64,8192]{1,0:T(8,128)(2,1)}) fusion(bf16[128,8192]{1,0:T(8,128)(2,1)} %mine_ref.1), kind=kLoop, calls=%fused_computation | loop fusion | bytes 4194304 | tf_op jit(solution)/shard_map/slice | solution.py:285
  3.7 2.5 %collective-permute-start.1 = (bf16[64,8192]{1,0:T(8,128)(2,1)}, bf16[64,8192]{1,0:T(8,128)(2,1)}, u32[]{:S(2)}, u32[]{:S(2)}) collective-permute-start(bf16[64,8192]{1,0:T(8,128)(2,1)} %get-tuple-element.57), channel_id=1, source_target_pairs={{0,4},{2,6},{4,8},{6,10},{8,12},{10,14},{12,0},{14,2},{1,5},{3,7},... | collective-permute-start | bytes 3145736 | tf_op jit(solution)/shard_map/ppermute | solution.py:307
  6.3 1.6 collective-permute-start
  7.8 1.4 copy.14.exps_ref
  9.3 30.4 %first.1 = (bf16[2048,8192]{1,0:T(8,128)(2,1)}, f32[256,2048]{1,0:T(8,128)S(1)}, bf16[256,2048]{1,0:T(8,128)(2,1)}) custom-call(s32[1]{0:T(128)} %bitcast.2.core_ref, bf16[128,8192]{1,0:T(8,128)(2,1)S(1)} %copy-done, bf16[128,8192]{1,0:T(8,128)(2,1)} %collective-permute-done.2.other_ref, f32[1,8192]{1,0:T(1,128)S(1)} %bitcast.11, ...), custom_call_target="tpu_custom_call" | custom-call | flops 1 | bytes 1 | tf_op jit(solution)/shard_map/first/pallas_call | solution.py:59
  39.7 1.3 copy-done.1
  41.0 1.3 collective-permute-start.9
  42.3 1.6 collective-permute-start.4
  43.9 11.2 %collective-permute-done.refs_1_ = bf16[64,8192]{1,0:T(8,128)(2,1)} collective-permute-done((bf16[64,8192]{1,0:T(8,128)(2,1)}, bf16[64,8192]{1,0:T(8,128)(2,1)}, u32[]{:S(2)}, u32[]{:S(2)}) %collective-permute-start) | collective-permute-done | bytes 1048608 | tf_op jit(solution)/shard_map/ppermute | solution.py:307
  55.1 2.1 %fusion.5 = (bf16[32,8192]{1,0:T(8,128)(2,1)}, bf16[32,8192]{1,0:T(8,128)(2,1)S(1)}) fusion(bf16[64,8192]{1,0:T(8,128)(2,1)} %collective-permute-done.refs_1_), kind=kLoop, calls=%fused_computation.5 | loop fusion | bytes 2097152 | tf_op jit(solution)/shard_map/slice | solution.py:285
  57.2 2.2 %fusion.6 = (bf16[32,8192]{1,0:T(8,128)(2,1)}, bf16[32,8192]{1,0:T(8,128)(2,1)}) fusion(bf16[64,8192]{1,0:T(8,128)(2,1)} %collective-permute-done.1.refs_0_), kind=kLoop, calls=%fused_computation.6 | loop fusion | bytes 2097152 | tf_op jit(solution)/shard_map/slice | solution.py:285
  59.9 0.8 copy-done.6
  61.3 1.1 collective-permute-done.8.refs_5_
  62.4 0.8 copy-done.8
  63.3 1.0 copy-done.7
  64.3 1.0 copy-done.9
  65.4 14.5 %multiply.5 = (f32[2,2,128,2048]{3,2,1,0:T(8,128)}, bf16[256,2048]{1,0:T(8,128)(2,1)S(1)}) custom-call(s32[1]{0:T(128)} %bitcast.4.mine_ref, s32[1]{0:T(128)} %bitcast.5.spot_ref, s32[1]{0:T(128)} %bitcast.2.core_ref, bf16[64,8192]{1,0:T(8,128)(2,1)} %collective-permute-done.1.refs_0_, bf16[64,8192]{1,0:T(8,128)(2,1)} %collective-permute-done.refs_1_, ...), custom_call_target="tpu_custom_call" | custom-call | flops 1 | bytes 1 | tf_op jit(solution)/shard_map/multiply/pallas_call | solution.py:202
  79.8 4.0 %collective-permute-start.12 = (bf16[256,2048]{1,0:T(8,128)(2,1)S(1)}, bf16[256,2048]{1,0:T(8,128)(2,1)S(1)}, u32[]{:S(2)}, u32[]{:S(2)}) collective-permute-start(bf16[256,2048]{1,0:T(8,128)(2,1)S(1)} %get-tuple-element.35), channel_id=1, source_target_pairs={{0,1},{2,3},{5,4},{7,6},{9,8},{11,10},{12,13},{14,15},{16,17},{18,... | collective-permute-start | bytes 3145736 | tf_op jit(solution)/shard_map/ppermute | solution.py:320
  83.9 1.8 place.5.refs_6_
  85.7 1.0 fusion.4
  86.7 13.2 %collective-permute-done.3.refs_1_ = bf16[64,8192]{1,0:T(8,128)(2,1)S(1)} collective-permute-done((bf16[64,8192]{1,0:T(8,128)(2,1)}, bf16[64,8192]{1,0:T(8,128)(2,1)S(1)}, u32[]{:S(2)}, u32[]{:S(2)}) %collective-permute-start.3) | collective-permute-done | bytes 1048608 | tf_op jit(solution)/shard_map/ppermute | solution.py:307
  99.9 0.9 fusion.3
  101.3 5.4 %collective-permute-done.12.refs_0_ = bf16[256,2048]{1,0:T(8,128)(2,1)S(1)} collective-permute-done((bf16[256,2048]{1,0:T(8,128)(2,1)S(1)}, bf16[256,2048]{1,0:T(8,128)(2,1)S(1)}, u32[]{:S(2)}, u32[]{:S(2)}) %collective-permute-start.12) | collective-permute-done | bytes 1048608 | tf_op jit(solution)/shard_map/ppermute | solution.py:320
  106.7 1.0 copy-done.4
  107.7 0.8 copy-done.10
  108.6 1.9 collective-permute-start.10
  110.5 1.0 copy-done.11
  111.6 17.7 %multiply.6 = (f32[2,2,128,2048]{3,2,1,0:T(8,128)}, bf16[256,2048]{1,0:T(8,128)(2,1)S(1)}) custom-call(s32[1]{0:T(128)} %bitcast.8.mine_ref, s32[1]{0:T(128)} %bitcast.9.spot_ref, s32[1]{0:T(128)} %bitcast.2.core_ref, bf16[64,8192]{1,0:T(8,128)(2,1)S(1)} %collective-permute-done.4.refs_0_, ...), custom_call_target="tpu_custom_call", output_to_operand_aliasing={{0}: (9, {})} | custom-call | flops 1 | bytes 1 | tf_op jit(solution)/shard_map/multiply/pallas_call | solution.py:202
  129.3 0.9 copy-done.18
  130.2 2.1 %fusion.2 = (bf16[16,8192]{1,0:T(8,128)(2,1)S(1)}, bf16[16,8192]{1,0:T(8,128)(2,1)}, bf16[16,8192]{1,0:T(8,128)(2,1)}, bf16[16,8192]{1,0:T(8,128)(2,1)}) fusion(bf16[64,8192]{1,0:T(8,128)(2,1)} %collective-permute-done.11.refs_0_), kind=kLoop, calls=%fused_computation.2 | loop fusion | bytes 2097152 | tf_op jit(solution)/shard_map/slice | solution.py:285
  133.4 0.7 collective-permute-done.17.refs_1_
  134.1 6.7 %collective-permute-start.21 = (bf16[256,2048]{1,0:T(8,128)(2,1)}, bf16[256,2048]{1,0:T(8,128)(2,1)S(1)}, u32[]{:S(2)}, u32[]{:S(2)}) collective-permute-start(bf16[256,2048]{1,0:T(8,128)(2,1)} %copy-done.18), channel_id=1, source_target_pairs={{0,1},{2,3},{4,5},{6,7},{9,8},{11,10},{13,12},{15,14},{16,17},{18,... | collective-permute-start | bytes 3145736 | tf_op jit(solution)/shard_map/ppermute | solution.py:320
  140.9 0.7 copy-done.12
  141.6 0.7 copy-done.14
  142.3 0.7 copy-done.16
  143.0 0.9 copy-done.13
  144.0 0.9 copy-done.15
  144.9 0.9 copy-done.17
  145.9 15.7 %multiply.7 = (f32[2,2,128,2048]{3,2,1,0:T(8,128)}, bf16[128,2048]{1,0:T(8,128)(2,1)S(1)}) custom-call(s32[1]{0:T(128)} %bitcast.mine_ref, s32[1]{0:T(128)} %bitcast.1.spot_ref, s32[1]{0:T(128)} %bitcast.2.core_ref, bf16[64,8192]{1,0:T(8,128)(2,1)} %collective-permute-done.11.refs_0_, ...), custom_call_target="tpu_custom_call", output_to_operand_aliasing={{0}: (8, {})} | custom-call | flops 1 | bytes 1 | tf_op jit(solution)/shard_map/multiply/pallas_call | solution.py:202
  161.6 1.5 collective-permute-start.27
  165.9 9.3 %multiply.8 = (f32[2,2,128,2048]{3,2,1,0:T(8,128)}, bf16[128,1024]{1,0:T(8,128)(2,1)S(1)}) custom-call(s32[1]{0:T(128)} %bitcast.mine_ref, s32[1]{0:T(128)} %bitcast.1.spot_ref, s32[1]{0:T(128)} %bitcast.2.core_ref, bf16[64,8192]{1,0:T(8,128)(2,1)S(1)} %collective-permute-done.10.refs_0_, ...), custom_call_target="tpu_custom_call", output_to_operand_aliasing={{0}: (8, {})} | custom-call | flops 1 | bytes 1 | tf_op jit(solution)/shard_map/multiply/pallas_call | solution.py:202
  175.2 1.3 collective-permute-start.26
  176.5 0.7 collective-permute-done.27.refs_0_
  177.2 9.3 %multiply.9 = (f32[2,2,128,2048]{3,2,1,0:T(8,128)}, bf16[128,1024]{1,0:T(8,128)(2,1)S(1)}) custom-call(s32[1]{0:T(128)} %bitcast.mine_ref, s32[1]{0:T(128)} %bitcast.1.spot_ref, s32[1]{0:T(128)} %bitcast.2.core_ref, bf16[64,8192]{1,0:T(8,128)(2,1)S(1)} %collective-permute-done.10.refs_0_, ...), custom_call_target="tpu_custom_call", output_to_operand_aliasing={{0}: (8, {})} | custom-call | flops 1 | bytes 1 | tf_op jit(solution)/shard_map/multiply/pallas_call | solution.py:202
  186.5 1.3 collective-permute-start.28
  187.9 2.3 %place.8.refs_2_ = f32[2,2,128,2048]{3,2,1,0:T(8,128)} custom-call(s32[1]{0:T(128)} %bitcast.mine_ref, s32[1]{0:T(128)} %bitcast.1.spot_ref, bf16[128,2048]{1,0:T(8,128)(2,1)S(1)} %collective-permute-done.27.refs_0_, f32[2,2,128,2048]{3,2,1,0:T(8,128)} %place.7.refs_1_), custom_call_target="tpu_custom_call", output_to_operand_aliasing={{}: (3, {})} | custom-call | flops 1 | bytes 1 | tf_op jit(solution)/shard_map/place/pallas_call | solution.py:266
  190.2 5.9 %collective-permute-done.28.refs_1_ = bf16[128,1024]{1,0:T(8,128)(2,1)S(1)} collective-permute-done((bf16[128,1024]{1,0:T(8,128)(2,1)S(1)}, bf16[128,1024]{1,0:T(8,128)(2,1)S(1)}, u32[]{:S(2)}, u32[]{:S(2)}) %collective-permute-start.28) | collective-permute-done | bytes 262176 | tf_op jit(solution)/shard_map/ppermute | solution.py:320
  196.1 2.3 %place.9 = f32[2,2,128,2048]{3,2,1,0:T(8,128)} custom-call(s32[1]{0:T(128)} %bitcast.mine_ref, s32[1]{0:T(128)} %bitcast.1.spot_ref, bf16[128,1024]{1,0:T(8,128)(2,1)S(1)} %collective-permute-done.26.refs_0_, bf16[128,1024]{1,0:T(8,128)(2,1)S(1)} %collective-permute-done.28.refs_1_, f32[2,2,128,2048]{3,2,1,0:T(8,128)} %place.8.refs_2_), custom_call_target="tpu_custom_call", output_to_operand_aliasing={{}: (4, {})} | custom-call | flops 1 | bytes 1 | tf_op jit(solution)/shard_map/place/pallas_call | solution.py:266
  (67 shorter events, 6.2 us)
Async XLA Ops:
  0.0 9.2 %copy-start = (bf16[128,8192]{1,0:T(8,128)(2,1)S(1)}, bf16[128,8192]{1,0:T(8,128)(2,1)}, u32[]{:S(2)}) copy-start(bf16[128,8192]{1,0:T(8,128)(2,1)} %mine_ref.1) | copy-start | bytes 6291460
  0.0 9.2 %copy-start.3 = (f32[8192]{0:T(1024)S(1)}, f32[8192]{0:T(1024)}, u32[]{:S(2)}) copy-start(f32[8192]{0:T(1024)} %param.7) | copy-start | bytes 98308
  0.0 9.2 %collective-permute-start.2 = (bf16[128,8192]{1,0:T(8,128)(2,1)}, bf16[128,8192]{1,0:T(8,128)(2,1)}, u32[]{:S(2)}, u32[]{:S(2)}) collective-permute-start(bf16[128,8192]{1,0:T(8,128)(2,1)} %mine_ref.1), channel_id=1, source_target_pairs={{0,2},{2,0},{4,6},{6,4},{8,10},{10,8},{12,14},{14,12},{1,3},{3,1},... | collective-permute-start | bytes 6291464 | tf_op jit(solution)/shard_map/ppermute | solution.py:311
  3.7 38.5 %collective-permute-start.1 = (bf16[64,8192]{1,0:T(8,128)(2,1)}, bf16[64,8192]{1,0:T(8,128)(2,1)}, u32[]{:S(2)}, u32[]{:S(2)}) collective-permute-start(bf16[64,8192]{1,0:T(8,128)(2,1)} %get-tuple-element.57), channel_id=1, source_target_pairs={{0,4},{2,6},{4,8},{6,10},{8,12},{10,14},{12,0},{14,2},{1,5},{3,7},... | collective-permute-start | bytes 3145736 | tf_op jit(solution)/shard_map/ppermute | solution.py:307
  6.3 48.8 %collective-permute-start = (bf16[64,8192]{1,0:T(8,128)(2,1)}, bf16[64,8192]{1,0:T(8,128)(2,1)}, u32[]{:S(2)}, u32[]{:S(2)}) collective-permute-start(bf16[64,8192]{1,0:T(8,128)(2,1)} %get-tuple-element.58), channel_id=1, source_target_pairs={{0,4},{2,6},{4,8},{6,10},{8,12},{10,14},{12,0},{14,2},{1,5},{3,7},... | collective-permute-start | bytes 3145736 | tf_op jit(solution)/shard_map/ppermute | solution.py:307
  39.7 1.3 copy-start.1
  41.0 42.9 %collective-permute-start.9 = (bf16[256,2048]{1,0:T(8,128)(2,1)}, bf16[256,2048]{1,0:T(8,128)(2,1)S(1)}, u32[]{:S(2)}, u32[]{:S(2)}) collective-permute-start(bf16[256,2048]{1,0:T(8,128)(2,1)} %get-tuple-element.31), channel_id=1, source_target_pairs={{1,0},{3,2},{5,4},{7,6},{8,9},{10,11},{12,13},{14,15},{17,16},{19,... | collective-permute-start | bytes 3145736 | tf_op jit(solution)/shard_map/ppermute | solution.py:320
  42.3 43.4 %collective-permute-start.4 = (bf16[64,8192]{1,0:T(8,128)(2,1)}, bf16[64,8192]{1,0:T(8,128)(2,1)S(1)}, u32[]{:S(2)}, u32[]{:S(2)}) collective-permute-start(bf16[64,8192]{1,0:T(8,128)(2,1)} %collective-permute-done.1.refs_0_), channel_id=1, source_target_pairs={{0,4},{2,6},{4,8},{6,10},{8,12},{10,14},{12,0},{14,2},{1,5},{3,7},... | collective-permute-start | bytes 3145736 | tf_op jit(solution)/shard_map/ppermute | solution.py:307
  57.2 2.8 %collective-permute-start.7 = (bf16[32,8192]{1,0:T(8,128)(2,1)S(1)}, bf16[32,8192]{1,0:T(8,128)(2,1)S(1)}, u32[]{:S(2)}, u32[]{:S(2)}) collective-permute-start(bf16[32,8192]{1,0:T(8,128)(2,1)S(1)} %get-tuple-element.72), channel_id=1, source_target_pairs={{0,2},{2,0},{4,6},{6,4},{8,10},{10,8},{12,14},{14,12},{1,3},{3,1},... | collective-permute-start | bytes 1572872 | tf_op jit(solution)/shard_map/ppermute | solution.py:311
  59.4 3.0 %collective-permute-start.8 = (bf16[32,8192]{1,0:T(8,128)(2,1)}, bf16[32,8192]{1,0:T(8,128)(2,1)S(1)}, u32[]{:S(2)}, u32[]{:S(2)}) collective-permute-start(bf16[32,8192]{1,0:T(8,128)(2,1)} %get-tuple-element.71), channel_id=1, source_target_pairs={{0,2},{2,0},{4,6},{6,4},{8,10},{10,8},{12,14},{14,12},{1,3},{3,1},... | collective-permute-start | bytes 1572872 | tf_op jit(solution)/shard_map/ppermute | solution.py:311
  59.9 3.3 %collective-permute-start.5 = (bf16[32,8192]{1,0:T(8,128)(2,1)}, bf16[32,8192]{1,0:T(8,128)(2,1)}, u32[]{:S(2)}, u32[]{:S(2)}) collective-permute-start(bf16[32,8192]{1,0:T(8,128)(2,1)} %get-tuple-element.74), channel_id=1, source_target_pairs={{0,2},{2,0},{4,6},{6,4},{8,10},{10,8},{12,14},{14,12},{1,3},{3,1},... | collective-permute-start | bytes 1572872 | tf_op jit(solution)/shard_map/ppermute | solution.py:311
  59.9 0.8 copy-start.6
  60.7 2.5 %collective-permute-start.6 = (bf16[32,8192]{1,0:T(8,128)(2,1)}, bf16[32,8192]{1,0:T(8,128)(2,1)}, u32[]{:S(2)}, u32[]{:S(2)}) collective-permute-start(bf16[32,8192]{1,0:T(8,128)(2,1)} %get-tuple-element.73), channel_id=1, source_target_pairs={{0,2},{2,0},{4,6},{6,4},{8,10},{10,8},{12,14},{14,12},{1,3},{3,1},... | collective-permute-start | bytes 1572872 | tf_op jit(solution)/shard_map/ppermute | solution.py:311
  62.4 0.8 copy-start.8
  63.2 36.7 %collective-permute-start.3 = (bf16[64,8192]{1,0:T(8,128)(2,1)}, bf16[64,8192]{1,0:T(8,128)(2,1)S(1)}, u32[]{:S(2)}, u32[]{:S(2)}) collective-permute-start(bf16[64,8192]{1,0:T(8,128)(2,1)} %collective-permute-done.refs_1_), channel_id=1, source_target_pairs={{0,4},{2,6},{4,8},{6,10},{8,12},{10,14},{12,0},{14,2},{1,5},{3,7},... | collective-permute-start | bytes 3145736 | tf_op jit(solution)/shard_map/ppermute | solution.py:307
  63.3 1.0 copy-start.7
  64.3 1.0 copy-start.9
  65.4 18.5 %copy-start.2 = (f32[256,2048]{1,0:T(8,128)S(1)}, f32[256,2048]{1,0:T(8,128)}, u32[]{:S(2)}) copy-start(f32[256,2048]{1,0:T(8,128)} %copy-done.1) | copy-start | bytes 6291460
  79.8 26.9 %collective-permute-start.12 = (bf16[256,2048]{1,0:T(8,128)(2,1)S(1)}, bf16[256,2048]{1,0:T(8,128)(2,1)S(1)}, u32[]{:S(2)}, u32[]{:S(2)}) collective-permute-start(bf16[256,2048]{1,0:T(8,128)(2,1)S(1)} %get-tuple-element.35), channel_id=1, source_target_pairs={{0,1},{2,3},{5,4},{7,6},{9,8},{11,10},{12,13},{14,15},{16,17},{18,... | collective-permute-start | bytes 3145736 | tf_op jit(solution)/shard_map/ppermute | solution.py:320
  85.7 44.6 %collective-permute-start.11 = (bf16[64,8192]{1,0:T(8,128)(2,1)S(1)}, bf16[64,8192]{1,0:T(8,128)(2,1)}, u32[]{:S(2)}, u32[]{:S(2)}) collective-permute-start(bf16[64,8192]{1,0:T(8,128)(2,1)S(1)} %collective-permute-done.4.refs_0_), channel_id=1, source_target_pairs={{0,4},{2,6},{4,8},{6,10},{8,12},{10,14},{12,0},{14,2},{1,5},{3,7},... | collective-permute-start | bytes 3145736 | tf_op jit(solution)/shard_map/ppermute | solution.py:307
  100.8 7.0 %collective-permute-start.15 = (bf16[32,8192]{1,0:T(8,128)(2,1)S(1)}, bf16[32,8192]{1,0:T(8,128)(2,1)S(1)}, u32[]{:S(2)}, u32[]{:S(2)}) collective-permute-start(bf16[32,8192]{1,0:T(8,128)(2,1)S(1)} %get-tuple-element.68), channel_id=1, source_target_pairs={{0,2},{2,0},{4,6},{6,4},{8,10},{10,8},{12,14},{14,12},{1,3},{3,1},... | collective-permute-start | bytes 1572872 | tf_op jit(solution)/shard_map/ppermute | solution.py:311
  100.8 9.7 %collective-permute-start.16 = (bf16[32,8192]{1,0:T(8,128)(2,1)}, bf16[32,8192]{1,0:T(8,128)(2,1)}, u32[]{:S(2)}, u32[]{:S(2)}) collective-permute-start(bf16[32,8192]{1,0:T(8,128)(2,1)} %get-tuple-element.67), channel_id=1, source_target_pairs={{0,2},{2,0},{4,6},{6,4},{8,10},{10,8},{12,14},{14,12},{1,3},{3,1},... | collective-permute-start | bytes 1572872 | tf_op jit(solution)/shard_map/ppermute | solution.py:311
  101.3 9.2 %collective-permute-start.13 = (bf16[32,8192]{1,0:T(8,128)(2,1)}, bf16[32,8192]{1,0:T(8,128)(2,1)}, u32[]{:S(2)}, u32[]{:S(2)}) collective-permute-start(bf16[32,8192]{1,0:T(8,128)(2,1)} %get-tuple-element.70), channel_id=1, source_target_pairs={{0,2},{2,0},{4,6},{6,4},{8,10},{10,8},{12,14},{14,12},{1,3},{3,1},... | collective-permute-start | bytes 1572872 | tf_op jit(solution)/shard_map/ppermute | solution.py:311
  106.7 1.0 copy-start.4
  107.7 2.8 %collective-permute-start.14 = (bf16[32,8192]{1,0:T(8,128)(2,1)}, bf16[32,8192]{1,0:T(8,128)(2,1)}, u32[]{:S(2)}, u32[]{:S(2)}) collective-permute-start(bf16[32,8192]{1,0:T(8,128)(2,1)} %get-tuple-element.69), channel_id=1, source_target_pairs={{0,2},{2,0},{4,6},{6,4},{8,10},{10,8},{12,14},{14,12},{1,3},{3,1},... | collective-permute-start | bytes 1572872 | tf_op jit(solution)/shard_map/ppermute | solution.py:311
  107.7 0.8 copy-start.10
  108.6 54.5 %collective-permute-start.10 = (bf16[64,8192]{1,0:T(8,128)(2,1)S(1)}, bf16[64,8192]{1,0:T(8,128)(2,1)S(1)}, u32[]{:S(2)}, u32[]{:S(2)}) collective-permute-start(bf16[64,8192]{1,0:T(8,128)(2,1)S(1)} %collective-permute-done.3.refs_1_), channel_id=1, source_target_pairs={{0,4},{2,6},{4,8},{6,10},{8,12},{10,14},{12,0},{14,2},{1,5},{3,7},... | collective-permute-start | bytes 3145736 | tf_op jit(solution)/shard_map/ppermute | solution.py:307
  110.5 1.0 copy-start.11
  111.6 17.7 %copy-start.5 = (bf16[256,2048]{1,0:T(8,128)(2,1)S(1)}, bf16[256,2048]{1,0:T(8,128)(2,1)}, u32[]{:S(2)}) copy-start(bf16[256,2048]{1,0:T(8,128)(2,1)} %copy-done.4) | copy-start | bytes 3145732
  129.3 1.0 copy-start.18
  132.3 1.7 collective-permute-start.17
  132.6 8.3 %collective-permute-start.18 = (bf16[16,8192]{1,0:T(8,128)(2,1)}, bf16[16,8192]{1,0:T(8,128)(2,1)S(1)}, u32[]{:S(2)}, u32[]{:S(2)}) collective-permute-start(bf16[16,8192]{1,0:T(8,128)(2,1)} %get-tuple-element.65), channel_id=1, source_target_pairs={{0,2},{2,0},{4,6},{6,4},{8,10},{10,8},{12,14},{14,12},{1,3},{3,1},... | collective-permute-start | bytes 786440 | tf_op jit(solution)/shard_map/ppermute | solution.py:311
  132.9 8.7 %collective-permute-start.19 = (bf16[16,8192]{1,0:T(8,128)(2,1)}, bf16[16,8192]{1,0:T(8,128)(2,1)S(1)}, u32[]{:S(2)}, u32[]{:S(2)}) collective-permute-start(bf16[16,8192]{1,0:T(8,128)(2,1)} %get-tuple-element.64), channel_id=1, source_target_pairs={{0,2},{2,0},{4,6},{6,4},{8,10},{10,8},{12,14},{14,12},{1,3},{3,1},... | collective-permute-start | bytes 786440 | tf_op jit(solution)/shard_map/ppermute | solution.py:311
  133.1 9.2 %collective-permute-start.20 = (bf16[16,8192]{1,0:T(8,128)(2,1)S(1)}, bf16[16,8192]{1,0:T(8,128)(2,1)S(1)}, u32[]{:S(2)}, u32[]{:S(2)}) collective-permute-start(bf16[16,8192]{1,0:T(8,128)(2,1)S(1)} %get-tuple-element.63), channel_id=1, source_target_pairs={{0,2},{2,0},{4,6},{6,4},{8,10},{10,8},{12,14},{14,12},{1,3},{3,1},... | collective-permute-start | bytes 786440 | tf_op jit(solution)/shard_map/ppermute | solution.py:311
  134.1 29.7 %collective-permute-start.21 = (bf16[256,2048]{1,0:T(8,128)(2,1)}, bf16[256,2048]{1,0:T(8,128)(2,1)S(1)}, u32[]{:S(2)}, u32[]{:S(2)}) collective-permute-start(bf16[256,2048]{1,0:T(8,128)(2,1)} %copy-done.18), channel_id=1, source_target_pairs={{0,1},{2,3},{4,5},{6,7},{9,8},{11,10},{13,12},{15,14},{16,17},{18,... | collective-permute-start | bytes 3145736 | tf_op jit(solution)/shard_map/ppermute | solution.py:320
  140.9 0.7 copy-start.12
  141.6 0.7 copy-start.14
  142.3 0.7 copy-start.16
  143.0 0.9 copy-start.13
  144.0 0.9 copy-start.15
  144.9 0.9 copy-start.17
  161.6 15.6 %collective-permute-start.27 = (bf16[128,2048]{1,0:T(8,128)(2,1)S(1)}, bf16[128,2048]{1,0:T(8,128)(2,1)S(1)}, u32[]{:S(2)}, u32[]{:S(2)}) collective-permute-start(bf16[128,2048]{1,0:T(8,128)(2,1)S(1)} %get-tuple-element.46), channel_id=1, source_target_pairs={{1,0},{3,2},{4,5},{6,7},{8,9},{10,11},{13,12},{15,14},{17,16},{19,... | collective-permute-start | bytes 1572872 | tf_op jit(solution)/shard_map/ppermute | solution.py:320
  163.2 1.6 collective-permute-start.22
  163.3 1.9 collective-permute-start.23
  163.8 1.8 collective-permute-start.24
  163.8 2.1 %collective-permute-start.25 = (bf16[16,8192]{1,0:T(8,128)(2,1)S(1)}, bf16[16,8192]{1,0:T(8,128)(2,1)S(1)}, u32[]{:S(2)}, u32[]{:S(2)}) collective-permute-start(bf16[16,8192]{1,0:T(8,128)(2,1)S(1)} %get-tuple-element.59), channel_id=1, source_target_pairs={{0,2},{2,0},{4,6},{6,4},{8,10},{10,8},{12,14},{14,12},{1,3},{3,1},... | collective-permute-start | bytes 786440 | tf_op jit(solution)/shard_map/ppermute | solution.py:311
  175.2 15.0 %collective-permute-start.26 = (bf16[128,1024]{1,0:T(8,128)(2,1)S(1)}, bf16[128,1024]{1,0:T(8,128)(2,1)S(1)}, u32[]{:S(2)}, u32[]{:S(2)}) collective-permute-start(bf16[128,1024]{1,0:T(8,128)(2,1)S(1)} %get-tuple-element.50), channel_id=1, source_target_pairs={{1,0},{3,2},{4,5},{6,7},{8,9},{10,11},{13,12},{15,14},{17,16},{19,... | collective-permute-start | bytes 786440 | tf_op jit(solution)/shard_map/ppermute | solution.py:320
  186.5 9.6 %collective-permute-start.28 = (bf16[128,1024]{1,0:T(8,128)(2,1)S(1)}, bf16[128,1024]{1,0:T(8,128)(2,1)S(1)}, u32[]{:S(2)}, u32[]{:S(2)}) collective-permute-start(bf16[128,1024]{1,0:T(8,128)(2,1)S(1)} %get-tuple-element.53), channel_id=1, source_target_pairs={{1,0},{3,2},{4,5},{6,7},{8,9},{10,11},{13,12},{15,14},{17,16},{19,... | collective-permute-start | bytes 786440 | tf_op jit(solution)/shard_map/ppermute | solution.py:320

commit v11 on v10

--- a/solution.py
+++ b/solution.py
@@ -217,7 +217,7 @@
             pltpu.SemaphoreType.DMA((count // tile,)),
         ],
         input_output_aliases={3 + len(mine) + len(other): 0} if given else {},
-        compiler_params=pltpu.CompilerParams(vmem_limit_bytes=27 * mib),
+        compiler_params=pltpu.CompilerParams(vmem_limit_bytes=26 * mib),
         cost_estimate=small,
         name="multiply",
     )(*where, core, *mine, *other, *given, fisher, train)
@@ -280,9 +280,25 @@
     )(*where, *operands)
 
 
+def cut_kernel(whole_ref, *refs):
+    rows = refs[0].shape[0]
+    for part, ref in enumerate(refs):
+        ref[...] = whole_ref[part * rows:(part + 1) * rows, :]
+
+
 def cut(whole, count):
-    rows = whole.shape[0] // count
-    return [whole[part * rows:(part + 1) * rows] for part in range(count)]
+    if count == 1:
+        return [whole]
+    piece = jax.ShapeDtypeStruct((whole.shape[0] // count, whole.shape[1]), whole.dtype)
+    return pl.pallas_call(
+        cut_kernel,
+        in_specs=[in_vmem],
+        out_specs=[in_vmem] * count,
+        out_shape=[piece] * count,
+        compiler_params=pltpu.CompilerParams(vmem_limit_bytes=6 * mib),
+        cost_estimate=small,
+        name="cut",
+    )(whole)
 
 
 def after(array, *others):

time: 199 us -> 201 us (1.010)
  Pallas kernels: 103 us -> 113 us
  local copies, waits for them, and re-layouts: 26.8 us -> 17.8 us
  waiting for transfers between devices: 40 us -> 43 us
    slice x7 -> x0, local copies, waits for them, and re-layouts: 11.7 us -> none  [cut(): return [whole[part * rows:(part + 1) * rows] for part in range(count)]]
    pallas_call x0 -> x7, Pallas kernels: none -> 7.95 us  [cut(): pl.pallas_call(cut_kernel, in_specs=[in_vmem], out_specs=[in_vmem] * coun...]
    ppermute x6, waiting for transfers between devices: 24.4 us -> 30.1 us  [shift(): return lax.ppermute(panel, 'blk', pairs)]
    ppermute x6, waiting for transfers between devices: 12 us -> 6.85 us  [exchange(): received.append(lax.ppermute(send, ('blk', 'dim'), pairs))]
    ppermute x6, starting transfers between devices: 16.1 us -> 12.6 us  [exchange(): received.append(lax.ppermute(send, ('blk', 'dim'), pairs))]
    unnamed x39, local copies, waits for them, and re-layouts: 15.1 us -> 17.8 us
    ppermute x17, waiting for transfers between devices: 3.61 us -> 6.11 us  [swap(): return [lax.ppermute(part, 'blk', pairs) for part in parts]]
  transfers between devices with their start and end apart: 29 -> 29, of which waited for: 12 -> 15; matrix products, arithmetic and copies ran while one was open for 7% -> 1% of each run, Pallas kernels for 51% -> 55%
where the time goes in v11:
time: 201 us; the launch traced here: 200 us
  Pallas kernels  113 us (56%)
  waiting for transfers between devices  43 us (21%)
  starting transfers between devices  26.4 us (13%)
  local copies, waits for them, and re-layouts  17.8 us (9%)
    pallas_call x5, Pallas kernels, multiply(): pl.pallas_call(functools.partial(multiply_kernel, counts, start, top), in...  66.9 us
    pallas_call x1, Pallas kernels, first(): pl.pallas_call(first_kernel, grid=(count // tile,), in_specs=[in_smem, pl...  30.4 us
    ppermute x6, waiting for transfers between devices, shift(): return lax.ppermute(panel, 'blk', pairs)  30.1 us
    unnamed x39, local copies, waits for them, and re-layouts  17.8 us
    ppermute x6, starting transfers between devices, exchange(): received.append(lax.ppermute(send, ('blk', 'dim'), pairs))  12.6 us
    ppermute x6, starting transfers between devices, shift(): return lax.ppermute(panel, 'blk', pairs)  9.73 us
    pallas_call x7, Pallas kernels, cut(): pl.pallas_call(cut_kernel, in_specs=[in_vmem], out_specs=[in_vmem] * coun...  7.95 us
    pallas_call x5, Pallas kernels, place(): pl.pallas_call(functools.partial(place_kernel, start, cols, len(kept)), i...  7.6 us
  transfers between devices with their start and end apart: 29, of which 15 were waited for; matrix products, arithmetic and copies ran while one was open for 1% of the time, Pallas kernels for 55%

profile of v11, /device:TPU:0, one launch (start us, length us, event | category | flops | bytes accessed | tf_op | source)
XLA Modules:
  0.0 200.3 jit_solution(9737422526529738242)
XLA Ops:
  0.5 1.6 copy-done
  2.0 1.4 cut.7
  3.5 2.6 %collective-permute-start.1 = (bf16[64,8192]{1,0:T(8,128)(2,1)}, bf16[64,8192]{1,0:T(8,128)(2,1)S(1)}, u32[]{:S(2)}, u32[]{:S(2)}) collective-permute-start(bf16[64,8192]{1,0:T(8,128)(2,1)} %get-tuple-element.50), channel_id=1, source_target_pairs={{0,4},{2,6},{4,8},{6,10},{8,12},{10,14},{12,0},{14,2},{1,5},{3,7},... | collective-permute-start | bytes 3145736 | tf_op jit(solution)/shard_map/ppermute | solution.py:323
  6.1 1.6 collective-permute-start
  7.6 2.4 %copy.14.exps_ref = s32[2048,64]{1,0:T(8,128)} copy(s32[2048,64]{0,1:T(8,128)} %param.5) | data formatting | bytes 1048576 | tf_op args[1]
  10.0 1.2 copy-done.2
  11.3 0.8 copy-done.5
  12.0 30.4 %first.1 = (bf16[2048,8192]{1,0:T(8,128)(2,1)}, f32[256,2048]{1,0:T(8,128)S(1)}, bf16[256,2048]{1,0:T(8,128)(2,1)}) custom-call(s32[1]{0:T(128)} %bitcast.2.core_ref, bf16[128,8192]{1,0:T(8,128)(2,1)S(1)} %copy-done.1, bf16[128,8192]{1,0:T(8,128)(2,1)} %collective-permute-done.2.other_ref, f32[1,8192]{1,0:T(1,128)S(1)} %bitcast.11, ...), custom_call_target="tpu_custom_call" | custom-call | flops 1 | bytes 1 | tf_op jit(solution)/shard_map/first/pallas_call | solution.py:59
  42.4 1.3 copy-done.3
  43.8 11.0 %collective-permute-done.whole_ref.refs_1_ = bf16[64,8192]{1,0:T(8,128)(2,1)} collective-permute-done((bf16[64,8192]{1,0:T(8,128)(2,1)}, bf16[64,8192]{1,0:T(8,128)(2,1)}, u32[]{:S(2)}, u32[]{:S(2)}) %collective-permute-start) | collective-permute-done | bytes 1048608 | tf_op jit(solution)/shard_map/ppermute | solution.py:323
  54.7 1.3 cut.9
  56.6 1.3 collective-permute-start.9
  57.9 4.3 %collective-permute-start.3 = (bf16[64,8192]{1,0:T(8,128)(2,1)}, bf16[64,8192]{1,0:T(8,128)(2,1)S(1)}, u32[]{:S(2)}, u32[]{:S(2)}) collective-permute-start(bf16[64,8192]{1,0:T(8,128)(2,1)} %collective-permute-done.whole_ref.refs_1_), channel_id=1, source_target_pairs={{0,4},{2,6},{4,8},{6,10},{8,12},{10,14},{12,0},{14,2},{1,5},{3,7},... | collective-permute-start | bytes 3145736 | tf_op jit(solution)/shard_map/ppermute | solution.py:323
  62.3 1.1 cut.8
  63.3 0.8 copy-done.7
  64.2 0.8 copy-done.9
  65.5 0.9 collective-permute-done.5.refs_2_
  66.4 1.0 collective-permute-done.6.refs_3_
  67.4 1.0 copy-done.8
  68.4 1.0 copy-done.10
  69.5 14.5 %multiply.5 = (f32[2,2,128,2048]{3,2,1,0:T(8,128)}, bf16[256,2048]{1,0:T(8,128)(2,1)}) custom-call(s32[1]{0:T(128)} %bitcast.4.mine_ref, s32[1]{0:T(128)} %bitcast.5.spot_ref, s32[1]{0:T(128)} %bitcast.2.core_ref, bf16[64,8192]{1,0:T(8,128)(2,1)S(1)} %collective-permute-done.1.whole_ref.refs_0_, bf16[64,8192]{1,0:T(8,128)(2,1)} %collective-permute-done.whole_ref.refs_1_, ...), custom_call_target="tpu_custom_call" | custom-call | flops 1 | bytes 1 | tf_op jit(solution)/shard_map/multiply/pallas_call | solution.py:202
  84.0 2.3 %collective-permute-start.12 = (bf16[256,2048]{1,0:T(8,128)(2,1)}, bf16[256,2048]{1,0:T(8,128)(2,1)}, u32[]{:S(2)}, u32[]{:S(2)}) collective-permute-start(bf16[256,2048]{1,0:T(8,128)(2,1)} %get-tuple-element.59), channel_id=1, source_target_pairs={{0,1},{2,3},{5,4},{7,6},{9,8},{11,10},{12,13},{14,15},{16,17},{18,... | collective-permute-start | bytes 3145736 | tf_op jit(solution)/shard_map/ppermute | solution.py:336
  86.3 2.9 %place.5.refs_6_ = f32[2,2,128,2048]{3,2,1,0:T(8,128)} custom-call(s32[1]{0:T(128)} %bitcast.6.mine_ref, s32[1]{0:T(128)} %bitcast.7.spot_ref, f32[256,2048]{1,0:T(8,128)S(1)} %copy-done.4, bf16[256,2048]{1,0:T(8,128)(2,1)} %collective-permute-done.9.refs_1_, f32[2,2,128,2048]{3,2,1,0:T(8,128)} %get-tuple-element.62.refs_2_), custom_call_target="tpu_custom_call", output_to_operand_aliasing={{}: (4, {})} | custom-call | flops 1 | bytes 1 | tf_op jit(solution)/shard_map/place/pallas_call | solution.py:266
  89.2 19.1 %collective-permute-done.3.whole_ref.refs_1_ = bf16[64,8192]{1,0:T(8,128)(2,1)S(1)} collective-permute-done((bf16[64,8192]{1,0:T(8,128)(2,1)}, bf16[64,8192]{1,0:T(8,128)(2,1)S(1)}, u32[]{:S(2)}, u32[]{:S(2)}) %collective-permute-start.3) | collective-permute-done | bytes 1048608 | tf_op jit(solution)/shard_map/ppermute | solution.py:323
  108.3 0.9 cut.11
  109.2 1.1 cut.10
  111.1 0.8 copy-done.11
  112.1 1.2 collective-permute-start.10
  113.4 0.7 collective-permute-done.14.refs_3_
  114.1 1.0 copy-done.12
  115.2 18.0 %multiply.6 = (f32[2,2,128,2048]{3,2,1,0:T(8,128)}, bf16[256,2048]{1,0:T(8,128)(2,1)}) custom-call(s32[1]{0:T(128)} %bitcast.8.mine_ref, s32[1]{0:T(128)} %bitcast.9.spot_ref, s32[1]{0:T(128)} %bitcast.2.core_ref, bf16[64,8192]{1,0:T(8,128)(2,1)S(1)} %collective-permute-done.4.whole_ref.refs_0_, ...), custom_call_target="tpu_custom_call", output_to_operand_aliasing={{0}: (9, {})} | custom-call | flops 1 | bytes 1 | tf_op jit(solution)/shard_map/multiply/pallas_call | solution.py:202
  133.2 5.2 %collective-permute-start.21 = (bf16[256,2048]{1,0:T(8,128)(2,1)}, bf16[256,2048]{1,0:T(8,128)(2,1)}, u32[]{:S(2)}, u32[]{:S(2)}) collective-permute-start(bf16[256,2048]{1,0:T(8,128)(2,1)} %get-tuple-element.70), channel_id=1, source_target_pairs={{0,1},{2,3},{4,5},{6,7},{9,8},{11,10},{13,12},{15,14},{16,17},{18,... | collective-permute-start | bytes 3145736 | tf_op jit(solution)/shard_map/ppermute | solution.py:336
  138.4 2.1 %cut.12 = (bf16[16,8192]{1,0:T(8,128)(2,1)S(1)}, bf16[16,8192]{1,0:T(8,128)(2,1)}, bf16[16,8192]{1,0:T(8,128)(2,1)}, bf16[16,8192]{1,0:T(8,128)(2,1)}) custom-call(bf16[64,8192]{1,0:T(8,128)(2,1)} %collective-permute-done.11.whole_ref.refs_0_), custom_call_target="tpu_custom_call" | custom-call | flops 1 | bytes 1 | tf_op jit(solution)/shard_map/cut/pallas_call | solution.py:293
  141.1 0.9 collective-permute-done.17.refs_1_
  144.0 0.7 copy-done.17
  144.8 0.9 copy-done.14
  145.7 0.9 copy-done.16
  146.7 0.9 copy-done.18
  147.6 15.7 %multiply.7 = (f32[2,2,128,2048]{3,2,1,0:T(8,128)}, bf16[128,2048]{1,0:T(8,128)(2,1)S(1)}) custom-call(s32[1]{0:T(128)} %bitcast.mine_ref, s32[1]{0:T(128)} %bitcast.1.spot_ref, s32[1]{0:T(128)} %bitcast.2.core_ref, bf16[64,8192]{1,0:T(8,128)(2,1)} %collective-permute-done.11.whole_ref.refs_0_, ...), custom_call_target="tpu_custom_call", output_to_operand_aliasing={{0}: (8, {})} | custom-call | flops 1 | bytes 1 | tf_op jit(solution)/shard_map/multiply/pallas_call | solution.py:202
  163.4 1.3 collective-permute-start.27
  167.5 9.3 %multiply.8 = (f32[2,2,128,2048]{3,2,1,0:T(8,128)}, bf16[128,1024]{1,0:T(8,128)(2,1)S(1)}) custom-call(s32[1]{0:T(128)} %bitcast.mine_ref, s32[1]{0:T(128)} %bitcast.1.spot_ref, s32[1]{0:T(128)} %bitcast.2.core_ref, bf16[64,8192]{1,0:T(8,128)(2,1)S(1)} %collective-permute-done.10.whole_ref.refs_0_, ...), custom_call_target="tpu_custom_call", output_to_operand_aliasing={{0}: (8, {})} | custom-call | flops 1 | bytes 1 | tf_op jit(solution)/shard_map/multiply/pallas_call | solution.py:202
  176.8 1.3 collective-permute-start.26
  178.1 1.1 collective-permute-done.27.refs_0_
  179.2 9.3 %multiply.9 = (f32[2,2,128,2048]{3,2,1,0:T(8,128)}, bf16[128,1024]{1,0:T(8,128)(2,1)S(1)}) custom-call(s32[1]{0:T(128)} %bitcast.mine_ref, s32[1]{0:T(128)} %bitcast.1.spot_ref, s32[1]{0:T(128)} %bitcast.2.core_ref, bf16[64,8192]{1,0:T(8,128)(2,1)S(1)} %collective-permute-done.10.whole_ref.refs_0_, ...), custom_call_target="tpu_custom_call", output_to_operand_aliasing={{0}: (8, {})} | custom-call | flops 1 | bytes 1 | tf_op jit(solution)/shard_map/multiply/pallas_call | solution.py:202
  188.6 1.3 collective-permute-start.28
  189.9 2.3 %place.8.refs_2_ = f32[2,2,128,2048]{3,2,1,0:T(8,128)} custom-call(s32[1]{0:T(128)} %bitcast.mine_ref, s32[1]{0:T(128)} %bitcast.1.spot_ref, bf16[128,2048]{1,0:T(8,128)(2,1)S(1)} %collective-permute-done.27.refs_0_, f32[2,2,128,2048]{3,2,1,0:T(8,128)} %place.7.refs_1_), custom_call_target="tpu_custom_call", output_to_operand_aliasing={{}: (3, {})} | custom-call | flops 1 | bytes 1 | tf_op jit(solution)/shard_map/place/pallas_call | solution.py:266
  192.3 5.7 %collective-permute-done.28.refs_1_ = bf16[128,1024]{1,0:T(8,128)(2,1)S(1)} collective-permute-done((bf16[128,1024]{1,0:T(8,128)(2,1)S(1)}, bf16[128,1024]{1,0:T(8,128)(2,1)S(1)}, u32[]{:S(2)}, u32[]{:S(2)}) %collective-permute-start.28) | collective-permute-done | bytes 262176 | tf_op jit(solution)/shard_map/ppermute | solution.py:336
  198.0 2.3 %place.9 = f32[2,2,128,2048]{3,2,1,0:T(8,128)} custom-call(s32[1]{0:T(128)} %bitcast.mine_ref, s32[1]{0:T(128)} %bitcast.1.spot_ref, bf16[128,1024]{1,0:T(8,128)(2,1)S(1)} %collective-permute-done.26.refs_0_, bf16[128,1024]{1,0:T(8,128)(2,1)S(1)} %collective-permute-done.28.refs_1_, f32[2,2,128,2048]{3,2,1,0:T(8,128)} %place.8.refs_2_), custom_call_target="tpu_custom_call", output_to_operand_aliasing={{}: (4, {})} | custom-call | flops 1 | bytes 1 | tf_op jit(solution)/shard_map/place/pallas_call | solution.py:266
  (67 shorter events, 8.3 us)
Async XLA Ops:
  0.0 10.0 %collective-permute-start.2 = (bf16[128,8192]{1,0:T(8,128)(2,1)}, bf16[128,8192]{1,0:T(8,128)(2,1)}, u32[]{:S(2)}, u32[]{:S(2)}) collective-permute-start(bf16[128,8192]{1,0:T(8,128)(2,1)} %mine_ref.1), channel_id=1, source_target_pairs={{0,2},{2,0},{4,6},{6,4},{8,10},{10,8},{12,14},{14,12},{1,3},{3,1},... | collective-permute-start | bytes 6291464 | tf_op jit(solution)/shard_map/ppermute | solution.py:327
  0.5 1.6 copy-start
  2.0 8.0 %copy-start.1 = (bf16[128,8192]{1,0:T(8,128)(2,1)S(1)}, bf16[128,8192]{1,0:T(8,128)(2,1)}, u32[]{:S(2)}) copy-start(bf16[128,8192]{1,0:T(8,128)(2,1)} %mine_ref.1) | copy-start | bytes 6291460
  3.5 40.3 %collective-permute-start.1 = (bf16[64,8192]{1,0:T(8,128)(2,1)}, bf16[64,8192]{1,0:T(8,128)(2,1)S(1)}, u32[]{:S(2)}, u32[]{:S(2)}) collective-permute-start(bf16[64,8192]{1,0:T(8,128)(2,1)} %get-tuple-element.50), channel_id=1, source_target_pairs={{0,4},{2,6},{4,8},{6,10},{8,12},{10,14},{12,0},{14,2},{1,5},{3,7},... | collective-permute-start | bytes 3145736 | tf_op jit(solution)/shard_map/ppermute | solution.py:323
  6.1 48.6 %collective-permute-start = (bf16[64,8192]{1,0:T(8,128)(2,1)}, bf16[64,8192]{1,0:T(8,128)(2,1)}, u32[]{:S(2)}, u32[]{:S(2)}) collective-permute-start(bf16[64,8192]{1,0:T(8,128)(2,1)} %get-tuple-element.49), channel_id=1, source_target_pairs={{0,4},{2,6},{4,8},{6,10},{8,12},{10,14},{12,0},{14,2},{1,5},{3,7},... | collective-permute-start | bytes 3145736 | tf_op jit(solution)/shard_map/ppermute | solution.py:323
  10.0 1.2 copy-start.2
  11.3 0.8 copy-start.5
  12.0 55.3 %copy-start.6 = (f32[8192]{0:T(1024)S(1)}, f32[8192]{0:T(1024)}, u32[]{:S(2)}) copy-start(f32[8192]{0:T(1024)} %param.7) | copy-start | bytes 98308
  42.4 1.3 copy-start.3
  56.0 7.3 %collective-permute-start.7 = (bf16[32,8192]{1,0:T(8,128)(2,1)S(1)}, bf16[32,8192]{1,0:T(8,128)(2,1)S(1)}, u32[]{:S(2)}, u32[]{:S(2)}) collective-permute-start(bf16[32,8192]{1,0:T(8,128)(2,1)S(1)} %get-tuple-element.56), channel_id=1, source_target_pairs={{0,2},{2,0},{4,6},{6,4},{8,10},{10,8},{12,14},{14,12},{1,3},{3,1},... | collective-permute-start | bytes 1572872 | tf_op jit(solution)/shard_map/ppermute | solution.py:327
  56.1 8.1 %collective-permute-start.8 = (bf16[32,8192]{1,0:T(8,128)(2,1)S(1)}, bf16[32,8192]{1,0:T(8,128)(2,1)S(1)}, u32[]{:S(2)}, u32[]{:S(2)}) collective-permute-start(bf16[32,8192]{1,0:T(8,128)(2,1)S(1)} %get-tuple-element.57), channel_id=1, source_target_pairs={{0,2},{2,0},{4,6},{6,4},{8,10},{10,8},{12,14},{14,12},{1,3},{3,1},... | collective-permute-start | bytes 1572872 | tf_op jit(solution)/shard_map/ppermute | solution.py:327
  56.6 29.7 %collective-permute-start.9 = (bf16[256,2048]{1,0:T(8,128)(2,1)}, bf16[256,2048]{1,0:T(8,128)(2,1)}, u32[]{:S(2)}, u32[]{:S(2)}) collective-permute-start(bf16[256,2048]{1,0:T(8,128)(2,1)} %get-tuple-element.51), channel_id=1, source_target_pairs={{1,0},{3,2},{5,4},{7,6},{8,9},{10,11},{12,13},{14,15},{17,16},{19,... | collective-permute-start | bytes 3145736 | tf_op jit(solution)/shard_map/ppermute | solution.py:336
  57.9 31.3 %collective-permute-start.4 = (bf16[64,8192]{1,0:T(8,128)(2,1)S(1)}, bf16[64,8192]{1,0:T(8,128)(2,1)S(1)}, u32[]{:S(2)}, u32[]{:S(2)}) collective-permute-start(bf16[64,8192]{1,0:T(8,128)(2,1)S(1)} %collective-permute-done.1.whole_ref.refs_0_), channel_id=1, source_target_pairs={{0,4},{2,6},{4,8},{6,10},{8,12},{10,14},{12,0},{14,2},{1,5},{3,7},... | collective-permute-start | bytes 3145736 | tf_op jit(solution)/shard_map/ppermute | solution.py:323
  57.9 50.4 %collective-permute-start.3 = (bf16[64,8192]{1,0:T(8,128)(2,1)}, bf16[64,8192]{1,0:T(8,128)(2,1)S(1)}, u32[]{:S(2)}, u32[]{:S(2)}) collective-permute-start(bf16[64,8192]{1,0:T(8,128)(2,1)} %collective-permute-done.whole_ref.refs_1_), channel_id=1, source_target_pairs={{0,4},{2,6},{4,8},{6,10},{8,12},{10,14},{12,0},{14,2},{1,5},{3,7},... | collective-permute-start | bytes 3145736 | tf_op jit(solution)/shard_map/ppermute | solution.py:323
  63.3 0.8 copy-start.7
  64.1 2.3 %collective-permute-start.5 = (bf16[32,8192]{1,0:T(8,128)(2,1)}, bf16[32,8192]{1,0:T(8,128)(2,1)}, u32[]{:S(2)}, u32[]{:S(2)}) collective-permute-start(bf16[32,8192]{1,0:T(8,128)(2,1)} %get-tuple-element.54), channel_id=1, source_target_pairs={{0,2},{2,0},{4,6},{6,4},{8,10},{10,8},{12,14},{14,12},{1,3},{3,1},... | collective-permute-start | bytes 1572872 | tf_op jit(solution)/shard_map/ppermute | solution.py:327
  64.2 0.8 copy-start.9
  65.0 2.4 %collective-permute-start.6 = (bf16[32,8192]{1,0:T(8,128)(2,1)}, bf16[32,8192]{1,0:T(8,128)(2,1)}, u32[]{:S(2)}, u32[]{:S(2)}) collective-permute-start(bf16[32,8192]{1,0:T(8,128)(2,1)} %get-tuple-element.55), channel_id=1, source_target_pairs={{0,2},{2,0},{4,6},{6,4},{8,10},{10,8},{12,14},{14,12},{1,3},{3,1},... | collective-permute-start | bytes 1572872 | tf_op jit(solution)/shard_map/ppermute | solution.py:327
  67.4 1.0 copy-start.8
  68.4 1.0 copy-start.10
  69.5 16.8 %copy-start.4 = (f32[256,2048]{1,0:T(8,128)S(1)}, f32[256,2048]{1,0:T(8,128)}, u32[]{:S(2)}) copy-start(f32[256,2048]{1,0:T(8,128)} %copy-done.3) | copy-start | bytes 6291460
  84.0 28.1 %collective-permute-start.12 = (bf16[256,2048]{1,0:T(8,128)(2,1)}, bf16[256,2048]{1,0:T(8,128)(2,1)}, u32[]{:S(2)}, u32[]{:S(2)}) collective-permute-start(bf16[256,2048]{1,0:T(8,128)(2,1)} %get-tuple-element.59), channel_id=1, source_target_pairs={{0,1},{2,3},{5,4},{7,6},{9,8},{11,10},{12,13},{14,15},{16,17},{18,... | collective-permute-start | bytes 3145736 | tf_op jit(solution)/shard_map/ppermute | solution.py:336
  109.2 1.9 collective-permute-start.15
  109.2 29.2 %collective-permute-start.11 = (bf16[64,8192]{1,0:T(8,128)(2,1)S(1)}, bf16[64,8192]{1,0:T(8,128)(2,1)}, u32[]{:S(2)}, u32[]{:S(2)}) collective-permute-start(bf16[64,8192]{1,0:T(8,128)(2,1)S(1)} %collective-permute-done.4.whole_ref.refs_0_), channel_id=1, source_target_pairs={{0,4},{2,6},{4,8},{6,10},{8,12},{10,14},{12,0},{14,2},{1,5},{3,7},... | collective-permute-start | bytes 3145736 | tf_op jit(solution)/shard_map/ppermute | solution.py:323
  110.3 3.0 %collective-permute-start.16 = (bf16[32,8192]{1,0:T(8,128)(2,1)}, bf16[32,8192]{1,0:T(8,128)(2,1)}, u32[]{:S(2)}, u32[]{:S(2)}) collective-permute-start(bf16[32,8192]{1,0:T(8,128)(2,1)} %get-tuple-element.69), channel_id=1, source_target_pairs={{0,2},{2,0},{4,6},{6,4},{8,10},{10,8},{12,14},{14,12},{1,3},{3,1},... | collective-permute-start | bytes 1572872 | tf_op jit(solution)/shard_map/ppermute | solution.py:327
  110.8 2.6 %collective-permute-start.13 = (bf16[32,8192]{1,0:T(8,128)(2,1)}, bf16[32,8192]{1,0:T(8,128)(2,1)}, u32[]{:S(2)}, u32[]{:S(2)}) collective-permute-start(bf16[32,8192]{1,0:T(8,128)(2,1)} %get-tuple-element.66), channel_id=1, source_target_pairs={{0,2},{2,0},{4,6},{6,4},{8,10},{10,8},{12,14},{14,12},{1,3},{3,1},... | collective-permute-start | bytes 1572872 | tf_op jit(solution)/shard_map/ppermute | solution.py:327
  111.1 0.8 copy-start.11
  111.9 2.3 %collective-permute-start.14 = (bf16[32,8192]{1,0:T(8,128)(2,1)}, bf16[32,8192]{1,0:T(8,128)(2,1)}, u32[]{:S(2)}, u32[]{:S(2)}) collective-permute-start(bf16[32,8192]{1,0:T(8,128)(2,1)} %get-tuple-element.67), channel_id=1, source_target_pairs={{0,2},{2,0},{4,6},{6,4},{8,10},{10,8},{12,14},{14,12},{1,3},{3,1},... | collective-permute-start | bytes 1572872 | tf_op jit(solution)/shard_map/ppermute | solution.py:327
  112.1 52.6 %collective-permute-start.10 = (bf16[64,8192]{1,0:T(8,128)(2,1)S(1)}, bf16[64,8192]{1,0:T(8,128)(2,1)S(1)}, u32[]{:S(2)}, u32[]{:S(2)}) collective-permute-start(bf16[64,8192]{1,0:T(8,128)(2,1)S(1)} %collective-permute-done.3.whole_ref.refs_1_), channel_id=1, source_target_pairs={{0,4},{2,6},{4,8},{6,10},{8,12},{10,14},{12,0},{14,2},{1,5},{3,7},... | collective-permute-start | bytes 3145736 | tf_op jit(solution)/shard_map/ppermute | solution.py:323
  114.1 1.0 copy-start.12
  133.2 32.3 %collective-permute-start.21 = (bf16[256,2048]{1,0:T(8,128)(2,1)}, bf16[256,2048]{1,0:T(8,128)(2,1)}, u32[]{:S(2)}, u32[]{:S(2)}) collective-permute-start(bf16[256,2048]{1,0:T(8,128)(2,1)} %get-tuple-element.70), channel_id=1, source_target_pairs={{0,1},{2,3},{4,5},{6,7},{9,8},{11,10},{13,12},{15,14},{16,17},{18,... | collective-permute-start | bytes 3145736 | tf_op jit(solution)/shard_map/ppermute | solution.py:336
  140.5 1.5 collective-permute-start.17
  140.6 2.0 %collective-permute-start.18 = (bf16[16,8192]{1,0:T(8,128)(2,1)}, bf16[16,8192]{1,0:T(8,128)(2,1)S(1)}, u32[]{:S(2)}, u32[]{:S(2)}) collective-permute-start(bf16[16,8192]{1,0:T(8,128)(2,1)} %get-tuple-element.75), channel_id=1, source_target_pairs={{0,2},{2,0},{4,6},{6,4},{8,10},{10,8},{12,14},{14,12},{1,3},{3,1},... | collective-permute-start | bytes 786440 | tf_op jit(solution)/shard_map/ppermute | solution.py:327
  141.0 2.3 %collective-permute-start.19 = (bf16[16,8192]{1,0:T(8,128)(2,1)}, bf16[16,8192]{1,0:T(8,128)(2,1)S(1)}, u32[]{:S(2)}, u32[]{:S(2)}) collective-permute-start(bf16[16,8192]{1,0:T(8,128)(2,1)} %get-tuple-element.76), channel_id=1, source_target_pairs={{0,2},{2,0},{4,6},{6,4},{8,10},{10,8},{12,14},{14,12},{1,3},{3,1},... | collective-permute-start | bytes 786440 | tf_op jit(solution)/shard_map/ppermute | solution.py:327
  142.0 2.0 collective-permute-start.20
  142.6 0.7 copy-start.13
  143.3 0.7 copy-start.15
  144.0 0.7 copy-start.17
  144.8 0.9 copy-start.14
  145.7 0.9 copy-start.16
  146.7 0.9 copy-start.18
  163.4 15.9 %collective-permute-start.27 = (bf16[128,2048]{1,0:T(8,128)(2,1)S(1)}, bf16[128,2048]{1,0:T(8,128)(2,1)S(1)}, u32[]{:S(2)}, u32[]{:S(2)}) collective-permute-start(bf16[128,2048]{1,0:T(8,128)(2,1)S(1)} %get-tuple-element.78), channel_id=1, source_target_pairs={{1,0},{3,2},{4,5},{6,7},{8,9},{10,11},{13,12},{15,14},{17,16},{19,... | collective-permute-start | bytes 1572872 | tf_op jit(solution)/shard_map/ppermute | solution.py:336
  164.8 1.6 collective-permute-start.22
  165.0 1.8 collective-permute-start.23
  165.3 1.8 collective-permute-start.24
  165.5 2.0 %collective-permute-start.25 = (bf16[16,8192]{1,0:T(8,128)(2,1)S(1)}, bf16[16,8192]{1,0:T(8,128)(2,1)S(1)}, u32[]{:S(2)}, u32[]{:S(2)}) collective-permute-start(bf16[16,8192]{1,0:T(8,128)(2,1)S(1)} %get-tuple-element.84), channel_id=1, source_target_pairs={{0,2},{2,0},{4,6},{6,4},{8,10},{10,8},{12,14},{14,12},{1,3},{3,1},... | collective-permute-start | bytes 786440 | tf_op jit(solution)/shard_map/ppermute | solution.py:327
  176.8 15.4 %collective-permute-start.26 = (bf16[128,1024]{1,0:T(8,128)(2,1)S(1)}, bf16[128,1024]{1,0:T(8,128)(2,1)S(1)}, u32[]{:S(2)}, u32[]{:S(2)}) collective-permute-start(bf16[128,1024]{1,0:T(8,128)(2,1)S(1)} %get-tuple-element.86), channel_id=1, source_target_pairs={{1,0},{3,2},{4,5},{6,7},{8,9},{10,11},{13,12},{15,14},{17,16},{19,... | collective-permute-start | bytes 786440 | tf_op jit(solution)/shard_map/ppermute | solution.py:336
  188.6 9.4 %collective-permute-start.28 = (bf16[128,1024]{1,0:T(8,128)(2,1)S(1)}, bf16[128,1024]{1,0:T(8,128)(2,1)S(1)}, u32[]{:S(2)}, u32[]{:S(2)}) collective-permute-start(bf16[128,1024]{1,0:T(8,128)(2,1)S(1)} %get-tuple-element.89), channel_id=1, source_target_pairs={{1,0},{3,2},{4,5},{6,7},{8,9},{10,11},{13,12},{15,14},{17,16},{19,... | collective-permute-start | bytes 786440 | tf_op jit(solution)/shard_map/ppermute | solution.py:336

commit v12 on v11

--- a/solution.py
+++ b/solution.py
@@ -94,7 +94,7 @@
     left, held, keep, send, in_sems, train_sems, keep_sems, send_sems = refs[4:]
     rows = sum(ref.shape[0] for ref in mine_refs)
     slots, tile, width = held.shape
-    tiles = keep.shape[1] // tile
+    tiles = keep_sems.shape[0]
     half = tile // 2
     depth = min(width, 1024)
     core = core_ref[0]
@@ -131,11 +131,14 @@
         scale = 1.0 / (fisher_ref[:, cols] + damping)
         left[:, cols] = (left[:, cols].astype(jnp.float32) * scale).astype(jnp.bfloat16)
 
-    def keeps(i):
+    def stores(i, of_mine):
+        slot = lax.rem(i, 2)
         cols = pl.ds(pl.multiple_of(i * tile, tile), tile)
+        if not of_mine:
+            return [pltpu.make_async_copy(send.at[slot], send_ref.at[:, cols], send_sems.at[i])]
         return [
             pltpu.make_async_copy(
-                keep.at[pl.ds(c * rows, rows), cols],
+                keep.at[slot, pl.ds(c * rows, rows)],
                 scores_ref.at[
                     spot_ref[0], c, pl.ds(start, rows),
                     pl.ds(pl.multiple_of(i * tile, tile) + top, tile),
@@ -145,13 +148,15 @@
             for c in range(cores)
         ]
 
-    def sends(i):
-        cols = pl.ds(pl.multiple_of(i * tile, tile), tile)
-        return [pltpu.make_async_copy(send.at[:, cols], send_ref.at[:, cols], send_sems.at[i])]
+    def wait_stores(i):
+        for flag in (0, 1):
+            @pl.when(mine_ref[0] == flag)
+            def _():
+                for store in stores(i, flag):
+                    store.wait()
 
     @pl.loop(0, tiles)
     def _(i):
-        cols = pl.ds(pl.multiple_of(i * tile, tile), tile)
         for fetch in fetches(i):
             fetch.wait()
         sums = lax.dot_general(
@@ -159,34 +164,29 @@
             preferred_element_type=jnp.float32,
         )
 
+        @pl.when(i >= 2)
+        def _():
+            wait_stores(i - 2)
+
         @pl.when(mine_ref[0] == 1)
         def _():
-            keep[:, cols] = sums
-            for copy in keeps(i):
-                copy.start()
+            keep[lax.rem(i, 2)] = sums
+            for store in stores(i, True):
+                store.start()
 
         @pl.when(mine_ref[0] == 0)
         def _():
-            send[:, cols] = sums.astype(jnp.bfloat16)
-            for copy in sends(i):
-                copy.start()
+            send[lax.rem(i, 2)] = sums.astype(jnp.bfloat16)
+            for store in stores(i, False):
+                store.start()
 
         @pl.when(i + slots < tiles)
         def _():
             for fetch in fetches(i + slots):
                 fetch.start()
 
-    @pl.loop(0, tiles)
-    def _(i):
-        @pl.when(mine_ref[0] == 1)
-        def _():
-            for copy in keeps(i):
-                copy.wait()
-
-        @pl.when(mine_ref[0] == 0)
-        def _():
-            for copy in sends(i):
-                copy.wait()
+    for i in range(max(tiles - 2, 0), tiles):
+        wait_stores(i)
 
 
 def multiply(scores, shape, where, core, mine, other, fisher, train, start, span=None):
@@ -195,7 +195,7 @@
     top, bottom = span or (0, train.shape[0])
     count = bottom - top
     tile = min(count, 256)
-    slots = 4
+    slots = 3
     block = (cores * rows, count)
     given = [] if scores is None else [scores]
     counts = (len(mine), len(other), len(given))
@@ -209,15 +209,15 @@
         scratch_shapes=[
             pltpu.VMEM((cores * rows, width), jnp.bfloat16),
             pltpu.VMEM((slots, tile, width), jnp.bfloat16),
-            pltpu.VMEM(block, jnp.float32),
-            pltpu.VMEM(block, jnp.bfloat16),
+            pltpu.VMEM((2, cores * rows, tile), jnp.float32),
+            pltpu.VMEM((2, cores * rows, tile), jnp.bfloat16),
             pltpu.SemaphoreType.DMA((len(mine) + len(other),)),
             pltpu.SemaphoreType.DMA((slots, 2)),
             pltpu.SemaphoreType.DMA((count // tile, cores)),
             pltpu.SemaphoreType.DMA((count // tile,)),
         ],
         input_output_aliases={3 + len(mine) + len(other): 0} if given else {},
-        compiler_params=pltpu.CompilerParams(vmem_limit_bytes=26 * mib),
+        compiler_params=pltpu.CompilerParams(vmem_limit_bytes=20 * mib),
         cost_estimate=small,
         name="multiply",
     )(*where, core, *mine, *other, *given, fisher, train)
@@ -342,51 +342,49 @@
         return mine, lax.rem(source, chips_per_owner)[None]
 
     hops = chips - 1
-    low_flow, high_flow = [shift(piece) for piece in cut(val_grads, 2)]
+    flow = shift(val_grads)
     train, keep, send = first(core, val_grads, *swap([val_grads]), fisher, grad_codes, scale_exps)
     scores, kept = None, [keep]
     for hop in range(1, hops):
         received = exchange(send, hop - 1)
-        low_piece = after(low_flow, send, *([] if scores is None else [scores]))
-        low_flow = shift(low_piece)
-        low_other = swap(cut(low_piece, 2))
-        high_piece = after(high_flow, low_piece)
-        high_flow = shift(high_piece)
-        high_other = swap(cut(high_piece, 2))
+        panel = after(flow, send, *([] if scores is None else [scores]))
+        if hop + 1 < hops:
+            flow = shift(panel)
+        else:
+            low_flow, high_piece = cut(panel, 2)
+            low_flow = shift(low_flow)
         if hop > 1:
-            low_piece = after(low_piece, *received)
+            panel = after(panel, *received)
         scores, send = multiply(
-            scores, shape, whose(hop), core, [low_piece, high_piece], [*low_other, *high_other],
-            fisher, train, 0,
+            scores, shape, whose(hop), core, [panel], swap([panel]), fisher, train, 0
         )
         received = [after(term, send) for term in received]
         scores = place(scores, whose(hop - 1), kept, received, [0] * len(received), 0)
         kept = []
+    high_flow = shift(after(high_piece, send))
     earlier = exchange(send, hops - 1)
     low_piece = after(low_flow, send, scores)
-    small = max(1, min(4, low_piece.shape[0] // 16))
     scores, send = multiply(
-        scores, shape, whose(hops), core, [low_piece], swap(cut(low_piece, small)), fisher, train, 0
+        scores, shape, whose(hops), core, [low_piece], swap(cut(low_piece, 2)), fisher, train, 0
     )
     received = exchange(send, hops)
-    high_piece = after(high_flow, send)
-    high_other = swap(cut(high_piece, small))
-    high_piece = after(high_piece, *earlier)
-    half = count // 2
+    high_piece = after(high_flow, send, *earlier)
+    high_other = swap([high_piece])
+    knee = count * 5 // 8
     halves = []
-    for top in (0, half):
+    for top, bottom in ((0, knee), (knee, count)):
         if top:
             high_piece = after(high_piece, send, *received)
         scores, send = multiply(
             scores, shape, whose(hops), core, [high_piece], high_other, fisher, train, own // 2,
-            (top, top + half),
+            (top, bottom),
         )
         halves.append(exchange(send, hops))
     earlier = [after(term, send) for term in earlier]
     scores = place(scores, whose(hops - 1), [], earlier, [0] * len(earlier), 0)
     received = [after(term, scores) for term in received]
     scores = place(scores, whose(hops), [], received, [0] * len(received), 0)
-    cols = [0] * len(received) + [half] * len(received)
+    cols = [0] * len(received) + [knee] * len(received)
     scores = place(scores, whose(hops), [], halves[0] + halves[1], cols, own // 2)
     return scores.reshape(chips_per_owner * cores * own, count)
 

time: 201 us -> 189 us (0.940)
  local copies, waits for them, and re-layouts: 17.8 us -> 7.86 us
  starting transfers between devices: 26.4 us -> 17.2 us
  waiting for transfers between devices: 43 us -> 52 us
    unnamed x39 -> x17, local copies, waits for them, and re-layouts: 17.8 us -> 7.86 us
    ppermute x6 -> x4, waiting for transfers between devices: 30.1 us -> 35.6 us  [shift(): return lax.ppermute(panel, 'blk', pairs)]
    pallas_call x7 -> x2, Pallas kernels: 7.95 us -> 2.59 us  [cut(): pl.pallas_call(cut_kernel, in_specs=[in_vmem], out_specs=[in_vmem] * coun...]
    ppermute x6 -> x4, starting transfers between devices: 9.73 us -> 4.81 us  [shift(): return lax.ppermute(panel, 'blk', pairs)]
    pallas_call x5, Pallas kernels: 66.9 us -> 71.5 us  [multiply(): pl.pallas_call(functools.partial(multiply_kernel, counts, start, top), in...]
    ppermute x17 -> x6, starting transfers between devices: 4.06 us -> 1.17 us  [swap(): return [lax.ppermute(part, 'blk', pairs) for part in parts]]
    ppermute x17 -> x6, waiting for transfers between devices: 6.11 us -> 8.51 us  [swap(): return [lax.ppermute(part, 'blk', pairs) for part in parts]]
  transfers between devices with their start and end apart: 29 -> 16, of which waited for: 15 -> 11; matrix products, arithmetic and copies ran while one was open for 1% -> 1% of each run, Pallas kernels for 55% -> 58%
where the time goes in v12:
time: 189 us; the launch traced here: 188 us
  Pallas kernels  111 us (59%)
  waiting for transfers between devices  52 us (28%)
  starting transfers between devices  17.2 us (9%)
  local copies, waits for them, and re-layouts  7.86 us (4%)
    pallas_call x5, Pallas kernels, multiply(): pl.pallas_call(functools.partial(multiply_kernel, counts, start, top), in...  71.5 us
    ppermute x4, waiting for transfers between devices, shift(): return lax.ppermute(panel, 'blk', pairs)  35.6 us
    pallas_call x1, Pallas kernels, first(): pl.pallas_call(first_kernel, grid=(count // tile,), in_specs=[in_smem, pl...  29.1 us
    ppermute x6, starting transfers between devices, exchange(): received.append(lax.ppermute(send, ('blk', 'dim'), pairs))  11.2 us
    ppermute x6, waiting for transfers between devices, swap(): return [lax.ppermute(part, 'blk', pairs) for part in parts]  8.51 us
    ppermute x6, waiting for transfers between devices, exchange(): received.append(lax.ppermute(send, ('blk', 'dim'), pairs))  7.98 us
    unnamed x17, local copies, waits for them, and re-layouts  7.86 us
    pallas_call x5, Pallas kernels, place(): pl.pallas_call(functools.partial(place_kernel, start, cols, len(kept)), i...  7.61 us
  transfers between devices with their start and end apart: 16, of which 11 were waited for; matrix products, arithmetic and copies ran while one was open for 1% of the time, Pallas kernels for 58%

profile of v12, /device:TPU:0, one launch (start us, length us, event | category | flops | bytes accessed | tf_op | source)
XLA Modules:
  0.0 188.2 jit_solution(7559123068500926110)
XLA Ops:
  0.0 0.5 collective-permute-start.1
  0.5 2.6 %collective-permute-start = (bf16[128,8192]{1,0:T(8,128)(2,1)}, bf16[128,8192]{1,0:T(8,128)(2,1)}, u32[]{:S(2)}, u32[]{:S(2)}) collective-permute-start(bf16[128,8192]{1,0:T(8,128)(2,1)} %mine_ref.1), channel_id=1, source_target_pairs={{0,4},{2,6},{4,8},{6,10},{8,12},{10,14},{12,0},{14,2},{1,5},{3,7},... | collective-permute-start | bytes 6291464 | tf_op jit(solution)/shard_map/ppermute | solution.py:323
  3.0 1.4 copy.14.exps_ref
  4.4 0.0 collective-permute-done.1.other_ref
  4.5 1.6 copy-done
  6.0 0.8 copy-done.3
  6.8 29.1 %first.1 = (bf16[2048,8192]{1,0:T(8,128)(2,1)}, f32[256,2048]{1,0:T(8,128)S(1)}, bf16[256,2048]{1,0:T(8,128)(2,1)S(1)}) custom-call(s32[1]{0:T(128)} %bitcast.2.core_ref, bf16[128,8192]{1,0:T(8,128)(2,1)S(1)} %copy-done, bf16[128,8192]{1,0:T(8,128)(2,1)S(1)} %collective-permute-done.1.other_ref, f32[1,8192]{1,0:T(1,128)S(1)} %bitcast.11, ...), custom_call_target="tpu_custom_call" | custom-call | flops 1 | bytes 1 | tf_op jit(solution)/shard_map/first/pallas_call | solution.py:59
  35.9 1.4 copy-done.1
  37.3 1.1 copy-done.7
  38.4 13.3 %collective-permute-done.refs_0_ = bf16[128,8192]{1,0:T(8,128)(2,1)} collective-permute-done((bf16[128,8192]{1,0:T(8,128)(2,1)}, bf16[128,8192]{1,0:T(8,128)(2,1)}, u32[]{:S(2)}, u32[]{:S(2)}) %collective-permute-start) | collective-permute-done | bytes 2097184 | tf_op jit(solution)/shard_map/ppermute | solution.py:323
  51.7 0.0 collective-permute-start.3
  51.7 0.0 collective-permute-start.2
  51.7 1.3 collective-permute-start.4
  53.0 3.2 %collective-permute-done.3.refs_1_ = bf16[128,8192]{1,0:T(8,128)(2,1)} collective-permute-done((bf16[128,8192]{1,0:T(8,128)(2,1)}, bf16[128,8192]{1,0:T(8,128)(2,1)}, u32[]{:S(2)}, u32[]{:S(2)}) %collective-permute-start.3) | collective-permute-done | bytes 2097184 | tf_op jit(solution)/shard_map/ppermute | solution.py:327
  56.2 17.6 %multiply.5 = (f32[2,2,128,2048]{3,2,1,0:T(8,128)}, bf16[256,2048]{1,0:T(8,128)(2,1)}) custom-call(s32[1]{0:T(128)} %bitcast.4.mine_ref, s32[1]{0:T(128)} %bitcast.5.spot_ref, s32[1]{0:T(128)} %bitcast.2.core_ref, bf16[128,8192]{1,0:T(8,128)(2,1)} %collective-permute-done.refs_0_, bf16[128,8192]{1,0:T(8,128)(2,1)} %collective-permute-done.3.refs_1_, ...), custom_call_target="tpu_custom_call" | custom-call | flops 1 | bytes 1 | tf_op jit(solution)/shard_map/multiply/pallas_call | solution.py:202
  73.7 3.6 %collective-permute-start.5 = (bf16[256,2048]{1,0:T(8,128)(2,1)}, bf16[256,2048]{1,0:T(8,128)(2,1)S(1)}, u32[]{:S(2)}, u32[]{:S(2)}) collective-permute-start(bf16[256,2048]{1,0:T(8,128)(2,1)} %get-tuple-element.36), channel_id=1, source_target_pairs={{0,1},{2,3},{5,4},{7,6},{9,8},{11,10},{12,13},{14,15},{16,17},{18,... | collective-permute-start | bytes 3145736 | tf_op jit(solution)/shard_map/ppermute | solution.py:336
  77.4 2.1 %collective-permute-done.4.refs_1_ = bf16[256,2048]{1,0:T(8,128)(2,1)} collective-permute-done((bf16[256,2048]{1,0:T(8,128)(2,1)}, bf16[256,2048]{1,0:T(8,128)(2,1)}, u32[]{:S(2)}, u32[]{:S(2)}) %collective-permute-start.4) | collective-permute-done | bytes 1048608 | tf_op jit(solution)/shard_map/ppermute | solution.py:336
  79.4 1.6 copy-done.2
  81.0 2.9 %place.5.refs_2_ = f32[2,2,128,2048]{3,2,1,0:T(8,128)} custom-call(s32[1]{0:T(128)} %bitcast.6.mine_ref, s32[1]{0:T(128)} %bitcast.7.spot_ref, f32[256,2048]{1,0:T(8,128)S(1)} %copy-done.2, bf16[256,2048]{1,0:T(8,128)(2,1)} %collective-permute-done.4.refs_1_, f32[2,2,128,2048]{3,2,1,0:T(8,128)} %get-tuple-element.39.refs_2_), custom_call_target="tpu_custom_call", output_to_operand_aliasing={{}: (4, {})} | custom-call | flops 1 | bytes 1 | tf_op jit(solution)/shard_map/place/pallas_call | solution.py:266
  83.9 17.8 %collective-permute-done.2.whole_ref.refs_0_ = bf16[128,8192]{1,0:T(8,128)(2,1)S(1)} collective-permute-done((bf16[128,8192]{1,0:T(8,128)(2,1)}, bf16[128,8192]{1,0:T(8,128)(2,1)S(1)}, u32[]{:S(2)}, u32[]{:S(2)}) %collective-permute-start.2) | collective-permute-done | bytes 2097184 | tf_op jit(solution)/shard_map/ppermute | solution.py:323
  101.7 1.5 cut.2
  103.3 0.1 copy-done.5
  103.4 1.1 collective-permute-start.8
  104.5 1.5 collective-permute-done.6.refs_1_
  106.0 17.2 %multiply.6 = (f32[2,2,128,2048]{3,2,1,0:T(8,128)}, bf16[256,2048]{1,0:T(8,128)(2,1)}) custom-call(s32[1]{0:T(128)} %bitcast.8.mine_ref, s32[1]{0:T(128)} %bitcast.9.spot_ref, s32[1]{0:T(128)} %bitcast.2.core_ref, bf16[128,8192]{1,0:T(8,128)(2,1)S(1)} %collective-permute-done.2.whole_ref.refs_0_, ...), custom_call_target="tpu_custom_call", output_to_operand_aliasing={{0}: (5, {})} | custom-call | flops 1 | bytes 1 | tf_op jit(solution)/shard_map/multiply/pallas_call | solution.py:202
  123.2 1.1 collective-permute-start.7
  124.3 2.5 %collective-permute-start.11 = (bf16[256,2048]{1,0:T(8,128)(2,1)}, bf16[256,2048]{1,0:T(8,128)(2,1)S(1)}, u32[]{:S(2)}, u32[]{:S(2)}) collective-permute-start(bf16[256,2048]{1,0:T(8,128)(2,1)} %get-tuple-element.43), channel_id=1, source_target_pairs={{0,1},{2,3},{4,5},{6,7},{9,8},{11,10},{13,12},{15,14},{16,17},{18,... | collective-permute-start | bytes 3145736 | tf_op jit(solution)/shard_map/ppermute | solution.py:336
  126.9 0.1 place.6.refs_3_
  126.9 4.5 %collective-permute-done.8.whole_ref.refs_0_ = bf16[64,8192]{1,0:T(8,128)(2,1)S(1)} collective-permute-done((bf16[64,8192]{1,0:T(8,128)(2,1)}, bf16[64,8192]{1,0:T(8,128)(2,1)S(1)}, u32[]{:S(2)}, u32[]{:S(2)}) %collective-permute-start.8) | collective-permute-done | bytes 1048608 | tf_op jit(solution)/shard_map/ppermute | solution.py:323
  131.4 1.0 cut.3
  132.4 0.0 collective-permute-start.10
  132.4 0.5 collective-permute-start.9
  132.9 1.7 collective-permute-done.10.refs_2_
  134.7 0.7 collective-permute-done.9.refs_1_
  135.4 18.0 %multiply.7 = (f32[2,2,128,2048]{3,2,1,0:T(8,128)}, bf16[128,2048]{1,0:T(8,128)(2,1)S(1)}) custom-call(s32[1]{0:T(128)} %bitcast.mine_ref, s32[1]{0:T(128)} %bitcast.1.spot_ref, s32[1]{0:T(128)} %bitcast.2.core_ref, bf16[64,8192]{1,0:T(8,128)(2,1)S(1)} %collective-permute-done.8.whole_ref.refs_0_, ...), custom_call_target="tpu_custom_call", output_to_operand_aliasing={{0}: (6, {})} | custom-call | flops 1 | bytes 1 | tf_op jit(solution)/shard_map/multiply/pallas_call | solution.py:202
  153.5 0.0 collective-permute-done.7.refs_0_
  153.5 0.2 collective-permute-start.12
  153.7 1.3 collective-permute-start.14
  155.0 1.2 collective-permute-done.12.refs_1_
  156.2 10.9 %multiply.8 = (f32[2,2,128,2048]{3,2,1,0:T(8,128)}, bf16[128,1280]{1,0:T(8,128)(2,1)S(1)}) custom-call(s32[1]{0:T(128)} %bitcast.mine_ref, s32[1]{0:T(128)} %bitcast.1.spot_ref, s32[1]{0:T(128)} %bitcast.2.core_ref, bf16[64,8192]{1,0:T(8,128)(2,1)S(1)} %collective-permute-done.7.refs_0_, ...), custom_call_target="tpu_custom_call", output_to_operand_aliasing={{0}: (5, {})} | custom-call | flops 1 | bytes 1 | tf_op jit(solution)/shard_map/multiply/pallas_call | solution.py:202
  167.2 1.3 collective-permute-start.13
  168.5 1.3 collective-permute-done.14.refs_0_
  169.8 7.8 %multiply.9 = (f32[2,2,128,2048]{3,2,1,0:T(8,128)}, bf16[128,768]{1,0:T(8,128)(2,1)S(1)}) custom-call(s32[1]{0:T(128)} %bitcast.mine_ref, s32[1]{0:T(128)} %bitcast.1.spot_ref, s32[1]{0:T(128)} %bitcast.2.core_ref, bf16[64,8192]{1,0:T(8,128)(2,1)S(1)} %collective-permute-done.7.refs_0_, ...), custom_call_target="tpu_custom_call", output_to_operand_aliasing={{0}: (5, {})} | custom-call | flops 1 | bytes 1 | tf_op jit(solution)/shard_map/multiply/pallas_call | solution.py:202
  177.6 1.3 collective-permute-start.15
  178.9 0.1 place.7.refs_1_
  178.9 2.3 %place.8.refs_2_ = f32[2,2,128,2048]{3,2,1,0:T(8,128)} custom-call(s32[1]{0:T(128)} %bitcast.mine_ref, s32[1]{0:T(128)} %bitcast.1.spot_ref, bf16[128,2048]{1,0:T(8,128)(2,1)S(1)} %collective-permute-done.14.refs_0_, f32[2,2,128,2048]{3,2,1,0:T(8,128)} %place.7.refs_1_), custom_call_target="tpu_custom_call", output_to_operand_aliasing={{}: (3, {})} | custom-call | flops 1 | bytes 1 | tf_op jit(solution)/shard_map/place/pallas_call | solution.py:266
  181.3 4.6 %collective-permute-done.15.refs_1_ = bf16[128,768]{1,0:T(8,128)(2,1)S(1)} collective-permute-done((bf16[128,768]{1,0:T(8,128)(2,1)S(1)}, bf16[128,768]{1,0:T(8,128)(2,1)S(1)}, u32[]{:S(2)}, u32[]{:S(2)}) %collective-permute-start.15) | collective-permute-done | bytes 196640 | tf_op jit(solution)/shard_map/ppermute | solution.py:336
  185.8 2.3 %place.9 = f32[2,2,128,2048]{3,2,1,0:T(8,128)} custom-call(s32[1]{0:T(128)} %bitcast.mine_ref, s32[1]{0:T(128)} %bitcast.1.spot_ref, bf16[128,1280]{1,0:T(8,128)(2,1)S(1)} %collective-permute-done.13.refs_0_, bf16[128,768]{1,0:T(8,128)(2,1)S(1)} %collective-permute-done.15.refs_1_, f32[2,2,128,2048]{3,2,1,0:T(8,128)} %place.8.refs_2_), custom_call_target="tpu_custom_call", output_to_operand_aliasing={{}: (4, {})} | custom-call | flops 1 | bytes 1 | tf_op jit(solution)/shard_map/place/pallas_call | solution.py:266
  (14 shorter events, 0.0 us)
Async XLA Ops:
  0.0 4.5 %collective-permute-start.1 = (bf16[128,8192]{1,0:T(8,128)(2,1)}, bf16[128,8192]{1,0:T(8,128)(2,1)S(1)}, u32[]{:S(2)}, u32[]{:S(2)}) collective-permute-start(bf16[128,8192]{1,0:T(8,128)(2,1)} %mine_ref.1), channel_id=1, source_target_pairs={{0,2},{2,0},{4,6},{6,4},{8,10},{10,8},{12,14},{14,12},{1,3},{3,1},... | collective-permute-start | bytes 6291464 | tf_op jit(solution)/shard_map/ppermute | solution.py:327
  0.5 51.2 %collective-permute-start = (bf16[128,8192]{1,0:T(8,128)(2,1)}, bf16[128,8192]{1,0:T(8,128)(2,1)}, u32[]{:S(2)}, u32[]{:S(2)}) collective-permute-start(bf16[128,8192]{1,0:T(8,128)(2,1)} %mine_ref.1), channel_id=1, source_target_pairs={{0,4},{2,6},{4,8},{6,10},{8,12},{10,14},{12,0},{14,2},{1,5},{3,7},... | collective-permute-start | bytes 6291464 | tf_op jit(solution)/shard_map/ppermute | solution.py:323
  4.5 1.6 copy-start
  6.0 0.8 copy-start.3
  6.8 49.4 %copy-start.4 = (f32[8192]{0:T(1024)S(1)}, f32[8192]{0:T(1024)}, u32[]{:S(2)}) copy-start(f32[8192]{0:T(1024)} %param.7) | copy-start | bytes 98308
  35.9 1.4 copy-start.1
  37.3 1.1 copy-start.7
  51.7 4.5 %collective-permute-start.3 = (bf16[128,8192]{1,0:T(8,128)(2,1)}, bf16[128,8192]{1,0:T(8,128)(2,1)}, u32[]{:S(2)}, u32[]{:S(2)}) collective-permute-start(bf16[128,8192]{1,0:T(8,128)(2,1)} %collective-permute-done.refs_0_), channel_id=1, source_target_pairs={{0,2},{2,0},{4,6},{6,4},{8,10},{10,8},{12,14},{14,12},{1,3},{3,1},... | collective-permute-start | bytes 6291464 | tf_op jit(solution)/shard_map/ppermute | solution.py:327
  51.7 50.1 %collective-permute-start.2 = (bf16[128,8192]{1,0:T(8,128)(2,1)}, bf16[128,8192]{1,0:T(8,128)(2,1)S(1)}, u32[]{:S(2)}, u32[]{:S(2)}) collective-permute-start(bf16[128,8192]{1,0:T(8,128)(2,1)} %collective-permute-done.refs_0_), channel_id=1, source_target_pairs={{0,4},{2,6},{4,8},{6,10},{8,12},{10,14},{12,0},{14,2},{1,5},{3,7},... | collective-permute-start | bytes 6291464 | tf_op jit(solution)/shard_map/ppermute | solution.py:323
  51.7 27.8 %collective-permute-start.4 = (bf16[256,2048]{1,0:T(8,128)(2,1)}, bf16[256,2048]{1,0:T(8,128)(2,1)}, u32[]{:S(2)}, u32[]{:S(2)}) collective-permute-start(bf16[256,2048]{1,0:T(8,128)(2,1)} %copy-done.7), channel_id=1, source_target_pairs={{1,0},{3,2},{5,4},{7,6},{8,9},{10,11},{12,13},{14,15},{17,16},{19,... | collective-permute-start | bytes 3145736 | tf_op jit(solution)/shard_map/ppermute | solution.py:336
  73.7 28.0 %collective-permute-start.5 = (bf16[256,2048]{1,0:T(8,128)(2,1)}, bf16[256,2048]{1,0:T(8,128)(2,1)S(1)}, u32[]{:S(2)}, u32[]{:S(2)}) collective-permute-start(bf16[256,2048]{1,0:T(8,128)(2,1)} %get-tuple-element.36), channel_id=1, source_target_pairs={{0,1},{2,3},{5,4},{7,6},{9,8},{11,10},{12,13},{14,15},{16,17},{18,... | collective-permute-start | bytes 3145736 | tf_op jit(solution)/shard_map/ppermute | solution.py:336
  79.4 1.6 copy-start.2
  101.7 1.7 copy-start.5
  101.7 4.3 %collective-permute-start.6 = (bf16[128,8192]{1,0:T(8,128)(2,1)S(1)}, bf16[128,8192]{1,0:T(8,128)(2,1)}, u32[]{:S(2)}, u32[]{:S(2)}) collective-permute-start(bf16[128,8192]{1,0:T(8,128)(2,1)S(1)} %collective-permute-done.2.whole_ref.refs_0_), channel_id=1, source_target_pairs={{0,2},{2,0},{4,6},{6,4},{8,10},{10,8},{12,14},{14,12},{1,3},{3,1},... | collective-permute-start | bytes 6291464 | tf_op jit(solution)/shard_map/ppermute | solution.py:327
  103.4 28.0 %collective-permute-start.8 = (bf16[64,8192]{1,0:T(8,128)(2,1)}, bf16[64,8192]{1,0:T(8,128)(2,1)S(1)}, u32[]{:S(2)}, u32[]{:S(2)}) collective-permute-start(bf16[64,8192]{1,0:T(8,128)(2,1)} %get-tuple-element.45), channel_id=1, source_target_pairs={{0,4},{2,6},{4,8},{6,10},{8,12},{10,14},{12,0},{14,2},{1,5},{3,7},... | collective-permute-start | bytes 3145736 | tf_op jit(solution)/shard_map/ppermute | solution.py:323
  106.0 20.8 %copy-start.6 = (bf16[256,2048]{1,0:T(8,128)(2,1)S(1)}, bf16[256,2048]{1,0:T(8,128)(2,1)}, u32[]{:S(2)}) copy-start(bf16[256,2048]{1,0:T(8,128)(2,1)} %copy-done.5) | copy-start | bytes 3145732
  123.2 30.3 %collective-permute-start.7 = (bf16[64,8192]{1,0:T(8,128)(2,1)}, bf16[64,8192]{1,0:T(8,128)(2,1)S(1)}, u32[]{:S(2)}, u32[]{:S(2)}) collective-permute-start(bf16[64,8192]{1,0:T(8,128)(2,1)} %get-tuple-element.44), channel_id=1, source_target_pairs={{0,4},{2,6},{4,8},{6,10},{8,12},{10,14},{12,0},{14,2},{1,5},{3,7},... | collective-permute-start | bytes 3145736 | tf_op jit(solution)/shard_map/ppermute | solution.py:323
  124.3 29.1 %collective-permute-start.11 = (bf16[256,2048]{1,0:T(8,128)(2,1)}, bf16[256,2048]{1,0:T(8,128)(2,1)S(1)}, u32[]{:S(2)}, u32[]{:S(2)}) collective-permute-start(bf16[256,2048]{1,0:T(8,128)(2,1)} %get-tuple-element.43), channel_id=1, source_target_pairs={{0,1},{2,3},{4,5},{6,7},{9,8},{11,10},{13,12},{15,14},{16,17},{18,... | collective-permute-start | bytes 3145736 | tf_op jit(solution)/shard_map/ppermute | solution.py:336
  132.4 2.3 %collective-permute-start.10 = (bf16[32,8192]{1,0:T(8,128)(2,1)}, bf16[32,8192]{1,0:T(8,128)(2,1)}, u32[]{:S(2)}, u32[]{:S(2)}) collective-permute-start(bf16[32,8192]{1,0:T(8,128)(2,1)} %get-tuple-element.50), channel_id=1, source_target_pairs={{0,2},{2,0},{4,6},{6,4},{8,10},{10,8},{12,14},{14,12},{1,3},{3,1},... | collective-permute-start | bytes 1572872 | tf_op jit(solution)/shard_map/ppermute | solution.py:327
  132.4 3.0 %collective-permute-start.9 = (bf16[32,8192]{1,0:T(8,128)(2,1)}, bf16[32,8192]{1,0:T(8,128)(2,1)}, u32[]{:S(2)}, u32[]{:S(2)}) collective-permute-start(bf16[32,8192]{1,0:T(8,128)(2,1)} %get-tuple-element.49), channel_id=1, source_target_pairs={{0,2},{2,0},{4,6},{6,4},{8,10},{10,8},{12,14},{14,12},{1,3},{3,1},... | collective-permute-start | bytes 1572872 | tf_op jit(solution)/shard_map/ppermute | solution.py:327
  153.5 2.7 %collective-permute-start.12 = (bf16[64,8192]{1,0:T(8,128)(2,1)S(1)}, bf16[64,8192]{1,0:T(8,128)(2,1)S(1)}, u32[]{:S(2)}, u32[]{:S(2)}) collective-permute-start(bf16[64,8192]{1,0:T(8,128)(2,1)S(1)} %collective-permute-done.7.refs_0_), channel_id=1, source_target_pairs={{0,2},{2,0},{4,6},{6,4},{8,10},{10,8},{12,14},{14,12},{1,3},{3,1},... | collective-permute-start | bytes 3145736 | tf_op jit(solution)/shard_map/ppermute | solution.py:327
  153.7 16.1 %collective-permute-start.14 = (bf16[128,2048]{1,0:T(8,128)(2,1)S(1)}, bf16[128,2048]{1,0:T(8,128)(2,1)S(1)}, u32[]{:S(2)}, u32[]{:S(2)}) collective-permute-start(bf16[128,2048]{1,0:T(8,128)(2,1)S(1)} %get-tuple-element.51), channel_id=1, source_target_pairs={{1,0},{3,2},{4,5},{6,7},{8,9},{10,11},{13,12},{15,14},{17,16},{19,... | collective-permute-start | bytes 1572872 | tf_op jit(solution)/shard_map/ppermute | solution.py:336
  167.2 18.7 %collective-permute-start.13 = (bf16[128,1280]{1,0:T(8,128)(2,1)S(1)}, bf16[128,1280]{1,0:T(8,128)(2,1)S(1)}, u32[]{:S(2)}, u32[]{:S(2)}) collective-permute-start(bf16[128,1280]{1,0:T(8,128)(2,1)S(1)} %get-tuple-element.54), channel_id=1, source_target_pairs={{1,0},{3,2},{4,5},{6,7},{8,9},{10,11},{13,12},{15,14},{17,16},{19,... | collective-permute-start | bytes 983048 | tf_op jit(solution)/shard_map/ppermute | solution.py:336
  177.6 8.3 %collective-permute-start.15 = (bf16[128,768]{1,0:T(8,128)(2,1)S(1)}, bf16[128,768]{1,0:T(8,128)(2,1)S(1)}, u32[]{:S(2)}, u32[]{:S(2)}) collective-permute-start(bf16[128,768]{1,0:T(8,128)(2,1)S(1)} %get-tuple-element.57), channel_id=1, source_target_pairs={{1,0},{3,2},{4,5},{6,7},{8,9},{10,11},{13,12},{15,14},{17,16},{19,... | collective-permute-start | bytes 589832 | tf_op jit(solution)/shard_map/ppermute | solution.py:336

commit v13 on v12

--- a/solution.py
+++ b/solution.py
@@ -195,7 +195,7 @@
     top, bottom = span or (0, train.shape[0])
     count = bottom - top
     tile = min(count, 256)
-    slots = 3
+    slots = 4
     block = (cores * rows, count)
     given = [] if scores is None else [scores]
     counts = (len(mine), len(other), len(given))
@@ -217,7 +217,7 @@
             pltpu.SemaphoreType.DMA((count // tile,)),
         ],
         input_output_aliases={3 + len(mine) + len(other): 0} if given else {},
-        compiler_params=pltpu.CompilerParams(vmem_limit_bytes=20 * mib),
+        compiler_params=pltpu.CompilerParams(vmem_limit_bytes=22 * mib),
         cost_estimate=small,
         name="multiply",
     )(*where, core, *mine, *other, *given, fisher, train)
@@ -351,8 +351,9 @@
         if hop + 1 < hops:
             flow = shift(panel)
         else:
-            low_flow, high_piece = cut(panel, 2)
-            low_flow = shift(low_flow)
+            low_piece, high_piece = cut(panel, 2)
+            flow = shift(low_piece)
+            panel = after(panel, low_piece)
         if hop > 1:
             panel = after(panel, *received)
         scores, send = multiply(
@@ -361,14 +362,14 @@
         received = [after(term, send) for term in received]
         scores = place(scores, whose(hop - 1), kept, received, [0] * len(received), 0)
         kept = []
-    high_flow = shift(after(high_piece, send))
     earlier = exchange(send, hops - 1)
-    low_piece = after(low_flow, send, scores)
+    low_piece = after(flow, send, scores)
+    flow = shift(after(high_piece, low_piece))
     scores, send = multiply(
-        scores, shape, whose(hops), core, [low_piece], swap(cut(low_piece, 2)), fisher, train, 0
+        scores, shape, whose(hops), core, [low_piece], swap([low_piece]), fisher, train, 0
     )
     received = exchange(send, hops)
-    high_piece = after(high_flow, send, *earlier)
+    high_piece = after(flow, send, *earlier)
     high_other = swap([high_piece])
     knee = count * 5 // 8
     halves = []

time: 189 us -> 194 us (1.026)
  waiting for transfers between devices: 52 us -> 60.1 us
    ppermute x4, waiting for transfers between devices: 35.6 us -> 44.3 us  [shift(): return lax.ppermute(panel, 'blk', pairs)]
    ppermute x4, starting transfers between devices: 4.81 us -> 2.58 us  [shift(): return lax.ppermute(panel, 'blk', pairs)]
    ppermute x6 -> x5, waiting for transfers between devices: 8.51 us -> 8.85 us  [swap(): return [lax.ppermute(part, 'blk', pairs) for part in parts]]
    unnamed x17 -> x13, local copies, waits for them, and re-layouts: 7.86 us -> 7.73 us
  transfers between devices with their start and end apart: 16 -> 15, of which waited for: 11 -> 10; matrix products, arithmetic and copies ran while one was open for 1% -> 1% of each run, Pallas kernels for 58% -> 56%
where the time goes in v13:
time: 194 us; the launch traced here: 193 us
  Pallas kernels  110 us (57%)
  waiting for transfers between devices  60.1 us (31%)
  starting transfers between devices  15.3 us (8%)
  local copies, waits for them, and re-layouts  7.73 us (4%)
    pallas_call x5, Pallas kernels, multiply(): pl.pallas_call(functools.partial(multiply_kernel, counts, start, top), in...  71.7 us
    ppermute x4, waiting for transfers between devices, shift(): return lax.ppermute(panel, 'blk', pairs)  44.3 us
    pallas_call x1, Pallas kernels, first(): pl.pallas_call(first_kernel, grid=(count // tile,), in_specs=[in_smem, pl...  29.1 us
    ppermute x6, starting transfers between devices, exchange(): received.append(lax.ppermute(send, ('blk', 'dim'), pairs))  12.2 us
    ppermute x5, waiting for transfers between devices, swap(): return [lax.ppermute(part, 'blk', pairs) for part in parts]  8.85 us
    unnamed x13, local copies, waits for them, and re-layouts  7.73 us
    pallas_call x5, Pallas kernels, place(): pl.pallas_call(functools.partial(place_kernel, start, cols, len(kept)), i...  7.61 us
    ppermute x6, waiting for transfers between devices, exchange(): received.append(lax.ppermute(send, ('blk', 'dim'), pairs))  6.96 us
  transfers between devices with their start and end apart: 15, of which 10 were waited for; matrix products, arithmetic and copies ran while one was open for 1% of the time, Pallas kernels for 56%

profile of v13, /device:TPU:0, one launch (start us, length us, event | category | flops | bytes accessed | tf_op | source)
XLA Modules:
  0.0 193.3 jit_solution(8434356842549441409)
XLA Ops:
  0.0 0.5 collective-permute-start.1
  0.5 2.6 %collective-permute-start = (bf16[128,8192]{1,0:T(8,128)(2,1)}, bf16[128,8192]{1,0:T(8,128)(2,1)}, u32[]{:S(2)}, u32[]{:S(2)}) collective-permute-start(bf16[128,8192]{1,0:T(8,128)(2,1)} %mine_ref.1), channel_id=1, source_target_pairs={{0,4},{2,6},{4,8},{6,10},{8,12},{10,14},{12,0},{14,2},{1,5},{3,7},... | collective-permute-start | bytes 6291464 | tf_op jit(solution)/shard_map/ppermute | solution.py:323
  3.0 1.4 copy.14.exps_ref
  4.4 0.0 collective-permute-done.1.other_ref
  4.5 1.6 copy-done
  6.0 0.8 copy-done.3
  6.8 29.1 %first.1 = (bf16[2048,8192]{1,0:T(8,128)(2,1)}, f32[256,2048]{1,0:T(8,128)S(1)}, bf16[256,2048]{1,0:T(8,128)(2,1)S(1)}) custom-call(s32[1]{0:T(128)} %bitcast.2.core_ref, bf16[128,8192]{1,0:T(8,128)(2,1)S(1)} %copy-done, bf16[128,8192]{1,0:T(8,128)(2,1)S(1)} %collective-permute-done.1.other_ref, f32[1,8192]{1,0:T(1,128)S(1)} %bitcast.11, ...), custom_call_target="tpu_custom_call" | custom-call | flops 1 | bytes 1 | tf_op jit(solution)/shard_map/first/pallas_call | solution.py:59
  35.9 1.4 copy-done.1
  37.3 1.0 copy-done.5
  38.4 13.3 %collective-permute-done.refs_0_ = bf16[128,8192]{1,0:T(8,128)(2,1)} collective-permute-done((bf16[128,8192]{1,0:T(8,128)(2,1)}, bf16[128,8192]{1,0:T(8,128)(2,1)}, u32[]{:S(2)}, u32[]{:S(2)}) %collective-permute-start) | collective-permute-done | bytes 2097184 | tf_op jit(solution)/shard_map/ppermute | solution.py:323
  51.7 0.0 collective-permute-start.3
  51.7 0.0 collective-permute-start.2
  51.7 1.3 collective-permute-start.4
  53.0 3.2 %collective-permute-done.3.refs_1_ = bf16[128,8192]{1,0:T(8,128)(2,1)} collective-permute-done((bf16[128,8192]{1,0:T(8,128)(2,1)}, bf16[128,8192]{1,0:T(8,128)(2,1)}, u32[]{:S(2)}, u32[]{:S(2)}) %collective-permute-start.3) | collective-permute-done | bytes 2097184 | tf_op jit(solution)/shard_map/ppermute | solution.py:327
  56.2 18.7 %multiply.5 = (f32[2,2,128,2048]{3,2,1,0:T(8,128)}, bf16[256,2048]{1,0:T(8,128)(2,1)}) custom-call(s32[1]{0:T(128)} %bitcast.4.mine_ref, s32[1]{0:T(128)} %bitcast.5.spot_ref, s32[1]{0:T(128)} %bitcast.2.core_ref, bf16[128,8192]{1,0:T(8,128)(2,1)} %collective-permute-done.refs_0_, bf16[128,8192]{1,0:T(8,128)(2,1)} %collective-permute-done.3.refs_1_, ...), custom_call_target="tpu_custom_call" | custom-call | flops 1 | bytes 1 | tf_op jit(solution)/shard_map/multiply/pallas_call | solution.py:202
  74.9 3.6 %collective-permute-start.6 = (bf16[256,2048]{1,0:T(8,128)(2,1)}, bf16[256,2048]{1,0:T(8,128)(2,1)S(1)}, u32[]{:S(2)}, u32[]{:S(2)}) collective-permute-start(bf16[256,2048]{1,0:T(8,128)(2,1)} %get-tuple-element.35), channel_id=1, source_target_pairs={{0,1},{2,3},{5,4},{7,6},{9,8},{11,10},{12,13},{14,15},{16,17},{18,... | collective-permute-start | bytes 3145736 | tf_op jit(solution)/shard_map/ppermute | solution.py:336
  78.5 0.9 collective-permute-done.4.refs_1_
  79.4 1.6 copy-done.2
  81.0 2.9 %place.5.refs_2_ = f32[2,2,128,2048]{3,2,1,0:T(8,128)} custom-call(s32[1]{0:T(128)} %bitcast.6.mine_ref, s32[1]{0:T(128)} %bitcast.7.spot_ref, f32[256,2048]{1,0:T(8,128)S(1)} %copy-done.2, bf16[256,2048]{1,0:T(8,128)(2,1)} %collective-permute-done.4.refs_1_, f32[2,2,128,2048]{3,2,1,0:T(8,128)} %get-tuple-element.38.refs_2_), custom_call_target="tpu_custom_call", output_to_operand_aliasing={{}: (4, {})} | custom-call | flops 1 | bytes 1 | tf_op jit(solution)/shard_map/place/pallas_call | solution.py:266
  83.9 17.8 %collective-permute-done.2.whole_ref.refs_0_ = bf16[128,8192]{1,0:T(8,128)(2,1)S(1)} collective-permute-done((bf16[128,8192]{1,0:T(8,128)(2,1)}, bf16[128,8192]{1,0:T(8,128)(2,1)S(1)}, u32[]{:S(2)}, u32[]{:S(2)}) %collective-permute-start.2) | collective-permute-done | bytes 2097184 | tf_op jit(solution)/shard_map/ppermute | solution.py:323
  101.7 1.5 cut.1
  103.2 0.0 collective-permute-done.6.refs_0_
  103.2 0.0 collective-permute-start.7
  103.2 0.0 collective-permute-start.5
  103.3 4.2 %collective-permute-done.7.refs_1_ = bf16[128,8192]{1,0:T(8,128)(2,1)} collective-permute-done((bf16[128,8192]{1,0:T(8,128)(2,1)S(1)}, bf16[128,8192]{1,0:T(8,128)(2,1)}, u32[]{:S(2)}, u32[]{:S(2)}) %collective-permute-start.7) | collective-permute-done | bytes 2097184 | tf_op jit(solution)/shard_map/ppermute | solution.py:327
  107.5 18.3 %multiply.6 = (f32[2,2,128,2048]{3,2,1,0:T(8,128)}, bf16[256,2048]{1,0:T(8,128)(2,1)}) custom-call(s32[1]{0:T(128)} %bitcast.8.mine_ref, s32[1]{0:T(128)} %bitcast.9.spot_ref, s32[1]{0:T(128)} %bitcast.2.core_ref, bf16[128,8192]{1,0:T(8,128)(2,1)S(1)} %collective-permute-done.2.whole_ref.refs_0_, ...), custom_call_target="tpu_custom_call", output_to_operand_aliasing={{0}: (5, {})} | custom-call | flops 1 | bytes 1 | tf_op jit(solution)/shard_map/multiply/pallas_call | solution.py:202
  125.8 0.1 place.6.refs_2_
  125.9 5.0 %collective-permute-done.5.refs_0_ = bf16[64,8192]{1,0:T(8,128)(2,1)} collective-permute-done((bf16[64,8192]{1,0:T(8,128)(2,1)}, bf16[64,8192]{1,0:T(8,128)(2,1)}, u32[]{:S(2)}, u32[]{:S(2)}) %collective-permute-start.5) | collective-permute-done | bytes 1048608 | tf_op jit(solution)/shard_map/ppermute | solution.py:323
  130.9 0.0 collective-permute-start.9
  130.9 0.0 collective-permute-start.8
  130.9 3.5 %collective-permute-start.10 = (bf16[256,2048]{1,0:T(8,128)(2,1)}, bf16[256,2048]{1,0:T(8,128)(2,1)S(1)}, u32[]{:S(2)}, u32[]{:S(2)}) collective-permute-start(bf16[256,2048]{1,0:T(8,128)(2,1)} %get-tuple-element.44), channel_id=1, source_target_pairs={{0,1},{2,3},{4,5},{6,7},{9,8},{11,10},{13,12},{15,14},{16,17},{18,... | collective-permute-start | bytes 3145736 | tf_op jit(solution)/shard_map/ppermute | solution.py:336
  134.5 0.0 collective-permute-done.9.refs_1_
  134.5 15.9 %multiply.7 = (f32[2,2,128,2048]{3,2,1,0:T(8,128)}, bf16[128,2048]{1,0:T(8,128)(2,1)S(1)}) custom-call(s32[1]{0:T(128)} %bitcast.mine_ref, s32[1]{0:T(128)} %bitcast.1.spot_ref, s32[1]{0:T(128)} %bitcast.2.core_ref, bf16[64,8192]{1,0:T(8,128)(2,1)} %collective-permute-done.5.refs_0_, ...), custom_call_target="tpu_custom_call", output_to_operand_aliasing={{0}: (5, {})} | custom-call | flops 1 | bytes 1 | tf_op jit(solution)/shard_map/multiply/pallas_call | solution.py:202
  150.4 8.1 %collective-permute-done.8.refs_0_ = bf16[64,8192]{1,0:T(8,128)(2,1)S(1)} collective-permute-done((bf16[64,8192]{1,0:T(8,128)(2,1)}, bf16[64,8192]{1,0:T(8,128)(2,1)S(1)}, u32[]{:S(2)}, u32[]{:S(2)}) %collective-permute-start.8) | collective-permute-done | bytes 1048608 | tf_op jit(solution)/shard_map/ppermute | solution.py:323
  158.5 0.0 collective-permute-done.10.refs_0_
  158.5 0.0 collective-permute-start.11
  158.5 1.3 collective-permute-start.13
  159.8 1.4 collective-permute-done.11.refs_1_
  161.2 10.9 %multiply.8 = (f32[2,2,128,2048]{3,2,1,0:T(8,128)}, bf16[128,1280]{1,0:T(8,128)(2,1)S(1)}) custom-call(s32[1]{0:T(128)} %bitcast.mine_ref, s32[1]{0:T(128)} %bitcast.1.spot_ref, s32[1]{0:T(128)} %bitcast.2.core_ref, bf16[64,8192]{1,0:T(8,128)(2,1)S(1)} %collective-permute-done.8.refs_0_, ...), custom_call_target="tpu_custom_call", output_to_operand_aliasing={{0}: (5, {})} | custom-call | flops 1 | bytes 1 | tf_op jit(solution)/shard_map/multiply/pallas_call | solution.py:202
  172.1 1.3 collective-permute-start.12
  173.4 1.3 collective-permute-done.13.refs_0_
  174.7 7.8 %multiply.9 = (f32[2,2,128,2048]{3,2,1,0:T(8,128)}, bf16[128,768]{1,0:T(8,128)(2,1)S(1)}) custom-call(s32[1]{0:T(128)} %bitcast.mine_ref, s32[1]{0:T(128)} %bitcast.1.spot_ref, s32[1]{0:T(128)} %bitcast.2.core_ref, bf16[64,8192]{1,0:T(8,128)(2,1)S(1)} %collective-permute-done.8.refs_0_, ...), custom_call_target="tpu_custom_call", output_to_operand_aliasing={{0}: (5, {})} | custom-call | flops 1 | bytes 1 | tf_op jit(solution)/shard_map/multiply/pallas_call | solution.py:202
  182.5 1.3 collective-permute-start.14
  183.8 0.1 place.7.refs_1_
  183.9 2.3 %place.8.refs_2_ = f32[2,2,128,2048]{3,2,1,0:T(8,128)} custom-call(s32[1]{0:T(128)} %bitcast.mine_ref, s32[1]{0:T(128)} %bitcast.1.spot_ref, bf16[128,2048]{1,0:T(8,128)(2,1)S(1)} %collective-permute-done.13.refs_0_, f32[2,2,128,2048]{3,2,1,0:T(8,128)} %place.7.refs_1_), custom_call_target="tpu_custom_call", output_to_operand_aliasing={{}: (3, {})} | custom-call | flops 1 | bytes 1 | tf_op jit(solution)/shard_map/place/pallas_call | solution.py:266
  186.2 4.8 %collective-permute-done.14.refs_1_ = bf16[128,768]{1,0:T(8,128)(2,1)S(1)} collective-permute-done((bf16[128,768]{1,0:T(8,128)(2,1)S(1)}, bf16[128,768]{1,0:T(8,128)(2,1)S(1)}, u32[]{:S(2)}, u32[]{:S(2)}) %collective-permute-start.14) | collective-permute-done | bytes 196640 | tf_op jit(solution)/shard_map/ppermute | solution.py:336
  191.0 0.0 collective-permute-done.12.refs_0_
  191.0 2.3 %place.9 = f32[2,2,128,2048]{3,2,1,0:T(8,128)} custom-call(s32[1]{0:T(128)} %bitcast.mine_ref, s32[1]{0:T(128)} %bitcast.1.spot_ref, bf16[128,1280]{1,0:T(8,128)(2,1)S(1)} %collective-permute-done.12.refs_0_, bf16[128,768]{1,0:T(8,128)(2,1)S(1)} %collective-permute-done.14.refs_1_, f32[2,2,128,2048]{3,2,1,0:T(8,128)} %place.8.refs_2_), custom_call_target="tpu_custom_call", output_to_operand_aliasing={{}: (4, {})} | custom-call | flops 1 | bytes 1 | tf_op jit(solution)/shard_map/place/pallas_call | solution.py:266
  (7 shorter events, 0.0 us)
Async XLA Ops:
  0.0 4.5 %collective-permute-start.1 = (bf16[128,8192]{1,0:T(8,128)(2,1)}, bf16[128,8192]{1,0:T(8,128)(2,1)S(1)}, u32[]{:S(2)}, u32[]{:S(2)}) collective-permute-start(bf16[128,8192]{1,0:T(8,128)(2,1)} %mine_ref.1), channel_id=1, source_target_pairs={{0,2},{2,0},{4,6},{6,4},{8,10},{10,8},{12,14},{14,12},{1,3},{3,1},... | collective-permute-start | bytes 6291464 | tf_op jit(solution)/shard_map/ppermute | solution.py:327
  0.5 51.2 %collective-permute-start = (bf16[128,8192]{1,0:T(8,128)(2,1)}, bf16[128,8192]{1,0:T(8,128)(2,1)}, u32[]{:S(2)}, u32[]{:S(2)}) collective-permute-start(bf16[128,8192]{1,0:T(8,128)(2,1)} %mine_ref.1), channel_id=1, source_target_pairs={{0,4},{2,6},{4,8},{6,10},{8,12},{10,14},{12,0},{14,2},{1,5},{3,7},... | collective-permute-start | bytes 6291464 | tf_op jit(solution)/shard_map/ppermute | solution.py:323
  4.5 1.6 copy-start
  6.0 0.8 copy-start.3
  6.8 49.4 %copy-start.4 = (f32[8192]{0:T(1024)S(1)}, f32[8192]{0:T(1024)}, u32[]{:S(2)}) copy-start(f32[8192]{0:T(1024)} %param.7) | copy-start | bytes 98308
  35.9 1.4 copy-start.1
  37.3 1.0 copy-start.5
  51.7 4.5 %collective-permute-start.3 = (bf16[128,8192]{1,0:T(8,128)(2,1)}, bf16[128,8192]{1,0:T(8,128)(2,1)}, u32[]{:S(2)}, u32[]{:S(2)}) collective-permute-start(bf16[128,8192]{1,0:T(8,128)(2,1)} %collective-permute-done.refs_0_), channel_id=1, source_target_pairs={{0,2},{2,0},{4,6},{6,4},{8,10},{10,8},{12,14},{14,12},{1,3},{3,1},... | collective-permute-start | bytes 6291464 | tf_op jit(solution)/shard_map/ppermute | solution.py:327
  51.7 50.1 %collective-permute-start.2 = (bf16[128,8192]{1,0:T(8,128)(2,1)}, bf16[128,8192]{1,0:T(8,128)(2,1)S(1)}, u32[]{:S(2)}, u32[]{:S(2)}) collective-permute-start(bf16[128,8192]{1,0:T(8,128)(2,1)} %collective-permute-done.refs_0_), channel_id=1, source_target_pairs={{0,4},{2,6},{4,8},{6,10},{8,12},{10,14},{12,0},{14,2},{1,5},{3,7},... | collective-permute-start | bytes 6291464 | tf_op jit(solution)/shard_map/ppermute | solution.py:323
  51.7 27.8 %collective-permute-start.4 = (bf16[256,2048]{1,0:T(8,128)(2,1)}, bf16[256,2048]{1,0:T(8,128)(2,1)}, u32[]{:S(2)}, u32[]{:S(2)}) collective-permute-start(bf16[256,2048]{1,0:T(8,128)(2,1)} %copy-done.5), channel_id=1, source_target_pairs={{1,0},{3,2},{5,4},{7,6},{8,9},{10,11},{12,13},{14,15},{17,16},{19,... | collective-permute-start | bytes 3145736 | tf_op jit(solution)/shard_map/ppermute | solution.py:336
  74.9 28.3 %collective-permute-start.6 = (bf16[256,2048]{1,0:T(8,128)(2,1)}, bf16[256,2048]{1,0:T(8,128)(2,1)S(1)}, u32[]{:S(2)}, u32[]{:S(2)}) collective-permute-start(bf16[256,2048]{1,0:T(8,128)(2,1)} %get-tuple-element.35), channel_id=1, source_target_pairs={{0,1},{2,3},{5,4},{7,6},{9,8},{11,10},{12,13},{14,15},{16,17},{18,... | collective-permute-start | bytes 3145736 | tf_op jit(solution)/shard_map/ppermute | solution.py:336
  79.4 1.6 copy-start.2
  103.2 4.3 %collective-permute-start.7 = (bf16[128,8192]{1,0:T(8,128)(2,1)S(1)}, bf16[128,8192]{1,0:T(8,128)(2,1)}, u32[]{:S(2)}, u32[]{:S(2)}) collective-permute-start(bf16[128,8192]{1,0:T(8,128)(2,1)S(1)} %collective-permute-done.2.whole_ref.refs_0_), channel_id=1, source_target_pairs={{0,2},{2,0},{4,6},{6,4},{8,10},{10,8},{12,14},{14,12},{1,3},{3,1},... | collective-permute-start | bytes 6291464 | tf_op jit(solution)/shard_map/ppermute | solution.py:327
  103.2 27.7 %collective-permute-start.5 = (bf16[64,8192]{1,0:T(8,128)(2,1)}, bf16[64,8192]{1,0:T(8,128)(2,1)}, u32[]{:S(2)}, u32[]{:S(2)}) collective-permute-start(bf16[64,8192]{1,0:T(8,128)(2,1)} %get-tuple-element.41), channel_id=1, source_target_pairs={{0,4},{2,6},{4,8},{6,10},{8,12},{10,14},{12,0},{14,2},{1,5},{3,7},... | collective-permute-start | bytes 3145736 | tf_op jit(solution)/shard_map/ppermute | solution.py:323
  130.9 3.5 %collective-permute-start.9 = (bf16[64,8192]{1,0:T(8,128)(2,1)}, bf16[64,8192]{1,0:T(8,128)(2,1)S(1)}, u32[]{:S(2)}, u32[]{:S(2)}) collective-permute-start(bf16[64,8192]{1,0:T(8,128)(2,1)} %collective-permute-done.5.refs_0_), channel_id=1, source_target_pairs={{0,2},{2,0},{4,6},{6,4},{8,10},{10,8},{12,14},{14,12},{1,3},{3,1},... | collective-permute-start | bytes 3145736 | tf_op jit(solution)/shard_map/ppermute | solution.py:327
  130.9 27.6 %collective-permute-start.8 = (bf16[64,8192]{1,0:T(8,128)(2,1)}, bf16[64,8192]{1,0:T(8,128)(2,1)S(1)}, u32[]{:S(2)}, u32[]{:S(2)}) collective-permute-start(bf16[64,8192]{1,0:T(8,128)(2,1)} %get-tuple-element.48), channel_id=1, source_target_pairs={{0,4},{2,6},{4,8},{6,10},{8,12},{10,14},{12,0},{14,2},{1,5},{3,7},... | collective-permute-start | bytes 3145736 | tf_op jit(solution)/shard_map/ppermute | solution.py:323
  130.9 27.6 %collective-permute-start.10 = (bf16[256,2048]{1,0:T(8,128)(2,1)}, bf16[256,2048]{1,0:T(8,128)(2,1)S(1)}, u32[]{:S(2)}, u32[]{:S(2)}) collective-permute-start(bf16[256,2048]{1,0:T(8,128)(2,1)} %get-tuple-element.44), channel_id=1, source_target_pairs={{0,1},{2,3},{4,5},{6,7},{9,8},{11,10},{13,12},{15,14},{16,17},{18,... | collective-permute-start | bytes 3145736 | tf_op jit(solution)/shard_map/ppermute | solution.py:336
  158.5 2.7 %collective-permute-start.11 = (bf16[64,8192]{1,0:T(8,128)(2,1)S(1)}, bf16[64,8192]{1,0:T(8,128)(2,1)S(1)}, u32[]{:S(2)}, u32[]{:S(2)}) collective-permute-start(bf16[64,8192]{1,0:T(8,128)(2,1)S(1)} %collective-permute-done.8.refs_0_), channel_id=1, source_target_pairs={{0,2},{2,0},{4,6},{6,4},{8,10},{10,8},{12,14},{14,12},{1,3},{3,1},... | collective-permute-start | bytes 3145736 | tf_op jit(solution)/shard_map/ppermute | solution.py:327
  158.5 16.2 %collective-permute-start.13 = (bf16[128,2048]{1,0:T(8,128)(2,1)S(1)}, bf16[128,2048]{1,0:T(8,128)(2,1)S(1)}, u32[]{:S(2)}, u32[]{:S(2)}) collective-permute-start(bf16[128,2048]{1,0:T(8,128)(2,1)S(1)} %get-tuple-element.49), channel_id=1, source_target_pairs={{1,0},{3,2},{4,5},{6,7},{8,9},{10,11},{13,12},{15,14},{17,16},{19,... | collective-permute-start | bytes 1572872 | tf_op jit(solution)/shard_map/ppermute | solution.py:336
  172.1 18.8 %collective-permute-start.12 = (bf16[128,1280]{1,0:T(8,128)(2,1)S(1)}, bf16[128,1280]{1,0:T(8,128)(2,1)S(1)}, u32[]{:S(2)}, u32[]{:S(2)}) collective-permute-start(bf16[128,1280]{1,0:T(8,128)(2,1)S(1)} %get-tuple-element.52), channel_id=1, source_target_pairs={{1,0},{3,2},{4,5},{6,7},{8,9},{10,11},{13,12},{15,14},{17,16},{19,... | collective-permute-start | bytes 983048 | tf_op jit(solution)/shard_map/ppermute | solution.py:336
  182.5 8.4 %collective-permute-start.14 = (bf16[128,768]{1,0:T(8,128)(2,1)S(1)}, bf16[128,768]{1,0:T(8,128)(2,1)S(1)}, u32[]{:S(2)}, u32[]{:S(2)}) collective-permute-start(bf16[128,768]{1,0:T(8,128)(2,1)S(1)} %get-tuple-element.55), channel_id=1, source_target_pairs={{1,0},{3,2},{4,5},{6,7},{8,9},{10,11},{13,12},{15,14},{17,16},{19,... | collective-permute-start | bytes 589832 | tf_op jit(solution)/shard_map/ppermute | solution.py:336

commit v14 on v13

--- a/solution.py
+++ b/solution.py
@@ -91,7 +91,7 @@
     refs = list(refs)
     mine_refs, other_refs, _ = [[refs.pop(0) for _ in range(size)] for size in counts]
     fisher_ref, train_ref, scores_ref, send_ref = refs[:4]
-    left, held, keep, send, in_sems, train_sems, keep_sems, send_sems = refs[4:]
+    left, held, keep, send, train_sems, keep_sems, send_sems = refs[4:]
     rows = sum(ref.shape[0] for ref in mine_refs)
     slots, tile, width = held.shape
     tiles = keep_sems.shape[0]
@@ -110,26 +110,20 @@
             for part in range(2)
         ]
 
-    loads = []
-    for group, place in ((mine_refs, core), (other_refs, 1 - core)):
-        offset = 0
-        for ref in group:
-            spot = pl.ds(pl.multiple_of(place * rows, rows) + offset, ref.shape[0])
-            loads.append(pltpu.make_async_copy(ref, left.at[spot], in_sems.at[len(loads)]))
-            offset += ref.shape[0]
-    for load in loads:
-        load.start()
     for i in range(min(slots, tiles)):
         for fetch in fetches(i):
             fetch.start()
-    for load in loads:
-        load.wait()
 
     @pl.loop(0, width // depth)
     def _(k):
         cols = pl.ds(pl.multiple_of(k * depth, depth), depth)
         scale = 1.0 / (fisher_ref[:, cols] + damping)
-        left[:, cols] = (left[:, cols].astype(jnp.float32) * scale).astype(jnp.bfloat16)
+        for group, place in ((mine_refs, core), (other_refs, 1 - core)):
+            offset = 0
+            for ref in group:
+                spot = pl.ds(pl.multiple_of(place * rows, rows) + offset, ref.shape[0])
+                left[spot, cols] = (ref[:, cols].astype(jnp.float32) * scale).astype(jnp.bfloat16)
+                offset += ref.shape[0]
 
     def stores(i, of_mine):
         slot = lax.rem(i, 2)
@@ -195,13 +189,13 @@
     top, bottom = span or (0, train.shape[0])
     count = bottom - top
     tile = min(count, 256)
-    slots = 4
+    slots = 3
     block = (cores * rows, count)
     given = [] if scores is None else [scores]
     counts = (len(mine), len(other), len(given))
     return pl.pallas_call(
         functools.partial(multiply_kernel, counts, start, top),
-        in_specs=[in_smem] * 3 + [anywhere] * sum(counts) + [in_vmem, anywhere],
+        in_specs=[in_smem] * 3 + [in_vmem] * sum(counts[:2]) + [anywhere] * len(given) + [in_vmem, anywhere],
         out_specs=[anywhere] * 2,
         out_shape=[
             jax.ShapeDtypeStruct(shape, jnp.float32), jax.ShapeDtypeStruct(block, jnp.bfloat16),
@@ -211,7 +205,6 @@
             pltpu.VMEM((slots, tile, width), jnp.bfloat16),
             pltpu.VMEM((2, cores * rows, tile), jnp.float32),
             pltpu.VMEM((2, cores * rows, tile), jnp.bfloat16),
-            pltpu.SemaphoreType.DMA((len(mine) + len(other),)),
             pltpu.SemaphoreType.DMA((slots, 2)),
             pltpu.SemaphoreType.DMA((count // tile, cores)),
             pltpu.SemaphoreType.DMA((count // tile,)),
@@ -363,13 +356,13 @@
         scores = place(scores, whose(hop - 1), kept, received, [0] * len(received), 0)
         kept = []
     earlier = exchange(send, hops - 1)
+    high_flow = shift(after(high_piece, send))
     low_piece = after(flow, send, scores)
-    flow = shift(after(high_piece, low_piece))
     scores, send = multiply(
-        scores, shape, whose(hops), core, [low_piece], swap([low_piece]), fisher, train, 0
+        scores, shape, whose(hops), core, [low_piece], swap(cut(low_piece, 2)), fisher, train, 0
     )
     received = exchange(send, hops)
-    high_piece = after(flow, send, *earlier)
+    high_piece = after(high_flow, send, *earlier)
     high_other = swap([high_piece])
     knee = count * 5 // 8
     halves = []

time: 194 us -> 189 us (0.974)
  Pallas kernels: 110 us -> 106 us
  waiting for transfers between devices: 60.1 us -> 58.1 us
    ppermute x4, waiting for transfers between devices: 44.3 us -> 36.9 us  [shift(): return lax.ppermute(panel, 'blk', pairs)]
    pallas_call x5, Pallas kernels: 71.7 us -> 66.6 us  [multiply(): pl.pallas_call(functools.partial(multiply_kernel, counts, start, top), in...]
    ppermute x6, waiting for transfers between devices: 6.96 us -> 9.85 us  [exchange(): received.append(lax.ppermute(send, ('blk', 'dim'), pairs))]
    ppermute x5 -> x6, waiting for transfers between devices: 8.85 us -> 11.4 us  [swap(): return [lax.ppermute(part, 'blk', pairs) for part in parts]]
    unnamed x13 -> x17, local copies, waits for them, and re-layouts: 7.73 us -> 8.71 us
  transfers between devices with their start and end apart: 15 -> 16, of which waited for: 10 -> 12; matrix products, arithmetic and copies ran while one was open for 1% -> 1% of each run, Pallas kernels for 56% -> 55%
where the time goes in v14:
time: 189 us
  Pallas kernels  106 us (56%)
  waiting for transfers between devices  58.1 us (31%)
  starting transfers between devices  16 us (8%)
  local copies, waits for them, and re-layouts  8.71 us (5%)
    pallas_call x5, Pallas kernels, multiply(): pl.pallas_call(functools.partial(multiply_kernel, counts, start, top), in...  66.6 us
    ppermute x4, waiting for transfers between devices, shift(): return lax.ppermute(panel, 'blk', pairs)  36.9 us
    pallas_call x1, Pallas kernels, first(): pl.pallas_call(first_kernel, grid=(count // tile,), in_specs=[in_smem, pl...  29.1 us
    ppermute x6, starting transfers between devices, exchange(): received.append(lax.ppermute(send, ('blk', 'dim'), pairs))  12.4 us
    ppermute x6, waiting for transfers between devices, swap(): return [lax.ppermute(part, 'blk', pairs) for part in parts]  11.4 us
    ppermute x6, waiting for transfers between devices, exchange(): received.append(lax.ppermute(send, ('blk', 'dim'), pairs))  9.85 us
    unnamed x17, local copies, waits for them, and re-layouts  8.71 us
    pallas_call x5, Pallas kernels, place(): pl.pallas_call(functools.partial(place_kernel, start, cols, len(kept)), i...  7.61 us
  transfers between devices with their start and end apart: 16, of which 12 were waited for; matrix products, arithmetic and copies ran while one was open for 1% of the time, Pallas kernels for 55%

profile of v14, /device:TPU:0, one launch (start us, length us, event | category | flops | bytes accessed | tf_op | source)
XLA Modules:
  0.0 188.8 jit_solution(14234699404834826561)
XLA Ops:
  0.0 0.5 collective-permute-start.1
  0.5 2.6 %collective-permute-start = (bf16[128,8192]{1,0:T(8,128)(2,1)}, bf16[128,8192]{1,0:T(8,128)(2,1)}, u32[]{:S(2)}, u32[]{:S(2)}) collective-permute-start(bf16[128,8192]{1,0:T(8,128)(2,1)} %mine_ref.1), channel_id=1, source_target_pairs={{0,4},{2,6},{4,8},{6,10},{8,12},{10,14},{12,0},{14,2},{1,5},{3,7},... | collective-permute-start | bytes 6291464 | tf_op jit(solution)/shard_map/ppermute | solution.py:316
  3.0 1.4 copy.14.exps_ref
  4.4 0.0 collective-permute-done.1.other_ref
  4.5 1.6 copy-done
  6.0 0.8 copy-done.3
  6.8 29.1 %first.1 = (bf16[2048,8192]{1,0:T(8,128)(2,1)}, f32[256,2048]{1,0:T(8,128)S(1)}, bf16[256,2048]{1,0:T(8,128)(2,1)S(1)}) custom-call(s32[1]{0:T(128)} %bitcast.2.core_ref, bf16[128,8192]{1,0:T(8,128)(2,1)S(1)} %copy-done, bf16[128,8192]{1,0:T(8,128)(2,1)S(1)} %collective-permute-done.1.other_ref, f32[1,8192]{1,0:T(1,128)S(1)} %bitcast.11, ...), custom_call_target="tpu_custom_call" | custom-call | flops 1 | bytes 1 | tf_op jit(solution)/shard_map/first/pallas_call | solution.py:59
  35.9 1.4 copy-done.1
  37.3 1.1 copy-done.7
  38.4 13.3 %collective-permute-done.refs_0_ = bf16[128,8192]{1,0:T(8,128)(2,1)} collective-permute-done((bf16[128,8192]{1,0:T(8,128)(2,1)}, bf16[128,8192]{1,0:T(8,128)(2,1)}, u32[]{:S(2)}, u32[]{:S(2)}) %collective-permute-start) | collective-permute-done | bytes 2097184 | tf_op jit(solution)/shard_map/ppermute | solution.py:316
  51.7 0.0 collective-permute-start.3
  51.7 0.0 collective-permute-start.2
  51.7 1.3 collective-permute-start.4
  53.0 3.2 %collective-permute-done.3.refs_1_ = bf16[128,8192]{1,0:T(8,128)(2,1)} collective-permute-done((bf16[128,8192]{1,0:T(8,128)(2,1)}, bf16[128,8192]{1,0:T(8,128)(2,1)}, u32[]{:S(2)}, u32[]{:S(2)}) %collective-permute-start.3) | collective-permute-done | bytes 2097184 | tf_op jit(solution)/shard_map/ppermute | solution.py:320
  56.2 16.0 %multiply.5 = (f32[2,2,128,2048]{3,2,1,0:T(8,128)}, bf16[256,2048]{1,0:T(8,128)(2,1)}) custom-call(s32[1]{0:T(128)} %bitcast.4.mine_ref, s32[1]{0:T(128)} %bitcast.5.spot_ref, s32[1]{0:T(128)} %bitcast.2.core_ref, bf16[128,8192]{1,0:T(8,128)(2,1)} %collective-permute-done.refs_0_, bf16[128,8192]{1,0:T(8,128)(2,1)} %collective-permute-done.3.refs_1_, ...), custom_call_target="tpu_custom_call" | custom-call | flops 1 | bytes 1 | tf_op jit(solution)/shard_map/multiply/pallas_call | solution.py:196
  72.2 3.6 %collective-permute-start.5 = (bf16[256,2048]{1,0:T(8,128)(2,1)}, bf16[256,2048]{1,0:T(8,128)(2,1)S(1)}, u32[]{:S(2)}, u32[]{:S(2)}) collective-permute-start(bf16[256,2048]{1,0:T(8,128)(2,1)} %get-tuple-element.37), channel_id=1, source_target_pairs={{0,1},{2,3},{5,4},{7,6},{9,8},{11,10},{12,13},{14,15},{16,17},{18,... | collective-permute-start | bytes 3145736 | tf_op jit(solution)/shard_map/ppermute | solution.py:329
  75.8 3.6 %collective-permute-done.4.refs_1_ = bf16[256,2048]{1,0:T(8,128)(2,1)} collective-permute-done((bf16[256,2048]{1,0:T(8,128)(2,1)}, bf16[256,2048]{1,0:T(8,128)(2,1)}, u32[]{:S(2)}, u32[]{:S(2)}) %collective-permute-start.4) | collective-permute-done | bytes 1048608 | tf_op jit(solution)/shard_map/ppermute | solution.py:329
  79.4 1.6 copy-done.2
  81.0 2.9 %place.5.refs_2_ = f32[2,2,128,2048]{3,2,1,0:T(8,128)} custom-call(s32[1]{0:T(128)} %bitcast.6.mine_ref, s32[1]{0:T(128)} %bitcast.7.spot_ref, f32[256,2048]{1,0:T(8,128)S(1)} %copy-done.2, bf16[256,2048]{1,0:T(8,128)(2,1)} %collective-permute-done.4.refs_1_, f32[2,2,128,2048]{3,2,1,0:T(8,128)} %get-tuple-element.40.refs_2_), custom_call_target="tpu_custom_call", output_to_operand_aliasing={{}: (4, {})} | custom-call | flops 1 | bytes 1 | tf_op jit(solution)/shard_map/place/pallas_call | solution.py:259
  83.9 17.8 %collective-permute-done.2.whole_ref.refs_0_ = bf16[128,8192]{1,0:T(8,128)(2,1)S(1)} collective-permute-done((bf16[128,8192]{1,0:T(8,128)(2,1)}, bf16[128,8192]{1,0:T(8,128)(2,1)S(1)}, u32[]{:S(2)}, u32[]{:S(2)}) %collective-permute-start.2) | collective-permute-done | bytes 2097184 | tf_op jit(solution)/shard_map/ppermute | solution.py:316
  101.7 1.4 cut.2
  103.2 0.0 collective-permute-done.5.refs_0_
  103.2 1.0 copy-done.5
  104.2 4.3 %collective-permute-done.6.refs_1_ = bf16[128,8192]{1,0:T(8,128)(2,1)} collective-permute-done((bf16[128,8192]{1,0:T(8,128)(2,1)S(1)}, bf16[128,8192]{1,0:T(8,128)(2,1)}, u32[]{:S(2)}, u32[]{:S(2)}) %collective-permute-start.6) | collective-permute-done | bytes 2097184 | tf_op jit(solution)/shard_map/ppermute | solution.py:320
  108.4 15.5 %multiply.6 = (f32[2,2,128,2048]{3,2,1,0:T(8,128)}, bf16[256,2048]{1,0:T(8,128)(2,1)}) custom-call(s32[1]{0:T(128)} %bitcast.8.mine_ref, s32[1]{0:T(128)} %bitcast.9.spot_ref, s32[1]{0:T(128)} %bitcast.2.core_ref, bf16[128,8192]{1,0:T(8,128)(2,1)S(1)} %collective-permute-done.2.whole_ref.refs_0_, ...), custom_call_target="tpu_custom_call", output_to_operand_aliasing={{0}: (5, {})} | custom-call | flops 1 | bytes 1 | tf_op jit(solution)/shard_map/multiply/pallas_call | solution.py:196
  123.9 0.1 collective-permute-start.7
  124.0 3.6 %collective-permute-start.11 = (bf16[256,2048]{1,0:T(8,128)(2,1)}, bf16[256,2048]{1,0:T(8,128)(2,1)S(1)}, u32[]{:S(2)}, u32[]{:S(2)}) collective-permute-start(bf16[256,2048]{1,0:T(8,128)(2,1)} %get-tuple-element.46), channel_id=1, source_target_pairs={{0,1},{2,3},{4,5},{6,7},{9,8},{11,10},{13,12},{15,14},{16,17},{18,... | collective-permute-start | bytes 3145736 | tf_op jit(solution)/shard_map/ppermute | solution.py:329
  127.6 0.1 place.6.refs_3_
  127.6 4.5 %collective-permute-done.8.whole_ref.refs_0_ = bf16[64,8192]{1,0:T(8,128)(2,1)S(1)} collective-permute-done((bf16[64,8192]{1,0:T(8,128)(2,1)}, bf16[64,8192]{1,0:T(8,128)(2,1)S(1)}, u32[]{:S(2)}, u32[]{:S(2)}) %collective-permute-start.8) | collective-permute-done | bytes 1048608 | tf_op jit(solution)/shard_map/ppermute | solution.py:316
  132.1 1.0 cut.3
  133.2 0.0 collective-permute-start.9
  133.2 0.5 collective-permute-start.10
  133.7 1.7 collective-permute-done.9.refs_1_
  135.4 0.7 collective-permute-done.10.refs_2_
  136.2 16.7 %multiply.7 = (f32[2,2,128,2048]{3,2,1,0:T(8,128)}, bf16[128,2048]{1,0:T(8,128)(2,1)S(1)}) custom-call(s32[1]{0:T(128)} %bitcast.mine_ref, s32[1]{0:T(128)} %bitcast.1.spot_ref, s32[1]{0:T(128)} %bitcast.2.core_ref, bf16[64,8192]{1,0:T(8,128)(2,1)S(1)} %collective-permute-done.8.whole_ref.refs_0_, ...), custom_call_target="tpu_custom_call", output_to_operand_aliasing={{0}: (6, {})} | custom-call | flops 1 | bytes 1 | tf_op jit(solution)/shard_map/multiply/pallas_call | solution.py:196
  152.9 1.3 collective-permute-done.7.refs_0_
  154.2 0.0 collective-permute-done.11.refs_0_
  154.2 1.3 collective-permute-start.14
  155.5 1.4 collective-permute-done.12.refs_1_
  156.9 10.8 %multiply.8 = (f32[2,2,128,2048]{3,2,1,0:T(8,128)}, bf16[128,1280]{1,0:T(8,128)(2,1)S(1)}) custom-call(s32[1]{0:T(128)} %bitcast.mine_ref, s32[1]{0:T(128)} %bitcast.1.spot_ref, s32[1]{0:T(128)} %bitcast.2.core_ref, bf16[64,8192]{1,0:T(8,128)(2,1)S(1)} %collective-permute-done.7.refs_0_, ...), custom_call_target="tpu_custom_call", output_to_operand_aliasing={{0}: (5, {})} | custom-call | flops 1 | bytes 1 | tf_op jit(solution)/shard_map/multiply/pallas_call | solution.py:196
  167.7 1.3 collective-permute-start.13
  169.0 1.5 collective-permute-done.14.refs_0_
  170.4 7.6 %multiply.9 = (f32[2,2,128,2048]{3,2,1,0:T(8,128)}, bf16[128,768]{1,0:T(8,128)(2,1)S(1)}) custom-call(s32[1]{0:T(128)} %bitcast.mine_ref, s32[1]{0:T(128)} %bitcast.1.spot_ref, s32[1]{0:T(128)} %bitcast.2.core_ref, bf16[64,8192]{1,0:T(8,128)(2,1)S(1)} %collective-permute-done.7.refs_0_, ...), custom_call_target="tpu_custom_call", output_to_operand_aliasing={{0}: (5, {})} | custom-call | flops 1 | bytes 1 | tf_op jit(solution)/shard_map/multiply/pallas_call | solution.py:196
  178.1 1.3 collective-permute-start.15
  179.4 0.1 place.7.refs_1_
  179.4 2.3 %place.8.refs_2_ = f32[2,2,128,2048]{3,2,1,0:T(8,128)} custom-call(s32[1]{0:T(128)} %bitcast.mine_ref, s32[1]{0:T(128)} %bitcast.1.spot_ref, bf16[128,2048]{1,0:T(8,128)(2,1)S(1)} %collective-permute-done.14.refs_0_, f32[2,2,128,2048]{3,2,1,0:T(8,128)} %place.7.refs_1_), custom_call_target="tpu_custom_call", output_to_operand_aliasing={{}: (3, {})} | custom-call | flops 1 | bytes 1 | tf_op jit(solution)/shard_map/place/pallas_call | solution.py:259
  181.7 4.8 %collective-permute-done.15.refs_1_ = bf16[128,768]{1,0:T(8,128)(2,1)S(1)} collective-permute-done((bf16[128,768]{1,0:T(8,128)(2,1)S(1)}, bf16[128,768]{1,0:T(8,128)(2,1)S(1)}, u32[]{:S(2)}, u32[]{:S(2)}) %collective-permute-start.15) | collective-permute-done | bytes 196640 | tf_op jit(solution)/shard_map/ppermute | solution.py:329
  186.5 2.3 %place.9 = f32[2,2,128,2048]{3,2,1,0:T(8,128)} custom-call(s32[1]{0:T(128)} %bitcast.mine_ref, s32[1]{0:T(128)} %bitcast.1.spot_ref, bf16[128,1280]{1,0:T(8,128)(2,1)S(1)} %collective-permute-done.13.refs_0_, bf16[128,768]{1,0:T(8,128)(2,1)S(1)} %collective-permute-done.15.refs_1_, f32[2,2,128,2048]{3,2,1,0:T(8,128)} %place.8.refs_2_), custom_call_target="tpu_custom_call", output_to_operand_aliasing={{}: (4, {})} | custom-call | flops 1 | bytes 1 | tf_op jit(solution)/shard_map/place/pallas_call | solution.py:259
  (14 shorter events, 0.0 us)
Async XLA Ops:
  0.0 4.5 %collective-permute-start.1 = (bf16[128,8192]{1,0:T(8,128)(2,1)}, bf16[128,8192]{1,0:T(8,128)(2,1)S(1)}, u32[]{:S(2)}, u32[]{:S(2)}) collective-permute-start(bf16[128,8192]{1,0:T(8,128)(2,1)} %mine_ref.1), channel_id=1, source_target_pairs={{0,2},{2,0},{4,6},{6,4},{8,10},{10,8},{12,14},{14,12},{1,3},{3,1},... | collective-permute-start | bytes 6291464 | tf_op jit(solution)/shard_map/ppermute | solution.py:320
  0.5 51.2 %collective-permute-start = (bf16[128,8192]{1,0:T(8,128)(2,1)}, bf16[128,8192]{1,0:T(8,128)(2,1)}, u32[]{:S(2)}, u32[]{:S(2)}) collective-permute-start(bf16[128,8192]{1,0:T(8,128)(2,1)} %mine_ref.1), channel_id=1, source_target_pairs={{0,4},{2,6},{4,8},{6,10},{8,12},{10,14},{12,0},{14,2},{1,5},{3,7},... | collective-permute-start | bytes 6291464 | tf_op jit(solution)/shard_map/ppermute | solution.py:316
  4.5 1.6 copy-start
  6.0 0.8 copy-start.3
  6.8 49.4 %copy-start.4 = (f32[8192]{0:T(1024)S(1)}, f32[8192]{0:T(1024)}, u32[]{:S(2)}) copy-start(f32[8192]{0:T(1024)} %param.7) | copy-start | bytes 98308
  35.9 1.4 copy-start.1
  37.3 1.1 copy-start.7
  51.7 4.5 %collective-permute-start.3 = (bf16[128,8192]{1,0:T(8,128)(2,1)}, bf16[128,8192]{1,0:T(8,128)(2,1)}, u32[]{:S(2)}, u32[]{:S(2)}) collective-permute-start(bf16[128,8192]{1,0:T(8,128)(2,1)} %collective-permute-done.refs_0_), channel_id=1, source_target_pairs={{0,2},{2,0},{4,6},{6,4},{8,10},{10,8},{12,14},{14,12},{1,3},{3,1},... | collective-permute-start | bytes 6291464 | tf_op jit(solution)/shard_map/ppermute | solution.py:320
  51.7 50.1 %collective-permute-start.2 = (bf16[128,8192]{1,0:T(8,128)(2,1)}, bf16[128,8192]{1,0:T(8,128)(2,1)S(1)}, u32[]{:S(2)}, u32[]{:S(2)}) collective-permute-start(bf16[128,8192]{1,0:T(8,128)(2,1)} %collective-permute-done.refs_0_), channel_id=1, source_target_pairs={{0,4},{2,6},{4,8},{6,10},{8,12},{10,14},{12,0},{14,2},{1,5},{3,7},... | collective-permute-start | bytes 6291464 | tf_op jit(solution)/shard_map/ppermute | solution.py:316
  51.7 27.8 %collective-permute-start.4 = (bf16[256,2048]{1,0:T(8,128)(2,1)}, bf16[256,2048]{1,0:T(8,128)(2,1)}, u32[]{:S(2)}, u32[]{:S(2)}) collective-permute-start(bf16[256,2048]{1,0:T(8,128)(2,1)} %copy-done.7), channel_id=1, source_target_pairs={{1,0},{3,2},{5,4},{7,6},{8,9},{10,11},{12,13},{14,15},{17,16},{19,... | collective-permute-start | bytes 3145736 | tf_op jit(solution)/shard_map/ppermute | solution.py:329
  72.2 31.0 %collective-permute-start.5 = (bf16[256,2048]{1,0:T(8,128)(2,1)}, bf16[256,2048]{1,0:T(8,128)(2,1)S(1)}, u32[]{:S(2)}, u32[]{:S(2)}) collective-permute-start(bf16[256,2048]{1,0:T(8,128)(2,1)} %get-tuple-element.37), channel_id=1, source_target_pairs={{0,1},{2,3},{5,4},{7,6},{9,8},{11,10},{12,13},{14,15},{16,17},{18,... | collective-permute-start | bytes 3145736 | tf_op jit(solution)/shard_map/ppermute | solution.py:329
  79.4 1.6 copy-start.2
  103.2 1.0 copy-start.5
  104.1 4.3 %collective-permute-start.6 = (bf16[128,8192]{1,0:T(8,128)(2,1)S(1)}, bf16[128,8192]{1,0:T(8,128)(2,1)}, u32[]{:S(2)}, u32[]{:S(2)}) collective-permute-start(bf16[128,8192]{1,0:T(8,128)(2,1)S(1)} %collective-permute-done.2.whole_ref.refs_0_), channel_id=1, source_target_pairs={{0,2},{2,0},{4,6},{6,4},{8,10},{10,8},{12,14},{14,12},{1,3},{3,1},... | collective-permute-start | bytes 6291464 | tf_op jit(solution)/shard_map/ppermute | solution.py:320
  104.1 28.0 %collective-permute-start.8 = (bf16[64,8192]{1,0:T(8,128)(2,1)}, bf16[64,8192]{1,0:T(8,128)(2,1)S(1)}, u32[]{:S(2)}, u32[]{:S(2)}) collective-permute-start(bf16[64,8192]{1,0:T(8,128)(2,1)} %get-tuple-element.43), channel_id=1, source_target_pairs={{0,4},{2,6},{4,8},{6,10},{8,12},{10,14},{12,0},{14,2},{1,5},{3,7},... | collective-permute-start | bytes 3145736 | tf_op jit(solution)/shard_map/ppermute | solution.py:316
  108.4 19.1 %copy-start.6 = (bf16[256,2048]{1,0:T(8,128)(2,1)S(1)}, bf16[256,2048]{1,0:T(8,128)(2,1)}, u32[]{:S(2)}) copy-start(bf16[256,2048]{1,0:T(8,128)(2,1)} %copy-done.5) | copy-start | bytes 3145732
  123.9 30.3 %collective-permute-start.7 = (bf16[64,8192]{1,0:T(8,128)(2,1)}, bf16[64,8192]{1,0:T(8,128)(2,1)S(1)}, u32[]{:S(2)}, u32[]{:S(2)}) collective-permute-start(bf16[64,8192]{1,0:T(8,128)(2,1)} %get-tuple-element.47), channel_id=1, source_target_pairs={{0,4},{2,6},{4,8},{6,10},{8,12},{10,14},{12,0},{14,2},{1,5},{3,7},... | collective-permute-start | bytes 3145736 | tf_op jit(solution)/shard_map/ppermute | solution.py:316
  124.0 30.2 %collective-permute-start.11 = (bf16[256,2048]{1,0:T(8,128)(2,1)}, bf16[256,2048]{1,0:T(8,128)(2,1)S(1)}, u32[]{:S(2)}, u32[]{:S(2)}) collective-permute-start(bf16[256,2048]{1,0:T(8,128)(2,1)} %get-tuple-element.46), channel_id=1, source_target_pairs={{0,1},{2,3},{4,5},{6,7},{9,8},{11,10},{13,12},{15,14},{16,17},{18,... | collective-permute-start | bytes 3145736 | tf_op jit(solution)/shard_map/ppermute | solution.py:329
  133.2 2.3 %collective-permute-start.9 = (bf16[32,8192]{1,0:T(8,128)(2,1)}, bf16[32,8192]{1,0:T(8,128)(2,1)}, u32[]{:S(2)}, u32[]{:S(2)}) collective-permute-start(bf16[32,8192]{1,0:T(8,128)(2,1)} %get-tuple-element.51), channel_id=1, source_target_pairs={{0,2},{2,0},{4,6},{6,4},{8,10},{10,8},{12,14},{14,12},{1,3},{3,1},... | collective-permute-start | bytes 1572872 | tf_op jit(solution)/shard_map/ppermute | solution.py:320
  133.2 3.0 %collective-permute-start.10 = (bf16[32,8192]{1,0:T(8,128)(2,1)}, bf16[32,8192]{1,0:T(8,128)(2,1)}, u32[]{:S(2)}, u32[]{:S(2)}) collective-permute-start(bf16[32,8192]{1,0:T(8,128)(2,1)} %get-tuple-element.52), channel_id=1, source_target_pairs={{0,2},{2,0},{4,6},{6,4},{8,10},{10,8},{12,14},{14,12},{1,3},{3,1},... | collective-permute-start | bytes 1572872 | tf_op jit(solution)/shard_map/ppermute | solution.py:320
  154.2 2.7 %collective-permute-start.12 = (bf16[64,8192]{1,0:T(8,128)(2,1)S(1)}, bf16[64,8192]{1,0:T(8,128)(2,1)S(1)}, u32[]{:S(2)}, u32[]{:S(2)}) collective-permute-start(bf16[64,8192]{1,0:T(8,128)(2,1)S(1)} %collective-permute-done.7.refs_0_), channel_id=1, source_target_pairs={{0,2},{2,0},{4,6},{6,4},{8,10},{10,8},{12,14},{14,12},{1,3},{3,1},... | collective-permute-start | bytes 3145736 | tf_op jit(solution)/shard_map/ppermute | solution.py:320
  154.2 16.2 %collective-permute-start.14 = (bf16[128,2048]{1,0:T(8,128)(2,1)S(1)}, bf16[128,2048]{1,0:T(8,128)(2,1)S(1)}, u32[]{:S(2)}, u32[]{:S(2)}) collective-permute-start(bf16[128,2048]{1,0:T(8,128)(2,1)S(1)} %get-tuple-element.53), channel_id=1, source_target_pairs={{1,0},{3,2},{4,5},{6,7},{8,9},{10,11},{13,12},{15,14},{17,16},{19,... | collective-permute-start | bytes 1572872 | tf_op jit(solution)/shard_map/ppermute | solution.py:329
  167.7 18.8 %collective-permute-start.13 = (bf16[128,1280]{1,0:T(8,128)(2,1)S(1)}, bf16[128,1280]{1,0:T(8,128)(2,1)S(1)}, u32[]{:S(2)}, u32[]{:S(2)}) collective-permute-start(bf16[128,1280]{1,0:T(8,128)(2,1)S(1)} %get-tuple-element.56), channel_id=1, source_target_pairs={{1,0},{3,2},{4,5},{6,7},{8,9},{10,11},{13,12},{15,14},{17,16},{19,... | collective-permute-start | bytes 983048 | tf_op jit(solution)/shard_map/ppermute | solution.py:329
  178.1 8.4 %collective-permute-start.15 = (bf16[128,768]{1,0:T(8,128)(2,1)S(1)}, bf16[128,768]{1,0:T(8,128)(2,1)S(1)}, u32[]{:S(2)}, u32[]{:S(2)}) collective-permute-start(bf16[128,768]{1,0:T(8,128)(2,1)S(1)} %get-tuple-element.59), channel_id=1, source_target_pairs={{1,0},{3,2},{4,5},{6,7},{8,9},{10,11},{13,12},{15,14},{17,16},{19,... | collective-permute-start | bytes 589832 | tf_op jit(solution)/shard_map/ppermute | solution.py:329

commit v15 on v14

--- a/solution.py
+++ b/solution.py
@@ -95,7 +95,8 @@
     rows = sum(ref.shape[0] for ref in mine_refs)
     slots, tile, width = held.shape
     tiles = keep_sems.shape[0]
-    half = tile // 2
+    parts = train_sems.shape[1]
+    share = tile // parts
     depth = min(width, 1024)
     core = core_ref[0]
 
@@ -103,11 +104,11 @@
         slot = lax.rem(i, slots)
         return [
             pltpu.make_async_copy(
-                train_ref.at[pl.ds(pl.multiple_of(i * tile, tile) + top + part * half, half)],
-                held.at[slot, pl.ds(part * half, half)],
+                train_ref.at[pl.ds(pl.multiple_of(i * tile, tile) + top + part * share, share)],
+                held.at[slot, pl.ds(part * share, share)],
                 train_sems.at[slot, part],
             )
-            for part in range(2)
+            for part in range(parts)
         ]
 
     for i in range(min(slots, tiles)):
@@ -205,7 +206,7 @@
             pltpu.VMEM((slots, tile, width), jnp.bfloat16),
             pltpu.VMEM((2, cores * rows, tile), jnp.float32),
             pltpu.VMEM((2, cores * rows, tile), jnp.bfloat16),
-            pltpu.SemaphoreType.DMA((slots, 2)),
+            pltpu.SemaphoreType.DMA((slots, 4)),
             pltpu.SemaphoreType.DMA((count // tile, cores)),
             pltpu.SemaphoreType.DMA((count // tile,)),
         ],
@@ -309,9 +310,15 @@
     fisher = fisher[None, :]
     shape = (chips_per_owner, cores, own, count)
 
+    ring = [*range(0, chips, 2), *reversed(range(1, chips, 2))]
+    origin = [
+        [ring[(ring.index(z) - hop) % chips] for z in range(chips)] for hop in range(chips)
+    ]
+
     def shift(panel):
         pairs = [
-            (z * cores + c, (z + 1) % chips * cores + c) for z in range(chips) for c in range(cores)
+            (ring[place] * cores + c, ring[(place + 1) % chips] * cores + c)
+            for place in range(chips) for c in range(cores)
         ]
         return lax.ppermute(panel, "blk", pairs)
 
@@ -324,13 +331,13 @@
         for step in range(1, owners):
             pairs = []
             for b in range(blks):
-                owner = (b // cores - by) % chips // chips_per_owner
+                owner = origin[by][b // cores] // chips_per_owner
                 pairs.append((b * owners + (owner + step) % owners, b * owners + owner))
             received.append(lax.ppermute(send, ("blk", "dim"), pairs))
         return received
 
     def whose(by):
-        source = lax.rem(chip - by + chips, chips)
+        source = sum(jnp.where(chip == z, origin[by][z], 0) for z in range(chips))
         mine = (source // chips_per_owner == me).astype(jnp.int32)[None]
         return mine, lax.rem(source, chips_per_owner)[None]
 
@@ -364,22 +371,15 @@
     received = exchange(send, hops)
     high_piece = after(high_flow, send, *earlier)
     high_other = swap([high_piece])
-    knee = count * 5 // 8
-    halves = []
-    for top, bottom in ((0, knee), (knee, count)):
-        if top:
-            high_piece = after(high_piece, send, *received)
-        scores, send = multiply(
-            scores, shape, whose(hops), core, [high_piece], high_other, fisher, train, own // 2,
-            (top, bottom),
-        )
-        halves.append(exchange(send, hops))
+    scores, send = multiply(
+        scores, shape, whose(hops), core, [high_piece], high_other, fisher, train, own // 2
+    )
+    last = exchange(send, hops)
     earlier = [after(term, send) for term in earlier]
     scores = place(scores, whose(hops - 1), [], earlier, [0] * len(earlier), 0)
     received = [after(term, scores) for term in received]
     scores = place(scores, whose(hops), [], received, [0] * len(received), 0)
-    cols = [0] * len(received) + [knee] * len(received)
-    scores = place(scores, whose(hops), [], halves[0] + halves[1], cols, own // 2)
+    scores = place(scores, whose(hops), [], last, [0] * len(last), own // 2)
     return scores.reshape(chips_per_owner * cores * own, count)
 
 

time: 189 us -> 187 us (0.989)
  starting transfers between devices: 16 us -> 21.6 us
  Pallas kernels: 106 us -> 101 us
  waiting for transfers between devices: 58.1 us -> 53.8 us
    ppermute x6 -> x5, waiting for transfers between devices: 9.85 us -> 23.2 us  [exchange(): received.append(lax.ppermute(send, ('blk', 'dim'), pairs))]
    ppermute x4, waiting for transfers between devices: 36.9 us -> 24.6 us  [shift(): return lax.ppermute(panel, 'blk', pairs)]
    ppermute x4, starting transfers between devices: 2.64 us -> 8.6 us  [shift(): return lax.ppermute(panel, 'blk', pairs)]
    ppermute x6, waiting for transfers between devices: 11.4 us -> 6.04 us  [swap(): return [lax.ppermute(part, 'blk', pairs) for part in parts]]
    pallas_call x5 -> x4, Pallas kernels: 66.6 us -> 62.9 us  [multiply(): pl.pallas_call(functools.partial(multiply_kernel, counts, start, top), in...]
    ppermute x6 -> x5, starting transfers between devices: 12.4 us -> 12 us  [exchange(): received.append(lax.ppermute(send, ('blk', 'dim'), pairs))]
  transfers between devices with their start and end apart: 16 -> 15, of which waited for: 12 -> 9; matrix products, arithmetic and copies ran while one was open for 1% -> 1% of each run, Pallas kernels for 55% -> 54%
where the time goes in v15:
time: 187 us; the launch traced here: 185 us
  Pallas kernels  101 us (54%)
  waiting for transfers between devices  53.8 us (29%)
  starting transfers between devices  21.6 us (12%)
  local copies, waits for them, and re-layouts  8.69 us (5%)
    pallas_call x4, Pallas kernels, multiply(): pl.pallas_call(functools.partial(multiply_kernel, counts, start, top), in...  62.9 us
    pallas_call x1, Pallas kernels, first(): pl.pallas_call(first_kernel, grid=(count // tile,), in_specs=[in_smem, pl...  29.1 us
    ppermute x4, waiting for transfers between devices, shift(): return lax.ppermute(panel, 'blk', pairs)  24.6 us
    ppermute x5, waiting for transfers between devices, exchange(): received.append(lax.ppermute(send, ('blk', 'dim'), pairs))  23.2 us
    ppermute x5, starting transfers between devices, exchange(): received.append(lax.ppermute(send, ('blk', 'dim'), pairs))  12 us
    unnamed x17, local copies, waits for them, and re-layouts  8.69 us
    ppermute x4, starting transfers between devices, shift(): return lax.ppermute(panel, 'blk', pairs)  8.6 us
    pallas_call x5, Pallas kernels, place(): pl.pallas_call(functools.partial(place_kernel, start, cols, len(kept)), i...  6.12 us
  transfers between devices with their start and end apart: 15, of which 9 were waited for; matrix products, arithmetic and copies ran while one was open for 1% of the time, Pallas kernels for 54%

profile of v15, /device:TPU:0, one launch (start us, length us, event | category | flops | bytes accessed | tf_op | source)
XLA Modules:
  0.0 185.0 jit_solution(16473228039472614233)
XLA Ops:
  0.0 0.5 collective-permute-start.1
  0.5 3.6 %collective-permute-start = (bf16[128,8192]{1,0:T(8,128)(2,1)}, bf16[128,8192]{1,0:T(8,128)(2,1)}, u32[]{:S(2)}, u32[]{:S(2)}) collective-permute-start(bf16[128,8192]{1,0:T(8,128)(2,1)} %mine_ref.1), channel_id=1, source_target_pairs={{0,8},{2,10},{8,12},{10,14},{12,4},{14,6},{4,0},{6,2},{1,9},{3,11}... | collective-permute-start | bytes 6291464 | tf_op jit(solution)/shard_map/ppermute | solution.py:323
  4.0 1.4 copy.13.exps_ref
  5.4 0.0 collective-permute-done.1.other_ref
  5.4 0.0 copy-start
  5.4 1.6 copy-done
  7.0 0.8 copy-done.5
  7.8 29.1 %first.1 = (bf16[2048,8192]{1,0:T(8,128)(2,1)}, f32[256,2048]{1,0:T(8,128)S(1)}, bf16[256,2048]{1,0:T(8,128)(2,1)S(1)}) custom-call(s32[1]{0:T(128)} %bitcast.2.core_ref, bf16[128,8192]{1,0:T(8,128)(2,1)S(1)} %copy-done, bf16[128,8192]{1,0:T(8,128)(2,1)S(1)} %collective-permute-done.1.other_ref, f32[1,8192]{1,0:T(1,128)S(1)} %bitcast.11, ...), custom_call_target="tpu_custom_call" | custom-call | flops 1 | bytes 1 | tf_op jit(solution)/shard_map/first/pallas_call | solution.py:59
  36.9 1.4 copy-done.1
  38.3 1.0 copy-done.7
  39.3 10.6 %collective-permute-done.refs_0_ = bf16[128,8192]{1,0:T(8,128)(2,1)} collective-permute-done((bf16[128,8192]{1,0:T(8,128)(2,1)}, bf16[128,8192]{1,0:T(8,128)(2,1)}, u32[]{:S(2)}, u32[]{:S(2)}) %collective-permute-start) | collective-permute-done | bytes 2097184 | tf_op jit(solution)/shard_map/ppermute | solution.py:323
  49.9 0.0 collective-permute-start.3
  49.9 3.4 %collective-permute-start.2 = (bf16[128,8192]{1,0:T(8,128)(2,1)}, bf16[128,8192]{1,0:T(8,128)(2,1)S(1)}, u32[]{:S(2)}, u32[]{:S(2)}) collective-permute-start(bf16[128,8192]{1,0:T(8,128)(2,1)} %collective-permute-done.refs_0_), channel_id=1, source_target_pairs={{0,8},{2,10},{8,12},{10,14},{12,4},{14,6},{4,0},{6,2},{1,9},{3,11}... | collective-permute-start | bytes 6291464 | tf_op jit(solution)/shard_map/ppermute | solution.py:323
  53.3 1.3 collective-permute-start.4
  54.6 0.0 collective-permute-done.3.refs_1_
  54.6 16.2 %multiply.4 = (f32[2,2,128,2048]{3,2,1,0:T(8,128)}, bf16[256,2048]{1,0:T(8,128)(2,1)}) custom-call(s32[1]{0:T(128)} %bitcast.4.mine_ref, s32[1]{0:T(128)} %bitcast.5.spot_ref, s32[1]{0:T(128)} %bitcast.2.core_ref, bf16[128,8192]{1,0:T(8,128)(2,1)} %collective-permute-done.refs_0_, bf16[128,8192]{1,0:T(8,128)(2,1)} %collective-permute-done.3.refs_1_, ...), custom_call_target="tpu_custom_call" | custom-call | flops 1 | bytes 1 | tf_op jit(solution)/shard_map/multiply/pallas_call | solution.py:197
  70.8 1.3 collective-permute-start.5
  72.1 9.4 %collective-permute-done.4.refs_1_ = bf16[256,2048]{1,0:T(8,128)(2,1)} collective-permute-done((bf16[256,2048]{1,0:T(8,128)(2,1)}, bf16[256,2048]{1,0:T(8,128)(2,1)}, u32[]{:S(2)}, u32[]{:S(2)}) %collective-permute-start.4) | collective-permute-done | bytes 1048608 | tf_op jit(solution)/shard_map/ppermute | solution.py:336
  81.5 1.6 copy-done.2
  83.1 2.9 %place.5.refs_2_ = f32[2,2,128,2048]{3,2,1,0:T(8,128)} custom-call(s32[1]{0:T(128)} %bitcast.6.mine_ref, s32[1]{0:T(128)} %bitcast.7.spot_ref, f32[256,2048]{1,0:T(8,128)S(1)} %copy-done.2, bf16[256,2048]{1,0:T(8,128)(2,1)} %collective-permute-done.4.refs_1_, f32[2,2,128,2048]{3,2,1,0:T(8,128)} %get-tuple-element.37.refs_2_), custom_call_target="tpu_custom_call", output_to_operand_aliasing={{}: (4, {})} | custom-call | flops 1 | bytes 1 | tf_op jit(solution)/shard_map/place/pallas_call | solution.py:260
  86.0 13.2 %collective-permute-done.2.whole_ref.refs_0_ = bf16[128,8192]{1,0:T(8,128)(2,1)S(1)} collective-permute-done((bf16[128,8192]{1,0:T(8,128)(2,1)}, bf16[128,8192]{1,0:T(8,128)(2,1)S(1)}, u32[]{:S(2)}, u32[]{:S(2)}) %collective-permute-start.2) | collective-permute-done | bytes 2097184 | tf_op jit(solution)/shard_map/ppermute | solution.py:323
  99.2 1.4 cut.2
  100.6 2.5 %collective-permute-done.5.refs_0_ = bf16[256,2048]{1,0:T(8,128)(2,1)S(1)} collective-permute-done((bf16[256,2048]{1,0:T(8,128)(2,1)}, bf16[256,2048]{1,0:T(8,128)(2,1)S(1)}, u32[]{:S(2)}, u32[]{:S(2)}) %collective-permute-start.5) | collective-permute-done | bytes 1048608 | tf_op jit(solution)/shard_map/ppermute | solution.py:336
  103.2 1.0 copy-done.3
  104.1 0.0 collective-permute-start.6
  104.1 0.7 collective-permute-start.8
  104.9 3.5 %collective-permute-done.6.refs_1_ = bf16[128,8192]{1,0:T(8,128)(2,1)} collective-permute-done((bf16[128,8192]{1,0:T(8,128)(2,1)S(1)}, bf16[128,8192]{1,0:T(8,128)(2,1)}, u32[]{:S(2)}, u32[]{:S(2)}) %collective-permute-start.6) | collective-permute-done | bytes 2097184 | tf_op jit(solution)/shard_map/ppermute | solution.py:327
  108.4 15.5 %multiply.5 = (f32[2,2,128,2048]{3,2,1,0:T(8,128)}, bf16[256,2048]{1,0:T(8,128)(2,1)}) custom-call(s32[1]{0:T(128)} %bitcast.8.mine_ref, s32[1]{0:T(128)} %bitcast.9.spot_ref, s32[1]{0:T(128)} %bitcast.2.core_ref, bf16[128,8192]{1,0:T(8,128)(2,1)S(1)} %collective-permute-done.2.whole_ref.refs_0_, ...), custom_call_target="tpu_custom_call", output_to_operand_aliasing={{0}: (5, {})} | custom-call | flops 1 | bytes 1 | tf_op jit(solution)/shard_map/multiply/pallas_call | solution.py:197
  123.9 0.9 collective-permute-start.7
  124.8 3.4 %collective-permute-start.11 = (bf16[256,2048]{1,0:T(8,128)(2,1)}, bf16[256,2048]{1,0:T(8,128)(2,1)S(1)}, u32[]{:S(2)}, u32[]{:S(2)}) collective-permute-start(bf16[256,2048]{1,0:T(8,128)(2,1)} %get-tuple-element.43), channel_id=1, source_target_pairs={{0,1},{2,3},{4,5},{6,7},{9,8},{11,10},{13,12},{15,14},{16,17},{18,... | collective-permute-start | bytes 3145736 | tf_op jit(solution)/shard_map/ppermute | solution.py:336
  128.2 3.1 %place.6.refs_3_ = f32[2,2,128,2048]{3,2,1,0:T(8,128)} custom-call(s32[1]{0:T(128)} %bitcast.4.mine_ref, s32[1]{0:T(128)} %bitcast.5.spot_ref, bf16[256,2048]{1,0:T(8,128)(2,1)S(1)} %copy-done.4, f32[2,2,128,2048]{3,2,1,0:T(8,128)} %get-tuple-element.46.refs_1_), custom_call_target="tpu_custom_call", output_to_operand_aliasing={{}: (3, {})} | custom-call | flops 1 | bytes 1 | tf_op jit(solution)/shard_map/place/pallas_call | solution.py:260
  131.3 0.0 collective-permute-done.8.whole_ref.refs_0_
  131.3 1.1 cut.3
  132.4 0.0 collective-permute-start.9
  132.4 0.5 collective-permute-start.10
  132.9 1.7 collective-permute-done.9.refs_1_
  134.6 0.7 collective-permute-done.10.refs_2_
  135.4 16.2 %multiply.6 = (f32[2,2,128,2048]{3,2,1,0:T(8,128)}, bf16[128,2048]{1,0:T(8,128)(2,1)S(1)}) custom-call(s32[1]{0:T(128)} %bitcast.mine_ref, s32[1]{0:T(128)} %bitcast.1.spot_ref, s32[1]{0:T(128)} %bitcast.2.core_ref, bf16[64,8192]{1,0:T(8,128)(2,1)S(1)} %collective-permute-done.8.whole_ref.refs_0_, ...), custom_call_target="tpu_custom_call", output_to_operand_aliasing={{0}: (6, {})} | custom-call | flops 1 | bytes 1 | tf_op jit(solution)/shard_map/multiply/pallas_call | solution.py:197
  151.6 0.8 collective-permute-done.7.refs_0_
  152.4 0.0 collective-permute-done.11.refs_0_
  152.4 2.8 %collective-permute-start.14 = (bf16[128,2048]{1,0:T(8,128)(2,1)S(1)}, bf16[128,2048]{1,0:T(8,128)(2,1)S(1)}, u32[]{:S(2)}, u32[]{:S(2)}) collective-permute-start(bf16[128,2048]{1,0:T(8,128)(2,1)S(1)} %get-tuple-element.50), channel_id=1, source_target_pairs={{0,1},{2,3},{5,4},{7,6},{8,9},{10,11},{13,12},{15,14},{16,17},{18,... | collective-permute-start | bytes 1572872 | tf_op jit(solution)/shard_map/ppermute | solution.py:336
  155.2 0.0 collective-permute-done.12.refs_1_
  155.2 15.0 %multiply.7 = (f32[2,2,128,2048]{3,2,1,0:T(8,128)}, bf16[128,2048]{1,0:T(8,128)(2,1)S(1)}) custom-call(s32[1]{0:T(128)} %bitcast.mine_ref, s32[1]{0:T(128)} %bitcast.1.spot_ref, s32[1]{0:T(128)} %bitcast.2.core_ref, bf16[64,8192]{1,0:T(8,128)(2,1)S(1)} %collective-permute-done.7.refs_0_, ...), custom_call_target="tpu_custom_call", output_to_operand_aliasing={{0}: (5, {})} | custom-call | flops 1 | bytes 1 | tf_op jit(solution)/shard_map/multiply/pallas_call | solution.py:197
  170.3 3.2 %collective-permute-start.13 = (bf16[128,2048]{1,0:T(8,128)(2,1)S(1)}, bf16[128,2048]{1,0:T(8,128)(2,1)S(1)}, u32[]{:S(2)}, u32[]{:S(2)}) collective-permute-start(bf16[128,2048]{1,0:T(8,128)(2,1)S(1)} %get-tuple-element.53), channel_id=1, source_target_pairs={{0,1},{2,3},{5,4},{7,6},{8,9},{10,11},{13,12},{15,14},{16,17},{18,... | collective-permute-start | bytes 1572872 | tf_op jit(solution)/shard_map/ppermute | solution.py:336
  173.5 0.1 place.7.refs_1_
  173.6 0.0 collective-permute-done.14.refs_0_
  173.6 0.1 place.8.refs_1_
  173.6 11.3 %collective-permute-done.13.refs_0_ = bf16[128,2048]{1,0:T(8,128)(2,1)S(1)} collective-permute-done((bf16[128,2048]{1,0:T(8,128)(2,1)S(1)}, bf16[128,2048]{1,0:T(8,128)(2,1)S(1)}, u32[]{:S(2)}, u32[]{:S(2)}) %collective-permute-start.13) | collective-permute-done | bytes 524320 | tf_op jit(solution)/shard_map/ppermute | solution.py:336
  (11 shorter events, 0.1 us)
Async XLA Ops:
  0.0 5.4 %collective-permute-start.1 = (bf16[128,8192]{1,0:T(8,128)(2,1)}, bf16[128,8192]{1,0:T(8,128)(2,1)S(1)}, u32[]{:S(2)}, u32[]{:S(2)}) collective-permute-start(bf16[128,8192]{1,0:T(8,128)(2,1)} %mine_ref.1), channel_id=1, source_target_pairs={{0,2},{2,0},{4,6},{6,4},{8,10},{10,8},{12,14},{14,12},{1,3},{3,1},... | collective-permute-start | bytes 6291464 | tf_op jit(solution)/shard_map/ppermute | solution.py:327
  0.5 49.5 %collective-permute-start = (bf16[128,8192]{1,0:T(8,128)(2,1)}, bf16[128,8192]{1,0:T(8,128)(2,1)}, u32[]{:S(2)}, u32[]{:S(2)}) collective-permute-start(bf16[128,8192]{1,0:T(8,128)(2,1)} %mine_ref.1), channel_id=1, source_target_pairs={{0,8},{2,10},{8,12},{10,14},{12,4},{14,6},{4,0},{6,2},{1,9},{3,11}... | collective-permute-start | bytes 6291464 | tf_op jit(solution)/shard_map/ppermute | solution.py:323
  5.4 1.6 copy-start
  7.0 0.8 copy-start.5
  7.8 46.8 %copy-start.6 = (f32[8192]{0:T(1024)S(1)}, f32[8192]{0:T(1024)}, u32[]{:S(2)}) copy-start(f32[8192]{0:T(1024)} %param.7) | copy-start | bytes 98308
  36.9 1.4 copy-start.1
  38.3 1.1 copy-start.7
  49.9 4.7 %collective-permute-start.3 = (bf16[128,8192]{1,0:T(8,128)(2,1)}, bf16[128,8192]{1,0:T(8,128)(2,1)}, u32[]{:S(2)}, u32[]{:S(2)}) collective-permute-start(bf16[128,8192]{1,0:T(8,128)(2,1)} %collective-permute-done.refs_0_), channel_id=1, source_target_pairs={{0,2},{2,0},{4,6},{6,4},{8,10},{10,8},{12,14},{14,12},{1,3},{3,1},... | collective-permute-start | bytes 6291464 | tf_op jit(solution)/shard_map/ppermute | solution.py:327
  49.9 49.3 %collective-permute-start.2 = (bf16[128,8192]{1,0:T(8,128)(2,1)}, bf16[128,8192]{1,0:T(8,128)(2,1)S(1)}, u32[]{:S(2)}, u32[]{:S(2)}) collective-permute-start(bf16[128,8192]{1,0:T(8,128)(2,1)} %collective-permute-done.refs_0_), channel_id=1, source_target_pairs={{0,8},{2,10},{8,12},{10,14},{12,4},{14,6},{4,0},{6,2},{1,9},{3,11}... | collective-permute-start | bytes 6291464 | tf_op jit(solution)/shard_map/ppermute | solution.py:323
  53.3 28.2 %collective-permute-start.4 = (bf16[256,2048]{1,0:T(8,128)(2,1)}, bf16[256,2048]{1,0:T(8,128)(2,1)}, u32[]{:S(2)}, u32[]{:S(2)}) collective-permute-start(bf16[256,2048]{1,0:T(8,128)(2,1)} %copy-done.7), channel_id=1, source_target_pairs={{1,0},{3,2},{5,4},{7,6},{8,9},{10,11},{12,13},{14,15},{17,16},{19,... | collective-permute-start | bytes 3145736 | tf_op jit(solution)/shard_map/ppermute | solution.py:336
  70.8 32.4 %collective-permute-start.5 = (bf16[256,2048]{1,0:T(8,128)(2,1)}, bf16[256,2048]{1,0:T(8,128)(2,1)S(1)}, u32[]{:S(2)}, u32[]{:S(2)}) collective-permute-start(bf16[256,2048]{1,0:T(8,128)(2,1)} %get-tuple-element.34), channel_id=1, source_target_pairs={{1,0},{3,2},{4,5},{6,7},{9,8},{11,10},{12,13},{14,15},{17,16},{19,... | collective-permute-start | bytes 3145736 | tf_op jit(solution)/shard_map/ppermute | solution.py:336
  81.5 1.6 copy-start.2
  103.2 1.0 copy-start.3
  104.1 4.3 %collective-permute-start.6 = (bf16[128,8192]{1,0:T(8,128)(2,1)S(1)}, bf16[128,8192]{1,0:T(8,128)(2,1)}, u32[]{:S(2)}, u32[]{:S(2)}) collective-permute-start(bf16[128,8192]{1,0:T(8,128)(2,1)S(1)} %collective-permute-done.2.whole_ref.refs_0_), channel_id=1, source_target_pairs={{0,2},{2,0},{4,6},{6,4},{8,10},{10,8},{12,14},{14,12},{1,3},{3,1},... | collective-permute-start | bytes 6291464 | tf_op jit(solution)/shard_map/ppermute | solution.py:327
  104.1 27.2 %collective-permute-start.8 = (bf16[64,8192]{1,0:T(8,128)(2,1)}, bf16[64,8192]{1,0:T(8,128)(2,1)S(1)}, u32[]{:S(2)}, u32[]{:S(2)}) collective-permute-start(bf16[64,8192]{1,0:T(8,128)(2,1)} %get-tuple-element.40), channel_id=1, source_target_pairs={{0,8},{2,10},{8,12},{10,14},{12,4},{14,6},{4,0},{6,2},{1,9},{3,11}... | collective-permute-start | bytes 3145736 | tf_op jit(solution)/shard_map/ppermute | solution.py:323
  108.4 19.8 %copy-start.4 = (bf16[256,2048]{1,0:T(8,128)(2,1)S(1)}, bf16[256,2048]{1,0:T(8,128)(2,1)}, u32[]{:S(2)}) copy-start(bf16[256,2048]{1,0:T(8,128)(2,1)} %copy-done.3) | copy-start | bytes 3145732
  123.9 28.4 %collective-permute-start.7 = (bf16[64,8192]{1,0:T(8,128)(2,1)}, bf16[64,8192]{1,0:T(8,128)(2,1)S(1)}, u32[]{:S(2)}, u32[]{:S(2)}) collective-permute-start(bf16[64,8192]{1,0:T(8,128)(2,1)} %get-tuple-element.44), channel_id=1, source_target_pairs={{0,8},{2,10},{8,12},{10,14},{12,4},{14,6},{4,0},{6,2},{1,9},{3,11}... | collective-permute-start | bytes 3145736 | tf_op jit(solution)/shard_map/ppermute | solution.py:323
  124.8 27.6 %collective-permute-start.11 = (bf16[256,2048]{1,0:T(8,128)(2,1)}, bf16[256,2048]{1,0:T(8,128)(2,1)S(1)}, u32[]{:S(2)}, u32[]{:S(2)}) collective-permute-start(bf16[256,2048]{1,0:T(8,128)(2,1)} %get-tuple-element.43), channel_id=1, source_target_pairs={{0,1},{2,3},{4,5},{6,7},{9,8},{11,10},{13,12},{15,14},{16,17},{18,... | collective-permute-start | bytes 3145736 | tf_op jit(solution)/shard_map/ppermute | solution.py:336
  132.4 2.3 %collective-permute-start.9 = (bf16[32,8192]{1,0:T(8,128)(2,1)}, bf16[32,8192]{1,0:T(8,128)(2,1)}, u32[]{:S(2)}, u32[]{:S(2)}) collective-permute-start(bf16[32,8192]{1,0:T(8,128)(2,1)} %get-tuple-element.48), channel_id=1, source_target_pairs={{0,2},{2,0},{4,6},{6,4},{8,10},{10,8},{12,14},{14,12},{1,3},{3,1},... | collective-permute-start | bytes 1572872 | tf_op jit(solution)/shard_map/ppermute | solution.py:327
  132.4 3.0 %collective-permute-start.10 = (bf16[32,8192]{1,0:T(8,128)(2,1)}, bf16[32,8192]{1,0:T(8,128)(2,1)}, u32[]{:S(2)}, u32[]{:S(2)}) collective-permute-start(bf16[32,8192]{1,0:T(8,128)(2,1)} %get-tuple-element.49), channel_id=1, source_target_pairs={{0,2},{2,0},{4,6},{6,4},{8,10},{10,8},{12,14},{14,12},{1,3},{3,1},... | collective-permute-start | bytes 1572872 | tf_op jit(solution)/shard_map/ppermute | solution.py:327
  152.4 2.8 %collective-permute-start.12 = (bf16[64,8192]{1,0:T(8,128)(2,1)S(1)}, bf16[64,8192]{1,0:T(8,128)(2,1)S(1)}, u32[]{:S(2)}, u32[]{:S(2)}) collective-permute-start(bf16[64,8192]{1,0:T(8,128)(2,1)S(1)} %collective-permute-done.7.refs_0_), channel_id=1, source_target_pairs={{0,2},{2,0},{4,6},{6,4},{8,10},{10,8},{12,14},{14,12},{1,3},{3,1},... | collective-permute-start | bytes 3145736 | tf_op jit(solution)/shard_map/ppermute | solution.py:327
  152.4 21.2 %collective-permute-start.14 = (bf16[128,2048]{1,0:T(8,128)(2,1)S(1)}, bf16[128,2048]{1,0:T(8,128)(2,1)S(1)}, u32[]{:S(2)}, u32[]{:S(2)}) collective-permute-start(bf16[128,2048]{1,0:T(8,128)(2,1)S(1)} %get-tuple-element.50), channel_id=1, source_target_pairs={{0,1},{2,3},{5,4},{7,6},{8,9},{10,11},{13,12},{15,14},{16,17},{18,... | collective-permute-start | bytes 1572872 | tf_op jit(solution)/shard_map/ppermute | solution.py:336
  170.3 14.7 %collective-permute-start.13 = (bf16[128,2048]{1,0:T(8,128)(2,1)S(1)}, bf16[128,2048]{1,0:T(8,128)(2,1)S(1)}, u32[]{:S(2)}, u32[]{:S(2)}) collective-permute-start(bf16[128,2048]{1,0:T(8,128)(2,1)S(1)} %get-tuple-element.53), channel_id=1, source_target_pairs={{0,1},{2,3},{5,4},{7,6},{8,9},{10,11},{13,12},{15,14},{16,17},{18,... | collective-permute-start | bytes 1572872 | tf_op jit(solution)/shard_map/ppermute | solution.py:336

commit v16 on v15

--- a/solution.py
+++ b/solution.py
@@ -192,6 +192,7 @@
     tile = min(count, 256)
     slots = 3
     block = (cores * rows, count)
+    grant = 4 * block[0] * width + 2 * slots * tile * width + 12 * block[0] * tile + 2 * mib
     given = [] if scores is None else [scores]
     counts = (len(mine), len(other), len(given))
     return pl.pallas_call(
@@ -211,7 +212,7 @@
             pltpu.SemaphoreType.DMA((count // tile,)),
         ],
         input_output_aliases={3 + len(mine) + len(other): 0} if given else {},
-        compiler_params=pltpu.CompilerParams(vmem_limit_bytes=22 * mib),
+        compiler_params=pltpu.CompilerParams(vmem_limit_bytes=grant),
         cost_estimate=small,
         name="multiply",
     )(*where, core, *mine, *other, *given, fisher, train)
@@ -371,15 +372,22 @@
     received = exchange(send, hops)
     high_piece = after(high_flow, send, *earlier)
     high_other = swap([high_piece])
-    scores, send = multiply(
-        scores, shape, whose(hops), core, [high_piece], high_other, fisher, train, own // 2
-    )
-    last = exchange(send, hops)
+    knee = count * 5 // 8
+    halves = []
+    for top, bottom in ((0, knee), (knee, count)):
+        if top:
+            high_piece = after(high_piece, send, *received)
+        scores, send = multiply(
+            scores, shape, whose(hops), core, [high_piece], high_other, fisher, train, own // 2,
+            (top, bottom),
+        )
+        halves.append(exchange(send, hops))
     earlier = [after(term, send) for term in earlier]
     scores = place(scores, whose(hops - 1), [], earlier, [0] * len(earlier), 0)
     received = [after(term, scores) for term in received]
     scores = place(scores, whose(hops), [], received, [0] * len(received), 0)
-    scores = place(scores, whose(hops), [], last, [0] * len(last), own // 2)
+    cols = [0] * len(halves[0]) + [knee] * len(halves[1])
+    scores = place(scores, whose(hops), [], halves[0] + halves[1], cols, own // 2)
     return scores.reshape(chips_per_owner * cores * own, count)
 
 

time: 187 us -> 204 us (1.091)
  local copies, waits for them, and re-layouts: 8.69 us -> 29.8 us
  waiting for transfers between devices: 53.8 us -> 47.2 us
    unnamed x17 -> x21, local copies, waits for them, and re-layouts: 8.69 us -> 29.8 us
    ppermute x5 -> x6, waiting for transfers between devices: 23.2 us -> 16.2 us  [exchange(): received.append(lax.ppermute(send, ('blk', 'dim'), pairs))]
    pallas_call x4 -> x5, Pallas kernels: 62.9 us -> 64.5 us  [multiply(): pl.pallas_call(functools.partial(multiply_kernel, counts, start, top), in...]
    ppermute x5 -> x6, starting transfers between devices: 12 us -> 11.2 us  [exchange(): received.append(lax.ppermute(send, ('blk', 'dim'), pairs))]
  transfers between devices with their start and end apart: 15 -> 16, of which waited for: 9 -> 9; matrix products, arithmetic and copies ran while one was open for 1% -> 1% of each run, Pallas kernels for 54% -> 51%
where the time goes in v16:
time: 204 us; the launch traced here: 200 us
  Pallas kernels  102 us (50%)
  waiting for transfers between devices  47.2 us (23%)
  local copies, waits for them, and re-layouts  29.8 us (15%)
  starting transfers between devices  20.9 us (10%)
    pallas_call x5, Pallas kernels, multiply(): pl.pallas_call(functools.partial(multiply_kernel, counts, start, top), in...  64.5 us
    unnamed x21, local copies, waits for them, and re-layouts  29.8 us
    pallas_call x1, Pallas kernels, first(): pl.pallas_call(first_kernel, grid=(count // tile,), in_specs=[in_smem, pl...  29.1 us
    ppermute x4, waiting for transfers between devices, shift(): return lax.ppermute(panel, 'blk', pairs)  23.8 us
    ppermute x6, waiting for transfers between devices, exchange(): received.append(lax.ppermute(send, ('blk', 'dim'), pairs))  16.2 us
    ppermute x6, starting transfers between devices, exchange(): received.append(lax.ppermute(send, ('blk', 'dim'), pairs))  11.2 us
    ppermute x4, starting transfers between devices, shift(): return lax.ppermute(panel, 'blk', pairs)  8.56 us
    ppermute x6, waiting for transfers between devices, swap(): return [lax.ppermute(part, 'blk', pairs) for part in parts]  7.19 us
  transfers between devices with their start and end apart: 16, of which 9 were waited for; matrix products, arithmetic and copies ran while one was open for 1% of the time, Pallas kernels for 51%

profile of v16, /device:TPU:0, one launch (start us, length us, event | category | flops | bytes accessed | tf_op | source)
XLA Modules:
  0.0 200.4 jit_solution(5948778557179879905)
XLA Ops:
  0.0 0.5 collective-permute-start.1
  0.5 3.6 %collective-permute-start = (bf16[128,8192]{1,0:T(8,128)(2,1)}, bf16[128,8192]{1,0:T(8,128)(2,1)}, u32[]{:S(2)}, u32[]{:S(2)}) collective-permute-start(bf16[128,8192]{1,0:T(8,128)(2,1)} %mine_ref.1), channel_id=1, source_target_pairs={{0,8},{2,10},{8,12},{10,14},{12,4},{14,6},{4,0},{6,2},{1,9},{3,11}... | collective-permute-start | bytes 6291464 | tf_op jit(solution)/shard_map/ppermute | solution.py:324
  4.0 1.4 copy.14.exps_ref
  5.4 0.0 collective-permute-done.1.other_ref
  5.4 0.0 copy-start.2
  5.4 1.6 copy-done.2
  7.0 0.8 copy-done.5
  7.8 29.1 %first.1 = (bf16[2048,8192]{1,0:T(8,128)(2,1)}, f32[256,2048]{1,0:T(8,128)S(1)}, bf16[256,2048]{1,0:T(8,128)(2,1)S(1)}) custom-call(s32[1]{0:T(128)} %bitcast.2.core_ref, bf16[128,8192]{1,0:T(8,128)(2,1)S(1)} %copy-done.2, bf16[128,8192]{1,0:T(8,128)(2,1)S(1)} %collective-permute-done.1.other_ref, f32[1,8192]{1,0:T(1,128)S(1)} %bitcast.11, ...), custom_call_target="tpu_custom_call" | custom-call | flops 1 | bytes 1 | tf_op jit(solution)/shard_map/first/pallas_call | solution.py:59
  36.9 1.3 copy-done.3
  38.3 1.0 copy-done.9
  39.3 10.6 %collective-permute-done.refs_0_ = bf16[128,8192]{1,0:T(8,128)(2,1)} collective-permute-done((bf16[128,8192]{1,0:T(8,128)(2,1)}, bf16[128,8192]{1,0:T(8,128)(2,1)}, u32[]{:S(2)}, u32[]{:S(2)}) %collective-permute-start) | collective-permute-done | bytes 2097184 | tf_op jit(solution)/shard_map/ppermute | solution.py:324
  49.9 0.0 collective-permute-start.3
  49.9 3.4 %collective-permute-start.2 = (bf16[128,8192]{1,0:T(8,128)(2,1)}, bf16[128,8192]{1,0:T(8,128)(2,1)S(1)}, u32[]{:S(2)}, u32[]{:S(2)}) collective-permute-start(bf16[128,8192]{1,0:T(8,128)(2,1)} %collective-permute-done.refs_0_), channel_id=1, source_target_pairs={{0,8},{2,10},{8,12},{10,14},{12,4},{14,6},{4,0},{6,2},{1,9},{3,11}... | collective-permute-start | bytes 6291464 | tf_op jit(solution)/shard_map/ppermute | solution.py:324
  53.3 1.3 collective-permute-start.4
  54.6 0.0 collective-permute-done.3.refs_1_
  54.6 16.2 %multiply.5 = (f32[2,2,128,2048]{3,2,1,0:T(8,128)}, bf16[256,2048]{1,0:T(8,128)(2,1)}) custom-call(s32[1]{0:T(128)} %bitcast.4.mine_ref, s32[1]{0:T(128)} %bitcast.5.spot_ref, s32[1]{0:T(128)} %bitcast.2.core_ref, bf16[128,8192]{1,0:T(8,128)(2,1)} %collective-permute-done.refs_0_, bf16[128,8192]{1,0:T(8,128)(2,1)} %collective-permute-done.3.refs_1_, ...), custom_call_target="tpu_custom_call" | custom-call | flops 1 | bytes 1 | tf_op jit(solution)/shard_map/multiply/pallas_call | solution.py:198
  70.8 1.3 collective-permute-start.5
  72.1 9.4 %collective-permute-done.4.refs_1_ = bf16[256,2048]{1,0:T(8,128)(2,1)} collective-permute-done((bf16[256,2048]{1,0:T(8,128)(2,1)}, bf16[256,2048]{1,0:T(8,128)(2,1)}, u32[]{:S(2)}, u32[]{:S(2)}) %collective-permute-start.4) | collective-permute-done | bytes 1048608 | tf_op jit(solution)/shard_map/ppermute | solution.py:337
  81.5 1.6 copy-done.4
  83.1 2.9 %place.5.refs_2_ = f32[2,2,128,2048]{3,2,1,0:T(8,128)} custom-call(s32[1]{0:T(128)} %bitcast.6.mine_ref, s32[1]{0:T(128)} %bitcast.7.spot_ref, f32[256,2048]{1,0:T(8,128)S(1)} %copy-done.4, bf16[256,2048]{1,0:T(8,128)(2,1)} %collective-permute-done.4.refs_1_, f32[2,2,128,2048]{3,2,1,0:T(8,128)} %get-tuple-element.40.refs_2_), custom_call_target="tpu_custom_call", output_to_operand_aliasing={{}: (4, {})} | custom-call | flops 1 | bytes 1 | tf_op jit(solution)/shard_map/place/pallas_call | solution.py:261
  86.0 13.2 %collective-permute-done.2.whole_ref.refs_0_ = bf16[128,8192]{1,0:T(8,128)(2,1)S(1)} collective-permute-done((bf16[128,8192]{1,0:T(8,128)(2,1)}, bf16[128,8192]{1,0:T(8,128)(2,1)S(1)}, u32[]{:S(2)}, u32[]{:S(2)}) %collective-permute-start.2) | collective-permute-done | bytes 2097184 | tf_op jit(solution)/shard_map/ppermute | solution.py:324
  99.2 1.4 cut.2
  100.6 2.5 %collective-permute-done.5.refs_0_ = bf16[256,2048]{1,0:T(8,128)(2,1)S(1)} collective-permute-done((bf16[256,2048]{1,0:T(8,128)(2,1)}, bf16[256,2048]{1,0:T(8,128)(2,1)S(1)}, u32[]{:S(2)}, u32[]{:S(2)}) %collective-permute-start.5) | collective-permute-done | bytes 1048608 | tf_op jit(solution)/shard_map/ppermute | solution.py:337
  103.2 1.0 copy-done.7
  104.1 0.7 collective-permute-start.8
  104.9 3.6 %collective-permute-done.6.refs_1_ = bf16[128,8192]{1,0:T(8,128)(2,1)} collective-permute-done((bf16[128,8192]{1,0:T(8,128)(2,1)S(1)}, bf16[128,8192]{1,0:T(8,128)(2,1)}, u32[]{:S(2)}, u32[]{:S(2)}) %collective-permute-start.6) | collective-permute-done | bytes 2097184 | tf_op jit(solution)/shard_map/ppermute | solution.py:328
  108.4 15.5 %multiply.6 = (f32[2,2,128,2048]{3,2,1,0:T(8,128)}, bf16[256,2048]{1,0:T(8,128)(2,1)}) custom-call(s32[1]{0:T(128)} %bitcast.8.mine_ref, s32[1]{0:T(128)} %bitcast.9.spot_ref, s32[1]{0:T(128)} %bitcast.2.core_ref, bf16[128,8192]{1,0:T(8,128)(2,1)S(1)} %collective-permute-done.2.whole_ref.refs_0_, ...), custom_call_target="tpu_custom_call", output_to_operand_aliasing={{0}: (5, {})} | custom-call | flops 1 | bytes 1 | tf_op jit(solution)/shard_map/multiply/pallas_call | solution.py:198
  124.0 0.9 collective-permute-start.7
  124.8 3.4 %collective-permute-start.11 = (bf16[256,2048]{1,0:T(8,128)(2,1)}, bf16[256,2048]{1,0:T(8,128)(2,1)S(1)}, u32[]{:S(2)}, u32[]{:S(2)}) collective-permute-start(bf16[256,2048]{1,0:T(8,128)(2,1)} %get-tuple-element.46), channel_id=1, source_target_pairs={{0,1},{2,3},{4,5},{6,7},{9,8},{11,10},{13,12},{15,14},{16,17},{18,... | collective-permute-start | bytes 3145736 | tf_op jit(solution)/shard_map/ppermute | solution.py:337
  128.2 3.1 %place.6.refs_3_ = f32[2,2,128,2048]{3,2,1,0:T(8,128)} custom-call(s32[1]{0:T(128)} %bitcast.4.mine_ref, s32[1]{0:T(128)} %bitcast.5.spot_ref, bf16[256,2048]{1,0:T(8,128)(2,1)S(1)} %copy-done.8, f32[2,2,128,2048]{3,2,1,0:T(8,128)} %get-tuple-element.49.refs_1_), custom_call_target="tpu_custom_call", output_to_operand_aliasing={{}: (3, {})} | custom-call | flops 1 | bytes 1 | tf_op jit(solution)/shard_map/place/pallas_call | solution.py:261
  131.3 1.1 cut.3
  132.4 0.5 collective-permute-start.10
  132.9 1.7 collective-permute-done.9.refs_1_
  134.6 0.7 collective-permute-done.10.refs_2_
  135.4 10.5 %copy-done = bf16[2048,8192]{1,0:T(8,128)(2,1)S(1)} copy-done((bf16[2048,8192]{1,0:T(8,128)(2,1)S(1)}, bf16[2048,8192]{1,0:T(8,128)(2,1)}, u32[]{:S(2)}) %copy-start) | copy-done | bytes 33554456
  145.9 16.7 %multiply.7 = (f32[2,2,128,2048]{3,2,1,0:T(8,128)}, bf16[128,2048]{1,0:T(8,128)(2,1)S(1)}) custom-call(s32[1]{0:T(128)} %bitcast.mine_ref, s32[1]{0:T(128)} %bitcast.1.spot_ref, s32[1]{0:T(128)} %bitcast.2.core_ref, bf16[64,8192]{1,0:T(8,128)(2,1)S(1)} %collective-permute-done.8.whole_ref.refs_0_, ...), custom_call_target="tpu_custom_call", output_to_operand_aliasing={{0}: (6, {})} | custom-call | flops 1 | bytes 1 | tf_op jit(solution)/shard_map/multiply/pallas_call | solution.py:198
  162.7 0.2 collective-permute-start.12
  162.9 1.4 collective-permute-start.14
  164.3 1.1 collective-permute-done.12.refs_1_
  165.4 10.5 %copy-done.1 = bf16[2048,8192]{1,0:T(8,128)(2,1)S(1)} copy-done((bf16[2048,8192]{1,0:T(8,128)(2,1)S(1)}, bf16[2048,8192]{1,0:T(8,128)(2,1)}, u32[]{:S(2)}) %copy-start.1) | copy-done | bytes 33554456
  176.0 9.9 %multiply.8 = (f32[2,2,128,2048]{3,2,1,0:T(8,128)}, bf16[128,1280]{1,0:T(8,128)(2,1)S(1)}) custom-call(s32[1]{0:T(128)} %bitcast.mine_ref, s32[1]{0:T(128)} %bitcast.1.spot_ref, s32[1]{0:T(128)} %bitcast.2.core_ref, bf16[64,8192]{1,0:T(8,128)(2,1)S(1)} %collective-permute-done.7.refs_0_, ...), custom_call_target="tpu_custom_call", output_to_operand_aliasing={{0}: (5, {})} | custom-call | flops 1 | bytes 1 | tf_op jit(solution)/shard_map/multiply/pallas_call | solution.py:198
  185.9 2.0 collective-permute-start.13
  187.9 6.2 %multiply.9 = (f32[2,2,128,2048]{3,2,1,0:T(8,128)}, bf16[128,768]{1,0:T(8,128)(2,1)S(1)}) custom-call(s32[1]{0:T(128)} %bitcast.mine_ref, s32[1]{0:T(128)} %bitcast.1.spot_ref, s32[1]{0:T(128)} %bitcast.2.core_ref, bf16[64,8192]{1,0:T(8,128)(2,1)S(1)} %collective-permute-done.7.refs_0_, ...), custom_call_target="tpu_custom_call", output_to_operand_aliasing={{0}: (5, {})} | custom-call | flops 1 | bytes 1 | tf_op jit(solution)/shard_map/multiply/pallas_call | solution.py:198
  194.1 1.9 collective-permute-start.15
  196.0 0.1 place.7.refs_1_
  196.0 0.1 place.8.refs_2_
  196.1 4.3 %collective-permute-done.15.refs_1_ = bf16[128,768]{1,0:T(8,128)(2,1)S(1)} collective-permute-done((bf16[128,768]{1,0:T(8,128)(2,1)S(1)}, bf16[128,768]{1,0:T(8,128)(2,1)S(1)}, u32[]{:S(2)}, u32[]{:S(2)}) %collective-permute-start.15) | collective-permute-done | bytes 196640 | tf_op jit(solution)/shard_map/ppermute | solution.py:337
  200.4 0.1 place.9
  (18 shorter events, 0.0 us)
Async XLA Ops:
  0.0 5.4 %collective-permute-start.1 = (bf16[128,8192]{1,0:T(8,128)(2,1)}, bf16[128,8192]{1,0:T(8,128)(2,1)S(1)}, u32[]{:S(2)}, u32[]{:S(2)}) collective-permute-start(bf16[128,8192]{1,0:T(8,128)(2,1)} %mine_ref.1), channel_id=1, source_target_pairs={{0,2},{2,0},{4,6},{6,4},{8,10},{10,8},{12,14},{14,12},{1,3},{3,1},... | collective-permute-start | bytes 6291464 | tf_op jit(solution)/shard_map/ppermute | solution.py:328
  0.5 49.5 %collective-permute-start = (bf16[128,8192]{1,0:T(8,128)(2,1)}, bf16[128,8192]{1,0:T(8,128)(2,1)}, u32[]{:S(2)}, u32[]{:S(2)}) collective-permute-start(bf16[128,8192]{1,0:T(8,128)(2,1)} %mine_ref.1), channel_id=1, source_target_pairs={{0,8},{2,10},{8,12},{10,14},{12,4},{14,6},{4,0},{6,2},{1,9},{3,11}... | collective-permute-start | bytes 6291464 | tf_op jit(solution)/shard_map/ppermute | solution.py:324
  5.4 1.6 copy-start.2
  7.0 0.8 copy-start.5
  7.8 46.8 %copy-start.6 = (f32[8192]{0:T(1024)S(1)}, f32[8192]{0:T(1024)}, u32[]{:S(2)}) copy-start(f32[8192]{0:T(1024)} %param.7) | copy-start | bytes 98308
  36.9 1.3 copy-start.3
  38.3 1.0 copy-start.9
  49.9 4.7 %collective-permute-start.3 = (bf16[128,8192]{1,0:T(8,128)(2,1)}, bf16[128,8192]{1,0:T(8,128)(2,1)}, u32[]{:S(2)}, u32[]{:S(2)}) collective-permute-start(bf16[128,8192]{1,0:T(8,128)(2,1)} %collective-permute-done.refs_0_), channel_id=1, source_target_pairs={{0,2},{2,0},{4,6},{6,4},{8,10},{10,8},{12,14},{14,12},{1,3},{3,1},... | collective-permute-start | bytes 6291464 | tf_op jit(solution)/shard_map/ppermute | solution.py:328
  49.9 49.3 %collective-permute-start.2 = (bf16[128,8192]{1,0:T(8,128)(2,1)}, bf16[128,8192]{1,0:T(8,128)(2,1)S(1)}, u32[]{:S(2)}, u32[]{:S(2)}) collective-permute-start(bf16[128,8192]{1,0:T(8,128)(2,1)} %collective-permute-done.refs_0_), channel_id=1, source_target_pairs={{0,8},{2,10},{8,12},{10,14},{12,4},{14,6},{4,0},{6,2},{1,9},{3,11}... | collective-permute-start | bytes 6291464 | tf_op jit(solution)/shard_map/ppermute | solution.py:324
  53.3 28.2 %collective-permute-start.4 = (bf16[256,2048]{1,0:T(8,128)(2,1)}, bf16[256,2048]{1,0:T(8,128)(2,1)}, u32[]{:S(2)}, u32[]{:S(2)}) collective-permute-start(bf16[256,2048]{1,0:T(8,128)(2,1)} %copy-done.9), channel_id=1, source_target_pairs={{1,0},{3,2},{5,4},{7,6},{8,9},{10,11},{12,13},{14,15},{17,16},{19,... | collective-permute-start | bytes 3145736 | tf_op jit(solution)/shard_map/ppermute | solution.py:337
  70.8 32.4 %collective-permute-start.5 = (bf16[256,2048]{1,0:T(8,128)(2,1)}, bf16[256,2048]{1,0:T(8,128)(2,1)S(1)}, u32[]{:S(2)}, u32[]{:S(2)}) collective-permute-start(bf16[256,2048]{1,0:T(8,128)(2,1)} %get-tuple-element.37), channel_id=1, source_target_pairs={{1,0},{3,2},{4,5},{6,7},{9,8},{11,10},{12,13},{14,15},{17,16},{19,... | collective-permute-start | bytes 3145736 | tf_op jit(solution)/shard_map/ppermute | solution.py:337
  81.5 1.6 copy-start.4
  103.2 1.0 copy-start.7
  104.1 4.3 %collective-permute-start.6 = (bf16[128,8192]{1,0:T(8,128)(2,1)S(1)}, bf16[128,8192]{1,0:T(8,128)(2,1)}, u32[]{:S(2)}, u32[]{:S(2)}) collective-permute-start(bf16[128,8192]{1,0:T(8,128)(2,1)S(1)} %collective-permute-done.2.whole_ref.refs_0_), channel_id=1, source_target_pairs={{0,2},{2,0},{4,6},{6,4},{8,10},{10,8},{12,14},{14,12},{1,3},{3,1},... | collective-permute-start | bytes 6291464 | tf_op jit(solution)/shard_map/ppermute | solution.py:328
  104.1 27.2 %collective-permute-start.8 = (bf16[64,8192]{1,0:T(8,128)(2,1)}, bf16[64,8192]{1,0:T(8,128)(2,1)S(1)}, u32[]{:S(2)}, u32[]{:S(2)}) collective-permute-start(bf16[64,8192]{1,0:T(8,128)(2,1)} %get-tuple-element.43), channel_id=1, source_target_pairs={{0,8},{2,10},{8,12},{10,14},{12,4},{14,6},{4,0},{6,2},{1,9},{3,11}... | collective-permute-start | bytes 3145736 | tf_op jit(solution)/shard_map/ppermute | solution.py:324
  108.4 19.8 %copy-start.8 = (bf16[256,2048]{1,0:T(8,128)(2,1)S(1)}, bf16[256,2048]{1,0:T(8,128)(2,1)}, u32[]{:S(2)}) copy-start(bf16[256,2048]{1,0:T(8,128)(2,1)} %copy-done.7) | copy-start | bytes 3145732
  124.0 38.7 %collective-permute-start.7 = (bf16[64,8192]{1,0:T(8,128)(2,1)}, bf16[64,8192]{1,0:T(8,128)(2,1)S(1)}, u32[]{:S(2)}, u32[]{:S(2)}) collective-permute-start(bf16[64,8192]{1,0:T(8,128)(2,1)} %get-tuple-element.47), channel_id=1, source_target_pairs={{0,8},{2,10},{8,12},{10,14},{12,4},{14,6},{4,0},{6,2},{1,9},{3,11}... | collective-permute-start | bytes 3145736 | tf_op jit(solution)/shard_map/ppermute | solution.py:324
  124.8 37.9 %collective-permute-start.11 = (bf16[256,2048]{1,0:T(8,128)(2,1)}, bf16[256,2048]{1,0:T(8,128)(2,1)S(1)}, u32[]{:S(2)}, u32[]{:S(2)}) collective-permute-start(bf16[256,2048]{1,0:T(8,128)(2,1)} %get-tuple-element.46), channel_id=1, source_target_pairs={{0,1},{2,3},{4,5},{6,7},{9,8},{11,10},{13,12},{15,14},{16,17},{18,... | collective-permute-start | bytes 3145736 | tf_op jit(solution)/shard_map/ppermute | solution.py:337
  132.4 2.3 %collective-permute-start.9 = (bf16[32,8192]{1,0:T(8,128)(2,1)}, bf16[32,8192]{1,0:T(8,128)(2,1)}, u32[]{:S(2)}, u32[]{:S(2)}) collective-permute-start(bf16[32,8192]{1,0:T(8,128)(2,1)} %get-tuple-element.51), channel_id=1, source_target_pairs={{0,2},{2,0},{4,6},{6,4},{8,10},{10,8},{12,14},{14,12},{1,3},{3,1},... | collective-permute-start | bytes 1572872 | tf_op jit(solution)/shard_map/ppermute | solution.py:328
  132.4 3.0 %collective-permute-start.10 = (bf16[32,8192]{1,0:T(8,128)(2,1)}, bf16[32,8192]{1,0:T(8,128)(2,1)}, u32[]{:S(2)}, u32[]{:S(2)}) collective-permute-start(bf16[32,8192]{1,0:T(8,128)(2,1)} %get-tuple-element.52), channel_id=1, source_target_pairs={{0,2},{2,0},{4,6},{6,4},{8,10},{10,8},{12,14},{14,12},{1,3},{3,1},... | collective-permute-start | bytes 1572872 | tf_op jit(solution)/shard_map/ppermute | solution.py:328
  135.4 10.5 %copy-start = (bf16[2048,8192]{1,0:T(8,128)(2,1)S(1)}, bf16[2048,8192]{1,0:T(8,128)(2,1)}, u32[]{:S(2)}) copy-start(bf16[2048,8192]{1,0:T(8,128)(2,1)} %get-tuple-element.36.refs_3_.refs_4_.refs_5_) | copy-start | bytes 100663296
  162.7 2.7 %collective-permute-start.12 = (bf16[64,8192]{1,0:T(8,128)(2,1)S(1)}, bf16[64,8192]{1,0:T(8,128)(2,1)S(1)}, u32[]{:S(2)}, u32[]{:S(2)}) collective-permute-start(bf16[64,8192]{1,0:T(8,128)(2,1)S(1)} %collective-permute-done.7.refs_0_), channel_id=1, source_target_pairs={{0,2},{2,0},{4,6},{6,4},{8,10},{10,8},{12,14},{14,12},{1,3},{3,1},... | collective-permute-start | bytes 3145736 | tf_op jit(solution)/shard_map/ppermute | solution.py:328
  162.9 25.0 %collective-permute-start.14 = (bf16[128,2048]{1,0:T(8,128)(2,1)S(1)}, bf16[128,2048]{1,0:T(8,128)(2,1)S(1)}, u32[]{:S(2)}, u32[]{:S(2)}) collective-permute-start(bf16[128,2048]{1,0:T(8,128)(2,1)S(1)} %get-tuple-element.53), channel_id=1, source_target_pairs={{0,1},{2,3},{5,4},{7,6},{8,9},{10,11},{13,12},{15,14},{16,17},{18,... | collective-permute-start | bytes 1572872 | tf_op jit(solution)/shard_map/ppermute | solution.py:337
  165.4 10.5 %copy-start.1 = (bf16[2048,8192]{1,0:T(8,128)(2,1)S(1)}, bf16[2048,8192]{1,0:T(8,128)(2,1)}, u32[]{:S(2)}) copy-start(bf16[2048,8192]{1,0:T(8,128)(2,1)} %get-tuple-element.36.refs_3_.refs_4_.refs_5_) | copy-start | bytes 100663296
  185.9 14.5 %collective-permute-start.13 = (bf16[128,1280]{1,0:T(8,128)(2,1)S(1)}, bf16[128,1280]{1,0:T(8,128)(2,1)S(1)}, u32[]{:S(2)}, u32[]{:S(2)}) collective-permute-start(bf16[128,1280]{1,0:T(8,128)(2,1)S(1)} %get-tuple-element.56), channel_id=1, source_target_pairs={{0,1},{2,3},{5,4},{7,6},{8,9},{10,11},{13,12},{15,14},{16,17},{18,... | collective-permute-start | bytes 983048 | tf_op jit(solution)/shard_map/ppermute | solution.py:337
  194.1 6.3 %collective-permute-start.15 = (bf16[128,768]{1,0:T(8,128)(2,1)S(1)}, bf16[128,768]{1,0:T(8,128)(2,1)S(1)}, u32[]{:S(2)}, u32[]{:S(2)}) collective-permute-start(bf16[128,768]{1,0:T(8,128)(2,1)S(1)} %get-tuple-element.59), channel_id=1, source_target_pairs={{0,1},{2,3},{5,4},{7,6},{8,9},{10,11},{13,12},{15,14},{16,17},{18,... | collective-permute-start | bytes 589832 | tf_op jit(solution)/shard_map/ppermute | solution.py:337

commit v17 on v16

--- a/solution.py
+++ b/solution.py
@@ -154,10 +154,15 @@
     def _(i):
         for fetch in fetches(i):
             fetch.wait()
-        sums = lax.dot_general(
-            left[...], held[lax.rem(i, slots)], (((1,), (1,)), ((), ())),
-            preferred_element_type=jnp.float32,
-        )
+        block = held[lax.rem(i, slots)]
+        if cores * rows <= 128:
+            sums = lax.dot_general(
+                block, left[...], (((1,), (1,)), ((), ())), preferred_element_type=jnp.float32
+            ).T
+        else:
+            sums = lax.dot_general(
+                left[...], block, (((1,), (1,)), ((), ())), preferred_element_type=jnp.float32
+            )
 
         @pl.when(i >= 2)
         def _():
@@ -192,7 +197,6 @@
     tile = min(count, 256)
     slots = 3
     block = (cores * rows, count)
-    grant = 4 * block[0] * width + 2 * slots * tile * width + 12 * block[0] * tile + 2 * mib
     given = [] if scores is None else [scores]
     counts = (len(mine), len(other), len(given))
     return pl.pallas_call(
@@ -212,7 +216,7 @@
             pltpu.SemaphoreType.DMA((count // tile,)),
         ],
         input_output_aliases={3 + len(mine) + len(other): 0} if given else {},
-        compiler_params=pltpu.CompilerParams(vmem_limit_bytes=grant),
+        compiler_params=pltpu.CompilerParams(vmem_limit_bytes=22 * mib),
         cost_estimate=small,
         name="multiply",
     )(*where, core, *mine, *other, *given, fisher, train)

time: 204 us -> 185 us (0.907)
  local copies, waits for them, and re-layouts: 29.8 us -> 8.71 us
  starting transfers between devices: 20.9 us -> 25.9 us
  Pallas kernels: 102 us -> 99.5 us
    unnamed x21 -> x17, local copies, waits for them, and re-layouts: 29.8 us -> 8.71 us
    ppermute x6, starting transfers between devices: 11.2 us -> 16.4 us  [exchange(): received.append(lax.ppermute(send, ('blk', 'dim'), pairs))]
    pallas_call x5, Pallas kernels: 64.5 us -> 61.8 us  [multiply(): pl.pallas_call(functools.partial(multiply_kernel, counts, start, top), in...]
    ppermute x4, waiting for transfers between devices: 23.8 us -> 26.3 us  [shift(): return lax.ppermute(panel, 'blk', pairs)]
  transfers between devices with their start and end apart: 16 -> 16, of which waited for: 9 -> 9; matrix products, arithmetic and copies ran while one was open for 1% -> 1% of each run, Pallas kernels for 51% -> 54%
where the time goes in v17:
time: 185 us; the launch traced here: 183 us
  Pallas kernels  99.5 us (54%)
  waiting for transfers between devices  48.1 us (26%)
  starting transfers between devices  25.9 us (14%)
  local copies, waits for them, and re-layouts  8.71 us (5%)
    pallas_call x5, Pallas kernels, multiply(): pl.pallas_call(functools.partial(multiply_kernel, counts, start, top), in...  61.8 us
    pallas_call x1, Pallas kernels, first(): pl.pallas_call(first_kernel, grid=(count // tile,), in_specs=[in_smem, pl...  29.1 us
    ppermute x4, waiting for transfers between devices, shift(): return lax.ppermute(panel, 'blk', pairs)  26.3 us
    ppermute x6, starting transfers between devices, exchange(): received.append(lax.ppermute(send, ('blk', 'dim'), pairs))  16.4 us
    ppermute x6, waiting for transfers between devices, exchange(): received.append(lax.ppermute(send, ('blk', 'dim'), pairs))  15.8 us
    unnamed x17, local copies, waits for them, and re-layouts  8.71 us
    ppermute x4, starting transfers between devices, shift(): return lax.ppermute(panel, 'blk', pairs)  8.58 us
    pallas_call x5, Pallas kernels, place(): pl.pallas_call(functools.partial(place_kernel, start, cols, len(kept)), i...  6.13 us
  transfers between devices with their start and end apart: 16, of which 9 were waited for; matrix products, arithmetic and copies ran while one was open for 1% of the time, Pallas kernels for 54%

profile of v17, /device:TPU:0, one launch (start us, length us, event | category | flops | bytes accessed | tf_op | source)
XLA Modules:
  0.0 182.6 jit_solution(1156546499608168434)
XLA Ops:
  0.0 0.5 collective-permute-start.1
  0.5 3.6 %collective-permute-start = (bf16[128,8192]{1,0:T(8,128)(2,1)}, bf16[128,8192]{1,0:T(8,128)(2,1)}, u32[]{:S(2)}, u32[]{:S(2)}) collective-permute-start(bf16[128,8192]{1,0:T(8,128)(2,1)} %mine_ref.1), channel_id=1, source_target_pairs={{0,8},{2,10},{8,12},{10,14},{12,4},{14,6},{4,0},{6,2},{1,9},{3,11}... | collective-permute-start | bytes 6291464 | tf_op jit(solution)/shard_map/ppermute | solution.py:328
  4.0 1.4 copy.14.exps_ref
  5.4 0.0 copy-start
  5.4 1.6 copy-done
  7.0 0.8 copy-done.3
  7.8 29.1 %first.1 = (bf16[2048,8192]{1,0:T(8,128)(2,1)}, f32[256,2048]{1,0:T(8,128)S(1)}, bf16[256,2048]{1,0:T(8,128)(2,1)S(1)}) custom-call(s32[1]{0:T(128)} %bitcast.2.core_ref, bf16[128,8192]{1,0:T(8,128)(2,1)S(1)} %copy-done, bf16[128,8192]{1,0:T(8,128)(2,1)S(1)} %collective-permute-done.1.other_ref, f32[1,8192]{1,0:T(1,128)S(1)} %bitcast.11, ...), custom_call_target="tpu_custom_call" | custom-call | flops 1 | bytes 1 | tf_op jit(solution)/shard_map/first/pallas_call | solution.py:59
  36.9 1.4 copy-done.1
  38.3 1.1 copy-done.7
  39.3 10.6 %collective-permute-done.refs_0_ = bf16[128,8192]{1,0:T(8,128)(2,1)} collective-permute-done((bf16[128,8192]{1,0:T(8,128)(2,1)}, bf16[128,8192]{1,0:T(8,128)(2,1)}, u32[]{:S(2)}, u32[]{:S(2)}) %collective-permute-start) | collective-permute-done | bytes 2097184 | tf_op jit(solution)/shard_map/ppermute | solution.py:328
  49.9 0.0 collective-permute-start.3
  49.9 3.4 %collective-permute-start.2 = (bf16[128,8192]{1,0:T(8,128)(2,1)}, bf16[128,8192]{1,0:T(8,128)(2,1)S(1)}, u32[]{:S(2)}, u32[]{:S(2)}) collective-permute-start(bf16[128,8192]{1,0:T(8,128)(2,1)} %collective-permute-done.refs_0_), channel_id=1, source_target_pairs={{0,8},{2,10},{8,12},{10,14},{12,4},{14,6},{4,0},{6,2},{1,9},{3,11}... | collective-permute-start | bytes 6291464 | tf_op jit(solution)/shard_map/ppermute | solution.py:328
  53.3 1.3 collective-permute-start.4
  54.6 0.0 collective-permute-done.3.refs_1_
  54.6 16.2 %multiply.5 = (f32[2,2,128,2048]{3,2,1,0:T(8,128)}, bf16[256,2048]{1,0:T(8,128)(2,1)}) custom-call(s32[1]{0:T(128)} %bitcast.4.mine_ref, s32[1]{0:T(128)} %bitcast.5.spot_ref, s32[1]{0:T(128)} %bitcast.2.core_ref, bf16[128,8192]{1,0:T(8,128)(2,1)} %collective-permute-done.refs_0_, bf16[128,8192]{1,0:T(8,128)(2,1)} %collective-permute-done.3.refs_1_, ...), custom_call_target="tpu_custom_call" | custom-call | flops 1 | bytes 1 | tf_op jit(solution)/shard_map/multiply/pallas_call | solution.py:202
  70.8 1.3 collective-permute-start.5
  72.1 9.4 %collective-permute-done.4.refs_1_ = bf16[256,2048]{1,0:T(8,128)(2,1)} collective-permute-done((bf16[256,2048]{1,0:T(8,128)(2,1)}, bf16[256,2048]{1,0:T(8,128)(2,1)}, u32[]{:S(2)}, u32[]{:S(2)}) %collective-permute-start.4) | collective-permute-done | bytes 1048608 | tf_op jit(solution)/shard_map/ppermute | solution.py:341
  81.5 1.6 copy-done.2
  83.1 2.9 %place.5.refs_2_ = f32[2,2,128,2048]{3,2,1,0:T(8,128)} custom-call(s32[1]{0:T(128)} %bitcast.6.mine_ref, s32[1]{0:T(128)} %bitcast.7.spot_ref, f32[256,2048]{1,0:T(8,128)S(1)} %copy-done.2, bf16[256,2048]{1,0:T(8,128)(2,1)} %collective-permute-done.4.refs_1_, f32[2,2,128,2048]{3,2,1,0:T(8,128)} %get-tuple-element.40.refs_2_), custom_call_target="tpu_custom_call", output_to_operand_aliasing={{}: (4, {})} | custom-call | flops 1 | bytes 1 | tf_op jit(solution)/shard_map/place/pallas_call | solution.py:265
  86.0 13.2 %collective-permute-done.2.whole_ref.refs_0_ = bf16[128,8192]{1,0:T(8,128)(2,1)S(1)} collective-permute-done((bf16[128,8192]{1,0:T(8,128)(2,1)}, bf16[128,8192]{1,0:T(8,128)(2,1)S(1)}, u32[]{:S(2)}, u32[]{:S(2)}) %collective-permute-start.2) | collective-permute-done | bytes 2097184 | tf_op jit(solution)/shard_map/ppermute | solution.py:328
  99.2 1.4 cut.2
  100.6 2.5 %collective-permute-done.5.refs_0_ = bf16[256,2048]{1,0:T(8,128)(2,1)S(1)} collective-permute-done((bf16[256,2048]{1,0:T(8,128)(2,1)}, bf16[256,2048]{1,0:T(8,128)(2,1)S(1)}, u32[]{:S(2)}, u32[]{:S(2)}) %collective-permute-start.5) | collective-permute-done | bytes 1048608 | tf_op jit(solution)/shard_map/ppermute | solution.py:341
  103.2 1.0 copy-done.5
  104.1 0.7 collective-permute-start.8
  104.9 3.5 %collective-permute-done.6.refs_1_ = bf16[128,8192]{1,0:T(8,128)(2,1)} collective-permute-done((bf16[128,8192]{1,0:T(8,128)(2,1)S(1)}, bf16[128,8192]{1,0:T(8,128)(2,1)}, u32[]{:S(2)}, u32[]{:S(2)}) %collective-permute-start.6) | collective-permute-done | bytes 2097184 | tf_op jit(solution)/shard_map/ppermute | solution.py:332
  108.4 15.5 %multiply.6 = (f32[2,2,128,2048]{3,2,1,0:T(8,128)}, bf16[256,2048]{1,0:T(8,128)(2,1)}) custom-call(s32[1]{0:T(128)} %bitcast.8.mine_ref, s32[1]{0:T(128)} %bitcast.9.spot_ref, s32[1]{0:T(128)} %bitcast.2.core_ref, bf16[128,8192]{1,0:T(8,128)(2,1)S(1)} %collective-permute-done.2.whole_ref.refs_0_, ...), custom_call_target="tpu_custom_call", output_to_operand_aliasing={{0}: (5, {})} | custom-call | flops 1 | bytes 1 | tf_op jit(solution)/shard_map/multiply/pallas_call | solution.py:202
  124.0 0.9 collective-permute-start.7
  124.8 3.4 %collective-permute-start.11 = (bf16[256,2048]{1,0:T(8,128)(2,1)}, bf16[256,2048]{1,0:T(8,128)(2,1)S(1)}, u32[]{:S(2)}, u32[]{:S(2)}) collective-permute-start(bf16[256,2048]{1,0:T(8,128)(2,1)} %get-tuple-element.46), channel_id=1, source_target_pairs={{0,1},{2,3},{4,5},{6,7},{9,8},{11,10},{13,12},{15,14},{16,17},{18,... | collective-permute-start | bytes 3145736 | tf_op jit(solution)/shard_map/ppermute | solution.py:341
  128.2 3.1 %place.6.refs_3_ = f32[2,2,128,2048]{3,2,1,0:T(8,128)} custom-call(s32[1]{0:T(128)} %bitcast.4.mine_ref, s32[1]{0:T(128)} %bitcast.5.spot_ref, bf16[256,2048]{1,0:T(8,128)(2,1)S(1)} %copy-done.6, f32[2,2,128,2048]{3,2,1,0:T(8,128)} %get-tuple-element.49.refs_1_), custom_call_target="tpu_custom_call", output_to_operand_aliasing={{}: (3, {})} | custom-call | flops 1 | bytes 1 | tf_op jit(solution)/shard_map/place/pallas_call | solution.py:265
  131.3 0.0 collective-permute-done.8.whole_ref.refs_0_
  131.3 1.1 cut.3
  132.4 0.5 collective-permute-start.10
  132.9 1.7 collective-permute-done.9.refs_1_
  134.6 0.7 collective-permute-done.10.refs_2_
  135.4 14.5 %multiply.7 = (f32[2,2,128,2048]{3,2,1,0:T(8,128)}, bf16[128,2048]{1,0:T(8,128)(2,1)S(1)}) custom-call(s32[1]{0:T(128)} %bitcast.mine_ref, s32[1]{0:T(128)} %bitcast.1.spot_ref, s32[1]{0:T(128)} %bitcast.2.core_ref, bf16[64,8192]{1,0:T(8,128)(2,1)S(1)} %collective-permute-done.8.whole_ref.refs_0_, ...), custom_call_target="tpu_custom_call", output_to_operand_aliasing={{0}: (6, {})} | custom-call | flops 1 | bytes 1 | tf_op jit(solution)/shard_map/multiply/pallas_call | solution.py:202
  149.9 2.5 %collective-permute-done.7.refs_0_ = bf16[64,8192]{1,0:T(8,128)(2,1)S(1)} collective-permute-done((bf16[64,8192]{1,0:T(8,128)(2,1)}, bf16[64,8192]{1,0:T(8,128)(2,1)S(1)}, u32[]{:S(2)}, u32[]{:S(2)}) %collective-permute-start.7) | collective-permute-done | bytes 1048608 | tf_op jit(solution)/shard_map/ppermute | solution.py:328
  152.4 0.0 collective-permute-done.11.refs_0_
  152.4 0.0 collective-permute-start.12
  152.4 2.8 %collective-permute-start.14 = (bf16[128,2048]{1,0:T(8,128)(2,1)S(1)}, bf16[128,2048]{1,0:T(8,128)(2,1)S(1)}, u32[]{:S(2)}, u32[]{:S(2)}) collective-permute-start(bf16[128,2048]{1,0:T(8,128)(2,1)S(1)} %get-tuple-element.53), channel_id=1, source_target_pairs={{0,1},{2,3},{5,4},{7,6},{8,9},{10,11},{13,12},{15,14},{16,17},{18,... | collective-permute-start | bytes 1572872 | tf_op jit(solution)/shard_map/ppermute | solution.py:341
  155.2 9.2 %multiply.8 = (f32[2,2,128,2048]{3,2,1,0:T(8,128)}, bf16[128,1280]{1,0:T(8,128)(2,1)S(1)}) custom-call(s32[1]{0:T(128)} %bitcast.mine_ref, s32[1]{0:T(128)} %bitcast.1.spot_ref, s32[1]{0:T(128)} %bitcast.2.core_ref, bf16[64,8192]{1,0:T(8,128)(2,1)S(1)} %collective-permute-done.7.refs_0_, ...), custom_call_target="tpu_custom_call", output_to_operand_aliasing={{0}: (5, {})} | custom-call | flops 1 | bytes 1 | tf_op jit(solution)/shard_map/multiply/pallas_call | solution.py:202
  164.4 3.3 %collective-permute-start.13 = (bf16[128,1280]{1,0:T(8,128)(2,1)S(1)}, bf16[128,1280]{1,0:T(8,128)(2,1)S(1)}, u32[]{:S(2)}, u32[]{:S(2)}) collective-permute-start(bf16[128,1280]{1,0:T(8,128)(2,1)S(1)} %get-tuple-element.56), channel_id=1, source_target_pairs={{0,1},{2,3},{5,4},{7,6},{8,9},{10,11},{13,12},{15,14},{16,17},{18,... | collective-permute-start | bytes 983048 | tf_op jit(solution)/shard_map/ppermute | solution.py:341
  167.7 0.0 collective-permute-done.14.refs_0_
  167.7 6.4 %multiply.9 = (f32[2,2,128,2048]{3,2,1,0:T(8,128)}, bf16[128,768]{1,0:T(8,128)(2,1)S(1)}) custom-call(s32[1]{0:T(128)} %bitcast.mine_ref, s32[1]{0:T(128)} %bitcast.1.spot_ref, s32[1]{0:T(128)} %bitcast.2.core_ref, bf16[64,8192]{1,0:T(8,128)(2,1)S(1)} %collective-permute-done.7.refs_0_, ...), custom_call_target="tpu_custom_call", output_to_operand_aliasing={{0}: (5, {})} | custom-call | flops 1 | bytes 1 | tf_op jit(solution)/shard_map/multiply/pallas_call | solution.py:202
  174.1 4.3 %collective-permute-start.15 = (bf16[128,768]{1,0:T(8,128)(2,1)S(1)}, bf16[128,768]{1,0:T(8,128)(2,1)S(1)}, u32[]{:S(2)}, u32[]{:S(2)}) collective-permute-start(bf16[128,768]{1,0:T(8,128)(2,1)S(1)} %get-tuple-element.59), channel_id=1, source_target_pairs={{0,1},{2,3},{5,4},{7,6},{8,9},{10,11},{13,12},{15,14},{16,17},{18,... | collective-permute-start | bytes 589832 | tf_op jit(solution)/shard_map/ppermute | solution.py:341
  178.5 0.1 place.7.refs_1_
  178.5 0.1 place.8.refs_2_
  178.6 3.9 %collective-permute-done.15.refs_1_ = bf16[128,768]{1,0:T(8,128)(2,1)S(1)} collective-permute-done((bf16[128,768]{1,0:T(8,128)(2,1)S(1)}, bf16[128,768]{1,0:T(8,128)(2,1)S(1)}, u32[]{:S(2)}, u32[]{:S(2)}) %collective-permute-start.15) | collective-permute-done | bytes 196640 | tf_op jit(solution)/shard_map/ppermute | solution.py:341
  182.5 0.1 place.9
  (14 shorter events, 0.0 us)
Async XLA Ops:
  0.0 5.4 %collective-permute-start.1 = (bf16[128,8192]{1,0:T(8,128)(2,1)}, bf16[128,8192]{1,0:T(8,128)(2,1)S(1)}, u32[]{:S(2)}, u32[]{:S(2)}) collective-permute-start(bf16[128,8192]{1,0:T(8,128)(2,1)} %mine_ref.1), channel_id=1, source_target_pairs={{0,2},{2,0},{4,6},{6,4},{8,10},{10,8},{12,14},{14,12},{1,3},{3,1},... | collective-permute-start | bytes 6291464 | tf_op jit(solution)/shard_map/ppermute | solution.py:332
  0.5 49.5 %collective-permute-start = (bf16[128,8192]{1,0:T(8,128)(2,1)}, bf16[128,8192]{1,0:T(8,128)(2,1)}, u32[]{:S(2)}, u32[]{:S(2)}) collective-permute-start(bf16[128,8192]{1,0:T(8,128)(2,1)} %mine_ref.1), channel_id=1, source_target_pairs={{0,8},{2,10},{8,12},{10,14},{12,4},{14,6},{4,0},{6,2},{1,9},{3,11}... | collective-permute-start | bytes 6291464 | tf_op jit(solution)/shard_map/ppermute | solution.py:328
  5.4 1.6 copy-start
  7.0 0.8 copy-start.3
  7.8 46.8 %copy-start.4 = (f32[8192]{0:T(1024)S(1)}, f32[8192]{0:T(1024)}, u32[]{:S(2)}) copy-start(f32[8192]{0:T(1024)} %param.7) | copy-start | bytes 98308
  36.9 1.4 copy-start.1
  38.3 1.1 copy-start.7
  49.9 4.7 %collective-permute-start.3 = (bf16[128,8192]{1,0:T(8,128)(2,1)}, bf16[128,8192]{1,0:T(8,128)(2,1)}, u32[]{:S(2)}, u32[]{:S(2)}) collective-permute-start(bf16[128,8192]{1,0:T(8,128)(2,1)} %collective-permute-done.refs_0_), channel_id=1, source_target_pairs={{0,2},{2,0},{4,6},{6,4},{8,10},{10,8},{12,14},{14,12},{1,3},{3,1},... | collective-permute-start | bytes 6291464 | tf_op jit(solution)/shard_map/ppermute | solution.py:332
  49.9 49.3 %collective-permute-start.2 = (bf16[128,8192]{1,0:T(8,128)(2,1)}, bf16[128,8192]{1,0:T(8,128)(2,1)S(1)}, u32[]{:S(2)}, u32[]{:S(2)}) collective-permute-start(bf16[128,8192]{1,0:T(8,128)(2,1)} %collective-permute-done.refs_0_), channel_id=1, source_target_pairs={{0,8},{2,10},{8,12},{10,14},{12,4},{14,6},{4,0},{6,2},{1,9},{3,11}... | collective-permute-start | bytes 6291464 | tf_op jit(solution)/shard_map/ppermute | solution.py:328
  53.3 28.2 %collective-permute-start.4 = (bf16[256,2048]{1,0:T(8,128)(2,1)}, bf16[256,2048]{1,0:T(8,128)(2,1)}, u32[]{:S(2)}, u32[]{:S(2)}) collective-permute-start(bf16[256,2048]{1,0:T(8,128)(2,1)} %copy-done.7), channel_id=1, source_target_pairs={{1,0},{3,2},{5,4},{7,6},{8,9},{10,11},{12,13},{14,15},{17,16},{19,... | collective-permute-start | bytes 3145736 | tf_op jit(solution)/shard_map/ppermute | solution.py:341
  70.8 32.4 %collective-permute-start.5 = (bf16[256,2048]{1,0:T(8,128)(2,1)}, bf16[256,2048]{1,0:T(8,128)(2,1)S(1)}, u32[]{:S(2)}, u32[]{:S(2)}) collective-permute-start(bf16[256,2048]{1,0:T(8,128)(2,1)} %get-tuple-element.37), channel_id=1, source_target_pairs={{1,0},{3,2},{4,5},{6,7},{9,8},{11,10},{12,13},{14,15},{17,16},{19,... | collective-permute-start | bytes 3145736 | tf_op jit(solution)/shard_map/ppermute | solution.py:341
  81.5 1.6 copy-start.2
  103.2 1.0 copy-start.5
  104.1 4.3 %collective-permute-start.6 = (bf16[128,8192]{1,0:T(8,128)(2,1)S(1)}, bf16[128,8192]{1,0:T(8,128)(2,1)}, u32[]{:S(2)}, u32[]{:S(2)}) collective-permute-start(bf16[128,8192]{1,0:T(8,128)(2,1)S(1)} %collective-permute-done.2.whole_ref.refs_0_), channel_id=1, source_target_pairs={{0,2},{2,0},{4,6},{6,4},{8,10},{10,8},{12,14},{14,12},{1,3},{3,1},... | collective-permute-start | bytes 6291464 | tf_op jit(solution)/shard_map/ppermute | solution.py:332
  104.1 27.2 %collective-permute-start.8 = (bf16[64,8192]{1,0:T(8,128)(2,1)}, bf16[64,8192]{1,0:T(8,128)(2,1)S(1)}, u32[]{:S(2)}, u32[]{:S(2)}) collective-permute-start(bf16[64,8192]{1,0:T(8,128)(2,1)} %get-tuple-element.43), channel_id=1, source_target_pairs={{0,8},{2,10},{8,12},{10,14},{12,4},{14,6},{4,0},{6,2},{1,9},{3,11}... | collective-permute-start | bytes 3145736 | tf_op jit(solution)/shard_map/ppermute | solution.py:328
  108.4 19.8 %copy-start.6 = (bf16[256,2048]{1,0:T(8,128)(2,1)S(1)}, bf16[256,2048]{1,0:T(8,128)(2,1)}, u32[]{:S(2)}) copy-start(bf16[256,2048]{1,0:T(8,128)(2,1)} %copy-done.5) | copy-start | bytes 3145732
  124.0 28.4 %collective-permute-start.7 = (bf16[64,8192]{1,0:T(8,128)(2,1)}, bf16[64,8192]{1,0:T(8,128)(2,1)S(1)}, u32[]{:S(2)}, u32[]{:S(2)}) collective-permute-start(bf16[64,8192]{1,0:T(8,128)(2,1)} %get-tuple-element.47), channel_id=1, source_target_pairs={{0,8},{2,10},{8,12},{10,14},{12,4},{14,6},{4,0},{6,2},{1,9},{3,11}... | collective-permute-start | bytes 3145736 | tf_op jit(solution)/shard_map/ppermute | solution.py:328
  124.8 27.6 %collective-permute-start.11 = (bf16[256,2048]{1,0:T(8,128)(2,1)}, bf16[256,2048]{1,0:T(8,128)(2,1)S(1)}, u32[]{:S(2)}, u32[]{:S(2)}) collective-permute-start(bf16[256,2048]{1,0:T(8,128)(2,1)} %get-tuple-element.46), channel_id=1, source_target_pairs={{0,1},{2,3},{4,5},{6,7},{9,8},{11,10},{13,12},{15,14},{16,17},{18,... | collective-permute-start | bytes 3145736 | tf_op jit(solution)/shard_map/ppermute | solution.py:341
  132.4 2.3 %collective-permute-start.9 = (bf16[32,8192]{1,0:T(8,128)(2,1)}, bf16[32,8192]{1,0:T(8,128)(2,1)}, u32[]{:S(2)}, u32[]{:S(2)}) collective-permute-start(bf16[32,8192]{1,0:T(8,128)(2,1)} %get-tuple-element.51), channel_id=1, source_target_pairs={{0,2},{2,0},{4,6},{6,4},{8,10},{10,8},{12,14},{14,12},{1,3},{3,1},... | collective-permute-start | bytes 1572872 | tf_op jit(solution)/shard_map/ppermute | solution.py:332
  132.4 3.0 %collective-permute-start.10 = (bf16[32,8192]{1,0:T(8,128)(2,1)}, bf16[32,8192]{1,0:T(8,128)(2,1)}, u32[]{:S(2)}, u32[]{:S(2)}) collective-permute-start(bf16[32,8192]{1,0:T(8,128)(2,1)} %get-tuple-element.52), channel_id=1, source_target_pairs={{0,2},{2,0},{4,6},{6,4},{8,10},{10,8},{12,14},{14,12},{1,3},{3,1},... | collective-permute-start | bytes 1572872 | tf_op jit(solution)/shard_map/ppermute | solution.py:332
  152.4 2.8 %collective-permute-start.12 = (bf16[64,8192]{1,0:T(8,128)(2,1)S(1)}, bf16[64,8192]{1,0:T(8,128)(2,1)S(1)}, u32[]{:S(2)}, u32[]{:S(2)}) collective-permute-start(bf16[64,8192]{1,0:T(8,128)(2,1)S(1)} %collective-permute-done.7.refs_0_), channel_id=1, source_target_pairs={{0,2},{2,0},{4,6},{6,4},{8,10},{10,8},{12,14},{14,12},{1,3},{3,1},... | collective-permute-start | bytes 3145736 | tf_op jit(solution)/shard_map/ppermute | solution.py:332
  152.4 15.3 %collective-permute-start.14 = (bf16[128,2048]{1,0:T(8,128)(2,1)S(1)}, bf16[128,2048]{1,0:T(8,128)(2,1)S(1)}, u32[]{:S(2)}, u32[]{:S(2)}) collective-permute-start(bf16[128,2048]{1,0:T(8,128)(2,1)S(1)} %get-tuple-element.53), channel_id=1, source_target_pairs={{0,1},{2,3},{5,4},{7,6},{8,9},{10,11},{13,12},{15,14},{16,17},{18,... | collective-permute-start | bytes 1572872 | tf_op jit(solution)/shard_map/ppermute | solution.py:341
  164.4 18.1 %collective-permute-start.13 = (bf16[128,1280]{1,0:T(8,128)(2,1)S(1)}, bf16[128,1280]{1,0:T(8,128)(2,1)S(1)}, u32[]{:S(2)}, u32[]{:S(2)}) collective-permute-start(bf16[128,1280]{1,0:T(8,128)(2,1)S(1)} %get-tuple-element.56), channel_id=1, source_target_pairs={{0,1},{2,3},{5,4},{7,6},{8,9},{10,11},{13,12},{15,14},{16,17},{18,... | collective-permute-start | bytes 983048 | tf_op jit(solution)/shard_map/ppermute | solution.py:341
  174.1 8.4 %collective-permute-start.15 = (bf16[128,768]{1,0:T(8,128)(2,1)S(1)}, bf16[128,768]{1,0:T(8,128)(2,1)S(1)}, u32[]{:S(2)}, u32[]{:S(2)}) collective-permute-start(bf16[128,768]{1,0:T(8,128)(2,1)S(1)} %get-tuple-element.59), channel_id=1, source_target_pairs={{0,1},{2,3},{5,4},{7,6},{8,9},{10,11},{13,12},{15,14},{16,17},{18,... | collective-permute-start | bytes 589832 | tf_op jit(solution)/shard_map/ppermute | solution.py:341

commit v18 on v17

--- a/solution.py
+++ b/solution.py
@@ -320,9 +320,9 @@
         [ring[(ring.index(z) - hop) % chips] for z in range(chips)] for hop in range(chips)
     ]
 
-    def shift(panel):
+    def shift(panel, by=1):
         pairs = [
-            (ring[place] * cores + c, ring[(place + 1) % chips] * cores + c)
+            (ring[place] * cores + c, ring[(place + by) % chips] * cores + c)
             for place in range(chips) for c in range(cores)
         ]
         return lax.ppermute(panel, "blk", pairs)
@@ -349,16 +349,15 @@
     hops = chips - 1
     flow = shift(val_grads)
     train, keep, send = first(core, val_grads, *swap([val_grads]), fisher, grad_codes, scale_exps)
+    low_piece, high_piece = cut(after(val_grads, send), 2)
     scores, kept = None, [keep]
     for hop in range(1, hops):
         received = exchange(send, hop - 1)
-        panel = after(flow, send, *([] if scores is None else [scores]))
+        panel = after(flow, send, *([] if scores is None else [scores, low_piece]))
         if hop + 1 < hops:
             flow = shift(panel)
         else:
-            low_piece, high_piece = cut(panel, 2)
-            flow = shift(low_piece)
-            panel = after(panel, low_piece)
+            flow = shift(after(low_piece, panel), -1)
         if hop > 1:
             panel = after(panel, *received)
         scores, send = multiply(
@@ -368,14 +367,14 @@
         scores = place(scores, whose(hop - 1), kept, received, [0] * len(received), 0)
         kept = []
     earlier = exchange(send, hops - 1)
-    high_flow = shift(after(high_piece, send))
+    high_flow = shift(after(high_piece, send), -1)
     low_piece = after(flow, send, scores)
     scores, send = multiply(
         scores, shape, whose(hops), core, [low_piece], swap(cut(low_piece, 2)), fisher, train, 0
     )
     received = exchange(send, hops)
     high_piece = after(high_flow, send, *earlier)
-    high_other = swap([high_piece])
+    high_other = swap(cut(high_piece, max(1, min(4, high_piece.shape[0] // 16))))
     knee = count * 5 // 8
     halves = []
     for top, bottom in ((0, knee), (knee, count)):

time: 185 us -> 182 us (0.984)
  starting transfers between devices: 25.9 us -> 20.2 us
  local copies, waits for them, and re-layouts: 8.71 us -> 11.7 us
    ppermute x6, starting transfers between devices: 16.4 us -> 11.1 us  [exchange(): received.append(lax.ppermute(send, ('blk', 'dim'), pairs))]
    unnamed x17 -> x23, local copies, waits for them, and re-layouts: 8.71 us -> 11.7 us
    ppermute x6 -> x9, waiting for transfers between devices: 6.05 us -> 8.59 us  [swap(): return [lax.ppermute(part, 'blk', pairs) for part in parts]]
    ppermute x6, waiting for transfers between devices: 15.8 us -> 13.8 us  [exchange(): received.append(lax.ppermute(send, ('blk', 'dim'), pairs))]
  transfers between devices with their start and end apart: 16 -> 19, of which waited for: 9 -> 13; matrix products, arithmetic and copies ran while one was open for 1% -> 1% of each run, Pallas kernels for 54% -> 55%
where the time goes in v18:
time: 182 us; the launch traced here: 179 us
  Pallas kernels  99.6 us (55%)
  waiting for transfers between devices  47.5 us (26%)
  starting transfers between devices  20.2 us (11%)
  local copies, waits for them, and re-layouts  11.7 us (6%)
    pallas_call x5, Pallas kernels, multiply(): pl.pallas_call(functools.partial(multiply_kernel, counts, start, top), in...  61.8 us
    pallas_call x1, Pallas kernels, first(): pl.pallas_call(first_kernel, grid=(count // tile,), in_specs=[in_smem, pl...  29.1 us
    ppermute x4, waiting for transfers between devices, shift(): return lax.ppermute(panel, 'blk', pairs)  25.2 us
    ppermute x6, waiting for transfers between devices, exchange(): received.append(lax.ppermute(send, ('blk', 'dim'), pairs))  13.8 us
    unnamed x23, local copies, waits for them, and re-layouts  11.7 us
    ppermute x6, starting transfers between devices, exchange(): received.append(lax.ppermute(send, ('blk', 'dim'), pairs))  11.1 us
    ppermute x9, waiting for transfers between devices, swap(): return [lax.ppermute(part, 'blk', pairs) for part in parts]  8.59 us
    ppermute x4, starting transfers between devices, shift(): return lax.ppermute(panel, 'blk', pairs)  7.03 us
  transfers between devices with their start and end apart: 19, of which 13 were waited for; matrix products, arithmetic and copies ran while one was open for 1% of the time, Pallas kernels for 55%

profile of v18, /device:TPU:0, one launch (start us, length us, event | category | flops | bytes accessed | tf_op | source)
XLA Modules:
  0.0 179.4 jit_solution(11366704115701949037)
XLA Ops:
  0.0 0.5 collective-permute-start
  0.5 3.6 %collective-permute-start.1 = (bf16[128,8192]{1,0:T(8,128)(2,1)}, bf16[128,8192]{1,0:T(8,128)(2,1)}, u32[]{:S(2)}, u32[]{:S(2)}) collective-permute-start(bf16[128,8192]{1,0:T(8,128)(2,1)} %whole_ref), channel_id=1, source_target_pairs={{0,8},{2,10},{8,12},{10,14},{12,4},{14,6},{4,0},{6,2},{1,9},{3,11}... | collective-permute-start | bytes 6291464 | tf_op jit(solution)/shard_map/ppermute | solution.py:328
  4.0 1.4 copy.14.exps_ref
  5.4 1.6 copy-done
  7.0 0.8 copy-done.6
  7.8 29.1 %first.1 = (bf16[2048,8192]{1,0:T(8,128)(2,1)}, f32[256,2048]{1,0:T(8,128)S(1)}, bf16[256,2048]{1,0:T(8,128)(2,1)S(1)}) custom-call(s32[1]{0:T(128)} %bitcast.2.core_ref, bf16[128,8192]{1,0:T(8,128)(2,1)S(1)} %copy-done, bf16[128,8192]{1,0:T(8,128)(2,1)S(1)} %collective-permute-done.other_ref, f32[1,8192]{1,0:T(1,128)S(1)} %bitcast.11, ...), custom_call_target="tpu_custom_call" | custom-call | flops 1 | bytes 1 | tf_op jit(solution)/shard_map/first/pallas_call | solution.py:59
  36.9 1.3 copy-done.4
  38.2 1.0 copy-done.10
  39.2 10.7 %collective-permute-done.1.refs_0_ = bf16[128,8192]{1,0:T(8,128)(2,1)} collective-permute-done((bf16[128,8192]{1,0:T(8,128)(2,1)}, bf16[128,8192]{1,0:T(8,128)(2,1)}, u32[]{:S(2)}, u32[]{:S(2)}) %collective-permute-start.1) | collective-permute-done | bytes 2097184 | tf_op jit(solution)/shard_map/ppermute | solution.py:328
  49.9 3.4 %collective-permute-start.2 = (bf16[128,8192]{1,0:T(8,128)(2,1)}, bf16[128,8192]{1,0:T(8,128)(2,1)}, u32[]{:S(2)}, u32[]{:S(2)}) collective-permute-start(bf16[128,8192]{1,0:T(8,128)(2,1)} %collective-permute-done.1.refs_0_), channel_id=1, source_target_pairs={{0,8},{2,10},{8,12},{10,14},{12,4},{14,6},{4,0},{6,2},{1,9},{3,11}... | collective-permute-start | bytes 6291464 | tf_op jit(solution)/shard_map/ppermute | solution.py:328
  53.3 1.3 collective-permute-start.4
  54.6 1.3 copy-done.2
  55.9 1.6 copy-done.3
  57.5 15.7 %multiply.5 = (f32[2,2,128,2048]{3,2,1,0:T(8,128)}, bf16[256,2048]{1,0:T(8,128)(2,1)}) custom-call(s32[1]{0:T(128)} %bitcast.6.mine_ref, s32[1]{0:T(128)} %bitcast.7.spot_ref, s32[1]{0:T(128)} %bitcast.2.core_ref, bf16[128,8192]{1,0:T(8,128)(2,1)} %collective-permute-done.1.refs_0_, bf16[128,8192]{1,0:T(8,128)(2,1)S(1)} %copy-done.3, ...), custom_call_target="tpu_custom_call" | custom-call | flops 1 | bytes 1 | tf_op jit(solution)/shard_map/multiply/pallas_call | solution.py:202
  73.2 1.3 collective-permute-start.5
  74.5 1.4 cut.3
  76.0 5.5 %collective-permute-done.4.refs_1_ = bf16[256,2048]{1,0:T(8,128)(2,1)} collective-permute-done((bf16[256,2048]{1,0:T(8,128)(2,1)}, bf16[256,2048]{1,0:T(8,128)(2,1)}, u32[]{:S(2)}, u32[]{:S(2)}) %collective-permute-start.4) | collective-permute-done | bytes 1048608 | tf_op jit(solution)/shard_map/ppermute | solution.py:341
  81.5 1.6 copy-done.5
  83.1 2.9 %place.5.refs_2_ = f32[2,2,128,2048]{3,2,1,0:T(8,128)} custom-call(s32[1]{0:T(128)} %bitcast.8.mine_ref, s32[1]{0:T(128)} %bitcast.9.spot_ref, f32[256,2048]{1,0:T(8,128)S(1)} %copy-done.5, bf16[256,2048]{1,0:T(8,128)(2,1)} %collective-permute-done.4.refs_1_, f32[2,2,128,2048]{3,2,1,0:T(8,128)} %get-tuple-element.47.refs_2_), custom_call_target="tpu_custom_call", output_to_operand_aliasing={{}: (4, {})} | custom-call | flops 1 | bytes 1 | tf_op jit(solution)/shard_map/place/pallas_call | solution.py:265
  86.0 13.2 %collective-permute-done.2.refs_0_ = bf16[128,8192]{1,0:T(8,128)(2,1)} collective-permute-done((bf16[128,8192]{1,0:T(8,128)(2,1)}, bf16[128,8192]{1,0:T(8,128)(2,1)}, u32[]{:S(2)}, u32[]{:S(2)}) %collective-permute-start.2) | collective-permute-done | bytes 2097184 | tf_op jit(solution)/shard_map/ppermute | solution.py:328
  99.2 4.0 %collective-permute-done.5.refs_0_ = bf16[256,2048]{1,0:T(8,128)(2,1)S(1)} collective-permute-done((bf16[256,2048]{1,0:T(8,128)(2,1)}, bf16[256,2048]{1,0:T(8,128)(2,1)S(1)}, u32[]{:S(2)}, u32[]{:S(2)}) %collective-permute-start.5) | collective-permute-done | bytes 1048608 | tf_op jit(solution)/shard_map/ppermute | solution.py:341
  103.2 4.5 %collective-permute-done.6.refs_1_ = bf16[128,8192]{1,0:T(8,128)(2,1)} collective-permute-done((bf16[128,8192]{1,0:T(8,128)(2,1)}, bf16[128,8192]{1,0:T(8,128)(2,1)}, u32[]{:S(2)}, u32[]{:S(2)}) %collective-permute-start.6) | collective-permute-done | bytes 2097184 | tf_op jit(solution)/shard_map/ppermute | solution.py:332
  107.7 16.0 %multiply.6 = (f32[2,2,128,2048]{3,2,1,0:T(8,128)}, bf16[256,2048]{1,0:T(8,128)(2,1)}) custom-call(s32[1]{0:T(128)} %bitcast.4.mine_ref, s32[1]{0:T(128)} %bitcast.5.spot_ref, s32[1]{0:T(128)} %bitcast.2.core_ref, bf16[128,8192]{1,0:T(8,128)(2,1)} %collective-permute-done.2.refs_0_, ...), custom_call_target="tpu_custom_call", output_to_operand_aliasing={{0}: (5, {})} | custom-call | flops 1 | bytes 1 | tf_op jit(solution)/shard_map/multiply/pallas_call | solution.py:202
  123.7 0.1 collective-permute-start.7
  123.8 3.0 %collective-permute-start.11 = (bf16[256,2048]{1,0:T(8,128)(2,1)}, bf16[256,2048]{1,0:T(8,128)(2,1)S(1)}, u32[]{:S(2)}, u32[]{:S(2)}) collective-permute-start(bf16[256,2048]{1,0:T(8,128)(2,1)} %get-tuple-element.51), channel_id=1, source_target_pairs={{0,1},{2,3},{4,5},{6,7},{9,8},{11,10},{13,12},{15,14},{16,17},{18,... | collective-permute-start | bytes 3145736 | tf_op jit(solution)/shard_map/ppermute | solution.py:341
  126.8 1.2 copy-done.9
  128.0 3.1 %place.6.refs_3_ = f32[2,2,128,2048]{3,2,1,0:T(8,128)} custom-call(s32[1]{0:T(128)} %bitcast.6.mine_ref, s32[1]{0:T(128)} %bitcast.7.spot_ref, bf16[256,2048]{1,0:T(8,128)(2,1)S(1)} %copy-done.9, f32[2,2,128,2048]{3,2,1,0:T(8,128)} %get-tuple-element.55.refs_1_), custom_call_target="tpu_custom_call", output_to_operand_aliasing={{}: (3, {})} | custom-call | flops 1 | bytes 1 | tf_op jit(solution)/shard_map/place/pallas_call | solution.py:265
  131.1 1.1 cut.4
  132.1 0.5 collective-permute-start.10
  132.6 1.7 collective-permute-done.9.refs_1_
  134.4 0.7 collective-permute-done.10.refs_2_
  135.1 14.5 %multiply.7 = (f32[2,2,128,2048]{3,2,1,0:T(8,128)}, bf16[128,2048]{1,0:T(8,128)(2,1)S(1)}) custom-call(s32[1]{0:T(128)} %bitcast.mine_ref, s32[1]{0:T(128)} %bitcast.1.spot_ref, s32[1]{0:T(128)} %bitcast.2.core_ref, bf16[64,8192]{1,0:T(8,128)(2,1)S(1)} %collective-permute-done.8.whole_ref.refs_0_, ...), custom_call_target="tpu_custom_call", output_to_operand_aliasing={{0}: (6, {})} | custom-call | flops 1 | bytes 1 | tf_op jit(solution)/shard_map/multiply/pallas_call | solution.py:202
  149.6 1.4 collective-permute-start.17
  151.1 1.3 collective-permute-done.7.whole_ref.refs_0_
  152.3 0.1 cut.5
  152.4 0.1 collective-permute-start.12
  152.5 0.5 collective-permute-start.13
  153.0 0.1 collective-permute-start.14
  153.0 0.4 collective-permute-start.15
  153.5 0.5 collective-permute-done.12.refs_1_
  154.0 0.4 collective-permute-done.13.refs_2_
  154.4 0.4 collective-permute-done.14.refs_3_
  154.7 0.4 collective-permute-done.15.refs_4_
  155.1 9.2 %multiply.8 = (f32[2,2,128,2048]{3,2,1,0:T(8,128)}, bf16[128,1280]{1,0:T(8,128)(2,1)S(1)}) custom-call(s32[1]{0:T(128)} %bitcast.mine_ref, s32[1]{0:T(128)} %bitcast.1.spot_ref, s32[1]{0:T(128)} %bitcast.2.core_ref, bf16[64,8192]{1,0:T(8,128)(2,1)S(1)} %collective-permute-done.7.whole_ref.refs_0_, ...), custom_call_target="tpu_custom_call", output_to_operand_aliasing={{0}: (8, {})} | custom-call | flops 1 | bytes 1 | tf_op jit(solution)/shard_map/multiply/pallas_call | solution.py:202
  164.3 2.2 %collective-permute-start.16 = (bf16[128,1280]{1,0:T(8,128)(2,1)S(1)}, bf16[128,1280]{1,0:T(8,128)(2,1)S(1)}, u32[]{:S(2)}, u32[]{:S(2)}) collective-permute-start(bf16[128,1280]{1,0:T(8,128)(2,1)S(1)} %get-tuple-element.66), channel_id=1, source_target_pairs={{0,1},{2,3},{5,4},{7,6},{8,9},{10,11},{13,12},{15,14},{16,17},{18,... | collective-permute-start | bytes 983048 | tf_op jit(solution)/shard_map/ppermute | solution.py:341
  166.5 6.4 %multiply.9 = (f32[2,2,128,2048]{3,2,1,0:T(8,128)}, bf16[128,768]{1,0:T(8,128)(2,1)S(1)}) custom-call(s32[1]{0:T(128)} %bitcast.mine_ref, s32[1]{0:T(128)} %bitcast.1.spot_ref, s32[1]{0:T(128)} %bitcast.2.core_ref, bf16[64,8192]{1,0:T(8,128)(2,1)S(1)} %collective-permute-done.7.whole_ref.refs_0_, ...), custom_call_target="tpu_custom_call", output_to_operand_aliasing={{0}: (8, {})} | custom-call | flops 1 | bytes 1 | tf_op jit(solution)/shard_map/multiply/pallas_call | solution.py:202
  173.0 1.9 %collective-permute-start.18 = (bf16[128,768]{1,0:T(8,128)(2,1)S(1)}, bf16[128,768]{1,0:T(8,128)(2,1)S(1)}, u32[]{:S(2)}, u32[]{:S(2)}) collective-permute-start(bf16[128,768]{1,0:T(8,128)(2,1)S(1)} %get-tuple-element.69), channel_id=1, source_target_pairs={{0,1},{2,3},{5,4},{7,6},{8,9},{10,11},{13,12},{15,14},{16,17},{18,... | collective-permute-start | bytes 589832 | tf_op jit(solution)/shard_map/ppermute | solution.py:341
  175.0 4.3 %collective-permute-done.18.refs_1_ = bf16[128,768]{1,0:T(8,128)(2,1)S(1)} collective-permute-done((bf16[128,768]{1,0:T(8,128)(2,1)S(1)}, bf16[128,768]{1,0:T(8,128)(2,1)S(1)}, u32[]{:S(2)}, u32[]{:S(2)}) %collective-permute-start.18) | collective-permute-done | bytes 196640 | tf_op jit(solution)/shard_map/ppermute | solution.py:341
  (27 shorter events, 0.2 us)
Async XLA Ops:
  0.0 5.4 %collective-permute-start = (bf16[128,8192]{1,0:T(8,128)(2,1)}, bf16[128,8192]{1,0:T(8,128)(2,1)S(1)}, u32[]{:S(2)}, u32[]{:S(2)}) collective-permute-start(bf16[128,8192]{1,0:T(8,128)(2,1)} %whole_ref), channel_id=1, source_target_pairs={{0,2},{2,0},{4,6},{6,4},{8,10},{10,8},{12,14},{14,12},{1,3},{3,1},... | collective-permute-start | bytes 6291464 | tf_op jit(solution)/shard_map/ppermute | solution.py:332
  0.5 49.5 %collective-permute-start.1 = (bf16[128,8192]{1,0:T(8,128)(2,1)}, bf16[128,8192]{1,0:T(8,128)(2,1)}, u32[]{:S(2)}, u32[]{:S(2)}) collective-permute-start(bf16[128,8192]{1,0:T(8,128)(2,1)} %whole_ref), channel_id=1, source_target_pairs={{0,8},{2,10},{8,12},{10,14},{12,4},{14,6},{4,0},{6,2},{1,9},{3,11}... | collective-permute-start | bytes 6291464 | tf_op jit(solution)/shard_map/ppermute | solution.py:328
  5.4 1.6 copy-start
  7.0 0.8 copy-start.6
  7.8 48.2 %copy-start.7 = (f32[8192]{0:T(1024)S(1)}, f32[8192]{0:T(1024)}, u32[]{:S(2)}) copy-start(f32[8192]{0:T(1024)} %param.7) | copy-start | bytes 98308
  36.9 1.3 copy-start.4
  38.2 1.0 copy-start.10
  49.9 4.7 %collective-permute-start.3 = (bf16[128,8192]{1,0:T(8,128)(2,1)}, bf16[128,8192]{1,0:T(8,128)(2,1)S(1)}, u32[]{:S(2)}, u32[]{:S(2)}) collective-permute-start(bf16[128,8192]{1,0:T(8,128)(2,1)} %collective-permute-done.1.refs_0_), channel_id=1, source_target_pairs={{0,2},{2,0},{4,6},{6,4},{8,10},{10,8},{12,14},{14,12},{1,3},{3,1},... | collective-permute-start | bytes 6291464 | tf_op jit(solution)/shard_map/ppermute | solution.py:332
  49.9 49.3 %collective-permute-start.2 = (bf16[128,8192]{1,0:T(8,128)(2,1)}, bf16[128,8192]{1,0:T(8,128)(2,1)}, u32[]{:S(2)}, u32[]{:S(2)}) collective-permute-start(bf16[128,8192]{1,0:T(8,128)(2,1)} %collective-permute-done.1.refs_0_), channel_id=1, source_target_pairs={{0,8},{2,10},{8,12},{10,14},{12,4},{14,6},{4,0},{6,2},{1,9},{3,11}... | collective-permute-start | bytes 6291464 | tf_op jit(solution)/shard_map/ppermute | solution.py:328
  53.3 28.2 %collective-permute-start.4 = (bf16[256,2048]{1,0:T(8,128)(2,1)}, bf16[256,2048]{1,0:T(8,128)(2,1)}, u32[]{:S(2)}, u32[]{:S(2)}) collective-permute-start(bf16[256,2048]{1,0:T(8,128)(2,1)} %copy-done.10), channel_id=1, source_target_pairs={{1,0},{3,2},{5,4},{7,6},{8,9},{10,11},{12,13},{14,15},{17,16},{19,... | collective-permute-start | bytes 3145736 | tf_op jit(solution)/shard_map/ppermute | solution.py:341
  54.6 1.3 copy-start.2
  55.9 1.6 copy-start.3
  57.5 17.0 %copy-start.1 = (bf16[128,8192]{1,0:T(8,128)(2,1)S(1)}, bf16[128,8192]{1,0:T(8,128)(2,1)}, u32[]{:S(2)}) copy-start(bf16[128,8192]{1,0:T(8,128)(2,1)} %whole_ref) | copy-start | bytes 6291460
  73.2 30.0 %collective-permute-start.5 = (bf16[256,2048]{1,0:T(8,128)(2,1)}, bf16[256,2048]{1,0:T(8,128)(2,1)S(1)}, u32[]{:S(2)}, u32[]{:S(2)}) collective-permute-start(bf16[256,2048]{1,0:T(8,128)(2,1)} %get-tuple-element.44), channel_id=1, source_target_pairs={{1,0},{3,2},{4,5},{6,7},{9,8},{11,10},{12,13},{14,15},{17,16},{19,... | collective-permute-start | bytes 3145736 | tf_op jit(solution)/shard_map/ppermute | solution.py:341
  81.5 1.6 copy-start.5
  103.2 20.6 %copy-start.8 = (bf16[256,2048]{1,0:T(8,128)(2,1)}, bf16[256,2048]{1,0:T(8,128)(2,1)S(1)}, u32[]{:S(2)}) copy-start(bf16[256,2048]{1,0:T(8,128)(2,1)S(1)} %collective-permute-done.5.refs_0_) | copy-start | bytes 3145732
  103.2 4.5 %collective-permute-start.6 = (bf16[128,8192]{1,0:T(8,128)(2,1)}, bf16[128,8192]{1,0:T(8,128)(2,1)}, u32[]{:S(2)}, u32[]{:S(2)}) collective-permute-start(bf16[128,8192]{1,0:T(8,128)(2,1)} %collective-permute-done.2.refs_0_), channel_id=1, source_target_pairs={{0,2},{2,0},{4,6},{6,4},{8,10},{10,8},{12,14},{14,12},{1,3},{3,1},... | collective-permute-start | bytes 6291464 | tf_op jit(solution)/shard_map/ppermute | solution.py:332
  103.2 27.9 %collective-permute-start.8 = (bf16[64,8192]{1,0:T(8,128)(2,1)}, bf16[64,8192]{1,0:T(8,128)(2,1)S(1)}, u32[]{:S(2)}, u32[]{:S(2)}) collective-permute-start(bf16[64,8192]{1,0:T(8,128)(2,1)} %get-tuple-element.53), channel_id=1, source_target_pairs={{0,4},{2,6},{8,0},{10,2},{12,8},{14,10},{4,12},{6,14},{1,5},{3,7},... | collective-permute-start | bytes 3145736 | tf_op jit(solution)/shard_map/ppermute | solution.py:328
  123.7 28.6 %collective-permute-start.7 = (bf16[64,8192]{1,0:T(8,128)(2,1)}, bf16[64,8192]{1,0:T(8,128)(2,1)S(1)}, u32[]{:S(2)}, u32[]{:S(2)}) collective-permute-start(bf16[64,8192]{1,0:T(8,128)(2,1)} %get-tuple-element.52), channel_id=1, source_target_pairs={{0,4},{2,6},{8,0},{10,2},{12,8},{14,10},{4,12},{6,14},{1,5},{3,7},... | collective-permute-start | bytes 3145736 | tf_op jit(solution)/shard_map/ppermute | solution.py:328
  123.8 28.5 %collective-permute-start.11 = (bf16[256,2048]{1,0:T(8,128)(2,1)}, bf16[256,2048]{1,0:T(8,128)(2,1)S(1)}, u32[]{:S(2)}, u32[]{:S(2)}) collective-permute-start(bf16[256,2048]{1,0:T(8,128)(2,1)} %get-tuple-element.51), channel_id=1, source_target_pairs={{0,1},{2,3},{4,5},{6,7},{9,8},{11,10},{13,12},{15,14},{16,17},{18,... | collective-permute-start | bytes 3145736 | tf_op jit(solution)/shard_map/ppermute | solution.py:341
  126.8 1.2 copy-start.9
  132.1 2.3 %collective-permute-start.9 = (bf16[32,8192]{1,0:T(8,128)(2,1)}, bf16[32,8192]{1,0:T(8,128)(2,1)}, u32[]{:S(2)}, u32[]{:S(2)}) collective-permute-start(bf16[32,8192]{1,0:T(8,128)(2,1)} %get-tuple-element.57), channel_id=1, source_target_pairs={{0,2},{2,0},{4,6},{6,4},{8,10},{10,8},{12,14},{14,12},{1,3},{3,1},... | collective-permute-start | bytes 1572872 | tf_op jit(solution)/shard_map/ppermute | solution.py:332
  132.1 3.0 %collective-permute-start.10 = (bf16[32,8192]{1,0:T(8,128)(2,1)}, bf16[32,8192]{1,0:T(8,128)(2,1)}, u32[]{:S(2)}, u32[]{:S(2)}) collective-permute-start(bf16[32,8192]{1,0:T(8,128)(2,1)} %get-tuple-element.58), channel_id=1, source_target_pairs={{0,2},{2,0},{4,6},{6,4},{8,10},{10,8},{12,14},{14,12},{1,3},{3,1},... | collective-permute-start | bytes 1572872 | tf_op jit(solution)/shard_map/ppermute | solution.py:332
  149.6 16.9 %collective-permute-start.17 = (bf16[128,2048]{1,0:T(8,128)(2,1)S(1)}, bf16[128,2048]{1,0:T(8,128)(2,1)S(1)}, u32[]{:S(2)}, u32[]{:S(2)}) collective-permute-start(bf16[128,2048]{1,0:T(8,128)(2,1)S(1)} %get-tuple-element.59), channel_id=1, source_target_pairs={{0,1},{2,3},{5,4},{7,6},{8,9},{10,11},{13,12},{15,14},{16,17},{18,... | collective-permute-start | bytes 1572872 | tf_op jit(solution)/shard_map/ppermute | solution.py:341
  152.4 1.6 collective-permute-start.12
  152.5 1.9 %collective-permute-start.13 = (bf16[16,8192]{1,0:T(8,128)(2,1)S(1)}, bf16[16,8192]{1,0:T(8,128)(2,1)S(1)}, u32[]{:S(2)}, u32[]{:S(2)}) collective-permute-start(bf16[16,8192]{1,0:T(8,128)(2,1)S(1)} %get-tuple-element.62), channel_id=1, source_target_pairs={{0,2},{2,0},{4,6},{6,4},{8,10},{10,8},{12,14},{14,12},{1,3},{3,1},... | collective-permute-start | bytes 786440 | tf_op jit(solution)/shard_map/ppermute | solution.py:332
  153.0 1.8 collective-permute-start.14
  153.0 2.1 %collective-permute-start.15 = (bf16[16,8192]{1,0:T(8,128)(2,1)S(1)}, bf16[16,8192]{1,0:T(8,128)(2,1)S(1)}, u32[]{:S(2)}, u32[]{:S(2)}) collective-permute-start(bf16[16,8192]{1,0:T(8,128)(2,1)S(1)} %get-tuple-element.64), channel_id=1, source_target_pairs={{0,2},{2,0},{4,6},{6,4},{8,10},{10,8},{12,14},{14,12},{1,3},{3,1},... | collective-permute-start | bytes 786440 | tf_op jit(solution)/shard_map/ppermute | solution.py:332
  164.3 15.0 %collective-permute-start.16 = (bf16[128,1280]{1,0:T(8,128)(2,1)S(1)}, bf16[128,1280]{1,0:T(8,128)(2,1)S(1)}, u32[]{:S(2)}, u32[]{:S(2)}) collective-permute-start(bf16[128,1280]{1,0:T(8,128)(2,1)S(1)} %get-tuple-element.66), channel_id=1, source_target_pairs={{0,1},{2,3},{5,4},{7,6},{8,9},{10,11},{13,12},{15,14},{16,17},{18,... | collective-permute-start | bytes 983048 | tf_op jit(solution)/shard_map/ppermute | solution.py:341
  173.0 6.3 %collective-permute-start.18 = (bf16[128,768]{1,0:T(8,128)(2,1)S(1)}, bf16[128,768]{1,0:T(8,128)(2,1)S(1)}, u32[]{:S(2)}, u32[]{:S(2)}) collective-permute-start(bf16[128,768]{1,0:T(8,128)(2,1)S(1)} %get-tuple-element.69), channel_id=1, source_target_pairs={{0,1},{2,3},{5,4},{7,6},{8,9},{10,11},{13,12},{15,14},{16,17},{18,... | collective-permute-start | bytes 589832 | tf_op jit(solution)/shard_map/ppermute | solution.py:341

commit v19 on v18

--- a/solution.py
+++ b/solution.py
@@ -353,7 +353,7 @@
     scores, kept = None, [keep]
     for hop in range(1, hops):
         received = exchange(send, hop - 1)
-        panel = after(flow, send, *([] if scores is None else [scores, low_piece]))
+        panel = after(flow, send, low_piece, *([] if scores is None else [scores]))
         if hop + 1 < hops:
             flow = shift(panel)
         else:
@@ -375,7 +375,7 @@
     received = exchange(send, hops)
     high_piece = after(high_flow, send, *earlier)
     high_other = swap(cut(high_piece, max(1, min(4, high_piece.shape[0] // 16))))
-    knee = count * 5 // 8
+    knee = count * 3 // 4
     halves = []
     for top, bottom in ((0, knee), (knee, count)):
         if top:

time: 182 us -> 182 us (level)
  local copies, waits for them, and re-layouts: 11.7 us -> 7.51 us
  waiting for transfers between devices: 47.5 us -> 51.6 us
    ppermute x6, waiting for transfers between devices: 13.8 us -> 18.7 us  [exchange(): received.append(lax.ppermute(send, ('blk', 'dim'), pairs))]
    unnamed x23 -> x17, local copies, waits for them, and re-layouts: 11.7 us -> 7.51 us
  transfers between devices with their start and end apart: 19 -> 19, of which waited for: 13 -> 14; matrix products, arithmetic and copies ran while one was open for 1% -> 1% of each run, Pallas kernels for 55% -> 56%
where the time goes in v19:
time: 182 us; the launch traced here: 179 us
  Pallas kernels  100 us (55%)
  waiting for transfers between devices  51.6 us (28%)
  starting transfers between devices  19.7 us (11%)
  local copies, waits for them, and re-layouts  7.51 us (4%)
    pallas_call x5, Pallas kernels, multiply(): pl.pallas_call(functools.partial(multiply_kernel, counts, start, top), in...  61.6 us
    pallas_call x1, Pallas kernels, first(): pl.pallas_call(first_kernel, grid=(count // tile,), in_specs=[in_smem, pl...  29.8 us
    ppermute x4, waiting for transfers between devices, shift(): return lax.ppermute(panel, 'blk', pairs)  24.3 us
    ppermute x6, waiting for transfers between devices, exchange(): received.append(lax.ppermute(send, ('blk', 'dim'), pairs))  18.7 us
    ppermute x6, starting transfers between devices, exchange(): received.append(lax.ppermute(send, ('blk', 'dim'), pairs))  10.7 us
    ppermute x9, waiting for transfers between devices, swap(): return [lax.ppermute(part, 'blk', pairs) for part in parts]  8.59 us
    unnamed x17, local copies, waits for them, and re-layouts  7.51 us
    ppermute x4, starting transfers between devices, shift(): return lax.ppermute(panel, 'blk', pairs)  6.92 us
  transfers between devices with their start and end apart: 19, of which 14 were waited for; matrix products, arithmetic and copies ran while one was open for 1% of the time, Pallas kernels for 56%

profile of v19, /device:TPU:0, one launch (start us, length us, event | category | flops | bytes accessed | tf_op | source)
XLA Modules:
  0.0 179.3 jit_solution(11827769932535073979)
XLA Ops:
  0.0 0.5 collective-permute-start
  0.5 3.6 %collective-permute-start.1 = (bf16[128,8192]{1,0:T(8,128)(2,1)}, bf16[128,8192]{1,0:T(8,128)(2,1)S(1)}, u32[]{:S(2)}, u32[]{:S(2)}) collective-permute-start(bf16[128,8192]{1,0:T(8,128)(2,1)} %whole_ref), channel_id=1, source_target_pairs={{0,8},{2,10},{8,12},{10,14},{12,4},{14,6},{4,0},{6,2},{1,9},{3,11}... | collective-permute-start | bytes 6291464 | tf_op jit(solution)/shard_map/ppermute | solution.py:328
  4.0 1.4 copy.14.exps_ref
  5.4 1.6 copy-done
  7.0 0.8 copy-done.3
  7.8 29.8 %first.1 = (bf16[2048,8192]{1,0:T(8,128)(2,1)}, f32[256,2048]{1,0:T(8,128)S(1)}, bf16[256,2048]{1,0:T(8,128)(2,1)S(1)}) custom-call(s32[1]{0:T(128)} %bitcast.2.core_ref, bf16[128,8192]{1,0:T(8,128)(2,1)S(1)} %copy-done, bf16[128,8192]{1,0:T(8,128)(2,1)} %collective-permute-done.other_ref, f32[1,8192]{1,0:T(1,128)S(1)} %bitcast.11, ...), custom_call_target="tpu_custom_call" | custom-call | flops 1 | bytes 1 | tf_op jit(solution)/shard_map/first/pallas_call | solution.py:59
  37.6 1.0 copy-done.7
  38.6 1.5 cut.3
  40.1 9.8 %collective-permute-done.1.refs_0_ = bf16[128,8192]{1,0:T(8,128)(2,1)S(1)} collective-permute-done((bf16[128,8192]{1,0:T(8,128)(2,1)}, bf16[128,8192]{1,0:T(8,128)(2,1)S(1)}, u32[]{:S(2)}, u32[]{:S(2)}) %collective-permute-start.1) | collective-permute-done | bytes 2097184 | tf_op jit(solution)/shard_map/ppermute | solution.py:328
  49.9 3.3 %collective-permute-start.2 = (bf16[128,8192]{1,0:T(8,128)(2,1)S(1)}, bf16[128,8192]{1,0:T(8,128)(2,1)}, u32[]{:S(2)}, u32[]{:S(2)}) collective-permute-start(bf16[128,8192]{1,0:T(8,128)(2,1)S(1)} %collective-permute-done.1.refs_0_), channel_id=1, source_target_pairs={{0,8},{2,10},{8,12},{10,14},{12,4},{14,6},{4,0},{6,2},{1,9},{3,11}... | collective-permute-start | bytes 6291464 | tf_op jit(solution)/shard_map/ppermute | solution.py:328
  53.2 1.3 collective-permute-start.4
  54.5 15.5 %multiply.5 = (f32[2,2,128,2048]{3,2,1,0:T(8,128)}, bf16[256,2048]{1,0:T(8,128)(2,1)}) custom-call(s32[1]{0:T(128)} %bitcast.6.mine_ref, s32[1]{0:T(128)} %bitcast.7.spot_ref, s32[1]{0:T(128)} %bitcast.2.core_ref, bf16[128,8192]{1,0:T(8,128)(2,1)S(1)} %collective-permute-done.1.refs_0_, bf16[128,8192]{1,0:T(8,128)(2,1)} %collective-permute-done.3.refs_1_, ...), custom_call_target="tpu_custom_call" | custom-call | flops 1 | bytes 1 | tf_op jit(solution)/shard_map/multiply/pallas_call | solution.py:202
  70.0 1.3 collective-permute-start.5
  71.4 10.0 %collective-permute-done.4.refs_1_ = bf16[256,2048]{1,0:T(8,128)(2,1)} collective-permute-done((bf16[256,2048]{1,0:T(8,128)(2,1)}, bf16[256,2048]{1,0:T(8,128)(2,1)}, u32[]{:S(2)}, u32[]{:S(2)}) %collective-permute-start.4) | collective-permute-done | bytes 1048608 | tf_op jit(solution)/shard_map/ppermute | solution.py:341
  81.4 1.6 copy-done.2
  83.0 2.9 %place.5.refs_2_ = f32[2,2,128,2048]{3,2,1,0:T(8,128)} custom-call(s32[1]{0:T(128)} %bitcast.8.mine_ref, s32[1]{0:T(128)} %bitcast.9.spot_ref, f32[256,2048]{1,0:T(8,128)S(1)} %copy-done.2, bf16[256,2048]{1,0:T(8,128)(2,1)} %collective-permute-done.4.refs_1_, f32[2,2,128,2048]{3,2,1,0:T(8,128)} %get-tuple-element.48.refs_2_), custom_call_target="tpu_custom_call", output_to_operand_aliasing={{}: (4, {})} | custom-call | flops 1 | bytes 1 | tf_op jit(solution)/shard_map/place/pallas_call | solution.py:265
  85.9 12.9 %collective-permute-done.2.refs_0_ = bf16[128,8192]{1,0:T(8,128)(2,1)} collective-permute-done((bf16[128,8192]{1,0:T(8,128)(2,1)S(1)}, bf16[128,8192]{1,0:T(8,128)(2,1)}, u32[]{:S(2)}, u32[]{:S(2)}) %collective-permute-start.2) | collective-permute-done | bytes 2097184 | tf_op jit(solution)/shard_map/ppermute | solution.py:328
  98.8 4.3 %collective-permute-done.5.refs_0_ = bf16[256,2048]{1,0:T(8,128)(2,1)S(1)} collective-permute-done((bf16[256,2048]{1,0:T(8,128)(2,1)}, bf16[256,2048]{1,0:T(8,128)(2,1)S(1)}, u32[]{:S(2)}, u32[]{:S(2)}) %collective-permute-start.5) | collective-permute-done | bytes 1048608 | tf_op jit(solution)/shard_map/ppermute | solution.py:341
  103.1 4.5 %collective-permute-done.6.refs_1_ = bf16[128,8192]{1,0:T(8,128)(2,1)} collective-permute-done((bf16[128,8192]{1,0:T(8,128)(2,1)}, bf16[128,8192]{1,0:T(8,128)(2,1)}, u32[]{:S(2)}, u32[]{:S(2)}) %collective-permute-start.6) | collective-permute-done | bytes 2097184 | tf_op jit(solution)/shard_map/ppermute | solution.py:332
  107.6 16.0 %multiply.6 = (f32[2,2,128,2048]{3,2,1,0:T(8,128)}, bf16[256,2048]{1,0:T(8,128)(2,1)}) custom-call(s32[1]{0:T(128)} %bitcast.4.mine_ref, s32[1]{0:T(128)} %bitcast.5.spot_ref, s32[1]{0:T(128)} %bitcast.2.core_ref, bf16[128,8192]{1,0:T(8,128)(2,1)} %collective-permute-done.2.refs_0_, ...), custom_call_target="tpu_custom_call", output_to_operand_aliasing={{0}: (5, {})} | custom-call | flops 1 | bytes 1 | tf_op jit(solution)/shard_map/multiply/pallas_call | solution.py:202
  123.6 0.1 collective-permute-start.7
  123.7 1.8 collective-permute-start.11
  125.5 1.2 copy-done.6
  126.7 3.1 %place.6.refs_3_ = f32[2,2,128,2048]{3,2,1,0:T(8,128)} custom-call(s32[1]{0:T(128)} %bitcast.6.mine_ref, s32[1]{0:T(128)} %bitcast.7.spot_ref, bf16[256,2048]{1,0:T(8,128)(2,1)S(1)} %copy-done.6, f32[2,2,128,2048]{3,2,1,0:T(8,128)} %get-tuple-element.55.refs_1_), custom_call_target="tpu_custom_call", output_to_operand_aliasing={{}: (3, {})} | custom-call | flops 1 | bytes 1 | tf_op jit(solution)/shard_map/place/pallas_call | solution.py:265
  129.7 0.4 collective-permute-done.8.whole_ref.refs_0_
  130.1 1.1 cut.4
  131.2 0.5 collective-permute-start.10
  131.7 1.7 collective-permute-done.9.refs_1_
  133.4 0.7 collective-permute-done.10.refs_2_
  134.2 14.5 %multiply.7 = (f32[2,2,128,2048]{3,2,1,0:T(8,128)}, bf16[128,2048]{1,0:T(8,128)(2,1)S(1)}) custom-call(s32[1]{0:T(128)} %bitcast.mine_ref, s32[1]{0:T(128)} %bitcast.1.spot_ref, s32[1]{0:T(128)} %bitcast.2.core_ref, bf16[64,8192]{1,0:T(8,128)(2,1)S(1)} %collective-permute-done.8.whole_ref.refs_0_, ...), custom_call_target="tpu_custom_call", output_to_operand_aliasing={{0}: (6, {})} | custom-call | flops 1 | bytes 1 | tf_op jit(solution)/shard_map/multiply/pallas_call | solution.py:202
  148.7 2.3 %collective-permute-start.17 = (bf16[128,2048]{1,0:T(8,128)(2,1)S(1)}, bf16[128,2048]{1,0:T(8,128)(2,1)S(1)}, u32[]{:S(2)}, u32[]{:S(2)}) collective-permute-start(bf16[128,2048]{1,0:T(8,128)(2,1)S(1)} %get-tuple-element.59), channel_id=1, source_target_pairs={{0,1},{2,3},{5,4},{7,6},{8,9},{10,11},{13,12},{15,14},{16,17},{18,... | collective-permute-start | bytes 1572872 | tf_op jit(solution)/shard_map/ppermute | solution.py:341
  151.0 1.2 collective-permute-done.7.whole_ref.refs_0_
  152.2 0.1 cut.5
  152.3 0.1 collective-permute-start.12
  152.4 0.5 collective-permute-start.13
  152.9 0.1 collective-permute-start.14
  152.9 0.4 collective-permute-start.15
  153.4 0.5 collective-permute-done.12.refs_1_
  153.9 0.4 collective-permute-done.13.refs_2_
  154.3 0.4 collective-permute-done.14.refs_3_
  154.6 0.4 collective-permute-done.15.refs_4_
  155.0 10.5 %multiply.8 = (f32[2,2,128,2048]{3,2,1,0:T(8,128)}, bf16[128,1536]{1,0:T(8,128)(2,1)S(1)}) custom-call(s32[1]{0:T(128)} %bitcast.mine_ref, s32[1]{0:T(128)} %bitcast.1.spot_ref, s32[1]{0:T(128)} %bitcast.2.core_ref, bf16[64,8192]{1,0:T(8,128)(2,1)S(1)} %collective-permute-done.7.whole_ref.refs_0_, ...), custom_call_target="tpu_custom_call", output_to_operand_aliasing={{0}: (8, {})} | custom-call | flops 1 | bytes 1 | tf_op jit(solution)/shard_map/multiply/pallas_call | solution.py:202
  165.6 2.2 %collective-permute-start.16 = (bf16[128,1536]{1,0:T(8,128)(2,1)S(1)}, bf16[128,1536]{1,0:T(8,128)(2,1)S(1)}, u32[]{:S(2)}, u32[]{:S(2)}) collective-permute-start(bf16[128,1536]{1,0:T(8,128)(2,1)S(1)} %get-tuple-element.66), channel_id=1, source_target_pairs={{0,1},{2,3},{5,4},{7,6},{8,9},{10,11},{13,12},{15,14},{16,17},{18,... | collective-permute-start | bytes 1179656 | tf_op jit(solution)/shard_map/ppermute | solution.py:341
  167.8 5.0 %multiply.9 = (f32[2,2,128,2048]{3,2,1,0:T(8,128)}, bf16[128,512]{1,0:T(8,128)(2,1)S(1)}) custom-call(s32[1]{0:T(128)} %bitcast.mine_ref, s32[1]{0:T(128)} %bitcast.1.spot_ref, s32[1]{0:T(128)} %bitcast.2.core_ref, bf16[64,8192]{1,0:T(8,128)(2,1)S(1)} %collective-permute-done.7.whole_ref.refs_0_, ...), custom_call_target="tpu_custom_call", output_to_operand_aliasing={{0}: (8, {})} | custom-call | flops 1 | bytes 1 | tf_op jit(solution)/shard_map/multiply/pallas_call | solution.py:202
  172.9 1.9 %collective-permute-start.18 = (bf16[128,512]{1,0:T(8,128)(2,1)S(1)}, bf16[128,512]{1,0:T(8,128)(2,1)S(1)}, u32[]{:S(2)}, u32[]{:S(2)}) collective-permute-start(bf16[128,512]{1,0:T(8,128)(2,1)S(1)} %get-tuple-element.69), channel_id=1, source_target_pairs={{0,1},{2,3},{5,4},{7,6},{8,9},{10,11},{13,12},{15,14},{16,17},{18,... | collective-permute-start | bytes 393224 | tf_op jit(solution)/shard_map/ppermute | solution.py:341
  174.8 0.1 place.7.refs_1_
  174.8 0.1 place.8.refs_2_
  174.9 4.3 %collective-permute-done.18.refs_1_ = bf16[128,512]{1,0:T(8,128)(2,1)S(1)} collective-permute-done((bf16[128,512]{1,0:T(8,128)(2,1)S(1)}, bf16[128,512]{1,0:T(8,128)(2,1)S(1)}, u32[]{:S(2)}, u32[]{:S(2)}) %collective-permute-start.18) | collective-permute-done | bytes 131104 | tf_op jit(solution)/shard_map/ppermute | solution.py:341
  (21 shorter events, 0.1 us)
Async XLA Ops:
  0.0 5.4 %collective-permute-start = (bf16[128,8192]{1,0:T(8,128)(2,1)}, bf16[128,8192]{1,0:T(8,128)(2,1)}, u32[]{:S(2)}, u32[]{:S(2)}) collective-permute-start(bf16[128,8192]{1,0:T(8,128)(2,1)} %whole_ref), channel_id=1, source_target_pairs={{0,2},{2,0},{4,6},{6,4},{8,10},{10,8},{12,14},{14,12},{1,3},{3,1},... | collective-permute-start | bytes 6291464 | tf_op jit(solution)/shard_map/ppermute | solution.py:332
  0.5 49.5 %collective-permute-start.1 = (bf16[128,8192]{1,0:T(8,128)(2,1)}, bf16[128,8192]{1,0:T(8,128)(2,1)S(1)}, u32[]{:S(2)}, u32[]{:S(2)}) collective-permute-start(bf16[128,8192]{1,0:T(8,128)(2,1)} %whole_ref), channel_id=1, source_target_pairs={{0,8},{2,10},{8,12},{10,14},{12,4},{14,6},{4,0},{6,2},{1,9},{3,11}... | collective-permute-start | bytes 6291464 | tf_op jit(solution)/shard_map/ppermute | solution.py:328
  5.4 1.6 copy-start
  7.0 0.8 copy-start.3
  7.8 46.7 %copy-start.4 = (f32[8192]{0:T(1024)S(1)}, f32[8192]{0:T(1024)}, u32[]{:S(2)}) copy-start(f32[8192]{0:T(1024)} %param.7) | copy-start | bytes 98308
  37.6 1.0 copy-start.7
  38.6 11.4 %copy-start.1 = (f32[256,2048]{1,0:T(8,128)}, f32[256,2048]{1,0:T(8,128)S(1)}, u32[]{:S(2)}) copy-start(f32[256,2048]{1,0:T(8,128)S(1)} %get-tuple-element.46.refs_0_) | copy-start | bytes 6291460
  49.9 4.6 %collective-permute-start.3 = (bf16[128,8192]{1,0:T(8,128)(2,1)S(1)}, bf16[128,8192]{1,0:T(8,128)(2,1)}, u32[]{:S(2)}, u32[]{:S(2)}) collective-permute-start(bf16[128,8192]{1,0:T(8,128)(2,1)S(1)} %collective-permute-done.1.refs_0_), channel_id=1, source_target_pairs={{0,2},{2,0},{4,6},{6,4},{8,10},{10,8},{12,14},{14,12},{1,3},{3,1},... | collective-permute-start | bytes 6291464 | tf_op jit(solution)/shard_map/ppermute | solution.py:332
  49.9 48.8 %collective-permute-start.2 = (bf16[128,8192]{1,0:T(8,128)(2,1)S(1)}, bf16[128,8192]{1,0:T(8,128)(2,1)}, u32[]{:S(2)}, u32[]{:S(2)}) collective-permute-start(bf16[128,8192]{1,0:T(8,128)(2,1)S(1)} %collective-permute-done.1.refs_0_), channel_id=1, source_target_pairs={{0,8},{2,10},{8,12},{10,14},{12,4},{14,6},{4,0},{6,2},{1,9},{3,11}... | collective-permute-start | bytes 6291464 | tf_op jit(solution)/shard_map/ppermute | solution.py:328
  53.2 28.2 %collective-permute-start.4 = (bf16[256,2048]{1,0:T(8,128)(2,1)}, bf16[256,2048]{1,0:T(8,128)(2,1)}, u32[]{:S(2)}, u32[]{:S(2)}) collective-permute-start(bf16[256,2048]{1,0:T(8,128)(2,1)} %copy-done.7), channel_id=1, source_target_pairs={{1,0},{3,2},{5,4},{7,6},{8,9},{10,11},{12,13},{14,15},{17,16},{19,... | collective-permute-start | bytes 3145736 | tf_op jit(solution)/shard_map/ppermute | solution.py:341
  70.0 33.0 %collective-permute-start.5 = (bf16[256,2048]{1,0:T(8,128)(2,1)}, bf16[256,2048]{1,0:T(8,128)(2,1)S(1)}, u32[]{:S(2)}, u32[]{:S(2)}) collective-permute-start(bf16[256,2048]{1,0:T(8,128)(2,1)} %get-tuple-element.45), channel_id=1, source_target_pairs={{1,0},{3,2},{4,5},{6,7},{9,8},{11,10},{12,13},{14,15},{17,16},{19,... | collective-permute-start | bytes 3145736 | tf_op jit(solution)/shard_map/ppermute | solution.py:341
  81.4 1.6 copy-start.2
  103.1 20.6 %copy-start.5 = (bf16[256,2048]{1,0:T(8,128)(2,1)}, bf16[256,2048]{1,0:T(8,128)(2,1)S(1)}, u32[]{:S(2)}) copy-start(bf16[256,2048]{1,0:T(8,128)(2,1)S(1)} %collective-permute-done.5.refs_0_) | copy-start | bytes 3145732
  103.1 4.5 %collective-permute-start.6 = (bf16[128,8192]{1,0:T(8,128)(2,1)}, bf16[128,8192]{1,0:T(8,128)(2,1)}, u32[]{:S(2)}, u32[]{:S(2)}) collective-permute-start(bf16[128,8192]{1,0:T(8,128)(2,1)} %collective-permute-done.2.refs_0_), channel_id=1, source_target_pairs={{0,2},{2,0},{4,6},{6,4},{8,10},{10,8},{12,14},{14,12},{1,3},{3,1},... | collective-permute-start | bytes 6291464 | tf_op jit(solution)/shard_map/ppermute | solution.py:332
  103.1 27.1 %collective-permute-start.8 = (bf16[64,8192]{1,0:T(8,128)(2,1)}, bf16[64,8192]{1,0:T(8,128)(2,1)S(1)}, u32[]{:S(2)}, u32[]{:S(2)}) collective-permute-start(bf16[64,8192]{1,0:T(8,128)(2,1)} %get-tuple-element.53), channel_id=1, source_target_pairs={{0,4},{2,6},{8,0},{10,2},{12,8},{14,10},{4,12},{6,14},{1,5},{3,7},... | collective-permute-start | bytes 3145736 | tf_op jit(solution)/shard_map/ppermute | solution.py:328
  123.6 28.6 %collective-permute-start.7 = (bf16[64,8192]{1,0:T(8,128)(2,1)}, bf16[64,8192]{1,0:T(8,128)(2,1)S(1)}, u32[]{:S(2)}, u32[]{:S(2)}) collective-permute-start(bf16[64,8192]{1,0:T(8,128)(2,1)} %get-tuple-element.52), channel_id=1, source_target_pairs={{0,4},{2,6},{8,0},{10,2},{12,8},{14,10},{4,12},{6,14},{1,5},{3,7},... | collective-permute-start | bytes 3145736 | tf_op jit(solution)/shard_map/ppermute | solution.py:328
  123.7 28.5 %collective-permute-start.11 = (bf16[256,2048]{1,0:T(8,128)(2,1)}, bf16[256,2048]{1,0:T(8,128)(2,1)S(1)}, u32[]{:S(2)}, u32[]{:S(2)}) collective-permute-start(bf16[256,2048]{1,0:T(8,128)(2,1)} %get-tuple-element.51), channel_id=1, source_target_pairs={{0,1},{2,3},{4,5},{6,7},{9,8},{11,10},{13,12},{15,14},{16,17},{18,... | collective-permute-start | bytes 3145736 | tf_op jit(solution)/shard_map/ppermute | solution.py:341
  125.4 1.2 copy-start.6
  131.2 2.3 %collective-permute-start.9 = (bf16[32,8192]{1,0:T(8,128)(2,1)}, bf16[32,8192]{1,0:T(8,128)(2,1)}, u32[]{:S(2)}, u32[]{:S(2)}) collective-permute-start(bf16[32,8192]{1,0:T(8,128)(2,1)} %get-tuple-element.57), channel_id=1, source_target_pairs={{0,2},{2,0},{4,6},{6,4},{8,10},{10,8},{12,14},{14,12},{1,3},{3,1},... | collective-permute-start | bytes 1572872 | tf_op jit(solution)/shard_map/ppermute | solution.py:332
  131.2 3.0 %collective-permute-start.10 = (bf16[32,8192]{1,0:T(8,128)(2,1)}, bf16[32,8192]{1,0:T(8,128)(2,1)}, u32[]{:S(2)}, u32[]{:S(2)}) collective-permute-start(bf16[32,8192]{1,0:T(8,128)(2,1)} %get-tuple-element.58), channel_id=1, source_target_pairs={{0,2},{2,0},{4,6},{6,4},{8,10},{10,8},{12,14},{14,12},{1,3},{3,1},... | collective-permute-start | bytes 1572872 | tf_op jit(solution)/shard_map/ppermute | solution.py:332
  148.7 19.1 %collective-permute-start.17 = (bf16[128,2048]{1,0:T(8,128)(2,1)S(1)}, bf16[128,2048]{1,0:T(8,128)(2,1)S(1)}, u32[]{:S(2)}, u32[]{:S(2)}) collective-permute-start(bf16[128,2048]{1,0:T(8,128)(2,1)S(1)} %get-tuple-element.59), channel_id=1, source_target_pairs={{0,1},{2,3},{5,4},{7,6},{8,9},{10,11},{13,12},{15,14},{16,17},{18,... | collective-permute-start | bytes 1572872 | tf_op jit(solution)/shard_map/ppermute | solution.py:341
  152.3 1.6 collective-permute-start.12
  152.4 1.9 %collective-permute-start.13 = (bf16[16,8192]{1,0:T(8,128)(2,1)S(1)}, bf16[16,8192]{1,0:T(8,128)(2,1)S(1)}, u32[]{:S(2)}, u32[]{:S(2)}) collective-permute-start(bf16[16,8192]{1,0:T(8,128)(2,1)S(1)} %get-tuple-element.62), channel_id=1, source_target_pairs={{0,2},{2,0},{4,6},{6,4},{8,10},{10,8},{12,14},{14,12},{1,3},{3,1},... | collective-permute-start | bytes 786440 | tf_op jit(solution)/shard_map/ppermute | solution.py:332
  152.9 1.8 collective-permute-start.14
  152.9 2.1 %collective-permute-start.15 = (bf16[16,8192]{1,0:T(8,128)(2,1)S(1)}, bf16[16,8192]{1,0:T(8,128)(2,1)S(1)}, u32[]{:S(2)}, u32[]{:S(2)}) collective-permute-start(bf16[16,8192]{1,0:T(8,128)(2,1)S(1)} %get-tuple-element.64), channel_id=1, source_target_pairs={{0,2},{2,0},{4,6},{6,4},{8,10},{10,8},{12,14},{14,12},{1,3},{3,1},... | collective-permute-start | bytes 786440 | tf_op jit(solution)/shard_map/ppermute | solution.py:332
  165.6 13.7 %collective-permute-start.16 = (bf16[128,1536]{1,0:T(8,128)(2,1)S(1)}, bf16[128,1536]{1,0:T(8,128)(2,1)S(1)}, u32[]{:S(2)}, u32[]{:S(2)}) collective-permute-start(bf16[128,1536]{1,0:T(8,128)(2,1)S(1)} %get-tuple-element.66), channel_id=1, source_target_pairs={{0,1},{2,3},{5,4},{7,6},{8,9},{10,11},{13,12},{15,14},{16,17},{18,... | collective-permute-start | bytes 1179656 | tf_op jit(solution)/shard_map/ppermute | solution.py:341
  172.9 6.4 %collective-permute-start.18 = (bf16[128,512]{1,0:T(8,128)(2,1)S(1)}, bf16[128,512]{1,0:T(8,128)(2,1)S(1)}, u32[]{:S(2)}, u32[]{:S(2)}) collective-permute-start(bf16[128,512]{1,0:T(8,128)(2,1)S(1)} %get-tuple-element.69), channel_id=1, source_target_pairs={{0,1},{2,3},{5,4},{7,6},{8,9},{10,11},{13,12},{15,14},{16,17},{18,... | collective-permute-start | bytes 393224 | tf_op jit(solution)/shard_map/ppermute | solution.py:341

commit v20 on v19

--- a/solution.py
+++ b/solution.py
@@ -195,7 +195,7 @@
     top, bottom = span or (0, train.shape[0])
     count = bottom - top
     tile = min(count, 256)
-    slots = 3
+    slots = 4 if cores * rows <= 128 else 3
     block = (cores * rows, count)
     given = [] if scores is None else [scores]
     counts = (len(mine), len(other), len(given))
@@ -375,7 +375,7 @@
     received = exchange(send, hops)
     high_piece = after(high_flow, send, *earlier)
     high_other = swap(cut(high_piece, max(1, min(4, high_piece.shape[0] // 16))))
-    knee = count * 3 // 4
+    knee = count * 5 // 8
     halves = []
     for top, bottom in ((0, knee), (knee, count)):
         if top:

time: 182 us -> 182 us (level)
  no operation moved by 1% of the time
where the time goes in v20:
time: 182 us; the launch traced here: 179 us
  Pallas kernels  100 us (55%)
  waiting for transfers between devices  51.5 us (28%)
  starting transfers between devices  19.7 us (11%)
  local copies, waits for them, and re-layouts  7.51 us (4%)
    pallas_call x5, Pallas kernels, multiply(): pl.pallas_call(functools.partial(multiply_kernel, counts, start, top), in...  61.7 us
    pallas_call x1, Pallas kernels, first(): pl.pallas_call(first_kernel, grid=(count // tile,), in_specs=[in_smem, pl...  29.8 us
    ppermute x4, waiting for transfers between devices, shift(): return lax.ppermute(panel, 'blk', pairs)  24.3 us
    ppermute x6, waiting for transfers between devices, exchange(): received.append(lax.ppermute(send, ('blk', 'dim'), pairs))  18.6 us
    ppermute x6, starting transfers between devices, exchange(): received.append(lax.ppermute(send, ('blk', 'dim'), pairs))  10.7 us
    ppermute x9, waiting for transfers between devices, swap(): return [lax.ppermute(part, 'blk', pairs) for part in parts]  8.59 us
    unnamed x17, local copies, waits for them, and re-layouts  7.51 us
    ppermute x4, starting transfers between devices, shift(): return lax.ppermute(panel, 'blk', pairs)  6.92 us
  transfers between devices with their start and end apart: 19, of which 14 were waited for; matrix products, arithmetic and copies ran while one was open for 1% of the time, Pallas kernels for 56%

profile of v20, /device:TPU:0, one launch (start us, length us, event | category | flops | bytes accessed | tf_op | source)
XLA Modules:
  0.0 179.3 jit_solution(3056099025079013835)
XLA Ops:
  0.0 0.5 collective-permute-start
  0.5 3.6 %collective-permute-start.1 = (bf16[128,8192]{1,0:T(8,128)(2,1)}, bf16[128,8192]{1,0:T(8,128)(2,1)S(1)}, u32[]{:S(2)}, u32[]{:S(2)}) collective-permute-start(bf16[128,8192]{1,0:T(8,128)(2,1)} %whole_ref), channel_id=1, source_target_pairs={{0,8},{2,10},{8,12},{10,14},{12,4},{14,6},{4,0},{6,2},{1,9},{3,11}... | collective-permute-start | bytes 6291464 | tf_op jit(solution)/shard_map/ppermute | solution.py:328
  4.0 1.4 copy.14.exps_ref
  5.4 1.6 copy-done
  7.0 0.8 copy-done.3
  7.8 29.8 %first.1 = (bf16[2048,8192]{1,0:T(8,128)(2,1)}, f32[256,2048]{1,0:T(8,128)S(1)}, bf16[256,2048]{1,0:T(8,128)(2,1)S(1)}) custom-call(s32[1]{0:T(128)} %bitcast.2.core_ref, bf16[128,8192]{1,0:T(8,128)(2,1)S(1)} %copy-done, bf16[128,8192]{1,0:T(8,128)(2,1)} %collective-permute-done.other_ref, f32[1,8192]{1,0:T(1,128)S(1)} %bitcast.11, ...), custom_call_target="tpu_custom_call" | custom-call | flops 1 | bytes 1 | tf_op jit(solution)/shard_map/first/pallas_call | solution.py:59
  37.6 1.0 copy-done.7
  38.6 1.5 cut.3
  40.1 9.8 %collective-permute-done.1.refs_0_ = bf16[128,8192]{1,0:T(8,128)(2,1)S(1)} collective-permute-done((bf16[128,8192]{1,0:T(8,128)(2,1)}, bf16[128,8192]{1,0:T(8,128)(2,1)S(1)}, u32[]{:S(2)}, u32[]{:S(2)}) %collective-permute-start.1) | collective-permute-done | bytes 2097184 | tf_op jit(solution)/shard_map/ppermute | solution.py:328
  49.9 3.3 %collective-permute-start.2 = (bf16[128,8192]{1,0:T(8,128)(2,1)S(1)}, bf16[128,8192]{1,0:T(8,128)(2,1)}, u32[]{:S(2)}, u32[]{:S(2)}) collective-permute-start(bf16[128,8192]{1,0:T(8,128)(2,1)S(1)} %collective-permute-done.1.refs_0_), channel_id=1, source_target_pairs={{0,8},{2,10},{8,12},{10,14},{12,4},{14,6},{4,0},{6,2},{1,9},{3,11}... | collective-permute-start | bytes 6291464 | tf_op jit(solution)/shard_map/ppermute | solution.py:328
  53.2 1.3 collective-permute-start.4
  54.5 15.5 %multiply.5 = (f32[2,2,128,2048]{3,2,1,0:T(8,128)}, bf16[256,2048]{1,0:T(8,128)(2,1)}) custom-call(s32[1]{0:T(128)} %bitcast.6.mine_ref, s32[1]{0:T(128)} %bitcast.7.spot_ref, s32[1]{0:T(128)} %bitcast.2.core_ref, bf16[128,8192]{1,0:T(8,128)(2,1)S(1)} %collective-permute-done.1.refs_0_, bf16[128,8192]{1,0:T(8,128)(2,1)} %collective-permute-done.3.refs_1_, ...), custom_call_target="tpu_custom_call" | custom-call | flops 1 | bytes 1 | tf_op jit(solution)/shard_map/multiply/pallas_call | solution.py:202
  70.0 1.3 collective-permute-start.5
  71.4 10.0 %collective-permute-done.4.refs_1_ = bf16[256,2048]{1,0:T(8,128)(2,1)} collective-permute-done((bf16[256,2048]{1,0:T(8,128)(2,1)}, bf16[256,2048]{1,0:T(8,128)(2,1)}, u32[]{:S(2)}, u32[]{:S(2)}) %collective-permute-start.4) | collective-permute-done | bytes 1048608 | tf_op jit(solution)/shard_map/ppermute | solution.py:341
  81.4 1.6 copy-done.2
  83.0 2.9 %place.5.refs_2_ = f32[2,2,128,2048]{3,2,1,0:T(8,128)} custom-call(s32[1]{0:T(128)} %bitcast.8.mine_ref, s32[1]{0:T(128)} %bitcast.9.spot_ref, f32[256,2048]{1,0:T(8,128)S(1)} %copy-done.2, bf16[256,2048]{1,0:T(8,128)(2,1)} %collective-permute-done.4.refs_1_, f32[2,2,128,2048]{3,2,1,0:T(8,128)} %get-tuple-element.48.refs_2_), custom_call_target="tpu_custom_call", output_to_operand_aliasing={{}: (4, {})} | custom-call | flops 1 | bytes 1 | tf_op jit(solution)/shard_map/place/pallas_call | solution.py:265
  85.9 12.9 %collective-permute-done.2.refs_0_ = bf16[128,8192]{1,0:T(8,128)(2,1)} collective-permute-done((bf16[128,8192]{1,0:T(8,128)(2,1)S(1)}, bf16[128,8192]{1,0:T(8,128)(2,1)}, u32[]{:S(2)}, u32[]{:S(2)}) %collective-permute-start.2) | collective-permute-done | bytes 2097184 | tf_op jit(solution)/shard_map/ppermute | solution.py:328
  98.8 4.3 %collective-permute-done.5.refs_0_ = bf16[256,2048]{1,0:T(8,128)(2,1)S(1)} collective-permute-done((bf16[256,2048]{1,0:T(8,128)(2,1)}, bf16[256,2048]{1,0:T(8,128)(2,1)S(1)}, u32[]{:S(2)}, u32[]{:S(2)}) %collective-permute-start.5) | collective-permute-done | bytes 1048608 | tf_op jit(solution)/shard_map/ppermute | solution.py:341
  103.1 4.5 %collective-permute-done.6.refs_1_ = bf16[128,8192]{1,0:T(8,128)(2,1)} collective-permute-done((bf16[128,8192]{1,0:T(8,128)(2,1)}, bf16[128,8192]{1,0:T(8,128)(2,1)}, u32[]{:S(2)}, u32[]{:S(2)}) %collective-permute-start.6) | collective-permute-done | bytes 2097184 | tf_op jit(solution)/shard_map/ppermute | solution.py:332
  107.6 16.0 %multiply.6 = (f32[2,2,128,2048]{3,2,1,0:T(8,128)}, bf16[256,2048]{1,0:T(8,128)(2,1)}) custom-call(s32[1]{0:T(128)} %bitcast.4.mine_ref, s32[1]{0:T(128)} %bitcast.5.spot_ref, s32[1]{0:T(128)} %bitcast.2.core_ref, bf16[128,8192]{1,0:T(8,128)(2,1)} %collective-permute-done.2.refs_0_, ...), custom_call_target="tpu_custom_call", output_to_operand_aliasing={{0}: (5, {})} | custom-call | flops 1 | bytes 1 | tf_op jit(solution)/shard_map/multiply/pallas_call | solution.py:202
  123.6 0.1 collective-permute-start.7
  123.7 1.8 collective-permute-start.11
  125.5 1.2 copy-done.6
  126.7 3.1 %place.6.refs_3_ = f32[2,2,128,2048]{3,2,1,0:T(8,128)} custom-call(s32[1]{0:T(128)} %bitcast.6.mine_ref, s32[1]{0:T(128)} %bitcast.7.spot_ref, bf16[256,2048]{1,0:T(8,128)(2,1)S(1)} %copy-done.6, f32[2,2,128,2048]{3,2,1,0:T(8,128)} %get-tuple-element.55.refs_1_), custom_call_target="tpu_custom_call", output_to_operand_aliasing={{}: (3, {})} | custom-call | flops 1 | bytes 1 | tf_op jit(solution)/shard_map/place/pallas_call | solution.py:265
  129.7 0.4 collective-permute-done.8.whole_ref.refs_0_
  130.1 1.1 cut.4
  131.2 0.5 collective-permute-start.10
  131.7 1.7 collective-permute-done.9.refs_1_
  133.4 0.7 collective-permute-done.10.refs_2_
  134.2 14.5 %multiply.7 = (f32[2,2,128,2048]{3,2,1,0:T(8,128)}, bf16[128,2048]{1,0:T(8,128)(2,1)S(1)}) custom-call(s32[1]{0:T(128)} %bitcast.mine_ref, s32[1]{0:T(128)} %bitcast.1.spot_ref, s32[1]{0:T(128)} %bitcast.2.core_ref, bf16[64,8192]{1,0:T(8,128)(2,1)S(1)} %collective-permute-done.8.whole_ref.refs_0_, ...), custom_call_target="tpu_custom_call", output_to_operand_aliasing={{0}: (6, {})} | custom-call | flops 1 | bytes 1 | tf_op jit(solution)/shard_map/multiply/pallas_call | solution.py:202
  148.7 2.3 %collective-permute-start.17 = (bf16[128,2048]{1,0:T(8,128)(2,1)S(1)}, bf16[128,2048]{1,0:T(8,128)(2,1)S(1)}, u32[]{:S(2)}, u32[]{:S(2)}) collective-permute-start(bf16[128,2048]{1,0:T(8,128)(2,1)S(1)} %get-tuple-element.59), channel_id=1, source_target_pairs={{0,1},{2,3},{5,4},{7,6},{8,9},{10,11},{13,12},{15,14},{16,17},{18,... | collective-permute-start | bytes 1572872 | tf_op jit(solution)/shard_map/ppermute | solution.py:341
  151.0 1.3 collective-permute-done.7.whole_ref.refs_0_
  152.2 0.1 cut.5
  152.3 0.1 collective-permute-start.12
  152.4 0.5 collective-permute-start.13
  152.9 0.1 collective-permute-start.14
  152.9 0.4 collective-permute-start.15
  153.4 0.5 collective-permute-done.12.refs_1_
  153.9 0.4 collective-permute-done.13.refs_2_
  154.3 0.4 collective-permute-done.14.refs_3_
  154.6 0.4 collective-permute-done.15.refs_4_
  155.0 9.2 %multiply.8 = (f32[2,2,128,2048]{3,2,1,0:T(8,128)}, bf16[128,1280]{1,0:T(8,128)(2,1)S(1)}) custom-call(s32[1]{0:T(128)} %bitcast.mine_ref, s32[1]{0:T(128)} %bitcast.1.spot_ref, s32[1]{0:T(128)} %bitcast.2.core_ref, bf16[64,8192]{1,0:T(8,128)(2,1)S(1)} %collective-permute-done.7.whole_ref.refs_0_, ...), custom_call_target="tpu_custom_call", output_to_operand_aliasing={{0}: (8, {})} | custom-call | flops 1 | bytes 1 | tf_op jit(solution)/shard_map/multiply/pallas_call | solution.py:202
  164.2 2.2 %collective-permute-start.16 = (bf16[128,1280]{1,0:T(8,128)(2,1)S(1)}, bf16[128,1280]{1,0:T(8,128)(2,1)S(1)}, u32[]{:S(2)}, u32[]{:S(2)}) collective-permute-start(bf16[128,1280]{1,0:T(8,128)(2,1)S(1)} %get-tuple-element.66), channel_id=1, source_target_pairs={{0,1},{2,3},{5,4},{7,6},{8,9},{10,11},{13,12},{15,14},{16,17},{18,... | collective-permute-start | bytes 983048 | tf_op jit(solution)/shard_map/ppermute | solution.py:341
  166.4 6.4 %multiply.9 = (f32[2,2,128,2048]{3,2,1,0:T(8,128)}, bf16[128,768]{1,0:T(8,128)(2,1)S(1)}) custom-call(s32[1]{0:T(128)} %bitcast.mine_ref, s32[1]{0:T(128)} %bitcast.1.spot_ref, s32[1]{0:T(128)} %bitcast.2.core_ref, bf16[64,8192]{1,0:T(8,128)(2,1)S(1)} %collective-permute-done.7.whole_ref.refs_0_, ...), custom_call_target="tpu_custom_call", output_to_operand_aliasing={{0}: (8, {})} | custom-call | flops 1 | bytes 1 | tf_op jit(solution)/shard_map/multiply/pallas_call | solution.py:202
  172.9 1.9 %collective-permute-start.18 = (bf16[128,768]{1,0:T(8,128)(2,1)S(1)}, bf16[128,768]{1,0:T(8,128)(2,1)S(1)}, u32[]{:S(2)}, u32[]{:S(2)}) collective-permute-start(bf16[128,768]{1,0:T(8,128)(2,1)S(1)} %get-tuple-element.69), channel_id=1, source_target_pairs={{0,1},{2,3},{5,4},{7,6},{8,9},{10,11},{13,12},{15,14},{16,17},{18,... | collective-permute-start | bytes 589832 | tf_op jit(solution)/shard_map/ppermute | solution.py:341
  174.8 0.1 place.7.refs_1_
  174.9 0.1 place.8.refs_2_
  174.9 4.3 %collective-permute-done.18.refs_1_ = bf16[128,768]{1,0:T(8,128)(2,1)S(1)} collective-permute-done((bf16[128,768]{1,0:T(8,128)(2,1)S(1)}, bf16[128,768]{1,0:T(8,128)(2,1)S(1)}, u32[]{:S(2)}, u32[]{:S(2)}) %collective-permute-start.18) | collective-permute-done | bytes 196640 | tf_op jit(solution)/shard_map/ppermute | solution.py:341
  (21 shorter events, 0.1 us)
Async XLA Ops:
  0.0 5.4 %collective-permute-start = (bf16[128,8192]{1,0:T(8,128)(2,1)}, bf16[128,8192]{1,0:T(8,128)(2,1)}, u32[]{:S(2)}, u32[]{:S(2)}) collective-permute-start(bf16[128,8192]{1,0:T(8,128)(2,1)} %whole_ref), channel_id=1, source_target_pairs={{0,2},{2,0},{4,6},{6,4},{8,10},{10,8},{12,14},{14,12},{1,3},{3,1},... | collective-permute-start | bytes 6291464 | tf_op jit(solution)/shard_map/ppermute | solution.py:332
  0.5 49.5 %collective-permute-start.1 = (bf16[128,8192]{1,0:T(8,128)(2,1)}, bf16[128,8192]{1,0:T(8,128)(2,1)S(1)}, u32[]{:S(2)}, u32[]{:S(2)}) collective-permute-start(bf16[128,8192]{1,0:T(8,128)(2,1)} %whole_ref), channel_id=1, source_target_pairs={{0,8},{2,10},{8,12},{10,14},{12,4},{14,6},{4,0},{6,2},{1,9},{3,11}... | collective-permute-start | bytes 6291464 | tf_op jit(solution)/shard_map/ppermute | solution.py:328
  5.4 1.6 copy-start
  7.0 0.8 copy-start.3
  7.8 46.7 %copy-start.4 = (f32[8192]{0:T(1024)S(1)}, f32[8192]{0:T(1024)}, u32[]{:S(2)}) copy-start(f32[8192]{0:T(1024)} %param.7) | copy-start | bytes 98308
  37.6 1.0 copy-start.7
  38.6 11.4 %copy-start.1 = (f32[256,2048]{1,0:T(8,128)}, f32[256,2048]{1,0:T(8,128)S(1)}, u32[]{:S(2)}) copy-start(f32[256,2048]{1,0:T(8,128)S(1)} %get-tuple-element.46.refs_0_) | copy-start | bytes 6291460
  49.9 4.6 %collective-permute-start.3 = (bf16[128,8192]{1,0:T(8,128)(2,1)S(1)}, bf16[128,8192]{1,0:T(8,128)(2,1)}, u32[]{:S(2)}, u32[]{:S(2)}) collective-permute-start(bf16[128,8192]{1,0:T(8,128)(2,1)S(1)} %collective-permute-done.1.refs_0_), channel_id=1, source_target_pairs={{0,2},{2,0},{4,6},{6,4},{8,10},{10,8},{12,14},{14,12},{1,3},{3,1},... | collective-permute-start | bytes 6291464 | tf_op jit(solution)/shard_map/ppermute | solution.py:332
  49.9 48.8 %collective-permute-start.2 = (bf16[128,8192]{1,0:T(8,128)(2,1)S(1)}, bf16[128,8192]{1,0:T(8,128)(2,1)}, u32[]{:S(2)}, u32[]{:S(2)}) collective-permute-start(bf16[128,8192]{1,0:T(8,128)(2,1)S(1)} %collective-permute-done.1.refs_0_), channel_id=1, source_target_pairs={{0,8},{2,10},{8,12},{10,14},{12,4},{14,6},{4,0},{6,2},{1,9},{3,11}... | collective-permute-start | bytes 6291464 | tf_op jit(solution)/shard_map/ppermute | solution.py:328
  53.2 28.2 %collective-permute-start.4 = (bf16[256,2048]{1,0:T(8,128)(2,1)}, bf16[256,2048]{1,0:T(8,128)(2,1)}, u32[]{:S(2)}, u32[]{:S(2)}) collective-permute-start(bf16[256,2048]{1,0:T(8,128)(2,1)} %copy-done.7), channel_id=1, source_target_pairs={{1,0},{3,2},{5,4},{7,6},{8,9},{10,11},{12,13},{14,15},{17,16},{19,... | collective-permute-start | bytes 3145736 | tf_op jit(solution)/shard_map/ppermute | solution.py:341
  70.0 33.0 %collective-permute-start.5 = (bf16[256,2048]{1,0:T(8,128)(2,1)}, bf16[256,2048]{1,0:T(8,128)(2,1)S(1)}, u32[]{:S(2)}, u32[]{:S(2)}) collective-permute-start(bf16[256,2048]{1,0:T(8,128)(2,1)} %get-tuple-element.45), channel_id=1, source_target_pairs={{1,0},{3,2},{4,5},{6,7},{9,8},{11,10},{12,13},{14,15},{17,16},{19,... | collective-permute-start | bytes 3145736 | tf_op jit(solution)/shard_map/ppermute | solution.py:341
  81.4 1.6 copy-start.2
  103.1 20.6 %copy-start.5 = (bf16[256,2048]{1,0:T(8,128)(2,1)}, bf16[256,2048]{1,0:T(8,128)(2,1)S(1)}, u32[]{:S(2)}) copy-start(bf16[256,2048]{1,0:T(8,128)(2,1)S(1)} %collective-permute-done.5.refs_0_) | copy-start | bytes 3145732
  103.1 4.5 %collective-permute-start.6 = (bf16[128,8192]{1,0:T(8,128)(2,1)}, bf16[128,8192]{1,0:T(8,128)(2,1)}, u32[]{:S(2)}, u32[]{:S(2)}) collective-permute-start(bf16[128,8192]{1,0:T(8,128)(2,1)} %collective-permute-done.2.refs_0_), channel_id=1, source_target_pairs={{0,2},{2,0},{4,6},{6,4},{8,10},{10,8},{12,14},{14,12},{1,3},{3,1},... | collective-permute-start | bytes 6291464 | tf_op jit(solution)/shard_map/ppermute | solution.py:332
  103.1 27.1 %collective-permute-start.8 = (bf16[64,8192]{1,0:T(8,128)(2,1)}, bf16[64,8192]{1,0:T(8,128)(2,1)S(1)}, u32[]{:S(2)}, u32[]{:S(2)}) collective-permute-start(bf16[64,8192]{1,0:T(8,128)(2,1)} %get-tuple-element.53), channel_id=1, source_target_pairs={{0,4},{2,6},{8,0},{10,2},{12,8},{14,10},{4,12},{6,14},{1,5},{3,7},... | collective-permute-start | bytes 3145736 | tf_op jit(solution)/shard_map/ppermute | solution.py:328
  123.6 28.6 %collective-permute-start.7 = (bf16[64,8192]{1,0:T(8,128)(2,1)}, bf16[64,8192]{1,0:T(8,128)(2,1)S(1)}, u32[]{:S(2)}, u32[]{:S(2)}) collective-permute-start(bf16[64,8192]{1,0:T(8,128)(2,1)} %get-tuple-element.52), channel_id=1, source_target_pairs={{0,4},{2,6},{8,0},{10,2},{12,8},{14,10},{4,12},{6,14},{1,5},{3,7},... | collective-permute-start | bytes 3145736 | tf_op jit(solution)/shard_map/ppermute | solution.py:328
  123.7 28.5 %collective-permute-start.11 = (bf16[256,2048]{1,0:T(8,128)(2,1)}, bf16[256,2048]{1,0:T(8,128)(2,1)S(1)}, u32[]{:S(2)}, u32[]{:S(2)}) collective-permute-start(bf16[256,2048]{1,0:T(8,128)(2,1)} %get-tuple-element.51), channel_id=1, source_target_pairs={{0,1},{2,3},{4,5},{6,7},{9,8},{11,10},{13,12},{15,14},{16,17},{18,... | collective-permute-start | bytes 3145736 | tf_op jit(solution)/shard_map/ppermute | solution.py:341
  125.4 1.2 copy-start.6
  131.2 2.3 %collective-permute-start.9 = (bf16[32,8192]{1,0:T(8,128)(2,1)}, bf16[32,8192]{1,0:T(8,128)(2,1)}, u32[]{:S(2)}, u32[]{:S(2)}) collective-permute-start(bf16[32,8192]{1,0:T(8,128)(2,1)} %get-tuple-element.57), channel_id=1, source_target_pairs={{0,2},{2,0},{4,6},{6,4},{8,10},{10,8},{12,14},{14,12},{1,3},{3,1},... | collective-permute-start | bytes 1572872 | tf_op jit(solution)/shard_map/ppermute | solution.py:332
  131.2 3.0 %collective-permute-start.10 = (bf16[32,8192]{1,0:T(8,128)(2,1)}, bf16[32,8192]{1,0:T(8,128)(2,1)}, u32[]{:S(2)}, u32[]{:S(2)}) collective-permute-start(bf16[32,8192]{1,0:T(8,128)(2,1)} %get-tuple-element.58), channel_id=1, source_target_pairs={{0,2},{2,0},{4,6},{6,4},{8,10},{10,8},{12,14},{14,12},{1,3},{3,1},... | collective-permute-start | bytes 1572872 | tf_op jit(solution)/shard_map/ppermute | solution.py:332
  148.7 17.7 %collective-permute-start.17 = (bf16[128,2048]{1,0:T(8,128)(2,1)S(1)}, bf16[128,2048]{1,0:T(8,128)(2,1)S(1)}, u32[]{:S(2)}, u32[]{:S(2)}) collective-permute-start(bf16[128,2048]{1,0:T(8,128)(2,1)S(1)} %get-tuple-element.59), channel_id=1, source_target_pairs={{0,1},{2,3},{5,4},{7,6},{8,9},{10,11},{13,12},{15,14},{16,17},{18,... | collective-permute-start | bytes 1572872 | tf_op jit(solution)/shard_map/ppermute | solution.py:341
  152.3 1.6 collective-permute-start.12
  152.4 1.9 %collective-permute-start.13 = (bf16[16,8192]{1,0:T(8,128)(2,1)S(1)}, bf16[16,8192]{1,0:T(8,128)(2,1)S(1)}, u32[]{:S(2)}, u32[]{:S(2)}) collective-permute-start(bf16[16,8192]{1,0:T(8,128)(2,1)S(1)} %get-tuple-element.62), channel_id=1, source_target_pairs={{0,2},{2,0},{4,6},{6,4},{8,10},{10,8},{12,14},{14,12},{1,3},{3,1},... | collective-permute-start | bytes 786440 | tf_op jit(solution)/shard_map/ppermute | solution.py:332
  152.9 1.8 collective-permute-start.14
  152.9 2.1 %collective-permute-start.15 = (bf16[16,8192]{1,0:T(8,128)(2,1)S(1)}, bf16[16,8192]{1,0:T(8,128)(2,1)S(1)}, u32[]{:S(2)}, u32[]{:S(2)}) collective-permute-start(bf16[16,8192]{1,0:T(8,128)(2,1)S(1)} %get-tuple-element.64), channel_id=1, source_target_pairs={{0,2},{2,0},{4,6},{6,4},{8,10},{10,8},{12,14},{14,12},{1,3},{3,1},... | collective-permute-start | bytes 786440 | tf_op jit(solution)/shard_map/ppermute | solution.py:332
  164.2 15.0 %collective-permute-start.16 = (bf16[128,1280]{1,0:T(8,128)(2,1)S(1)}, bf16[128,1280]{1,0:T(8,128)(2,1)S(1)}, u32[]{:S(2)}, u32[]{:S(2)}) collective-permute-start(bf16[128,1280]{1,0:T(8,128)(2,1)S(1)} %get-tuple-element.66), channel_id=1, source_target_pairs={{0,1},{2,3},{5,4},{7,6},{8,9},{10,11},{13,12},{15,14},{16,17},{18,... | collective-permute-start | bytes 983048 | tf_op jit(solution)/shard_map/ppermute | solution.py:341
  172.9 6.4 %collective-permute-start.18 = (bf16[128,768]{1,0:T(8,128)(2,1)S(1)}, bf16[128,768]{1,0:T(8,128)(2,1)S(1)}, u32[]{:S(2)}, u32[]{:S(2)}) collective-permute-start(bf16[128,768]{1,0:T(8,128)(2,1)S(1)} %get-tuple-element.69), channel_id=1, source_target_pairs={{0,1},{2,3},{5,4},{7,6},{8,9},{10,11},{13,12},{15,14},{16,17},{18,... | collective-permute-start | bytes 589832 | tf_op jit(solution)/shard_map/ppermute | solution.py:341

commit v21 on v18

--- a/solution.py
+++ b/solution.py
@@ -155,7 +155,7 @@
         for fetch in fetches(i):
             fetch.wait()
         block = held[lax.rem(i, slots)]
-        if cores * rows <= 128:
+        if cores * rows <= 256:
             sums = lax.dot_general(
                 block, left[...], (((1,), (1,)), ((), ())), preferred_element_type=jnp.float32
             ).T

time: 182 us -> 183 us (level)
  transfers between devices with their start and end apart: 19 -> 19, of which waited for: 13 -> 13; matrix products, arithmetic and copies ran while one was open for 1% -> 1% of each run, Pallas kernels for 55% -> 56%
where the time goes in v21:
time: 183 us; the launch traced here: 180 us
  Pallas kernels  101 us (55%)
  waiting for transfers between devices  46.1 us (25%)
  starting transfers between devices  21.4 us (12%)
  local copies, waits for them, and re-layouts  11.7 us (6%)
    pallas_call x5, Pallas kernels, multiply(): pl.pallas_call(functools.partial(multiply_kernel, counts, start, top), in...  62.8 us
    pallas_call x1, Pallas kernels, first(): pl.pallas_call(first_kernel, grid=(count // tile,), in_specs=[in_smem, pl...  29.1 us
    ppermute x4, waiting for transfers between devices, shift(): return lax.ppermute(panel, 'blk', pairs)  24.2 us
    ppermute x6, waiting for transfers between devices, exchange(): received.append(lax.ppermute(send, ('blk', 'dim'), pairs))  13.3 us
    ppermute x6, starting transfers between devices, exchange(): received.append(lax.ppermute(send, ('blk', 'dim'), pairs))  12.4 us
    unnamed x23, local copies, waits for them, and re-layouts  11.7 us
    ppermute x9, waiting for transfers between devices, swap(): return [lax.ppermute(part, 'blk', pairs) for part in parts]  8.59 us
    ppermute x4, starting transfers between devices, shift(): return lax.ppermute(panel, 'blk', pairs)  7.03 us
  transfers between devices with their start and end apart: 19, of which 13 were waited for; matrix products, arithmetic and copies ran while one was open for 1% of the time, Pallas kernels for 56%

profile of v21, /device:TPU:0, one launch (start us, length us, event | category | flops | bytes accessed | tf_op | source)
XLA Modules:
  0.0 180.2 jit_solution(17528089326350317393)
XLA Ops:
  0.0 0.5 collective-permute-start
  0.5 3.6 %collective-permute-start.1 = (bf16[128,8192]{1,0:T(8,128)(2,1)}, bf16[128,8192]{1,0:T(8,128)(2,1)}, u32[]{:S(2)}, u32[]{:S(2)}) collective-permute-start(bf16[128,8192]{1,0:T(8,128)(2,1)} %whole_ref), channel_id=1, source_target_pairs={{0,8},{2,10},{8,12},{10,14},{12,4},{14,6},{4,0},{6,2},{1,9},{3,11}... | collective-permute-start | bytes 6291464 | tf_op jit(solution)/shard_map/ppermute | solution.py:328
  4.0 1.4 copy.14.exps_ref
  5.4 1.6 copy-done
  7.0 0.8 copy-done.6
  7.8 29.1 %first.1 = (bf16[2048,8192]{1,0:T(8,128)(2,1)}, f32[256,2048]{1,0:T(8,128)S(1)}, bf16[256,2048]{1,0:T(8,128)(2,1)S(1)}) custom-call(s32[1]{0:T(128)} %bitcast.2.core_ref, bf16[128,8192]{1,0:T(8,128)(2,1)S(1)} %copy-done, bf16[128,8192]{1,0:T(8,128)(2,1)S(1)} %collective-permute-done.other_ref, f32[1,8192]{1,0:T(1,128)S(1)} %bitcast.11, ...), custom_call_target="tpu_custom_call" | custom-call | flops 1 | bytes 1 | tf_op jit(solution)/shard_map/first/pallas_call | solution.py:59
  36.9 1.3 copy-done.4
  38.2 1.0 copy-done.10
  39.2 10.7 %collective-permute-done.1.refs_0_ = bf16[128,8192]{1,0:T(8,128)(2,1)} collective-permute-done((bf16[128,8192]{1,0:T(8,128)(2,1)}, bf16[128,8192]{1,0:T(8,128)(2,1)}, u32[]{:S(2)}, u32[]{:S(2)}) %collective-permute-start.1) | collective-permute-done | bytes 2097184 | tf_op jit(solution)/shard_map/ppermute | solution.py:328
  49.9 3.4 %collective-permute-start.2 = (bf16[128,8192]{1,0:T(8,128)(2,1)}, bf16[128,8192]{1,0:T(8,128)(2,1)}, u32[]{:S(2)}, u32[]{:S(2)}) collective-permute-start(bf16[128,8192]{1,0:T(8,128)(2,1)} %collective-permute-done.1.refs_0_), channel_id=1, source_target_pairs={{0,8},{2,10},{8,12},{10,14},{12,4},{14,6},{4,0},{6,2},{1,9},{3,11}... | collective-permute-start | bytes 6291464 | tf_op jit(solution)/shard_map/ppermute | solution.py:328
  53.3 1.3 collective-permute-start.4
  54.6 1.3 copy-done.2
  55.9 1.6 copy-done.3
  57.5 16.2 %multiply.5 = (f32[2,2,128,2048]{3,2,1,0:T(8,128)}, bf16[256,2048]{1,0:T(8,128)(2,1)}) custom-call(s32[1]{0:T(128)} %bitcast.6.mine_ref, s32[1]{0:T(128)} %bitcast.7.spot_ref, s32[1]{0:T(128)} %bitcast.2.core_ref, bf16[128,8192]{1,0:T(8,128)(2,1)} %collective-permute-done.1.refs_0_, bf16[128,8192]{1,0:T(8,128)(2,1)S(1)} %copy-done.3, ...), custom_call_target="tpu_custom_call" | custom-call | flops 1 | bytes 1 | tf_op jit(solution)/shard_map/multiply/pallas_call | solution.py:202
  73.7 1.3 collective-permute-start.5
  75.1 1.4 cut.3
  76.5 5.0 %collective-permute-done.4.refs_1_ = bf16[256,2048]{1,0:T(8,128)(2,1)} collective-permute-done((bf16[256,2048]{1,0:T(8,128)(2,1)}, bf16[256,2048]{1,0:T(8,128)(2,1)}, u32[]{:S(2)}, u32[]{:S(2)}) %collective-permute-start.4) | collective-permute-done | bytes 1048608 | tf_op jit(solution)/shard_map/ppermute | solution.py:341
  81.5 1.6 copy-done.5
  83.1 2.9 %place.5.refs_2_ = f32[2,2,128,2048]{3,2,1,0:T(8,128)} custom-call(s32[1]{0:T(128)} %bitcast.8.mine_ref, s32[1]{0:T(128)} %bitcast.9.spot_ref, f32[256,2048]{1,0:T(8,128)S(1)} %copy-done.5, bf16[256,2048]{1,0:T(8,128)(2,1)} %collective-permute-done.4.refs_1_, f32[2,2,128,2048]{3,2,1,0:T(8,128)} %get-tuple-element.47.refs_2_), custom_call_target="tpu_custom_call", output_to_operand_aliasing={{}: (4, {})} | custom-call | flops 1 | bytes 1 | tf_op jit(solution)/shard_map/place/pallas_call | solution.py:265
  86.0 13.2 %collective-permute-done.2.refs_0_ = bf16[128,8192]{1,0:T(8,128)(2,1)} collective-permute-done((bf16[128,8192]{1,0:T(8,128)(2,1)}, bf16[128,8192]{1,0:T(8,128)(2,1)}, u32[]{:S(2)}, u32[]{:S(2)}) %collective-permute-start.2) | collective-permute-done | bytes 2097184 | tf_op jit(solution)/shard_map/ppermute | solution.py:328
  99.2 4.0 %collective-permute-done.5.refs_0_ = bf16[256,2048]{1,0:T(8,128)(2,1)S(1)} collective-permute-done((bf16[256,2048]{1,0:T(8,128)(2,1)}, bf16[256,2048]{1,0:T(8,128)(2,1)S(1)}, u32[]{:S(2)}, u32[]{:S(2)}) %collective-permute-start.5) | collective-permute-done | bytes 1048608 | tf_op jit(solution)/shard_map/ppermute | solution.py:341
  103.2 4.5 %collective-permute-done.6.refs_1_ = bf16[128,8192]{1,0:T(8,128)(2,1)} collective-permute-done((bf16[128,8192]{1,0:T(8,128)(2,1)}, bf16[128,8192]{1,0:T(8,128)(2,1)}, u32[]{:S(2)}, u32[]{:S(2)}) %collective-permute-start.6) | collective-permute-done | bytes 2097184 | tf_op jit(solution)/shard_map/ppermute | solution.py:332
  107.7 16.6 %multiply.6 = (f32[2,2,128,2048]{3,2,1,0:T(8,128)}, bf16[256,2048]{1,0:T(8,128)(2,1)}) custom-call(s32[1]{0:T(128)} %bitcast.4.mine_ref, s32[1]{0:T(128)} %bitcast.5.spot_ref, s32[1]{0:T(128)} %bitcast.2.core_ref, bf16[128,8192]{1,0:T(8,128)(2,1)} %collective-permute-done.2.refs_0_, ...), custom_call_target="tpu_custom_call", output_to_operand_aliasing={{0}: (5, {})} | custom-call | flops 1 | bytes 1 | tf_op jit(solution)/shard_map/multiply/pallas_call | solution.py:202
  124.2 0.1 collective-permute-start.7
  124.3 3.5 %collective-permute-start.11 = (bf16[256,2048]{1,0:T(8,128)(2,1)}, bf16[256,2048]{1,0:T(8,128)(2,1)S(1)}, u32[]{:S(2)}, u32[]{:S(2)}) collective-permute-start(bf16[256,2048]{1,0:T(8,128)(2,1)} %get-tuple-element.51), channel_id=1, source_target_pairs={{0,1},{2,3},{4,5},{6,7},{9,8},{11,10},{13,12},{15,14},{16,17},{18,... | collective-permute-start | bytes 3145736 | tf_op jit(solution)/shard_map/ppermute | solution.py:341
  127.8 1.2 copy-done.9
  129.0 3.1 %place.6.refs_3_ = f32[2,2,128,2048]{3,2,1,0:T(8,128)} custom-call(s32[1]{0:T(128)} %bitcast.6.mine_ref, s32[1]{0:T(128)} %bitcast.7.spot_ref, bf16[256,2048]{1,0:T(8,128)(2,1)S(1)} %copy-done.9, f32[2,2,128,2048]{3,2,1,0:T(8,128)} %get-tuple-element.55.refs_1_), custom_call_target="tpu_custom_call", output_to_operand_aliasing={{}: (3, {})} | custom-call | flops 1 | bytes 1 | tf_op jit(solution)/shard_map/place/pallas_call | solution.py:265
  132.1 1.1 cut.4
  133.1 0.5 collective-permute-start.10
  133.7 1.7 collective-permute-done.9.refs_1_
  135.4 0.7 collective-permute-done.10.refs_2_
  136.1 14.5 %multiply.7 = (f32[2,2,128,2048]{3,2,1,0:T(8,128)}, bf16[128,2048]{1,0:T(8,128)(2,1)S(1)}) custom-call(s32[1]{0:T(128)} %bitcast.mine_ref, s32[1]{0:T(128)} %bitcast.1.spot_ref, s32[1]{0:T(128)} %bitcast.2.core_ref, bf16[64,8192]{1,0:T(8,128)(2,1)S(1)} %collective-permute-done.8.whole_ref.refs_0_, ...), custom_call_target="tpu_custom_call", output_to_operand_aliasing={{0}: (6, {})} | custom-call | flops 1 | bytes 1 | tf_op jit(solution)/shard_map/multiply/pallas_call | solution.py:202
  150.7 1.3 collective-permute-start.17
  152.0 0.3 collective-permute-done.7.whole_ref.refs_0_
  152.3 0.1 cut.5
  152.4 0.1 collective-permute-start.12
  152.5 0.5 collective-permute-start.13
  153.0 0.1 collective-permute-start.14
  153.0 0.4 collective-permute-start.15
  153.5 0.5 collective-permute-done.12.refs_1_
  154.0 0.4 collective-permute-done.13.refs_2_
  154.4 0.4 collective-permute-done.14.refs_3_
  154.7 0.4 collective-permute-done.15.refs_4_
  155.1 9.2 %multiply.8 = (f32[2,2,128,2048]{3,2,1,0:T(8,128)}, bf16[128,1280]{1,0:T(8,128)(2,1)S(1)}) custom-call(s32[1]{0:T(128)} %bitcast.mine_ref, s32[1]{0:T(128)} %bitcast.1.spot_ref, s32[1]{0:T(128)} %bitcast.2.core_ref, bf16[64,8192]{1,0:T(8,128)(2,1)S(1)} %collective-permute-done.7.whole_ref.refs_0_, ...), custom_call_target="tpu_custom_call", output_to_operand_aliasing={{0}: (8, {})} | custom-call | flops 1 | bytes 1 | tf_op jit(solution)/shard_map/multiply/pallas_call | solution.py:202
  164.3 3.1 %collective-permute-start.16 = (bf16[128,1280]{1,0:T(8,128)(2,1)S(1)}, bf16[128,1280]{1,0:T(8,128)(2,1)S(1)}, u32[]{:S(2)}, u32[]{:S(2)}) collective-permute-start(bf16[128,1280]{1,0:T(8,128)(2,1)S(1)} %get-tuple-element.66), channel_id=1, source_target_pairs={{0,1},{2,3},{5,4},{7,6},{8,9},{10,11},{13,12},{15,14},{16,17},{18,... | collective-permute-start | bytes 983048 | tf_op jit(solution)/shard_map/ppermute | solution.py:341
  167.4 6.4 %multiply.9 = (f32[2,2,128,2048]{3,2,1,0:T(8,128)}, bf16[128,768]{1,0:T(8,128)(2,1)S(1)}) custom-call(s32[1]{0:T(128)} %bitcast.mine_ref, s32[1]{0:T(128)} %bitcast.1.spot_ref, s32[1]{0:T(128)} %bitcast.2.core_ref, bf16[64,8192]{1,0:T(8,128)(2,1)S(1)} %collective-permute-done.7.whole_ref.refs_0_, ...), custom_call_target="tpu_custom_call", output_to_operand_aliasing={{0}: (8, {})} | custom-call | flops 1 | bytes 1 | tf_op jit(solution)/shard_map/multiply/pallas_call | solution.py:202
  173.8 1.9 %collective-permute-start.18 = (bf16[128,768]{1,0:T(8,128)(2,1)S(1)}, bf16[128,768]{1,0:T(8,128)(2,1)S(1)}, u32[]{:S(2)}, u32[]{:S(2)}) collective-permute-start(bf16[128,768]{1,0:T(8,128)(2,1)S(1)} %get-tuple-element.69), channel_id=1, source_target_pairs={{0,1},{2,3},{5,4},{7,6},{8,9},{10,11},{13,12},{15,14},{16,17},{18,... | collective-permute-start | bytes 589832 | tf_op jit(solution)/shard_map/ppermute | solution.py:341
  175.9 4.3 %collective-permute-done.18.refs_1_ = bf16[128,768]{1,0:T(8,128)(2,1)S(1)} collective-permute-done((bf16[128,768]{1,0:T(8,128)(2,1)S(1)}, bf16[128,768]{1,0:T(8,128)(2,1)S(1)}, u32[]{:S(2)}, u32[]{:S(2)}) %collective-permute-start.18) | collective-permute-done | bytes 196640 | tf_op jit(solution)/shard_map/ppermute | solution.py:341
  (27 shorter events, 0.2 us)
Async XLA Ops:
  0.0 5.4 %collective-permute-start = (bf16[128,8192]{1,0:T(8,128)(2,1)}, bf16[128,8192]{1,0:T(8,128)(2,1)S(1)}, u32[]{:S(2)}, u32[]{:S(2)}) collective-permute-start(bf16[128,8192]{1,0:T(8,128)(2,1)} %whole_ref), channel_id=1, source_target_pairs={{0,2},{2,0},{4,6},{6,4},{8,10},{10,8},{12,14},{14,12},{1,3},{3,1},... | collective-permute-start | bytes 6291464 | tf_op jit(solution)/shard_map/ppermute | solution.py:332
  0.5 49.5 %collective-permute-start.1 = (bf16[128,8192]{1,0:T(8,128)(2,1)}, bf16[128,8192]{1,0:T(8,128)(2,1)}, u32[]{:S(2)}, u32[]{:S(2)}) collective-permute-start(bf16[128,8192]{1,0:T(8,128)(2,1)} %whole_ref), channel_id=1, source_target_pairs={{0,8},{2,10},{8,12},{10,14},{12,4},{14,6},{4,0},{6,2},{1,9},{3,11}... | collective-permute-start | bytes 6291464 | tf_op jit(solution)/shard_map/ppermute | solution.py:328
  5.4 1.6 copy-start
  7.0 0.8 copy-start.6
  7.8 48.2 %copy-start.7 = (f32[8192]{0:T(1024)S(1)}, f32[8192]{0:T(1024)}, u32[]{:S(2)}) copy-start(f32[8192]{0:T(1024)} %param.7) | copy-start | bytes 98308
  36.9 1.3 copy-start.4
  38.2 1.0 copy-start.10
  49.9 4.7 %collective-permute-start.3 = (bf16[128,8192]{1,0:T(8,128)(2,1)}, bf16[128,8192]{1,0:T(8,128)(2,1)S(1)}, u32[]{:S(2)}, u32[]{:S(2)}) collective-permute-start(bf16[128,8192]{1,0:T(8,128)(2,1)} %collective-permute-done.1.refs_0_), channel_id=1, source_target_pairs={{0,2},{2,0},{4,6},{6,4},{8,10},{10,8},{12,14},{14,12},{1,3},{3,1},... | collective-permute-start | bytes 6291464 | tf_op jit(solution)/shard_map/ppermute | solution.py:332
  49.9 49.3 %collective-permute-start.2 = (bf16[128,8192]{1,0:T(8,128)(2,1)}, bf16[128,8192]{1,0:T(8,128)(2,1)}, u32[]{:S(2)}, u32[]{:S(2)}) collective-permute-start(bf16[128,8192]{1,0:T(8,128)(2,1)} %collective-permute-done.1.refs_0_), channel_id=1, source_target_pairs={{0,8},{2,10},{8,12},{10,14},{12,4},{14,6},{4,0},{6,2},{1,9},{3,11}... | collective-permute-start | bytes 6291464 | tf_op jit(solution)/shard_map/ppermute | solution.py:328
  53.3 28.2 %collective-permute-start.4 = (bf16[256,2048]{1,0:T(8,128)(2,1)}, bf16[256,2048]{1,0:T(8,128)(2,1)}, u32[]{:S(2)}, u32[]{:S(2)}) collective-permute-start(bf16[256,2048]{1,0:T(8,128)(2,1)} %copy-done.10), channel_id=1, source_target_pairs={{1,0},{3,2},{5,4},{7,6},{8,9},{10,11},{12,13},{14,15},{17,16},{19,... | collective-permute-start | bytes 3145736 | tf_op jit(solution)/shard_map/ppermute | solution.py:341
  54.6 1.3 copy-start.2
  55.9 1.6 copy-start.3
  57.5 17.5 %copy-start.1 = (bf16[128,8192]{1,0:T(8,128)(2,1)S(1)}, bf16[128,8192]{1,0:T(8,128)(2,1)}, u32[]{:S(2)}) copy-start(bf16[128,8192]{1,0:T(8,128)(2,1)} %whole_ref) | copy-start | bytes 6291460
  73.7 29.4 %collective-permute-start.5 = (bf16[256,2048]{1,0:T(8,128)(2,1)}, bf16[256,2048]{1,0:T(8,128)(2,1)S(1)}, u32[]{:S(2)}, u32[]{:S(2)}) collective-permute-start(bf16[256,2048]{1,0:T(8,128)(2,1)} %get-tuple-element.44), channel_id=1, source_target_pairs={{1,0},{3,2},{4,5},{6,7},{9,8},{11,10},{12,13},{14,15},{17,16},{19,... | collective-permute-start | bytes 3145736 | tf_op jit(solution)/shard_map/ppermute | solution.py:341
  81.5 1.6 copy-start.5
  103.2 21.1 %copy-start.8 = (bf16[256,2048]{1,0:T(8,128)(2,1)}, bf16[256,2048]{1,0:T(8,128)(2,1)S(1)}, u32[]{:S(2)}) copy-start(bf16[256,2048]{1,0:T(8,128)(2,1)S(1)} %collective-permute-done.5.refs_0_) | copy-start | bytes 3145732
  103.2 4.5 %collective-permute-start.6 = (bf16[128,8192]{1,0:T(8,128)(2,1)}, bf16[128,8192]{1,0:T(8,128)(2,1)}, u32[]{:S(2)}, u32[]{:S(2)}) collective-permute-start(bf16[128,8192]{1,0:T(8,128)(2,1)} %collective-permute-done.2.refs_0_), channel_id=1, source_target_pairs={{0,2},{2,0},{4,6},{6,4},{8,10},{10,8},{12,14},{14,12},{1,3},{3,1},... | collective-permute-start | bytes 6291464 | tf_op jit(solution)/shard_map/ppermute | solution.py:332
  103.2 28.9 %collective-permute-start.8 = (bf16[64,8192]{1,0:T(8,128)(2,1)}, bf16[64,8192]{1,0:T(8,128)(2,1)S(1)}, u32[]{:S(2)}, u32[]{:S(2)}) collective-permute-start(bf16[64,8192]{1,0:T(8,128)(2,1)} %get-tuple-element.53), channel_id=1, source_target_pairs={{0,4},{2,6},{8,0},{10,2},{12,8},{14,10},{4,12},{6,14},{1,5},{3,7},... | collective-permute-start | bytes 3145736 | tf_op jit(solution)/shard_map/ppermute | solution.py:328
  124.2 28.1 %collective-permute-start.7 = (bf16[64,8192]{1,0:T(8,128)(2,1)}, bf16[64,8192]{1,0:T(8,128)(2,1)S(1)}, u32[]{:S(2)}, u32[]{:S(2)}) collective-permute-start(bf16[64,8192]{1,0:T(8,128)(2,1)} %get-tuple-element.52), channel_id=1, source_target_pairs={{0,4},{2,6},{8,0},{10,2},{12,8},{14,10},{4,12},{6,14},{1,5},{3,7},... | collective-permute-start | bytes 3145736 | tf_op jit(solution)/shard_map/ppermute | solution.py:328
  124.3 28.0 %collective-permute-start.11 = (bf16[256,2048]{1,0:T(8,128)(2,1)}, bf16[256,2048]{1,0:T(8,128)(2,1)S(1)}, u32[]{:S(2)}, u32[]{:S(2)}) collective-permute-start(bf16[256,2048]{1,0:T(8,128)(2,1)} %get-tuple-element.51), channel_id=1, source_target_pairs={{0,1},{2,3},{4,5},{6,7},{9,8},{11,10},{13,12},{15,14},{16,17},{18,... | collective-permute-start | bytes 3145736 | tf_op jit(solution)/shard_map/ppermute | solution.py:341
  127.8 1.2 copy-start.9
  133.1 2.3 %collective-permute-start.9 = (bf16[32,8192]{1,0:T(8,128)(2,1)}, bf16[32,8192]{1,0:T(8,128)(2,1)}, u32[]{:S(2)}, u32[]{:S(2)}) collective-permute-start(bf16[32,8192]{1,0:T(8,128)(2,1)} %get-tuple-element.57), channel_id=1, source_target_pairs={{0,2},{2,0},{4,6},{6,4},{8,10},{10,8},{12,14},{14,12},{1,3},{3,1},... | collective-permute-start | bytes 1572872 | tf_op jit(solution)/shard_map/ppermute | solution.py:332
  133.1 3.0 %collective-permute-start.10 = (bf16[32,8192]{1,0:T(8,128)(2,1)}, bf16[32,8192]{1,0:T(8,128)(2,1)}, u32[]{:S(2)}, u32[]{:S(2)}) collective-permute-start(bf16[32,8192]{1,0:T(8,128)(2,1)} %get-tuple-element.58), channel_id=1, source_target_pairs={{0,2},{2,0},{4,6},{6,4},{8,10},{10,8},{12,14},{14,12},{1,3},{3,1},... | collective-permute-start | bytes 1572872 | tf_op jit(solution)/shard_map/ppermute | solution.py:332
  150.7 16.7 %collective-permute-start.17 = (bf16[128,2048]{1,0:T(8,128)(2,1)S(1)}, bf16[128,2048]{1,0:T(8,128)(2,1)S(1)}, u32[]{:S(2)}, u32[]{:S(2)}) collective-permute-start(bf16[128,2048]{1,0:T(8,128)(2,1)S(1)} %get-tuple-element.59), channel_id=1, source_target_pairs={{0,1},{2,3},{5,4},{7,6},{8,9},{10,11},{13,12},{15,14},{16,17},{18,... | collective-permute-start | bytes 1572872 | tf_op jit(solution)/shard_map/ppermute | solution.py:341
  152.4 1.6 collective-permute-start.12
  152.5 1.9 %collective-permute-start.13 = (bf16[16,8192]{1,0:T(8,128)(2,1)S(1)}, bf16[16,8192]{1,0:T(8,128)(2,1)S(1)}, u32[]{:S(2)}, u32[]{:S(2)}) collective-permute-start(bf16[16,8192]{1,0:T(8,128)(2,1)S(1)} %get-tuple-element.62), channel_id=1, source_target_pairs={{0,2},{2,0},{4,6},{6,4},{8,10},{10,8},{12,14},{14,12},{1,3},{3,1},... | collective-permute-start | bytes 786440 | tf_op jit(solution)/shard_map/ppermute | solution.py:332
  153.0 1.8 collective-permute-start.14
  153.0 2.1 %collective-permute-start.15 = (bf16[16,8192]{1,0:T(8,128)(2,1)S(1)}, bf16[16,8192]{1,0:T(8,128)(2,1)S(1)}, u32[]{:S(2)}, u32[]{:S(2)}) collective-permute-start(bf16[16,8192]{1,0:T(8,128)(2,1)S(1)} %get-tuple-element.64), channel_id=1, source_target_pairs={{0,2},{2,0},{4,6},{6,4},{8,10},{10,8},{12,14},{14,12},{1,3},{3,1},... | collective-permute-start | bytes 786440 | tf_op jit(solution)/shard_map/ppermute | solution.py:332
  164.3 15.9 %collective-permute-start.16 = (bf16[128,1280]{1,0:T(8,128)(2,1)S(1)}, bf16[128,1280]{1,0:T(8,128)(2,1)S(1)}, u32[]{:S(2)}, u32[]{:S(2)}) collective-permute-start(bf16[128,1280]{1,0:T(8,128)(2,1)S(1)} %get-tuple-element.66), channel_id=1, source_target_pairs={{0,1},{2,3},{5,4},{7,6},{8,9},{10,11},{13,12},{15,14},{16,17},{18,... | collective-permute-start | bytes 983048 | tf_op jit(solution)/shard_map/ppermute | solution.py:341
  173.8 6.3 %collective-permute-start.18 = (bf16[128,768]{1,0:T(8,128)(2,1)S(1)}, bf16[128,768]{1,0:T(8,128)(2,1)S(1)}, u32[]{:S(2)}, u32[]{:S(2)}) collective-permute-start(bf16[128,768]{1,0:T(8,128)(2,1)S(1)} %get-tuple-element.69), channel_id=1, source_target_pairs={{0,1},{2,3},{5,4},{7,6},{8,9},{10,11},{13,12},{15,14},{16,17},{18,... | collective-permute-start | bytes 589832 | tf_op jit(solution)/shard_map/ppermute | solution.py:341
